TPU v7x, 32 devices: a whole 2x2x4 slice. The times are simulated.
32 devices in a mesh: hst: 8 (over z, y), local: 4 (over x, core).
Axes of the slice: x: 2, y: 2, z: 4, core: 2. Of those that a mesh axis runs over, the one named last changes fastest.
Arguments:
- grads: bfloat16 [8, 4, 16, 49152], P('hst', 'local'), may hold values from -0.29882812 to 0.29882812
- master: float32 [16, 49152], P('local', 'hst'), may hold values from -3 to 3
- moment_one: float32 [16, 49152], P('local', 'hst'), may hold values from -3 to 3
- moment_two: float32 [16, 49152], P('local', 'hst'), may hold values from 0.01 to 2
Outputs:
- grad_total: float32 [16, 49152], P('local', 'hst')
- new_master: float32 [16, 49152], P('local', 'hst')
- new_one: float32 [16, 49152], P('local', 'hst')
- new_two: float32 [16, 49152], P('local', 'hst')
- secondary: bfloat16 [16, 49152], P('local')
All inputs are finite; a program needn't handle non-finite values.
Results may differ from a plain program's by a relative error of at most 0.001.
Values may be sent and summed in bfloat16 or wider, within the bound.
No kernel may reach another device: no remote copies, remote signals or barrier semaphores. Data moves between devices by JAX's collectives and lax.ppermute only.
A program may use at most 64 MiB of HBM per device.

v0:
```python
import jax
import jax.numpy as jnp
from jax import lax
from jax.sharding import PartitionSpec as P

beta_one = 0.9
beta_two = 0.95
learn_rate = 0.02
decay_rate = 0.1
epsilon = 1e-08
correct_one = 1.0 - (0.9**50) ** 2
correct_two = 1.0 - (0.95**50) ** 2


def local(grads, master, moment_one, moment_two):
    local_count = lax.axis_size("local")
    host_count = lax.axis_size("hst")
    gradient = grads[0, 0]
    total_rows = gradient.shape[0]
    total_cols = gradient.shape[1]
    row_block = total_rows // local_count
    col_block = total_cols // host_count
    pieces = lax.all_to_all(
        gradient.reshape(local_count, row_block, total_cols),
        "local",
        split_axis=0,
        concat_axis=0,
        tiled=True,
    )
    partial_sum = jnp.sum(pieces.astype(jnp.float32), axis=0)
    arrived = lax.all_to_all(
        partial_sum.reshape(row_block, host_count, col_block),
        "hst",
        split_axis=1,
        concat_axis=1,
        tiled=True,
    )
    grad_total = jnp.sum(arrived, axis=1)
    new_one = beta_one * moment_one + (1.0 - beta_one) * grad_total
    new_two = beta_two * moment_two + (1.0 - beta_two) * grad_total * grad_total
    update = new_one / correct_one / (jnp.sqrt(new_two / correct_two) + epsilon)
    new_master = master - learn_rate * (update + decay_rate * master)
    secondary = lax.all_gather(new_master.astype(jnp.bfloat16), "hst", axis=1, tiled=True)
    return (grad_total, new_master, new_one, new_two, secondary)


def solution(mesh):
    return jax.shard_map(
        local,
        mesh=mesh,
        in_specs=(
            P("hst", "local", None, None),
            P("local", "hst"),
            P("local", "hst"),
            P("local", "hst"),
        ),
        out_specs=(
            P("local", "hst"),
            P("local", "hst"),
            P("local", "hst"),
            P("local", "hst"),
            P("local", None),
        ),
        check_vma=False,
    )
```

profile of v0, /device:TPU:0, one launch (start us, length us, event | category | flops | bytes accessed | tf_op | source)
XLA Modules:
  0.0 85.8 jit_solution(3247194534327098498)
XLA Ops:
  0.6 1.7 %reshape_squeeze.3 = bf16[4,4,49152]{2,1,0:T(4,128)(2,1)S(1)} reshape(bf16[1,1,16,49152]{3,2,1,0:T(8,128)(2,1)} %param.4) | data formatting | bytes 3145728 | tf_op jit(solution)/shard_map/reshape;squeeze | solution.py:24
  2.4 24.1 %all_to_all.10 = bf16[4,4,49152]{2,1,0:T(4,128)(2,1)S(1)} all-to-all(bf16[4,4,49152]{2,1,0:T(4,128)(2,1)S(1)} %reshape_squeeze.3), channel_id=1, replica_groups=mesh['hst'=8,'local'=4] {'local'}, dimensions={0} | all-to-all | bytes 3145728 | tf_op jit(solution)/shard_map/all_to_all | solution.py:23
  26.5 0.8 convert_reduce_fusion
  27.3 0.0 copy-start.1
  27.3 0.0 copy-start.2
  27.3 0.0 copy-start.3
  27.3 25.5 %all_to_all.11 = f32[4,8,6144]{2,0,1:T(4,128)S(1)} all-to-all(f32[4,8,6144]{2,0,1:T(4,128)S(1)} %bitcast.3), channel_id=1, replica_groups=mesh['hst'=8,'local'=4] {'hst'}, dimensions={1} | all-to-all | bytes 1572864 | tf_op jit(solution)/shard_map/all_to_all | solution.py:31
  52.8 0.1 reduce_sum.19
  53.0 0.0 copy-done.1
  53.0 0.0 copy-done.2
  53.0 0.0 copy-done.3
  53.0 0.0 copy-start
  53.0 0.9 %fusion.1 = (bf16[4,6144]{1,0:T(4,128)(2,1)S(1)}, f32[4,6144]{1,0:T(4,128)}, f32[4,6144]{1,0:T(4,128)}, f32[4,6144]{1,0:T(4,128)}) fusion(f32[4,6144]{1,0:T(4,128)S(1)} %copy-done.1, f32[4,6144]{1,0:T(4,128)S(1)} %reduce_sum.19, f32[4,6144]{1,0:T(4,128)S(1)} %copy-done.2, f32[4,6144]{1,0:T(4,128)S(1)} %copy-done.3), kind=kLoop, calls=%fused_computation.5 | loop fusion | flops 393216 | bytes 737280 | tf_op jit(solution)/shard_map/convert_element_type | solution.py:43
  53.9 31.2 %all_gather.3 = bf16[4,49152]{1,0:T(4,128)(2,1)S(1)} all-gather(bf16[4,6144]{1,0:T(4,128)(2,1)S(1)} %get-tuple-element.5), channel_id=1, replica_groups=mesh['hst'=8,'local'=4] {'hst'}, dimensions={1}, use_global_device_ids=true | all-gather | bytes 442368 | tf_op jit(solution)/shard_map/all_gather | solution.py:43
  85.1 0.7 copy.10
  85.8 0.0 copy-done
Async XLA Ops:
  27.3 25.7 %copy-start.1 = (f32[4,6144]{1,0:T(4,128)S(1)}, f32[4,6144]{1,0:T(4,128)}, u32[]{:S(2)}) copy-start(f32[4,6144]{1,0:T(4,128)} %param.5) | copy-start | bytes 294916
  27.3 25.7 %copy-start.2 = (f32[4,6144]{1,0:T(4,128)S(1)}, f32[4,6144]{1,0:T(4,128)}, u32[]{:S(2)}) copy-start(f32[4,6144]{1,0:T(4,128)} %param.6) | copy-start | bytes 294916
  27.3 25.7 %copy-start.3 = (f32[4,6144]{1,0:T(4,128)S(1)}, f32[4,6144]{1,0:T(4,128)}, u32[]{:S(2)}) copy-start(f32[4,6144]{1,0:T(4,128)} %param.7) | copy-start | bytes 294916
  53.0 32.8 %copy-start = (f32[4,6144]{1,0:T(4,128)}, f32[4,6144]{1,0:T(4,128)S(1)}, u32[]{:S(2)}) copy-start(f32[4,6144]{1,0:T(4,128)S(1)} %reduce_sum.19) | copy-start | bytes 294916
where the time goes:
time: 86 us; the launch traced here: 85.8 us
  blocking collectives  80.8 us (94%)
  local copies, waits for them, and re-layouts  2.5 us (3%)
  other arithmetic  1.79 us (2%)
    all_gather x1, blocking collectives, local(): lax.all_gather(new_master.astype(jnp.bfloat16), 'hst', axis=1, tiled=True)  31.2 us
    all_to_all x1, blocking collectives, local(): lax.all_to_all(partial_sum.reshape(row_block, host_count, col_block), 'hs...  25.5 us
    all_to_all x1, blocking collectives, local(): lax.all_to_all(gradient.reshape(local_count, row_block, total_cols), 'loc...  24.1 us
    another operation x1, local copies, waits for them, and re-layouts, local(): gradient.reshape(local_count, row_block, total_cols)  1.73 us

commit v1 on v0

--- a/solution.py
+++ b/solution.py
@@ -12,6 +12,15 @@
 correct_two = 1.0 - (0.95**50) ** 2
 
 
+def exchange(axis, count, make):
+    me = lax.axis_index(axis)
+    got = [make(me)]
+    for step in range(1, count):
+        pairs = [(i, i ^ step) for i in range(count)]
+        got.append(lax.ppermute(make(me ^ step), axis, pairs))
+    return got
+
+
 def local(grads, master, moment_one, moment_two):
     local_count = lax.axis_size("local")
     host_count = lax.axis_size("hst")
@@ -20,27 +29,40 @@
     total_cols = gradient.shape[1]
     row_block = total_rows // local_count
     col_block = total_cols // host_count
-    pieces = lax.all_to_all(
-        gradient.reshape(local_count, row_block, total_cols),
-        "local",
-        split_axis=0,
-        concat_axis=0,
-        tiled=True,
-    )
-    partial_sum = jnp.sum(pieces.astype(jnp.float32), axis=0)
-    arrived = lax.all_to_all(
-        partial_sum.reshape(row_block, host_count, col_block),
-        "hst",
-        split_axis=1,
-        concat_axis=1,
-        tiled=True,
-    )
-    grad_total = jnp.sum(arrived, axis=1)
+    split = gradient.reshape(local_count, row_block, total_cols)
+    pieces = exchange("local", local_count, lambda j: lax.dynamic_index_in_dim(split, j, 0, keepdims=False))
+    partial_sum = sum(p.astype(jnp.float32) for p in pieces)
+    if host_count <= 16:
+        arrived = exchange(
+            "hst",
+            host_count,
+            lambda j: lax.dynamic_slice_in_dim(partial_sum, j * col_block, col_block, 1),
+        )
+        grad_total = sum(arrived)
+    else:
+        arrived = lax.all_to_all(
+            partial_sum.reshape(row_block, host_count, col_block),
+            "hst",
+            split_axis=1,
+            concat_axis=1,
+            tiled=True,
+        )
+        grad_total = jnp.sum(arrived, axis=1)
     new_one = beta_one * moment_one + (1.0 - beta_one) * grad_total
     new_two = beta_two * moment_two + (1.0 - beta_two) * grad_total * grad_total
     update = new_one / correct_one / (jnp.sqrt(new_two / correct_two) + epsilon)
     new_master = master - learn_rate * (update + decay_rate * master)
-    secondary = lax.all_gather(new_master.astype(jnp.bfloat16), "hst", axis=1, tiled=True)
+    mine = new_master.astype(jnp.bfloat16)
+    if host_count <= 16:
+        me = lax.axis_index("hst")
+        secondary = jnp.zeros((row_block, total_cols), jnp.bfloat16)
+        secondary = lax.dynamic_update_slice_in_dim(secondary, mine, me * col_block, 1)
+        for step in range(1, host_count):
+            pairs = [(i, i ^ step) for i in range(host_count)]
+            block = lax.ppermute(mine, "hst", pairs)
+            secondary = lax.dynamic_update_slice_in_dim(secondary, block, (me ^ step) * col_block, 1)
+    else:
+        secondary = lax.all_gather(mine, "hst", axis=1, tiled=True)
     return (grad_total, new_master, new_one, new_two, secondary)
 
 

time: 86 us -> 67.1 us (0.78)
  blocking collectives: 80.8 us -> 0 us
  waiting for transfers between devices: 0 us -> 32.1 us
  starting transfers between devices: 0 us -> 28.5 us
    all_to_all x2 -> x0, blocking collectives: 49.6 us -> none  [the longest x1 25.5 us: local(): lax.all_to_all(partial_sum.reshape(row_block, host_count, col_block), 'hs...]
    ppermute x0 -> x17, waiting for transfers between devices: none -> 32.1 us  [the longest x10 27.8 us: exchange(): got.append(lax.ppermute(make(me ^ step), axis, pairs))]
    all_gather x1 -> x0, blocking collectives: 31.2 us -> none  [local(): lax.all_gather(new_master.astype(jnp.bfloat16), 'hst', axis=1, tiled=True)]
    ppermute x0 -> x17, starting transfers between devices: none -> 28.5 us  [the longest x10 14.4 us: exchange(): got.append(lax.ppermute(make(me ^ step), axis, pairs))]
    add x0 -> x1, other arithmetic: none -> 1.35 us  [local(): partial_sum = sum((p.astype(jnp.float32) for p in pieces))]
    dynamic_update_slice x0 -> x1, other arithmetic: none -> 0.94 us  [local(): lax.dynamic_update_slice_in_dim(secondary, mine, me * col_block, 1)]
    reduce_sum x2 -> x0, other arithmetic: 0.92 us -> none  [the longest x1 0.79 us: local(): partial_sum = jnp.sum(pieces.astype(jnp.float32), axis=0)]
    convert_element_type x1 -> x0, other arithmetic: 0.86 us -> none  [local(): new_master.astype(jnp.bfloat16)]
  transfers between devices with their start and end apart: 0 -> 17, of which waited for: 0 -> 5; matrix products, arithmetic and copies ran while one was open for 0% -> 0% of each run, Pallas kernels for 0% -> 0%
where the time goes in v1:
time: 67.1 us; the launch traced here: 67 us
  waiting for transfers between devices  32.1 us (48%)
  starting transfers between devices  28.5 us (42%)
  local copies, waits for them, and re-layouts  3.28 us (5%)
  other arithmetic  2.3 us (3%)
  between operations  0.79 us (1%)
    ppermute x10, waiting for transfers between devices, exchange(): got.append(lax.ppermute(make(me ^ step), axis, pairs))  27.8 us
    ppermute x10, starting transfers between devices, exchange(): got.append(lax.ppermute(make(me ^ step), axis, pairs))  14.4 us
    ppermute x7, starting transfers between devices, local(): block = lax.ppermute(mine, 'hst', pairs)  14.2 us
    ppermute x7, waiting for transfers between devices, local(): block = lax.ppermute(mine, 'hst', pairs)  4.23 us
    another operation x1, local copies, waits for them, and re-layouts, local(): split = gradient.reshape(local_count, row_block, total_cols)  1.73 us
    add x1, other arithmetic, local(): partial_sum = sum((p.astype(jnp.float32) for p in pieces))  1.35 us
  transfers between devices with their start and end apart: 17, of which 5 were waited for; matrix products, arithmetic and copies ran while one was open for 0% of the time, Pallas kernels for 0%

profile of v1, /device:TPU:0, one launch (start us, length us, event | category | flops | bytes accessed | tf_op | source)
XLA Modules:
  0.0 67.0 jit_solution(8917967194294447625)
XLA Ops:
  0.6 1.7 %reshape_squeeze.3 = bf16[4,4,49152]{2,1,0:T(4,128)(2,1)S(1)} reshape(bf16[1,1,16,49152]{3,2,1,0:T(8,128)(2,1)} %param.4) | data formatting | bytes 3145728 | tf_op jit(solution)/shard_map/reshape;squeeze | solution.py:32
  2.4 0.4 dynamic-slice_bitcast_fusion.2
  2.8 0.5 collective-permute-start
  3.3 2.6 %collective-permute-start.1 = (bf16[4,49152]{1,0:T(4,128)(2,1)S(1)}, bf16[4,49152]{1,0:T(4,128)(2,1)S(1)}, u32[]{:S(2)}, u32[]{:S(2)}) collective-permute-start(bf16[4,49152]{1,0:T(4,128)(2,1)S(1)} %get-tuple-element.13), channel_id=1, source_target_pairs={{0,2},{1,3},{2,0},{3,1},{4,6},{5,7},{6,4},{7,5},{8,10},{9,11},{10,... | collective-permute-start | bytes 1179656 | tf_op jit(solution)/shard_map/ppermute | solution.py:20
  5.9 0.1 collective-permute-start.2
  6.0 9.9 %collective-permute-done.1 = bf16[4,49152]{1,0:T(4,128)(2,1)S(1)} collective-permute-done((bf16[4,49152]{1,0:T(4,128)(2,1)S(1)}, bf16[4,49152]{1,0:T(4,128)(2,1)S(1)}, u32[]{:S(2)}, u32[]{:S(2)}) %collective-permute-start.1) | collective-permute-done | bytes 393248 | tf_op jit(solution)/shard_map/ppermute | solution.py:20
  15.9 8.0 %collective-permute-done.2 = bf16[4,49152]{1,0:T(4,128)(2,1)} collective-permute-done((bf16[4,49152]{1,0:T(4,128)(2,1)S(1)}, bf16[4,49152]{1,0:T(4,128)(2,1)}, u32[]{:S(2)}, u32[]{:S(2)}) %collective-permute-start.2) | collective-permute-done | bytes 393248 | tf_op jit(solution)/shard_map/ppermute | solution.py:20
  23.9 1.4 %fusion.1 = f32[4,49152]{1,0:T(4,128)S(1)} fusion(bf16[4,49152]{1,0:T(4,128)(2,1)} %collective-permute-done.2, bf16[4,49152]{1,0:T(4,128)(2,1)S(1)} %collective-permute-done.1, bf16[4,49152]{1,0:T(4,128)(2,1)S(1)} %collective-permute-done, bf16[4,4,49152]{2,1,0:T(4,128)(2,1)S(1)} %reshape_squeeze.3, s32[]{:T(128)S(6)} %select_n.45), kind=kLoop, calls=%fused_computation.2 | loop fusion | flops 1376256 | bytes 2359300 | tf_op jit(solution)/shard_map/add | solution.py:34
  25.2 0.1 constant_dynamic-slice_fusion.6
  25.3 1.7 %collective-permute-start.3 = (f32[4,6144]{1,0:T(4,128)S(1)}, f32[4,6144]{1,0:T(4,128)S(1)}, u32[]{:S(2)}, u32[]{:S(2)}) collective-permute-start(f32[4,6144]{1,0:T(4,128)S(1)} %get-tuple-element.14), channel_id=1, source_target_pairs={{0,4},{4,0},{8,12},{12,8},{16,20},{20,16},{24,28},{28,24},{1,5},{5... | collective-permute-start | bytes 294920 | tf_op jit(solution)/shard_map/ppermute | solution.py:20
  27.0 1.6 %collective-permute-start.4 = (f32[4,6144]{1,0:T(4,128)S(1)}, f32[4,6144]{1,0:T(4,128)S(1)}, u32[]{:S(2)}, u32[]{:S(2)}) collective-permute-start(f32[4,6144]{1,0:T(4,128)S(1)} %get-tuple-element.20), channel_id=1, source_target_pairs={{0,8},{4,12},{8,0},{12,4},{16,24},{20,28},{24,16},{28,20},{1,9},{5... | collective-permute-start | bytes 294920 | tf_op jit(solution)/shard_map/ppermute | solution.py:20
  28.5 0.3 collective-permute-start.5
  28.9 2.7 %collective-permute-start.6 = (f32[4,6144]{1,0:T(4,128)S(1)}, f32[4,6144]{1,0:T(4,128)S(1)}, u32[]{:S(2)}, u32[]{:S(2)}) collective-permute-start(f32[4,6144]{1,0:T(4,128)S(1)} %get-tuple-element.18), channel_id=1, source_target_pairs={{0,16},{4,20},{8,24},{12,28},{16,0},{20,4},{24,8},{28,12},{1,17},{... | collective-permute-start | bytes 294920 | tf_op jit(solution)/shard_map/ppermute | solution.py:20
  31.5 1.3 %collective-permute-start.7 = (f32[4,6144]{1,0:T(4,128)S(1)}, f32[4,6144]{1,0:T(4,128)S(1)}, u32[]{:S(2)}, u32[]{:S(2)}) collective-permute-start(f32[4,6144]{1,0:T(4,128)S(1)} %get-tuple-element.17), channel_id=1, source_target_pairs={{0,20},{4,16},{8,28},{12,24},{16,4},{20,0},{24,12},{28,8},{1,21},{... | collective-permute-start | bytes 294920 | tf_op jit(solution)/shard_map/ppermute | solution.py:20
  32.8 0.0 collective-permute-done.3
  32.8 3.6 %collective-permute-start.8 = (f32[4,6144]{1,0:T(4,128)S(1)}, f32[4,6144]{1,0:T(4,128)S(1)}, u32[]{:S(2)}, u32[]{:S(2)}) collective-permute-start(f32[4,6144]{1,0:T(4,128)S(1)} %get-tuple-element.16), channel_id=1, source_target_pairs={{0,24},{4,28},{8,16},{12,20},{16,8},{20,12},{24,0},{28,4},{1,25},{... | collective-permute-start | bytes 294920 | tf_op jit(solution)/shard_map/ppermute | solution.py:20
  36.4 0.1 collective-permute-start.9
  36.5 0.0 collective-permute-done.5
  36.5 0.0 collective-permute-done.6
  36.5 9.9 %collective-permute-done.7 = f32[4,6144]{1,0:T(4,128)S(1)} collective-permute-done((f32[4,6144]{1,0:T(4,128)S(1)}, f32[4,6144]{1,0:T(4,128)S(1)}, u32[]{:S(2)}, u32[]{:S(2)}) %collective-permute-start.7) | collective-permute-done | bytes 98336 | tf_op jit(solution)/shard_map/ppermute | solution.py:20
  46.5 0.1 broadcast_in_dim.3
  46.6 0.9 %constant_dynamic-update-slice_fusion.7 = (bf16[4,49152]{1,0:T(4,128)(2,1)S(1)}, bf16[4,6144]{1,0:T(4,128)(2,1)S(1)}, f32[4,6144]{1,0:T(4,128)}, f32[4,6144]{1,0...) fusion(bf16[4,49152]{1,0:T(4,128)(2,1)S(1)} %broadcast_in_dim.3, s32[]{:T(128)S(6)} %select_n.49, ...), kind=kLoop, calls=%fused_computation.18 | loop fusion | flops 565248 | bytes 1572868 | tf_op jit(solution)/shard_map/dynamic_update_slice | solution.py:59
  47.6 1.5 %collective-permute-start.10 = (bf16[4,6144]{1,0:T(4,128)(2,1)S(1)}, bf16[4,6144]{1,0:T(4,128)(2,1)S(1)}, u32[]{:S(2)}, u32[]{:S(2)}) collective-permute-start(bf16[4,6144]{1,0:T(4,128)(2,1)S(1)} %get-tuple-element.6), channel_id=1, source_target_pairs={{0,4},{4,0},{8,12},{12,8},{16,20},{20,16},{24,28},{28,24},{1,5},{5... | collective-permute-start | bytes 147464 | tf_op jit(solution)/shard_map/ppermute | solution.py:62
  49.0 3.8 %collective-permute-start.11 = (bf16[4,6144]{1,0:T(4,128)(2,1)S(1)}, bf16[4,6144]{1,0:T(4,128)(2,1)S(1)}, u32[]{:S(2)}, u32[]{:S(2)}) collective-permute-start(bf16[4,6144]{1,0:T(4,128)(2,1)S(1)} %get-tuple-element.6), channel_id=1, source_target_pairs={{0,8},{4,12},{8,0},{12,4},{16,24},{20,28},{24,16},{28,20},{1,9},{5... | collective-permute-start | bytes 147464 | tf_op jit(solution)/shard_map/ppermute | solution.py:62
  52.9 0.4 collective-permute-start.12
  53.3 3.7 %collective-permute-start.13 = (bf16[4,6144]{1,0:T(4,128)(2,1)S(1)}, bf16[4,6144]{1,0:T(4,128)(2,1)S(1)}, u32[]{:S(2)}, u32[]{:S(2)}) collective-permute-start(bf16[4,6144]{1,0:T(4,128)(2,1)S(1)} %get-tuple-element.6), channel_id=1, source_target_pairs={{0,16},{4,20},{8,24},{12,28},{16,0},{20,4},{24,8},{28,12},{1,17},{... | collective-permute-start | bytes 147464 | tf_op jit(solution)/shard_map/ppermute | solution.py:62
  56.9 2.4 %collective-permute-start.15 = (bf16[4,6144]{1,0:T(4,128)(2,1)S(1)}, bf16[4,6144]{1,0:T(4,128)(2,1)S(1)}, u32[]{:S(2)}, u32[]{:S(2)}) collective-permute-start(bf16[4,6144]{1,0:T(4,128)(2,1)S(1)} %get-tuple-element.6), channel_id=1, source_target_pairs={{0,24},{4,28},{8,16},{12,20},{16,8},{20,12},{24,0},{28,4},{1,25},{... | collective-permute-start | bytes 147464 | tf_op jit(solution)/shard_map/ppermute | solution.py:62
  59.3 2.4 %collective-permute-start.16 = (bf16[4,6144]{1,0:T(4,128)(2,1)S(1)}, bf16[4,6144]{1,0:T(4,128)(2,1)S(1)}, u32[]{:S(2)}, u32[]{:S(2)}) collective-permute-start(bf16[4,6144]{1,0:T(4,128)(2,1)S(1)} %get-tuple-element.6), channel_id=1, source_target_pairs={{0,28},{4,24},{8,20},{12,16},{16,12},{20,8},{24,4},{28,0},{1,29},{... | collective-permute-start | bytes 147464 | tf_op jit(solution)/shard_map/ppermute | solution.py:62
  61.9 2.6 %collective-permute-done.14 = bf16[4,6144]{1,0:T(4,128)(2,1)S(1)} collective-permute-done((bf16[4,6144]{1,0:T(4,128)(2,1)S(1)}, bf16[4,6144]{1,0:T(4,128)(2,1)S(1)}, u32[]{:S(2)}, u32[]{:S(2)}) %collective-permute-start.14) | collective-permute-done | bytes 49184 | tf_op jit(solution)/shard_map/ppermute | solution.py:62
  64.5 1.7 %collective-permute-done.16 = bf16[4,6144]{1,0:T(4,128)(2,1)S(1)} collective-permute-done((bf16[4,6144]{1,0:T(4,128)(2,1)S(1)}, bf16[4,6144]{1,0:T(4,128)(2,1)S(1)}, u32[]{:S(2)}, u32[]{:S(2)}) %collective-permute-start.16) | collective-permute-done | bytes 49184 | tf_op jit(solution)/shard_map/ppermute | solution.py:62
  66.2 0.0 copy-start
  66.2 0.7 %copy-done = bf16[4,49152]{1,0:T(4,128)(2,1)} copy-done((bf16[4,49152]{1,0:T(4,128)(2,1)}, bf16[4,49152]{1,0:T(4,128)(2,1)S(1)}, u32[]{:S(2)}) %copy-start) | copy-done | bytes 393240
  (23 shorter events, 0.3 us)
Async XLA Ops:
  2.8 3.2 %collective-permute-start = (bf16[4,49152]{1,0:T(4,128)(2,1)S(1)}, bf16[4,49152]{1,0:T(4,128)(2,1)S(1)}, u32[]{:S(2)}, u32[]{:S(2)}) collective-permute-start(bf16[4,49152]{1,0:T(4,128)(2,1)S(1)} %get-tuple-element.11), channel_id=1, source_target_pairs={{0,1},{1,0},{2,3},{3,2},{4,5},{5,4},{6,7},{7,6},{8,9},{9,8},{10,11... | collective-permute-start | bytes 1179656 | tf_op jit(solution)/shard_map/ppermute | solution.py:20
  3.3 12.5 %collective-permute-start.1 = (bf16[4,49152]{1,0:T(4,128)(2,1)S(1)}, bf16[4,49152]{1,0:T(4,128)(2,1)S(1)}, u32[]{:S(2)}, u32[]{:S(2)}) collective-permute-start(bf16[4,49152]{1,0:T(4,128)(2,1)S(1)} %get-tuple-element.13), channel_id=1, source_target_pairs={{0,2},{1,3},{2,0},{3,1},{4,6},{5,7},{6,4},{7,5},{8,10},{9,11},{10,... | collective-permute-start | bytes 1179656 | tf_op jit(solution)/shard_map/ppermute | solution.py:20
  5.9 18.0 %collective-permute-start.2 = (bf16[4,49152]{1,0:T(4,128)(2,1)S(1)}, bf16[4,49152]{1,0:T(4,128)(2,1)}, u32[]{:S(2)}, u32[]{:S(2)}) collective-permute-start(bf16[4,49152]{1,0:T(4,128)(2,1)S(1)} %get-tuple-element.12), channel_id=1, source_target_pairs={{0,3},{1,2},{2,1},{3,0},{4,7},{5,6},{6,5},{7,4},{8,11},{9,10},{10,... | collective-permute-start | bytes 1179656 | tf_op jit(solution)/shard_map/ppermute | solution.py:20
  6.0 40.6 %copy-start.1 = (f32[4,6144]{1,0:T(4,128)S(1)}, f32[4,6144]{1,0:T(4,128)}, u32[]{:S(2)}) copy-start(f32[4,6144]{1,0:T(4,128)} %param.5) | copy-start | bytes 294916
  6.0 40.6 %copy-start.2 = (f32[4,6144]{1,0:T(4,128)S(1)}, f32[4,6144]{1,0:T(4,128)}, u32[]{:S(2)}) copy-start(f32[4,6144]{1,0:T(4,128)} %param.6) | copy-start | bytes 294916
  6.0 40.6 %copy-start.3 = (f32[4,6144]{1,0:T(4,128)S(1)}, f32[4,6144]{1,0:T(4,128)}, u32[]{:S(2)}) copy-start(f32[4,6144]{1,0:T(4,128)} %param.7) | copy-start | bytes 294916
  25.3 7.5 %collective-permute-start.3 = (f32[4,6144]{1,0:T(4,128)S(1)}, f32[4,6144]{1,0:T(4,128)S(1)}, u32[]{:S(2)}, u32[]{:S(2)}) collective-permute-start(f32[4,6144]{1,0:T(4,128)S(1)} %get-tuple-element.14), channel_id=1, source_target_pairs={{0,4},{4,0},{8,12},{12,8},{16,20},{20,16},{24,28},{28,24},{1,5},{5... | collective-permute-start | bytes 294920 | tf_op jit(solution)/shard_map/ppermute | solution.py:20
  27.0 9.5 %collective-permute-start.4 = (f32[4,6144]{1,0:T(4,128)S(1)}, f32[4,6144]{1,0:T(4,128)S(1)}, u32[]{:S(2)}, u32[]{:S(2)}) collective-permute-start(f32[4,6144]{1,0:T(4,128)S(1)} %get-tuple-element.20), channel_id=1, source_target_pairs={{0,8},{4,12},{8,0},{12,4},{16,24},{20,28},{24,16},{28,20},{1,9},{5... | collective-permute-start | bytes 294920 | tf_op jit(solution)/shard_map/ppermute | solution.py:20
  28.5 8.0 %collective-permute-start.5 = (f32[4,6144]{1,0:T(4,128)S(1)}, f32[4,6144]{1,0:T(4,128)S(1)}, u32[]{:S(2)}, u32[]{:S(2)}) collective-permute-start(f32[4,6144]{1,0:T(4,128)S(1)} %get-tuple-element.19), channel_id=1, source_target_pairs={{0,12},{4,8},{8,4},{12,0},{16,28},{20,24},{24,20},{28,16},{1,13},{... | collective-permute-start | bytes 294920 | tf_op jit(solution)/shard_map/ppermute | solution.py:20
  28.9 7.7 %collective-permute-start.6 = (f32[4,6144]{1,0:T(4,128)S(1)}, f32[4,6144]{1,0:T(4,128)S(1)}, u32[]{:S(2)}, u32[]{:S(2)}) collective-permute-start(f32[4,6144]{1,0:T(4,128)S(1)} %get-tuple-element.18), channel_id=1, source_target_pairs={{0,16},{4,20},{8,24},{12,28},{16,0},{20,4},{24,8},{28,12},{1,17},{... | collective-permute-start | bytes 294920 | tf_op jit(solution)/shard_map/ppermute | solution.py:20
  31.5 14.9 %collective-permute-start.7 = (f32[4,6144]{1,0:T(4,128)S(1)}, f32[4,6144]{1,0:T(4,128)S(1)}, u32[]{:S(2)}, u32[]{:S(2)}) collective-permute-start(f32[4,6144]{1,0:T(4,128)S(1)} %get-tuple-element.17), channel_id=1, source_target_pairs={{0,20},{4,16},{8,28},{12,24},{16,4},{20,0},{24,12},{28,8},{1,21},{... | collective-permute-start | bytes 294920 | tf_op jit(solution)/shard_map/ppermute | solution.py:20
  32.8 13.6 %collective-permute-start.8 = (f32[4,6144]{1,0:T(4,128)S(1)}, f32[4,6144]{1,0:T(4,128)S(1)}, u32[]{:S(2)}, u32[]{:S(2)}) collective-permute-start(f32[4,6144]{1,0:T(4,128)S(1)} %get-tuple-element.16), channel_id=1, source_target_pairs={{0,24},{4,28},{8,16},{12,20},{16,8},{20,12},{24,0},{28,4},{1,25},{... | collective-permute-start | bytes 294920 | tf_op jit(solution)/shard_map/ppermute | solution.py:20
  36.4 10.0 %collective-permute-start.9 = (f32[4,6144]{1,0:T(4,128)S(1)}, f32[4,6144]{1,0:T(4,128)S(1)}, u32[]{:S(2)}, u32[]{:S(2)}) collective-permute-start(f32[4,6144]{1,0:T(4,128)S(1)} %get-tuple-element.15), channel_id=1, source_target_pairs={{0,28},{4,24},{8,20},{12,16},{16,12},{20,8},{24,4},{28,0},{1,29},{... | collective-permute-start | bytes 294920 | tf_op jit(solution)/shard_map/ppermute | solution.py:20
  47.6 9.4 %collective-permute-start.10 = (bf16[4,6144]{1,0:T(4,128)(2,1)S(1)}, bf16[4,6144]{1,0:T(4,128)(2,1)S(1)}, u32[]{:S(2)}, u32[]{:S(2)}) collective-permute-start(bf16[4,6144]{1,0:T(4,128)(2,1)S(1)} %get-tuple-element.6), channel_id=1, source_target_pairs={{0,4},{4,0},{8,12},{12,8},{16,20},{20,16},{24,28},{28,24},{1,5},{5... | collective-permute-start | bytes 147464 | tf_op jit(solution)/shard_map/ppermute | solution.py:62
  49.0 10.3 %collective-permute-start.11 = (bf16[4,6144]{1,0:T(4,128)(2,1)S(1)}, bf16[4,6144]{1,0:T(4,128)(2,1)S(1)}, u32[]{:S(2)}, u32[]{:S(2)}) collective-permute-start(bf16[4,6144]{1,0:T(4,128)(2,1)S(1)} %get-tuple-element.6), channel_id=1, source_target_pairs={{0,8},{4,12},{8,0},{12,4},{16,24},{20,28},{24,16},{28,20},{1,9},{5... | collective-permute-start | bytes 147464 | tf_op jit(solution)/shard_map/ppermute | solution.py:62
  52.9 8.9 %collective-permute-start.12 = (bf16[4,6144]{1,0:T(4,128)(2,1)S(1)}, bf16[4,6144]{1,0:T(4,128)(2,1)S(1)}, u32[]{:S(2)}, u32[]{:S(2)}) collective-permute-start(bf16[4,6144]{1,0:T(4,128)(2,1)S(1)} %get-tuple-element.6), channel_id=1, source_target_pairs={{0,12},{4,8},{8,4},{12,0},{16,28},{20,24},{24,20},{28,16},{1,13},{... | collective-permute-start | bytes 147464 | tf_op jit(solution)/shard_map/ppermute | solution.py:62
  53.3 8.6 %collective-permute-start.13 = (bf16[4,6144]{1,0:T(4,128)(2,1)S(1)}, bf16[4,6144]{1,0:T(4,128)(2,1)S(1)}, u32[]{:S(2)}, u32[]{:S(2)}) collective-permute-start(bf16[4,6144]{1,0:T(4,128)(2,1)S(1)} %get-tuple-element.6), channel_id=1, source_target_pairs={{0,16},{4,20},{8,24},{12,28},{16,0},{20,4},{24,8},{28,12},{1,17},{... | collective-permute-start | bytes 147464 | tf_op jit(solution)/shard_map/ppermute | solution.py:62
  56.9 7.5 %collective-permute-start.14 = (bf16[4,6144]{1,0:T(4,128)(2,1)S(1)}, bf16[4,6144]{1,0:T(4,128)(2,1)S(1)}, u32[]{:S(2)}, u32[]{:S(2)}) collective-permute-start(bf16[4,6144]{1,0:T(4,128)(2,1)S(1)} %get-tuple-element.6), channel_id=1, source_target_pairs={{0,20},{4,16},{8,28},{12,24},{16,4},{20,0},{24,12},{28,8},{1,21},{... | collective-permute-start | bytes 147464 | tf_op jit(solution)/shard_map/ppermute | solution.py:62
  56.9 7.5 %collective-permute-start.15 = (bf16[4,6144]{1,0:T(4,128)(2,1)S(1)}, bf16[4,6144]{1,0:T(4,128)(2,1)S(1)}, u32[]{:S(2)}, u32[]{:S(2)}) collective-permute-start(bf16[4,6144]{1,0:T(4,128)(2,1)S(1)} %get-tuple-element.6), channel_id=1, source_target_pairs={{0,24},{4,28},{8,16},{12,20},{16,8},{20,12},{24,0},{28,4},{1,25},{... | collective-permute-start | bytes 147464 | tf_op jit(solution)/shard_map/ppermute | solution.py:62
  59.3 6.9 %collective-permute-start.16 = (bf16[4,6144]{1,0:T(4,128)(2,1)S(1)}, bf16[4,6144]{1,0:T(4,128)(2,1)S(1)}, u32[]{:S(2)}, u32[]{:S(2)}) collective-permute-start(bf16[4,6144]{1,0:T(4,128)(2,1)S(1)} %get-tuple-element.6), channel_id=1, source_target_pairs={{0,28},{4,24},{8,20},{12,16},{16,12},{20,8},{24,4},{28,0},{1,29},{... | collective-permute-start | bytes 147464 | tf_op jit(solution)/shard_map/ppermute | solution.py:62
  66.2 0.7 %copy-start = (bf16[4,49152]{1,0:T(4,128)(2,1)}, bf16[4,49152]{1,0:T(4,128)(2,1)S(1)}, u32[]{:S(2)}) copy-start(bf16[4,49152]{1,0:T(4,128)(2,1)S(1)} %constant_dynamic-update-slice_fusion) | copy-start | bytes 1179652

commit v2 on v0

--- a/solution.py
+++ b/solution.py
@@ -11,17 +11,64 @@
 correct_one = 1.0 - (0.9**50) ** 2
 correct_two = 1.0 - (0.95**50) ** 2
 
+wire_scale = 4096.0
 
-def local(grads, master, moment_one, moment_two):
+
+def swap(value, axis, flip):
+    count = lax.axis_size(axis)
+    return lax.ppermute(value, axis, [(i, i ^ flip) for i in range(count)])
+
+
+def narrow(value):
+    return (value * wire_scale).astype(jnp.float16)
+
+
+def widen(value):
+    return value.astype(jnp.float32) * (1.0 / wire_scale)
+
+
+def pick(value, index, dim):
+    return lax.dynamic_index_in_dim(value, index, dim, keepdims=False)
+
+
+def reduce_blocks(gradient):
+    rows, cols = gradient.shape
+    row_block, col_block = rows // 4, cols // 8
+    me_local, me_host = lax.axis_index("local"), lax.axis_index("hst")
+    x, core = me_local // 2, me_local % 2
+    z, y = me_host // 2, me_host % 2
+
+    other = swap(gradient, "local", 1)
+
+    def mine(g):
+        g = g.reshape(2, 2 * row_block, cols)
+        return jnp.where(core == 0, g[:, :row_block], g[:, row_block:]).astype(jnp.float32)
+
+    pair = (mine(gradient) + mine(other)).reshape(2, row_block, 8, col_block)
+    pair = pair.transpose(0, 2, 1, 3).reshape(2, 2, 2, 2, row_block, col_block)
+    low, high = pair[:, 0], pair[:, 1]
+    low_in = swap(narrow(pick(low, 1 - x, 0)), "local", 2)
+    high_in = swap(narrow(pick(high, 1 - y, 2)), "hst", 1)
+    low = pick(low, x, 0) + widen(low_in)
+    high = pick(high, y, 2) + widen(high_in)
+    low_in = swap(narrow(pick(low, 1 - y, 1)), "hst", 1)
+    high_in = swap(narrow(pick(high, 1 - x, 0)), "local", 2)
+    low = pick(low, y, 1) + widen(low_in)
+    high = pick(high, x, 0) + widen(high_in)
+    blocks = jnp.concatenate([low, high], axis=0)
+    total = pick(blocks, z, 0)
+    for step in (1, 2, 3):
+        total = total + widen(swap(narrow(pick(blocks, z ^ step, 0)), "hst", 2 * step))
+    return total
+
+
+def reduce_general(gradient):
     local_count = lax.axis_size("local")
     host_count = lax.axis_size("hst")
-    gradient = grads[0, 0]
-    total_rows = gradient.shape[0]
-    total_cols = gradient.shape[1]
-    row_block = total_rows // local_count
-    col_block = total_cols // host_count
+    rows, cols = gradient.shape
+    row_block, col_block = rows // local_count, cols // host_count
     pieces = lax.all_to_all(
-        gradient.reshape(local_count, row_block, total_cols),
+        gradient.reshape(local_count, row_block, cols),
         "local",
         split_axis=0,
         concat_axis=0,
@@ -35,12 +82,34 @@
         concat_axis=1,
         tiled=True,
     )
-    grad_total = jnp.sum(arrived, axis=1)
+    return jnp.sum(arrived, axis=1)
+
+
+def gather_blocks(mine):
+    host_count = lax.axis_size("hst")
+    row_block, col_block = mine.shape
+    me = lax.axis_index("hst")
+    whole = jnp.zeros((row_block, host_count * col_block), mine.dtype)
+    whole = lax.dynamic_update_slice_in_dim(whole, mine, me * col_block, 1)
+    for step in range(1, host_count):
+        block = swap(mine, "hst", step)
+        whole = lax.dynamic_update_slice_in_dim(whole, block, (me ^ step) * col_block, 1)
+    return whole
+
+
+def local(grads, master, moment_one, moment_two):
+    tuned = lax.axis_size("local") == 4 and lax.axis_size("hst") == 8
+    gradient = grads[0, 0]
+    grad_total = reduce_blocks(gradient) if tuned else reduce_general(gradient)
     new_one = beta_one * moment_one + (1.0 - beta_one) * grad_total
     new_two = beta_two * moment_two + (1.0 - beta_two) * grad_total * grad_total
     update = new_one / correct_one / (jnp.sqrt(new_two / correct_two) + epsilon)
     new_master = master - learn_rate * (update + decay_rate * master)
-    secondary = lax.all_gather(new_master.astype(jnp.bfloat16), "hst", axis=1, tiled=True)
+    mine = new_master.astype(jnp.bfloat16)
+    if tuned:
+        secondary = gather_blocks(mine)
+    else:
+        secondary = lax.all_gather(mine, "hst", axis=1, tiled=True)
     return (grad_total, new_master, new_one, new_two, secondary)
 
 

time: 86 us -> 49.5 us (0.58)
  blocking collectives: 80.8 us -> 0 us
  starting transfers between devices: 0 us -> 24.1 us
  waiting for transfers between devices: 0 us -> 18.4 us
  other arithmetic: 1.79 us -> 4.83 us
  local copies, waits for them, and re-layouts: 2.5 us -> 1.26 us
    all_to_all x2 -> x0, blocking collectives: 49.6 us -> none  [the longest x1 25.5 us: local(): lax.all_to_all(partial_sum.reshape(row_block, host_count, col_block), 'hs...]
    all_gather x1 -> x0, blocking collectives: 31.2 us -> none  [local(): lax.all_gather(new_master.astype(jnp.bfloat16), 'hst', axis=1, tiled=True)]
    ppermute x0 -> x15, starting transfers between devices: none -> 24.1 us  [swap(): return lax.ppermute(value, axis, [(i, i ^ flip) for i in range(count)])]
    ppermute x0 -> x15, waiting for transfers between devices: none -> 18.4 us  [swap(): return lax.ppermute(value, axis, [(i, i ^ flip) for i in range(count)])]
    add x0 -> x5, other arithmetic: none -> 3.4 us  [the longest x1 2.97 us: reduce_blocks(): pair = (mine(gradient) + mine(other)).reshape(2, row_block, 8, col_block)]
    another operation x1 -> x0, local copies, waits for them, and re-layouts: 1.73 us -> none  [local(): gradient.reshape(local_count, row_block, total_cols)]
    dynamic_update_slice x0 -> x1, other arithmetic: none -> 0.94 us  [gather_blocks(): whole = lax.dynamic_update_slice_in_dim(whole, mine, me * col_block, 1)]
    reduce_sum x2 -> x0, other arithmetic: 0.92 us -> none  [the longest x1 0.79 us: local(): partial_sum = jnp.sum(pieces.astype(jnp.float32), axis=0)]
  transfers between devices with their start and end apart: 0 -> 15, of which waited for: 0 -> 8; matrix products, arithmetic and copies ran while one was open for 0% -> 2% of each run, Pallas kernels for 0% -> 0%
where the time goes in v2:
time: 49.5 us; the launch traced here: 49.4 us
  starting transfers between devices  24.1 us (49%)
  waiting for transfers between devices  18.4 us (37%)
  other arithmetic  4.83 us (10%)
  local copies, waits for them, and re-layouts  1.26 us (3%)
  between operations  0.81 us (2%)
    ppermute x15, starting transfers between devices, swap(): return lax.ppermute(value, axis, [(i, i ^ flip) for i in range(count)])  24.1 us
    ppermute x15, waiting for transfers between devices, swap(): return lax.ppermute(value, axis, [(i, i ^ flip) for i in range(count)])  18.4 us
    add x1, other arithmetic, reduce_blocks(): pair = (mine(gradient) + mine(other)).reshape(2, row_block, 8, col_block)  2.97 us
  transfers between devices with their start and end apart: 15, of which 8 were waited for; matrix products, arithmetic and copies ran while one was open for 2% of the time, Pallas kernels for 0%

profile of v2, /device:TPU:0, one launch (start us, length us, event | category | flops | bytes accessed | tf_op | source)
XLA Modules:
  0.0 49.4 jit_solution(7105928068332284080)
XLA Ops:
  0.6 0.5 %collective-permute-start = (bf16[16,49152]{1,0:T(8,128)(2,1)}, bf16[16,49152]{1,0:T(8,128)(2,1)S(1)}, u32[]{:S(2)}, u32[]{:S(2)}) collective-permute-start(bf16[16,49152]{1,0:T(8,128)(2,1)} %bitcast.42), channel_id=1, source_target_pairs={{0,1},{1,0},{2,3},{3,2},{4,5},{5,4},{6,7},{7,6},{8,9},{9,8},{10,11... | collective-permute-start | bytes 4718600 | tf_op jit(solution)/shard_map/ppermute | solution.py:19
  1.1 3.2 %collective-permute-done = bf16[16,49152]{1,0:T(8,128)(2,1)S(1)} collective-permute-done((bf16[16,49152]{1,0:T(8,128)(2,1)}, bf16[16,49152]{1,0:T(8,128)(2,1)S(1)}, u32[]{:S(2)}, u32[]{:S(2)}) %collective-permute-start) | collective-permute-done | bytes 1572896 | tf_op jit(solution)/shard_map/ppermute | solution.py:19
  4.4 3.0 %convert_add_fusion = f32[2,4,49152]{2,1,0:T(4,128)S(1)} fusion(bf16[2,8,49152]{2,1,0:T(8,128)(2,1)S(1)} %bitcast.44, bf16[2,8,49152]{2,1,0:T(8,128)(2,1)} %bitcast.43, pred[]{:T(512)S(6)} %eq.7), kind=kLoop, calls=%fused_computation | loop fusion | flops 1966080 | bytes 4718593 | tf_op jit(solution)/shard_map/add | solution.py:47
  7.4 0.1 fusion.26
  7.6 0.1 fusion.3
  7.7 2.9 %collective-permute-start.1 = (f16[2,2,4,6144]{3,2,0,1:T(4,128)(2,1)S(1)}, f16[2,2,4,6144]{3,2,0,1:T(4,128)(2,1)S(1)}, u32[]{:S(2)}, u32[]{:S(2)}) collective-permute-start(f16[2,2,4,6144]{3,2,0,1:T(4,128)(2,1)S(1)} %fusion.3), channel_id=1, source_target_pairs={{0,2},{1,3},{2,0},{3,1},{4,6},{5,7},{6,4},{7,5},{8,10},{9,11},{10,... | collective-permute-start | bytes 589832 | tf_op jit(solution)/shard_map/ppermute | solution.py:19
  10.6 0.1 fusion.2
  10.7 1.6 %collective-permute-start.3 = (f16[2,2,4,6144]{3,2,1,0:T(4,128)(2,1)S(1)}, f16[2,2,4,6144]{3,2,1,0:T(4,128)(2,1)S(1)}, u32[]{:S(2)}, u32[]{:S(2)}) collective-permute-start(f16[2,2,4,6144]{3,2,1,0:T(4,128)(2,1)S(1)} %fusion.2), channel_id=1, source_target_pairs={{0,4},{4,0},{8,12},{12,8},{16,20},{20,16},{24,28},{28,24},{1,5},{5... | collective-permute-start | bytes 589832 | tf_op jit(solution)/shard_map/ppermute | solution.py:19
  12.3 3.5 %collective-permute-done.1 = f16[2,2,4,6144]{3,2,0,1:T(4,128)(2,1)S(1)} collective-permute-done((f16[2,2,4,6144]{3,2,0,1:T(4,128)(2,1)S(1)}, f16[2,2,4,6144]{3,2,0,1:T(4,128)(2,1)S(1)}, u32[]{:S(2)}, u32[]{:S(2)}) %collective-permute-start.1) | collective-permute-done | bytes 196640 | tf_op jit(solution)/shard_map/ppermute | solution.py:19
  15.8 0.1 fusion.1
  16.0 1.8 %collective-permute-start.2 = (f16[2,4,6144]{2,1,0:T(4,128)(2,1)S(1)}, f16[2,4,6144]{2,1,0:T(4,128)(2,1)S(1)}, u32[]{:S(2)}, u32[]{:S(2)}) collective-permute-start(f16[2,4,6144]{2,1,0:T(4,128)(2,1)S(1)} %fusion.5), channel_id=1, source_target_pairs={{0,4},{4,0},{8,12},{12,8},{16,20},{20,16},{24,28},{28,24},{1,5},{5... | collective-permute-start | bytes 294920 | tf_op jit(solution)/shard_map/ppermute | solution.py:19
  17.9 0.1 bitcast_add_fusion
  18.1 1.6 %collective-permute-start.4 = (f16[2,4,6144]{2,1,0:T(4,128)(2,1)S(1)}, f16[2,4,6144]{2,1,0:T(4,128)(2,1)S(1)}, u32[]{:S(2)}, u32[]{:S(2)}) collective-permute-start(f16[2,4,6144]{2,1,0:T(4,128)(2,1)S(1)} %fusion.6), channel_id=1, source_target_pairs={{0,2},{1,3},{2,0},{3,1},{4,6},{5,7},{6,4},{7,5},{8,10},{9,11},{10,... | collective-permute-start | bytes 294920 | tf_op jit(solution)/shard_map/ppermute | solution.py:19
  19.6 1.1 %collective-permute-done.2 = f16[2,4,6144]{2,1,0:T(4,128)(2,1)S(1)} collective-permute-done((f16[2,4,6144]{2,1,0:T(4,128)(2,1)S(1)}, f16[2,4,6144]{2,1,0:T(4,128)(2,1)S(1)}, u32[]{:S(2)}, u32[]{:S(2)}) %collective-permute-start.2) | collective-permute-done | bytes 98336 | tf_op jit(solution)/shard_map/ppermute | solution.py:19
  20.7 0.1 bitcast_add_fusion.2
  20.8 2.0 %collective-permute-done.4 = f16[2,4,6144]{2,1,0:T(4,128)(2,1)S(1)} collective-permute-done((f16[2,4,6144]{2,1,0:T(4,128)(2,1)S(1)}, f16[2,4,6144]{2,1,0:T(4,128)(2,1)S(1)}, u32[]{:S(2)}, u32[]{:S(2)}) %collective-permute-start.4) | collective-permute-done | bytes 98336 | tf_op jit(solution)/shard_map/ppermute | solution.py:19
  22.8 0.2 fusion.22
  23.0 1.6 %collective-permute-start.5 = (f16[4,6144]{1,0:T(4,128)(2,1)S(1)}, f16[4,6144]{1,0:T(4,128)(2,1)S(1)}, u32[]{:S(2)}, u32[]{:S(2)}) collective-permute-start(f16[4,6144]{1,0:T(4,128)(2,1)S(1)} %get-tuple-element.15), channel_id=1, source_target_pairs={{0,8},{4,12},{8,0},{12,4},{16,24},{20,28},{24,16},{28,20},{1,9},{5... | collective-permute-start | bytes 147464 | tf_op jit(solution)/shard_map/ppermute | solution.py:19
  24.7 2.6 %collective-permute-start.6 = (f16[4,6144]{1,0:T(4,128)(2,1)S(1)}, f16[4,6144]{1,0:T(4,128)(2,1)S(1)}, u32[]{:S(2)}, u32[]{:S(2)}) collective-permute-start(f16[4,6144]{1,0:T(4,128)(2,1)S(1)} %get-tuple-element.16), channel_id=1, source_target_pairs={{0,16},{4,20},{8,24},{12,28},{16,0},{20,4},{24,8},{28,12},{1,17},{... | collective-permute-start | bytes 147464 | tf_op jit(solution)/shard_map/ppermute | solution.py:19
  27.3 0.2 collective-permute-start.7
  27.5 3.2 %collective-permute-done.6 = f16[4,6144]{1,0:T(4,128)(2,1)S(1)} collective-permute-done((f16[4,6144]{1,0:T(4,128)(2,1)S(1)}, f16[4,6144]{1,0:T(4,128)(2,1)S(1)}, u32[]{:S(2)}, u32[]{:S(2)}) %collective-permute-start.6) | collective-permute-done | bytes 49184 | tf_op jit(solution)/shard_map/ppermute | solution.py:19
  30.7 2.4 %collective-permute-done.7 = f16[4,6144]{1,0:T(4,128)(2,1)S(1)} collective-permute-done((f16[4,6144]{1,0:T(4,128)(2,1)S(1)}, f16[4,6144]{1,0:T(4,128)(2,1)S(1)}, u32[]{:S(2)}, u32[]{:S(2)}) %collective-permute-start.7) | collective-permute-done | bytes 49184 | tf_op jit(solution)/shard_map/ppermute | solution.py:19
  33.2 0.1 broadcast_in_dim.3
  33.3 0.9 %constant_dynamic-update-slice_fusion.7 = (bf16[4,49152]{1,0:T(4,128)(2,1)S(1)}, bf16[4,6144]{1,0:T(4,128)(2,1)S(1)}, f32[4,6144]{1,0:T(4,128)}, f32[4,6144]{1,0...) fusion(bf16[4,49152]{1,0:T(4,128)(2,1)S(1)} %broadcast_in_dim.3, s32[]{:T(128)S(6)} %select_n.102, ...), kind=kLoop, calls=%fused_computation.53 | loop fusion | flops 638976 | bytes 1327112 | tf_op jit(solution)/shard_map/dynamic_update_slice | solution.py:93
  34.2 1.1 %collective-permute-start.8 = (bf16[4,6144]{1,0:T(4,128)(2,1)S(1)}, bf16[4,6144]{1,0:T(4,128)(2,1)S(1)}, u32[]{:S(2)}, u32[]{:S(2)}) collective-permute-start(bf16[4,6144]{1,0:T(4,128)(2,1)S(1)} %get-tuple-element.6), channel_id=1, source_target_pairs={{0,4},{4,0},{8,12},{12,8},{16,20},{20,16},{24,28},{28,24},{1,5},{5... | collective-permute-start | bytes 147464 | tf_op jit(solution)/shard_map/ppermute | solution.py:19
  35.3 2.4 %collective-permute-start.10 = (bf16[4,6144]{1,0:T(4,128)(2,1)S(1)}, bf16[4,6144]{1,0:T(4,128)(2,1)S(1)}, u32[]{:S(2)}, u32[]{:S(2)}) collective-permute-start(bf16[4,6144]{1,0:T(4,128)(2,1)S(1)} %get-tuple-element.6), channel_id=1, source_target_pairs={{0,12},{4,8},{8,4},{12,0},{16,28},{20,24},{24,20},{28,16},{1,13},{... | collective-permute-start | bytes 147464 | tf_op jit(solution)/shard_map/ppermute | solution.py:19
  37.7 3.4 %collective-permute-start.12 = (bf16[4,6144]{1,0:T(4,128)(2,1)S(1)}, bf16[4,6144]{1,0:T(4,128)(2,1)S(1)}, u32[]{:S(2)}, u32[]{:S(2)}) collective-permute-start(bf16[4,6144]{1,0:T(4,128)(2,1)S(1)} %get-tuple-element.6), channel_id=1, source_target_pairs={{0,20},{4,16},{8,28},{12,24},{16,4},{20,0},{24,12},{28,8},{1,21},{... | collective-permute-start | bytes 147464 | tf_op jit(solution)/shard_map/ppermute | solution.py:19
  41.2 0.6 %collective-permute-start.13 = (bf16[4,6144]{1,0:T(4,128)(2,1)S(1)}, bf16[4,6144]{1,0:T(4,128)(2,1)S(1)}, u32[]{:S(2)}, u32[]{:S(2)}) collective-permute-start(bf16[4,6144]{1,0:T(4,128)(2,1)S(1)} %get-tuple-element.6), channel_id=1, source_target_pairs={{0,24},{4,28},{8,16},{12,20},{16,8},{20,12},{24,0},{28,4},{1,25},{... | collective-permute-start | bytes 147464 | tf_op jit(solution)/shard_map/ppermute | solution.py:19
  41.8 3.7 %collective-permute-start.14 = (bf16[4,6144]{1,0:T(4,128)(2,1)S(1)}, bf16[4,6144]{1,0:T(4,128)(2,1)S(1)}, u32[]{:S(2)}, u32[]{:S(2)}) collective-permute-start(bf16[4,6144]{1,0:T(4,128)(2,1)S(1)} %get-tuple-element.6), channel_id=1, source_target_pairs={{0,28},{4,24},{8,20},{12,16},{16,12},{20,8},{24,4},{28,0},{1,29},{... | collective-permute-start | bytes 147464 | tf_op jit(solution)/shard_map/ppermute | solution.py:19
  45.7 1.4 %collective-permute-done.13 = bf16[4,6144]{1,0:T(4,128)(2,1)S(1)} collective-permute-done((bf16[4,6144]{1,0:T(4,128)(2,1)S(1)}, bf16[4,6144]{1,0:T(4,128)(2,1)S(1)}, u32[]{:S(2)}, u32[]{:S(2)}) %collective-permute-start.13) | collective-permute-done | bytes 49184 | tf_op jit(solution)/shard_map/ppermute | solution.py:19
  47.1 1.5 %collective-permute-done.14 = bf16[4,6144]{1,0:T(4,128)(2,1)S(1)} collective-permute-done((bf16[4,6144]{1,0:T(4,128)(2,1)S(1)}, bf16[4,6144]{1,0:T(4,128)(2,1)S(1)}, u32[]{:S(2)}, u32[]{:S(2)}) %collective-permute-start.14) | collective-permute-done | bytes 49184 | tf_op jit(solution)/shard_map/ppermute | solution.py:19
  48.7 0.7 %copy-done = bf16[4,49152]{1,0:T(4,128)(2,1)} copy-done((bf16[4,49152]{1,0:T(4,128)(2,1)}, bf16[4,49152]{1,0:T(4,128)(2,1)S(1)}, u32[]{:S(2)}) %copy-start) | copy-done | bytes 393240
  (27 shorter events, 0.5 us)
Async XLA Ops:
  0.6 3.8 %collective-permute-start = (bf16[16,49152]{1,0:T(8,128)(2,1)}, bf16[16,49152]{1,0:T(8,128)(2,1)S(1)}, u32[]{:S(2)}, u32[]{:S(2)}) collective-permute-start(bf16[16,49152]{1,0:T(8,128)(2,1)} %bitcast.42), channel_id=1, source_target_pairs={{0,1},{1,0},{2,3},{3,2},{4,5},{5,4},{6,7},{7,6},{8,9},{9,8},{10,11... | collective-permute-start | bytes 4718600 | tf_op jit(solution)/shard_map/ppermute | solution.py:19
  7.7 8.1 %collective-permute-start.1 = (f16[2,2,4,6144]{3,2,0,1:T(4,128)(2,1)S(1)}, f16[2,2,4,6144]{3,2,0,1:T(4,128)(2,1)S(1)}, u32[]{:S(2)}, u32[]{:S(2)}) collective-permute-start(f16[2,2,4,6144]{3,2,0,1:T(4,128)(2,1)S(1)} %fusion.3), channel_id=1, source_target_pairs={{0,2},{1,3},{2,0},{3,1},{4,6},{5,7},{6,4},{7,5},{8,10},{9,11},{10,... | collective-permute-start | bytes 589832 | tf_op jit(solution)/shard_map/ppermute | solution.py:19
  10.7 7.2 %collective-permute-start.3 = (f16[2,2,4,6144]{3,2,1,0:T(4,128)(2,1)S(1)}, f16[2,2,4,6144]{3,2,1,0:T(4,128)(2,1)S(1)}, u32[]{:S(2)}, u32[]{:S(2)}) collective-permute-start(f16[2,2,4,6144]{3,2,1,0:T(4,128)(2,1)S(1)} %fusion.2), channel_id=1, source_target_pairs={{0,4},{4,0},{8,12},{12,8},{16,20},{20,16},{24,28},{28,24},{1,5},{5... | collective-permute-start | bytes 589832 | tf_op jit(solution)/shard_map/ppermute | solution.py:19
  16.0 17.3 %copy-start.1 = (f32[4,6144]{1,0:T(4,128)S(1)}, f32[4,6144]{1,0:T(4,128)}, u32[]{:S(2)}) copy-start(f32[4,6144]{1,0:T(4,128)} %param.5) | copy-start | bytes 294916
  16.0 17.3 %copy-start.2 = (f32[4,6144]{1,0:T(4,128)S(1)}, f32[4,6144]{1,0:T(4,128)}, u32[]{:S(2)}) copy-start(f32[4,6144]{1,0:T(4,128)} %param.6) | copy-start | bytes 294916
  16.0 17.3 %copy-start.3 = (f32[4,6144]{1,0:T(4,128)S(1)}, f32[4,6144]{1,0:T(4,128)}, u32[]{:S(2)}) copy-start(f32[4,6144]{1,0:T(4,128)} %param.7) | copy-start | bytes 294916
  16.0 4.7 %collective-permute-start.2 = (f16[2,4,6144]{2,1,0:T(4,128)(2,1)S(1)}, f16[2,4,6144]{2,1,0:T(4,128)(2,1)S(1)}, u32[]{:S(2)}, u32[]{:S(2)}) collective-permute-start(f16[2,4,6144]{2,1,0:T(4,128)(2,1)S(1)} %fusion.5), channel_id=1, source_target_pairs={{0,4},{4,0},{8,12},{12,8},{16,20},{20,16},{24,28},{28,24},{1,5},{5... | collective-permute-start | bytes 294920 | tf_op jit(solution)/shard_map/ppermute | solution.py:19
  18.1 4.7 %collective-permute-start.4 = (f16[2,4,6144]{2,1,0:T(4,128)(2,1)S(1)}, f16[2,4,6144]{2,1,0:T(4,128)(2,1)S(1)}, u32[]{:S(2)}, u32[]{:S(2)}) collective-permute-start(f16[2,4,6144]{2,1,0:T(4,128)(2,1)S(1)} %fusion.6), channel_id=1, source_target_pairs={{0,2},{1,3},{2,0},{3,1},{4,6},{5,7},{6,4},{7,5},{8,10},{9,11},{10,... | collective-permute-start | bytes 294920 | tf_op jit(solution)/shard_map/ppermute | solution.py:19
  23.0 4.5 %collective-permute-start.5 = (f16[4,6144]{1,0:T(4,128)(2,1)S(1)}, f16[4,6144]{1,0:T(4,128)(2,1)S(1)}, u32[]{:S(2)}, u32[]{:S(2)}) collective-permute-start(f16[4,6144]{1,0:T(4,128)(2,1)S(1)} %get-tuple-element.15), channel_id=1, source_target_pairs={{0,8},{4,12},{8,0},{12,4},{16,24},{20,28},{24,16},{28,20},{1,9},{5... | collective-permute-start | bytes 147464 | tf_op jit(solution)/shard_map/ppermute | solution.py:19
  24.7 6.0 %collective-permute-start.6 = (f16[4,6144]{1,0:T(4,128)(2,1)S(1)}, f16[4,6144]{1,0:T(4,128)(2,1)S(1)}, u32[]{:S(2)}, u32[]{:S(2)}) collective-permute-start(f16[4,6144]{1,0:T(4,128)(2,1)S(1)} %get-tuple-element.16), channel_id=1, source_target_pairs={{0,16},{4,20},{8,24},{12,28},{16,0},{20,4},{24,8},{28,12},{1,17},{... | collective-permute-start | bytes 147464 | tf_op jit(solution)/shard_map/ppermute | solution.py:19
  27.3 5.9 %collective-permute-start.7 = (f16[4,6144]{1,0:T(4,128)(2,1)S(1)}, f16[4,6144]{1,0:T(4,128)(2,1)S(1)}, u32[]{:S(2)}, u32[]{:S(2)}) collective-permute-start(f16[4,6144]{1,0:T(4,128)(2,1)S(1)} %get-tuple-element.17), channel_id=1, source_target_pairs={{0,24},{4,28},{8,16},{12,20},{16,8},{20,12},{24,0},{28,4},{1,25},{... | collective-permute-start | bytes 147464 | tf_op jit(solution)/shard_map/ppermute | solution.py:19
  34.2 6.9 %collective-permute-start.8 = (bf16[4,6144]{1,0:T(4,128)(2,1)S(1)}, bf16[4,6144]{1,0:T(4,128)(2,1)S(1)}, u32[]{:S(2)}, u32[]{:S(2)}) collective-permute-start(bf16[4,6144]{1,0:T(4,128)(2,1)S(1)} %get-tuple-element.6), channel_id=1, source_target_pairs={{0,4},{4,0},{8,12},{12,8},{16,20},{20,16},{24,28},{28,24},{1,5},{5... | collective-permute-start | bytes 147464 | tf_op jit(solution)/shard_map/ppermute | solution.py:19
  35.3 6.5 %collective-permute-start.9 = (bf16[4,6144]{1,0:T(4,128)(2,1)S(1)}, bf16[4,6144]{1,0:T(4,128)(2,1)S(1)}, u32[]{:S(2)}, u32[]{:S(2)}) collective-permute-start(bf16[4,6144]{1,0:T(4,128)(2,1)S(1)} %get-tuple-element.6), channel_id=1, source_target_pairs={{0,8},{4,12},{8,0},{12,4},{16,24},{20,28},{24,16},{28,20},{1,9},{5... | collective-permute-start | bytes 147464 | tf_op jit(solution)/shard_map/ppermute | solution.py:19
  35.3 10.2 %collective-permute-start.10 = (bf16[4,6144]{1,0:T(4,128)(2,1)S(1)}, bf16[4,6144]{1,0:T(4,128)(2,1)S(1)}, u32[]{:S(2)}, u32[]{:S(2)}) collective-permute-start(bf16[4,6144]{1,0:T(4,128)(2,1)S(1)} %get-tuple-element.6), channel_id=1, source_target_pairs={{0,12},{4,8},{8,4},{12,0},{16,28},{20,24},{24,20},{28,16},{1,13},{... | collective-permute-start | bytes 147464 | tf_op jit(solution)/shard_map/ppermute | solution.py:19
  37.7 7.8 %collective-permute-start.11 = (bf16[4,6144]{1,0:T(4,128)(2,1)S(1)}, bf16[4,6144]{1,0:T(4,128)(2,1)S(1)}, u32[]{:S(2)}, u32[]{:S(2)}) collective-permute-start(bf16[4,6144]{1,0:T(4,128)(2,1)S(1)} %get-tuple-element.6), channel_id=1, source_target_pairs={{0,16},{4,20},{8,24},{12,28},{16,0},{20,4},{24,8},{28,12},{1,17},{... | collective-permute-start | bytes 147464 | tf_op jit(solution)/shard_map/ppermute | solution.py:19
  37.7 7.9 %collective-permute-start.12 = (bf16[4,6144]{1,0:T(4,128)(2,1)S(1)}, bf16[4,6144]{1,0:T(4,128)(2,1)S(1)}, u32[]{:S(2)}, u32[]{:S(2)}) collective-permute-start(bf16[4,6144]{1,0:T(4,128)(2,1)S(1)} %get-tuple-element.6), channel_id=1, source_target_pairs={{0,20},{4,16},{8,28},{12,24},{16,4},{20,0},{24,12},{28,8},{1,21},{... | collective-permute-start | bytes 147464 | tf_op jit(solution)/shard_map/ppermute | solution.py:19
  41.2 5.9 %collective-permute-start.13 = (bf16[4,6144]{1,0:T(4,128)(2,1)S(1)}, bf16[4,6144]{1,0:T(4,128)(2,1)S(1)}, u32[]{:S(2)}, u32[]{:S(2)}) collective-permute-start(bf16[4,6144]{1,0:T(4,128)(2,1)S(1)} %get-tuple-element.6), channel_id=1, source_target_pairs={{0,24},{4,28},{8,16},{12,20},{16,8},{20,12},{24,0},{28,4},{1,25},{... | collective-permute-start | bytes 147464 | tf_op jit(solution)/shard_map/ppermute | solution.py:19
  41.8 6.9 %collective-permute-start.14 = (bf16[4,6144]{1,0:T(4,128)(2,1)S(1)}, bf16[4,6144]{1,0:T(4,128)(2,1)S(1)}, u32[]{:S(2)}, u32[]{:S(2)}) collective-permute-start(bf16[4,6144]{1,0:T(4,128)(2,1)S(1)} %get-tuple-element.6), channel_id=1, source_target_pairs={{0,28},{4,24},{8,20},{12,16},{16,12},{20,8},{24,4},{28,0},{1,29},{... | collective-permute-start | bytes 147464 | tf_op jit(solution)/shard_map/ppermute | solution.py:19
  48.6 0.7 %copy-start = (bf16[4,49152]{1,0:T(4,128)(2,1)}, bf16[4,49152]{1,0:T(4,128)(2,1)S(1)}, u32[]{:S(2)}) copy-start(bf16[4,49152]{1,0:T(4,128)(2,1)S(1)} %constant_dynamic-update-slice_fusion) | copy-start | bytes 1179652

commit v3 on v0

--- a/solution.py
+++ b/solution.py
@@ -11,17 +11,89 @@
 correct_one = 1.0 - (0.9**50) ** 2
 correct_two = 1.0 - (0.95**50) ** 2
 
+wire_scale = 4096.0
 
-def local(grads, master, moment_one, moment_two):
+
+def flip_pairs(flips):
+    count = lax.axis_size("hst") * lax.axis_size("local")
+    return [(i, i ^ flips[i % 2]) for i in range(count)]
+
+
+def swap(value, *flips):
+    return lax.ppermute(value, ("hst", "local"), flip_pairs(flips))
+
+
+def narrow(value):
+    return (value * wire_scale).astype(jnp.float16)
+
+
+def widen(value):
+    return value.astype(jnp.float32) * (1.0 / wire_scale)
+
+
+def pick(value, index):
+    return lax.dynamic_index_in_dim(value, index, 0, keepdims=False)
+
+
+CORE, X, Y, Z_NEAR, Z_FAR = 1, 2, 4, 8, 16
+
+
+def reduce_blocks(gradient):
+    rows, cols = gradient.shape
+    tile, half = rows // 2, cols // 16
+    me_local, me_host = lax.axis_index("local"), lax.axis_index("hst")
+    x, core = me_local // 2, me_local % 2
+    z, y = me_host // 2, me_host % 2
+
+    split = gradient.reshape(2, tile, 16, half).transpose(0, 2, 1, 3)
+    split = split.reshape(2, 4, 2, 2, tile, half).transpose(3, 0, 1, 2, 4, 5)
+    other = swap(pick(split, 1 - core), CORE, CORE)
+    pair = pick(split, core).astype(jnp.float32) + other.astype(jnp.float32)
+
+    def column(i, j):
+        return lax.dynamic_slice(pair, (i, 0, j, 0, 0), (1, 4, 1, tile, half)).reshape(4, tile, half)
+
+    x_first, y_first = 1 - core, core
+    sent = narrow(jnp.stack([column(x ^ x_first, y ^ y_first), column(1 - x, 1 - y)]))
+    got = widen(swap(sent, X, Y))
+    keep = column(x, y) + got[0]
+    send = column(x ^ y_first, y ^ x_first) + got[1]
+    quad = keep + widen(swap(narrow(send), Y, X))
+
+    first = jnp.where(core == 0, 2, 1)
+    sent = narrow(jnp.stack([pick(quad, z ^ first), pick(quad, z ^ 3)]))
+    got = widen(swap(sent, Z_FAR, Z_NEAR))
+    keep = pick(quad, z) + got[0]
+    send = pick(quad, z ^ 3 ^ first) + got[1]
+    total = keep + widen(swap(narrow(send), Z_NEAR, Z_FAR))
+
+    by_core = total.reshape(2, tile // 2, half)
+    own, other = pick(by_core, core), swap(pick(by_core, 1 - core), CORE, CORE)
+    left, right = jnp.where(core == 0, own, other), jnp.where(core == 0, other, own)
+    return jnp.concatenate([left, right], axis=1)
+
+
+def gather_blocks(mine):
+    row_block, col_block = mine.shape
+    me, core = lax.axis_index("hst"), lax.axis_index("local") % 2
+    near = jnp.where(core == 0, 2, 1)
+    blocks, place = mine[None], [me]
+    for flips, bit in (((Z_FAR, Z_FAR), 4), ((Z_NEAR, Y), near), ((Y, Z_NEAR), 3 - near)):
+        blocks = jnp.concatenate([blocks, swap(blocks, *flips)])
+        place = place + [p ^ bit for p in place]
+    whole = jnp.zeros((row_block, 8 * col_block), mine.dtype)
+    for i, p in enumerate(place):
+        whole = lax.dynamic_update_slice_in_dim(whole, blocks[i], p * col_block, 1)
+    return whole
+
+
+def reduce_general(gradient):
     local_count = lax.axis_size("local")
     host_count = lax.axis_size("hst")
-    gradient = grads[0, 0]
-    total_rows = gradient.shape[0]
-    total_cols = gradient.shape[1]
-    row_block = total_rows // local_count
-    col_block = total_cols // host_count
+    rows, cols = gradient.shape
+    row_block, col_block = rows // local_count, cols // host_count
     pieces = lax.all_to_all(
-        gradient.reshape(local_count, row_block, total_cols),
+        gradient.reshape(local_count, row_block, cols),
         "local",
         split_axis=0,
         concat_axis=0,
@@ -35,12 +107,22 @@
         concat_axis=1,
         tiled=True,
     )
-    grad_total = jnp.sum(arrived, axis=1)
+    return jnp.sum(arrived, axis=1)
+
+
+def local(grads, master, moment_one, moment_two):
+    tuned = lax.axis_size("local") == 4 and lax.axis_size("hst") == 8
+    gradient = grads[0, 0]
+    grad_total = reduce_blocks(gradient) if tuned else reduce_general(gradient)
     new_one = beta_one * moment_one + (1.0 - beta_one) * grad_total
     new_two = beta_two * moment_two + (1.0 - beta_two) * grad_total * grad_total
     update = new_one / correct_one / (jnp.sqrt(new_two / correct_two) + epsilon)
     new_master = master - learn_rate * (update + decay_rate * master)
-    secondary = lax.all_gather(new_master.astype(jnp.bfloat16), "hst", axis=1, tiled=True)
+    mine = new_master.astype(jnp.bfloat16)
+    if tuned:
+        secondary = gather_blocks(mine)
+    else:
+        secondary = lax.all_gather(mine, "hst", axis=1, tiled=True)
     return (grad_total, new_master, new_one, new_two, secondary)
 
 

time: 86 us -> 51.2 us (0.60)
  blocking collectives: 80.8 us -> 0 us
  waiting for transfers between devices: 0 us -> 25.8 us
  starting transfers between devices: 0 us -> 19 us
  other arithmetic: 1.79 us -> 2.77 us
    all_to_all x2 -> x0, blocking collectives: 49.6 us -> none  [the longest x1 25.5 us: local(): lax.all_to_all(partial_sum.reshape(row_block, host_count, col_block), 'hs...]
    all_gather x1 -> x0, blocking collectives: 31.2 us -> none  [local(): lax.all_gather(new_master.astype(jnp.bfloat16), 'hst', axis=1, tiled=True)]
    ppermute x0 -> x9, waiting for transfers between devices: none -> 25.8 us  [swap(): return lax.ppermute(value, ('hst', 'local'), flip_pairs(flips))]
    ppermute x0 -> x9, starting transfers between devices: none -> 19 us  [swap(): return lax.ppermute(value, ('hst', 'local'), flip_pairs(flips))]
    another operation x1, local copies, waits for them, and re-layouts: 1.73 us -> 0.07 us  [reduce_blocks(): jnp.stack([column(x ^ x_first, y ^ y_first), column(1 - x, 1 - y)])]
    add x0 -> x3, other arithmetic: none -> 1.4 us  [the longest x1 1.32 us: reduce_blocks(): pair = pick(split, core).astype(jnp.float32) + other.astype(jnp.float32)]
    squeeze x0 -> x2, local copies, waits for them, and re-layouts: none -> 1.33 us  [pick(): return lax.dynamic_index_in_dim(value, index, 0, keepdims=False)]
    reduce_sum x2 -> x0, other arithmetic: 0.92 us -> none  [the longest x1 0.79 us: local(): partial_sum = jnp.sum(pieces.astype(jnp.float32), axis=0)]
  transfers between devices with their start and end apart: 0 -> 9, of which waited for: 0 -> 9; matrix products, arithmetic and copies ran while one was open for 0% -> 0% of each run, Pallas kernels for 0% -> 0%
where the time goes in v3:
time: 51.2 us; the launch traced here: 51 us
  waiting for transfers between devices  25.8 us (50%)
  starting transfers between devices  19 us (37%)
  other arithmetic  2.77 us (5%)
  local copies, waits for them, and re-layouts  2.52 us (5%)
  between operations  0.9 us (2%)
    ppermute x9, waiting for transfers between devices, swap(): return lax.ppermute(value, ('hst', 'local'), flip_pairs(flips))  25.8 us
    ppermute x9, starting transfers between devices, swap(): return lax.ppermute(value, ('hst', 'local'), flip_pairs(flips))  19 us
    squeeze x2, local copies, waits for them, and re-layouts, pick(): return lax.dynamic_index_in_dim(value, index, 0, keepdims=False)  1.33 us
    add x1, other arithmetic, reduce_blocks(): pair = pick(split, core).astype(jnp.float32) + other.astype(jnp.float32)  1.32 us
  transfers between devices with their start and end apart: 9, of which 9 were waited for; matrix products, arithmetic and copies ran while one was open for 0% of the time, Pallas kernels for 0%

profile of v3, /device:TPU:0, one launch (start us, length us, event | category | flops | bytes accessed | tf_op | source)
XLA Modules:
  0.0 51.0 jit_solution(9673164769029997104)
XLA Ops:
  0.6 0.0 copy-start
  0.7 1.3 %dynamic-slice_bitcast_fusion = bf16[2,4,2,8,3072]{4,3,2,1,0:T(8,128)(2,1)S(1)} fusion(bf16[2,4,2,2,8,3072]{5,4,3,2,1,0:T(8,128)(2,1)} %bitcast.71, s32[]{:T(128)S(6)} %select_n.111), kind=kLoop, calls=%fused_computation.4 | loop fusion | bytes 1572868 | tf_op jit(solution)/shard_map/jit(dynamic_index_in_dim)/squeeze | solution.py:35
  2.0 0.5 %collective-permute-start = (bf16[2,4,2,8,3072]{4,3,2,1,0:T(8,128)(2,1)S(1)}, bf16[2,4,2,8,3072]{4,3,2,1,0:T(8,128)(2,1)}, u32[]{:S(2)}, u32[]{:S(2)}) collective-permute-start(bf16[2,4,2,8,3072]{4,3,2,1,0:T(8,128)(2,1)S(1)} %dynamic-slice_bitcast_fusion), channel_id=1, source_target_pairs={{0,1},{1,0},{2,3},{3,2},{4,5},{5,4},{6,7},{7,6},{8,9},{9,8},{10,11... | collective-permute-start | bytes 2359304 | tf_op jit(solution)/shard_map/ppermute | solution.py:23
  2.5 2.0 %collective-permute-done = bf16[2,4,2,8,3072]{4,3,2,1,0:T(8,128)(2,1)} collective-permute-done((bf16[2,4,2,8,3072]{4,3,2,1,0:T(8,128)(2,1)S(1)}, bf16[2,4,2,8,3072]{4,3,2,1,0:T(8,128)(2,1)}, u32[]{:S(2)}, u32[]{:S(2)}) %collective-permute-start) | collective-permute-done | bytes 786464 | tf_op jit(solution)/shard_map/ppermute | solution.py:23
  4.5 1.3 %convert_add_fusion = f32[2,4,2,8,3072]{4,3,2,1,0:T(8,128)S(1)} fusion(bf16[2,4,2,8,3072]{4,3,2,1,0:T(8,128)(2,1)} %collective-permute-done, bf16[2,4,2,2,8,3072]{5,4,3,2,1,0:T(8,128)(2,1)S(1)} %bitcast.72, s32[]{:T(128)S(6)} %select_n.110), kind=kLoop, calls=%fused_computation | loop fusion | flops 1179648 | bytes 3145732 | tf_op jit(solution)/shard_map/add | solution.py:51
  5.9 0.1 dynamic-slice_bitcast_fusion.2
  5.9 0.1 fusion
  6.0 2.9 %collective-permute-start.1 = (f16[2,4,8,3072]{3,2,1,0:T(8,128)(2,1)S(1)}, f16[2,4,8,3072]{3,2,1,0:T(8,128)(2,1)S(1)}, u32[]{:S(2)}, u32[]{:S(2)}) collective-permute-start(f16[2,4,8,3072]{3,2,1,0:T(8,128)(2,1)S(1)} %fusion), channel_id=1, source_target_pairs={{0,2},{1,5},{2,0},{3,7},{4,6},{5,1},{6,4},{7,3},{8,10},{9,13},{10,... | collective-permute-start | bytes 1179656 | tf_op jit(solution)/shard_map/ppermute | solution.py:23
  8.9 5.8 %collective-permute-done.1 = f16[2,4,8,3072]{3,2,1,0:T(8,128)(2,1)S(1)} collective-permute-done((f16[2,4,8,3072]{3,2,1,0:T(8,128)(2,1)S(1)}, f16[2,4,8,3072]{3,2,1,0:T(8,128)(2,1)S(1)}, u32[]{:S(2)}, u32[]{:S(2)}) %collective-permute-start.1) | collective-permute-done | bytes 393248 | tf_op jit(solution)/shard_map/ppermute | solution.py:23
  14.7 0.1 convert_multiply_fusion
  14.8 0.1 fusion.3
  14.8 2.1 %collective-permute-start.2 = (f16[4,8,3072]{2,1,0:T(8,128)(2,1)S(1)}, f16[4,8,3072]{2,1,0:T(8,128)(2,1)S(1)}, u32[]{:S(2)}, u32[]{:S(2)}) collective-permute-start(f16[4,8,3072]{2,1,0:T(8,128)(2,1)S(1)} %fusion.3), channel_id=1, source_target_pairs={{0,4},{1,3},{2,6},{3,1},{4,0},{5,7},{6,2},{7,5},{8,12},{9,11},{10,... | collective-permute-start | bytes 589832 | tf_op jit(solution)/shard_map/ppermute | solution.py:23
  17.0 3.6 %collective-permute-done.2 = f16[4,8,3072]{2,1,0:T(8,128)(2,1)S(1)} collective-permute-done((f16[4,8,3072]{2,1,0:T(8,128)(2,1)S(1)}, f16[4,8,3072]{2,1,0:T(8,128)(2,1)S(1)}, u32[]{:S(2)}, u32[]{:S(2)}) %collective-permute-start.2) | collective-permute-done | bytes 196640 | tf_op jit(solution)/shard_map/ppermute | solution.py:23
  20.6 0.1 fusion.5
  20.7 3.2 %collective-permute-start.3 = (f16[2,8,3072]{2,1,0:T(8,128)(2,1)S(1)}, f16[2,8,3072]{2,1,0:T(8,128)(2,1)S(1)}, u32[]{:S(2)}, u32[]{:S(2)}) collective-permute-start(f16[2,8,3072]{2,1,0:T(8,128)(2,1)S(1)} %fusion.6), channel_id=1, source_target_pairs={{0,16},{1,9},{2,18},{3,11},{4,20},{5,13},{6,22},{7,15},{8,24},{9,1... | collective-permute-start | bytes 294920 | tf_op jit(solution)/shard_map/ppermute | solution.py:23
  23.9 2.6 %collective-permute-done.3 = f16[2,8,3072]{2,1,0:T(8,128)(2,1)S(1)} collective-permute-done((f16[2,8,3072]{2,1,0:T(8,128)(2,1)S(1)}, f16[2,8,3072]{2,1,0:T(8,128)(2,1)S(1)}, u32[]{:S(2)}, u32[]{:S(2)}) %collective-permute-start.3) | collective-permute-done | bytes 98336 | tf_op jit(solution)/shard_map/ppermute | solution.py:23
  26.5 3.2 %collective-permute-start.4 = (f16[8,3072]{1,0:T(8,128)(2,1)S(1)}, f16[8,3072]{1,0:T(8,128)(2,1)S(1)}, u32[]{:S(2)}, u32[]{:S(2)}) collective-permute-start(f16[8,3072]{1,0:T(8,128)(2,1)S(1)} %fusion.12), channel_id=1, source_target_pairs={{0,8},{1,17},{2,10},{3,19},{4,12},{5,21},{6,14},{7,23},{8,0},{9,25... | collective-permute-start | bytes 147464 | tf_op jit(solution)/shard_map/ppermute | solution.py:23
  29.7 2.1 %collective-permute-done.4 = f16[8,3072]{1,0:T(8,128)(2,1)S(1)} collective-permute-done((f16[8,3072]{1,0:T(8,128)(2,1)S(1)}, f16[8,3072]{1,0:T(8,128)(2,1)S(1)}, u32[]{:S(2)}, u32[]{:S(2)}) %collective-permute-start.4) | collective-permute-done | bytes 49184 | tf_op jit(solution)/shard_map/ppermute | solution.py:23
  31.9 0.1 collective-permute-start.5
  32.0 1.2 %collective-permute-done.5 = f32[4,3072]{1,0:T(4,128)S(1)} collective-permute-done((f32[4,3072]{1,0:T(4,128)S(1)}, f32[4,3072]{1,0:T(4,128)S(1)}, u32[]{:S(2)}, u32[]{:S(2)}) %collective-permute-start.5) | collective-permute-done | bytes 49184 | tf_op jit(solution)/shard_map/ppermute | solution.py:23
  33.2 0.8 %convert_bitcast_fusion = (bf16[1,4,6144]{2,1,0:T(4,128)(2,1)S(1)}, f32[4,6144]{1,0:T(4,128)S(1)}, f32[4,6144]{1,0:T(4,128)}, f32[4,6144]{1,0:T(4,128)}, f32[4,6144]{1,0:T(4,128)}) fusion(f32[4,6144]{1,0:T(4,128)S(1)} %copy-done.3, f32[4,6144]{1,0:T(4,128)S(1)} %copy-done.4, f32[4,6144]{1,0:T(4,128)S(1)} %copy-done.5, f32[4,3072]{1,0:T(4,128)S(1)} %get-tuple-element.15, ...), kind=kLoop, calls=%fused_computation.47 | loop fusion | flops 417792 | bytes 835584 | tf_op jit(solution)/shard_map/broadcast_in_dim | solution.py:80
  34.1 3.4 %collective-permute-start.6 = (bf16[1,4,6144]{2,1,0:T(4,128)(2,1)S(1)}, bf16[1,4,6144]{2,1,0:T(4,128)(2,1)S(1)}, u32[]{:S(2)}, u32[]{:S(2)}) collective-permute-start(bf16[1,4,6144]{2,1,0:T(4,128)(2,1)S(1)} %get-tuple-element.5), channel_id=1, source_target_pairs={{0,16},{1,17},{2,18},{3,19},{4,20},{5,21},{6,22},{7,23},{8,24},{9,... | collective-permute-start | bytes 147464 | tf_op jit(solution)/shard_map/ppermute | solution.py:23
  37.4 0.1 broadcast_in_dim.6
  37.6 1.9 %collective-permute-done.6 = bf16[1,4,6144]{2,1,0:T(4,128)(2,1)S(1)} collective-permute-done((bf16[1,4,6144]{2,1,0:T(4,128)(2,1)S(1)}, bf16[1,4,6144]{2,1,0:T(4,128)(2,1)S(1)}, u32[]{:S(2)}, u32[]{:S(2)}) %collective-permute-start.6) | collective-permute-done | bytes 49184 | tf_op jit(solution)/shard_map/ppermute | solution.py:23
  39.5 0.1 pad_maximum_fusion.2
  39.6 2.1 %collective-permute-start.7 = (bf16[2,4,6144]{2,1,0:T(4,128)(2,1)S(1)}, bf16[2,4,6144]{2,1,0:T(4,128)(2,1)S(1)}, u32[]{:S(2)}, u32[]{:S(2)}) collective-permute-start(bf16[2,4,6144]{2,1,0:T(4,128)(2,1)S(1)} %pad_maximum_fusion.2), channel_id=1, source_target_pairs={{0,8},{1,5},{2,10},{3,7},{4,12},{5,1},{6,14},{7,3},{8,0},{9,13},{1... | collective-permute-start | bytes 294920 | tf_op jit(solution)/shard_map/ppermute | solution.py:23
  41.7 2.6 %collective-permute-done.7 = bf16[2,4,6144]{2,1,0:T(4,128)(2,1)S(1)} collective-permute-done((bf16[2,4,6144]{2,1,0:T(4,128)(2,1)S(1)}, bf16[2,4,6144]{2,1,0:T(4,128)(2,1)S(1)}, u32[]{:S(2)}, u32[]{:S(2)}) %collective-permute-start.7) | collective-permute-done | bytes 98336 | tf_op jit(solution)/shard_map/ppermute | solution.py:23
  44.3 0.1 pad_maximum_fusion
  44.4 1.6 %collective-permute-start.8 = (bf16[4,4,6144]{2,1,0:T(4,128)(2,1)S(1)}, bf16[4,4,6144]{2,1,0:T(4,128)(2,1)S(1)}, u32[]{:S(2)}, u32[]{:S(2)}) collective-permute-start(bf16[4,4,6144]{2,1,0:T(4,128)(2,1)S(1)} %pad_maximum_fusion), channel_id=1, source_target_pairs={{0,4},{1,9},{2,6},{3,11},{4,0},{5,13},{6,2},{7,15},{8,12},{9,1},{1... | collective-permute-start | bytes 589832 | tf_op jit(solution)/shard_map/ppermute | solution.py:23
  46.1 4.1 %collective-permute-done.8 = bf16[4,4,6144]{2,1,0:T(4,128)(2,1)S(1)} collective-permute-done((bf16[4,4,6144]{2,1,0:T(4,128)(2,1)S(1)}, bf16[4,4,6144]{2,1,0:T(4,128)(2,1)S(1)}, u32[]{:S(2)}, u32[]{:S(2)}) %collective-permute-start.8) | collective-permute-done | bytes 196640 | tf_op jit(solution)/shard_map/ppermute | solution.py:23
  50.3 0.0 copy-start.1
  50.3 0.7 %copy-done.1 = bf16[4,49152]{1,0:T(4,128)(2,1)} copy-done((bf16[4,49152]{1,0:T(4,128)(2,1)}, bf16[4,49152]{1,0:T(4,128)(2,1)S(1)}, u32[]{:S(2)}) %copy-start.1) | copy-done | bytes 393240
  (25 shorter events, 0.4 us)
Async XLA Ops:
  0.6 3.9 %copy-start = (bf16[1,1,16,49152]{3,2,1,0:T(8,128)(2,1)S(1)}, bf16[1,1,16,49152]{3,2,1,0:T(8,128)(2,1)}, u32[]{:S(2)}) copy-start(bf16[1,1,16,49152]{3,2,1,0:T(8,128)(2,1)} %param.4) | copy-start | bytes 4718596
  2.0 2.6 %collective-permute-start = (bf16[2,4,2,8,3072]{4,3,2,1,0:T(8,128)(2,1)S(1)}, bf16[2,4,2,8,3072]{4,3,2,1,0:T(8,128)(2,1)}, u32[]{:S(2)}, u32[]{:S(2)}) collective-permute-start(bf16[2,4,2,8,3072]{4,3,2,1,0:T(8,128)(2,1)S(1)} %dynamic-slice_bitcast_fusion), channel_id=1, source_target_pairs={{0,1},{1,0},{2,3},{3,2},{4,5},{5,4},{6,7},{7,6},{8,9},{9,8},{10,11... | collective-permute-start | bytes 2359304 | tf_op jit(solution)/shard_map/ppermute | solution.py:23
  6.0 8.7 %collective-permute-start.1 = (f16[2,4,8,3072]{3,2,1,0:T(8,128)(2,1)S(1)}, f16[2,4,8,3072]{3,2,1,0:T(8,128)(2,1)S(1)}, u32[]{:S(2)}, u32[]{:S(2)}) collective-permute-start(f16[2,4,8,3072]{3,2,1,0:T(8,128)(2,1)S(1)} %fusion), channel_id=1, source_target_pairs={{0,2},{1,5},{2,0},{3,7},{4,6},{5,1},{6,4},{7,3},{8,10},{9,13},{10,... | collective-permute-start | bytes 1179656 | tf_op jit(solution)/shard_map/ppermute | solution.py:23
  14.8 5.8 %collective-permute-start.2 = (f16[4,8,3072]{2,1,0:T(8,128)(2,1)S(1)}, f16[4,8,3072]{2,1,0:T(8,128)(2,1)S(1)}, u32[]{:S(2)}, u32[]{:S(2)}) collective-permute-start(f16[4,8,3072]{2,1,0:T(8,128)(2,1)S(1)} %fusion.3), channel_id=1, source_target_pairs={{0,4},{1,3},{2,6},{3,1},{4,0},{5,7},{6,2},{7,5},{8,12},{9,11},{10,... | collective-permute-start | bytes 589832 | tf_op jit(solution)/shard_map/ppermute | solution.py:23
  17.0 16.2 %copy-start.3 = (f32[4,6144]{1,0:T(4,128)S(1)}, f32[4,6144]{1,0:T(4,128)}, u32[]{:S(2)}) copy-start(f32[4,6144]{1,0:T(4,128)} %param.5) | copy-start | bytes 294916
  17.0 16.2 %copy-start.4 = (f32[4,6144]{1,0:T(4,128)S(1)}, f32[4,6144]{1,0:T(4,128)}, u32[]{:S(2)}) copy-start(f32[4,6144]{1,0:T(4,128)} %param.6) | copy-start | bytes 294916
  17.0 16.2 %copy-start.5 = (f32[4,6144]{1,0:T(4,128)S(1)}, f32[4,6144]{1,0:T(4,128)}, u32[]{:S(2)}) copy-start(f32[4,6144]{1,0:T(4,128)} %param.7) | copy-start | bytes 294916
  20.7 5.8 %collective-permute-start.3 = (f16[2,8,3072]{2,1,0:T(8,128)(2,1)S(1)}, f16[2,8,3072]{2,1,0:T(8,128)(2,1)S(1)}, u32[]{:S(2)}, u32[]{:S(2)}) collective-permute-start(f16[2,8,3072]{2,1,0:T(8,128)(2,1)S(1)} %fusion.6), channel_id=1, source_target_pairs={{0,16},{1,9},{2,18},{3,11},{4,20},{5,13},{6,22},{7,15},{8,24},{9,1... | collective-permute-start | bytes 294920 | tf_op jit(solution)/shard_map/ppermute | solution.py:23
  26.5 5.2 %collective-permute-start.4 = (f16[8,3072]{1,0:T(8,128)(2,1)S(1)}, f16[8,3072]{1,0:T(8,128)(2,1)S(1)}, u32[]{:S(2)}, u32[]{:S(2)}) collective-permute-start(f16[8,3072]{1,0:T(8,128)(2,1)S(1)} %fusion.12), channel_id=1, source_target_pairs={{0,8},{1,17},{2,10},{3,19},{4,12},{5,21},{6,14},{7,23},{8,0},{9,25... | collective-permute-start | bytes 147464 | tf_op jit(solution)/shard_map/ppermute | solution.py:23
  31.9 1.3 %collective-permute-start.5 = (f32[4,3072]{1,0:T(4,128)S(1)}, f32[4,3072]{1,0:T(4,128)S(1)}, u32[]{:S(2)}, u32[]{:S(2)}) collective-permute-start(f32[4,3072]{1,0:T(4,128)S(1)} %dynamic-slice_bitcast_fusion.3), channel_id=1, source_target_pairs={{0,1},{1,0},{2,3},{3,2},{4,5},{5,4},{6,7},{7,6},{8,9},{9,8},{10,11... | collective-permute-start | bytes 147464 | tf_op jit(solution)/shard_map/ppermute | solution.py:23
  34.1 16.2 %copy-start.2 = (f32[4,6144]{1,0:T(4,128)}, f32[4,6144]{1,0:T(4,128)S(1)}, u32[]{:S(2)}) copy-start(f32[4,6144]{1,0:T(4,128)S(1)} %get-tuple-element.6) | copy-start | bytes 294916
  34.1 5.4 %collective-permute-start.6 = (bf16[1,4,6144]{2,1,0:T(4,128)(2,1)S(1)}, bf16[1,4,6144]{2,1,0:T(4,128)(2,1)S(1)}, u32[]{:S(2)}, u32[]{:S(2)}) collective-permute-start(bf16[1,4,6144]{2,1,0:T(4,128)(2,1)S(1)} %get-tuple-element.5), channel_id=1, source_target_pairs={{0,16},{1,17},{2,18},{3,19},{4,20},{5,21},{6,22},{7,23},{8,24},{9,... | collective-permute-start | bytes 147464 | tf_op jit(solution)/shard_map/ppermute | solution.py:23
  39.6 4.7 %collective-permute-start.7 = (bf16[2,4,6144]{2,1,0:T(4,128)(2,1)S(1)}, bf16[2,4,6144]{2,1,0:T(4,128)(2,1)S(1)}, u32[]{:S(2)}, u32[]{:S(2)}) collective-permute-start(bf16[2,4,6144]{2,1,0:T(4,128)(2,1)S(1)} %pad_maximum_fusion.2), channel_id=1, source_target_pairs={{0,8},{1,5},{2,10},{3,7},{4,12},{5,1},{6,14},{7,3},{8,0},{9,13},{1... | collective-permute-start | bytes 294920 | tf_op jit(solution)/shard_map/ppermute | solution.py:23
  44.4 5.7 %collective-permute-start.8 = (bf16[4,4,6144]{2,1,0:T(4,128)(2,1)S(1)}, bf16[4,4,6144]{2,1,0:T(4,128)(2,1)S(1)}, u32[]{:S(2)}, u32[]{:S(2)}) collective-permute-start(bf16[4,4,6144]{2,1,0:T(4,128)(2,1)S(1)} %pad_maximum_fusion), channel_id=1, source_target_pairs={{0,4},{1,9},{2,6},{3,11},{4,0},{5,13},{6,2},{7,15},{8,12},{9,1},{1... | collective-permute-start | bytes 589832 | tf_op jit(solution)/shard_map/ppermute | solution.py:23
  50.3 0.7 %copy-start.1 = (bf16[4,49152]{1,0:T(4,128)(2,1)}, bf16[4,49152]{1,0:T(4,128)(2,1)S(1)}, u32[]{:S(2)}) copy-start(bf16[4,49152]{1,0:T(4,128)(2,1)S(1)} %fusion.13) | copy-start | bytes 1179652

commit v4 on v3

--- a/solution.py
+++ b/solution.py
@@ -60,12 +60,9 @@
     send = column(x ^ y_first, y ^ x_first) + got[1]
     quad = keep + widen(swap(narrow(send), Y, X))
 
-    first = jnp.where(core == 0, 2, 1)
-    sent = narrow(jnp.stack([pick(quad, z ^ first), pick(quad, z ^ 3)]))
-    got = widen(swap(sent, Z_FAR, Z_NEAR))
-    keep = pick(quad, z) + got[0]
-    send = pick(quad, z ^ 3 ^ first) + got[1]
-    total = keep + widen(swap(narrow(send), Z_NEAR, Z_FAR))
+    total = pick(quad, z)
+    for step, flip in ((3, Z_FAR + Z_NEAR), (2, Z_FAR), (1, Z_NEAR)):
+        total = total + widen(swap(narrow(pick(quad, z ^ step)), flip, flip))
 
     by_core = total.reshape(2, tile // 2, half)
     own, other = pick(by_core, core), swap(pick(by_core, 1 - core), CORE, CORE)
@@ -75,16 +72,8 @@
 
 def gather_blocks(mine):
     row_block, col_block = mine.shape
-    me, core = lax.axis_index("hst"), lax.axis_index("local") % 2
-    near = jnp.where(core == 0, 2, 1)
-    blocks, place = mine[None], [me]
-    for flips, bit in (((Z_FAR, Z_FAR), 4), ((Z_NEAR, Y), near), ((Y, Z_NEAR), 3 - near)):
-        blocks = jnp.concatenate([blocks, swap(blocks, *flips)])
-        place = place + [p ^ bit for p in place]
-    whole = jnp.zeros((row_block, 8 * col_block), mine.dtype)
-    for i, p in enumerate(place):
-        whole = lax.dynamic_update_slice_in_dim(whole, blocks[i], p * col_block, 1)
-    return whole
+    whole = lax.all_gather(mine, "hst", axis=0, tiled=False)
+    return whole.transpose(1, 0, 2).reshape(row_block, 8 * col_block)
 
 
 def reduce_general(gradient):

time: 51.2 us -> 64.2 us (1.25)
  blocking collectives: 0 us -> 31 us
  waiting for transfers between devices: 25.8 us -> 17 us
  starting transfers between devices: 19 us -> 10.4 us
    all_gather x0 -> x1, blocking collectives: none -> 31 us  [gather_blocks(): whole = lax.all_gather(mine, 'hst', axis=0, tiled=False)]
    ppermute x9 -> x7, waiting for transfers between devices: 25.8 us -> 17 us  [swap(): return lax.ppermute(value, ('hst', 'local'), flip_pairs(flips))]
    ppermute x9 -> x7, starting transfers between devices: 19 us -> 10.4 us  [swap(): return lax.ppermute(value, ('hst', 'local'), flip_pairs(flips))]
    unnamed x0 -> x1, other arithmetic: none -> 0.87 us
    broadcast_in_dim x1 -> x0, other arithmetic: 0.84 us -> none  [gather_blocks(): blocks, place = (mine[None], [me])]
  transfers between devices with their start and end apart: 9 -> 7, of which waited for: 9 -> 7; matrix products, arithmetic and copies ran while one was open for 0% -> 0% of each run, Pallas kernels for 0% -> 0%
where the time goes in v4:
time: 64.2 us; the launch traced here: 64 us
  blocking collectives  31 us (48%)
  waiting for transfers between devices  17 us (26%)
  starting transfers between devices  10.4 us (16%)
  other arithmetic  2.55 us (4%)
  local copies, waits for them, and re-layouts  2.19 us (3%)
  between operations  0.81 us (1%)
    all_gather x1, blocking collectives, gather_blocks(): whole = lax.all_gather(mine, 'hst', axis=0, tiled=False)  31 us
    ppermute x7, waiting for transfers between devices, swap(): return lax.ppermute(value, ('hst', 'local'), flip_pairs(flips))  17 us
    ppermute x7, starting transfers between devices, swap(): return lax.ppermute(value, ('hst', 'local'), flip_pairs(flips))  10.4 us
    squeeze x2, local copies, waits for them, and re-layouts, pick(): return lax.dynamic_index_in_dim(value, index, 0, keepdims=False)  1.33 us
    add x1, other arithmetic, reduce_blocks(): pair = pick(split, core).astype(jnp.float32) + other.astype(jnp.float32)  1.32 us
  transfers between devices with their start and end apart: 7, of which 7 were waited for; matrix products, arithmetic and copies ran while one was open for 0% of the time, Pallas kernels for 0%

profile of v4, /device:TPU:0, one launch (start us, length us, event | category | flops | bytes accessed | tf_op | source)
XLA Modules:
  0.0 64.0 jit_solution(10673251792516531263)
XLA Ops:
  0.6 0.0 copy-start
  0.7 1.3 %dynamic-slice_bitcast_fusion = bf16[2,4,2,8,3072]{4,3,2,1,0:T(8,128)(2,1)S(1)} fusion(bf16[2,4,2,2,8,3072]{5,4,3,2,1,0:T(8,128)(2,1)} %bitcast.55, s32[]{:T(128)S(6)} %select_n.80), kind=kLoop, calls=%fused_computation.4 | loop fusion | bytes 1572868 | tf_op jit(solution)/shard_map/jit(dynamic_index_in_dim)/squeeze | solution.py:35
  2.0 0.5 collective-permute-start
  2.5 2.0 %collective-permute-done = bf16[2,4,2,8,3072]{4,3,2,1,0:T(8,128)(2,1)} collective-permute-done((bf16[2,4,2,8,3072]{4,3,2,1,0:T(8,128)(2,1)S(1)}, bf16[2,4,2,8,3072]{4,3,2,1,0:T(8,128)(2,1)}, u32[]{:S(2)}, u32[]{:S(2)}) %collective-permute-start) | collective-permute-done | bytes 786464 | tf_op jit(solution)/shard_map/ppermute | solution.py:23
  4.5 0.0 copy-done
  4.5 1.3 %convert_add_fusion = f32[2,4,2,8,3072]{4,3,2,1,0:T(8,128)S(1)} fusion(bf16[2,4,2,8,3072]{4,3,2,1,0:T(8,128)(2,1)} %collective-permute-done, bf16[2,4,2,2,8,3072]{5,4,3,2,1,0:T(8,128)(2,1)S(1)} %bitcast.56, s32[]{:T(128)S(6)} %select_n.79), kind=kLoop, calls=%fused_computation | loop fusion | flops 1179648 | bytes 3145732 | tf_op jit(solution)/shard_map/add | solution.py:51
  5.9 0.1 dynamic-slice_bitcast_fusion.2
  5.9 0.1 fusion
  6.0 2.9 %collective-permute-start.1 = (f16[2,4,8,3072]{3,2,1,0:T(8,128)(2,1)S(1)}, f16[2,4,8,3072]{3,2,1,0:T(8,128)(2,1)S(1)}, u32[]{:S(2)}, u32[]{:S(2)}) collective-permute-start(f16[2,4,8,3072]{3,2,1,0:T(8,128)(2,1)S(1)} %fusion), channel_id=1, source_target_pairs={{0,2},{1,5},{2,0},{3,7},{4,6},{5,1},{6,4},{7,3},{8,10},{9,13},{10,... | collective-permute-start | bytes 1179656 | tf_op jit(solution)/shard_map/ppermute | solution.py:23
  8.9 5.8 %collective-permute-done.1 = f16[2,4,8,3072]{3,2,1,0:T(8,128)(2,1)S(1)} collective-permute-done((f16[2,4,8,3072]{3,2,1,0:T(8,128)(2,1)S(1)}, f16[2,4,8,3072]{3,2,1,0:T(8,128)(2,1)S(1)}, u32[]{:S(2)}, u32[]{:S(2)}) %collective-permute-start.1) | collective-permute-done | bytes 393248 | tf_op jit(solution)/shard_map/ppermute | solution.py:23
  14.7 0.1 convert_multiply_fusion
  14.8 0.1 fusion.3
  14.8 0.0 copy-start.1
  14.9 0.0 copy-start.2
  14.9 0.0 copy-start.3
  14.9 2.1 %collective-permute-start.2 = (f16[4,8,3072]{2,1,0:T(8,128)(2,1)S(1)}, f16[4,8,3072]{2,1,0:T(8,128)(2,1)S(1)}, u32[]{:S(2)}, u32[]{:S(2)}) collective-permute-start(f16[4,8,3072]{2,1,0:T(8,128)(2,1)S(1)} %fusion.3), channel_id=1, source_target_pairs={{0,4},{1,3},{2,6},{3,1},{4,0},{5,7},{6,2},{7,5},{8,12},{9,11},{10,... | collective-permute-start | bytes 589832 | tf_op jit(solution)/shard_map/ppermute | solution.py:23
  17.0 3.6 %collective-permute-done.2 = f16[4,8,3072]{2,1,0:T(8,128)(2,1)S(1)} collective-permute-done((f16[4,8,3072]{2,1,0:T(8,128)(2,1)S(1)}, f16[4,8,3072]{2,1,0:T(8,128)(2,1)S(1)}, u32[]{:S(2)}, u32[]{:S(2)}) %collective-permute-start.2) | collective-permute-done | bytes 196640 | tf_op jit(solution)/shard_map/ppermute | solution.py:23
  20.7 0.1 fusion.5
  20.8 4.2 %collective-permute-start.3 = (f16[8,3072]{1,0:T(8,128)(2,1)S(1)}, f16[8,3072]{1,0:T(8,128)(2,1)S(1)}, u32[]{:S(2)}, u32[]{:S(2)}) collective-permute-start(f16[8,3072]{1,0:T(8,128)(2,1)S(1)} %get-tuple-element.12), channel_id=1, source_target_pairs={{0,24},{1,25},{2,26},{3,27},{4,28},{5,29},{6,30},{7,31},{8,16},{9,... | collective-permute-start | bytes 147464 | tf_op jit(solution)/shard_map/ppermute | solution.py:23
  24.9 0.0 collective-permute-start.5
  24.9 0.6 collective-permute-start.4
  25.6 1.5 %collective-permute-done.3 = f16[8,3072]{1,0:T(8,128)(2,1)S(1)} collective-permute-done((f16[8,3072]{1,0:T(8,128)(2,1)S(1)}, f16[8,3072]{1,0:T(8,128)(2,1)S(1)}, u32[]{:S(2)}, u32[]{:S(2)}) %collective-permute-start.3) | collective-permute-done | bytes 49184 | tf_op jit(solution)/shard_map/ppermute | solution.py:23
  27.0 2.0 %collective-permute-done.5 = f16[8,3072]{1,0:T(8,128)(2,1)S(1)} collective-permute-done((f16[8,3072]{1,0:T(8,128)(2,1)S(1)}, f16[8,3072]{1,0:T(8,128)(2,1)S(1)}, u32[]{:S(2)}, u32[]{:S(2)}) %collective-permute-start.5) | collective-permute-done | bytes 49184 | tf_op jit(solution)/shard_map/ppermute | solution.py:23
  29.0 0.9 %collective-permute-done.4 = f16[8,3072]{1,0:T(8,128)(2,1)S(1)} collective-permute-done((f16[8,3072]{1,0:T(8,128)(2,1)S(1)}, f16[8,3072]{1,0:T(8,128)(2,1)S(1)}, u32[]{:S(2)}, u32[]{:S(2)}) %collective-permute-start.4) | collective-permute-done | bytes 49184 | tf_op jit(solution)/shard_map/ppermute | solution.py:23
  30.0 0.1 collective-permute-start.6
  30.1 1.2 %collective-permute-done.6 = f32[4,3072]{1,0:T(4,128)S(1)} collective-permute-done((f32[4,3072]{1,0:T(4,128)S(1)}, f32[4,3072]{1,0:T(4,128)S(1)}, u32[]{:S(2)}, u32[]{:S(2)}) %collective-permute-start.6) | collective-permute-done | bytes 49184 | tf_op jit(solution)/shard_map/ppermute | solution.py:23
  31.3 0.0 copy-done.1
  31.3 0.0 copy-done.2
  31.4 0.0 copy-done.3
  31.4 0.9 %convert_bitcast_fusion = (bf16[1,4,6144]{2,1,0:T(4,128)(2,1)S(1)}, f32[4,6144]{1,0:T(4,128)}, f32[4,6144]{1,0:T(4,128)}, f32[4,6144]{1,0:T(4,128)}, f32[4,6144]{1,0:T(4,128)}) fusion(f32[4,6144]{1,0:T(4,128)S(1)} %copy-done.1, f32[4,6144]{1,0:T(4,128)S(1)} %copy-done.2, f32[4,6144]{1,0:T(4,128)S(1)} %copy-done.3, f32[4,3072]{1,0:T(4,128)S(1)} %get-tuple-element.16, ...), kind=kLoop, calls=%fused_computation.30 | loop fusion | flops 417792 | bytes 835584
  32.2 31.0 %all-gather.1 = bf16[8,4,6144]{2,1,0:T(4,128)(2,1)S(1)} all-gather(bf16[1,4,6144]{2,1,0:T(4,128)(2,1)S(1)} %get-tuple-element.5), channel_id=2, replica_groups=mesh['hst'=8,'local'=4] {'hst'}, dimensions={0}, use_global_device_ids=true | all-gather | bytes 442368 | tf_op jit(solution)/shard_map/all_gather | solution.py:75
  63.2 0.7 %copy.11 = bf16[4,49152]{1,0:T(4,128)(2,1)} copy(bf16[4,49152]{1,0:T(4,128)(2,1)S(1)} %bitcast.54) | data formatting | bytes 786432
  (5 shorter events, 0.1 us)
Async XLA Ops:
  0.6 3.9 %copy-start = (bf16[1,1,16,49152]{3,2,1,0:T(8,128)(2,1)S(1)}, bf16[1,1,16,49152]{3,2,1,0:T(8,128)(2,1)}, u32[]{:S(2)}) copy-start(bf16[1,1,16,49152]{3,2,1,0:T(8,128)(2,1)} %param.4) | copy-start | bytes 4718596
  2.0 2.6 %collective-permute-start = (bf16[2,4,2,8,3072]{4,3,2,1,0:T(8,128)(2,1)S(1)}, bf16[2,4,2,8,3072]{4,3,2,1,0:T(8,128)(2,1)}, u32[]{:S(2)}, u32[]{:S(2)}) collective-permute-start(bf16[2,4,2,8,3072]{4,3,2,1,0:T(8,128)(2,1)S(1)} %dynamic-slice_bitcast_fusion), channel_id=1, source_target_pairs={{0,1},{1,0},{2,3},{3,2},{4,5},{5,4},{6,7},{7,6},{8,9},{9,8},{10,11... | collective-permute-start | bytes 2359304 | tf_op jit(solution)/shard_map/ppermute | solution.py:23
  6.0 8.7 %collective-permute-start.1 = (f16[2,4,8,3072]{3,2,1,0:T(8,128)(2,1)S(1)}, f16[2,4,8,3072]{3,2,1,0:T(8,128)(2,1)S(1)}, u32[]{:S(2)}, u32[]{:S(2)}) collective-permute-start(f16[2,4,8,3072]{3,2,1,0:T(8,128)(2,1)S(1)} %fusion), channel_id=1, source_target_pairs={{0,2},{1,5},{2,0},{3,7},{4,6},{5,1},{6,4},{7,3},{8,10},{9,13},{10,... | collective-permute-start | bytes 1179656 | tf_op jit(solution)/shard_map/ppermute | solution.py:23
  14.8 16.5 %copy-start.1 = (f32[4,6144]{1,0:T(4,128)S(1)}, f32[4,6144]{1,0:T(4,128)}, u32[]{:S(2)}) copy-start(f32[4,6144]{1,0:T(4,128)} %param.5) | copy-start | bytes 294916
  14.9 16.5 %copy-start.2 = (f32[4,6144]{1,0:T(4,128)S(1)}, f32[4,6144]{1,0:T(4,128)}, u32[]{:S(2)}) copy-start(f32[4,6144]{1,0:T(4,128)} %param.6) | copy-start | bytes 294916
  14.9 16.5 %copy-start.3 = (f32[4,6144]{1,0:T(4,128)S(1)}, f32[4,6144]{1,0:T(4,128)}, u32[]{:S(2)}) copy-start(f32[4,6144]{1,0:T(4,128)} %param.7) | copy-start | bytes 294916
  14.9 5.8 %collective-permute-start.2 = (f16[4,8,3072]{2,1,0:T(8,128)(2,1)S(1)}, f16[4,8,3072]{2,1,0:T(8,128)(2,1)S(1)}, u32[]{:S(2)}, u32[]{:S(2)}) collective-permute-start(f16[4,8,3072]{2,1,0:T(8,128)(2,1)S(1)} %fusion.3), channel_id=1, source_target_pairs={{0,4},{1,3},{2,6},{3,1},{4,0},{5,7},{6,2},{7,5},{8,12},{9,11},{10,... | collective-permute-start | bytes 589832 | tf_op jit(solution)/shard_map/ppermute | solution.py:23
  20.8 6.3 %collective-permute-start.3 = (f16[8,3072]{1,0:T(8,128)(2,1)S(1)}, f16[8,3072]{1,0:T(8,128)(2,1)S(1)}, u32[]{:S(2)}, u32[]{:S(2)}) collective-permute-start(f16[8,3072]{1,0:T(8,128)(2,1)S(1)} %get-tuple-element.12), channel_id=1, source_target_pairs={{0,24},{1,25},{2,26},{3,27},{4,28},{5,29},{6,30},{7,31},{8,16},{9,... | collective-permute-start | bytes 147464 | tf_op jit(solution)/shard_map/ppermute | solution.py:23
  24.9 4.1 %collective-permute-start.5 = (f16[8,3072]{1,0:T(8,128)(2,1)S(1)}, f16[8,3072]{1,0:T(8,128)(2,1)S(1)}, u32[]{:S(2)}, u32[]{:S(2)}) collective-permute-start(f16[8,3072]{1,0:T(8,128)(2,1)S(1)} %get-tuple-element.13), channel_id=1, source_target_pairs={{0,8},{1,9},{2,10},{3,11},{4,12},{5,13},{6,14},{7,15},{8,0},{9,1},... | collective-permute-start | bytes 147464 | tf_op jit(solution)/shard_map/ppermute | solution.py:23
  24.9 5.0 %collective-permute-start.4 = (f16[8,3072]{1,0:T(8,128)(2,1)S(1)}, f16[8,3072]{1,0:T(8,128)(2,1)S(1)}, u32[]{:S(2)}, u32[]{:S(2)}) collective-permute-start(f16[8,3072]{1,0:T(8,128)(2,1)S(1)} %get-tuple-element.14), channel_id=1, source_target_pairs={{0,16},{1,17},{2,18},{3,19},{4,20},{5,21},{6,22},{7,23},{8,24},{9,... | collective-permute-start | bytes 147464 | tf_op jit(solution)/shard_map/ppermute | solution.py:23
  30.0 1.3 %collective-permute-start.6 = (f32[4,3072]{1,0:T(4,128)S(1)}, f32[4,3072]{1,0:T(4,128)S(1)}, u32[]{:S(2)}, u32[]{:S(2)}) collective-permute-start(f32[4,3072]{1,0:T(4,128)S(1)} %dynamic-slice_bitcast_fusion.3), channel_id=1, source_target_pairs={{0,1},{1,0},{2,3},{3,2},{4,5},{5,4},{6,7},{7,6},{8,9},{9,8},{10,11... | collective-permute-start | bytes 147464 | tf_op jit(solution)/shard_map/ppermute | solution.py:23

commit v5 on v4

--- a/solution.py
+++ b/solution.py
@@ -47,22 +47,23 @@
 
     split = gradient.reshape(2, tile, 16, half).transpose(0, 2, 1, 3)
     split = split.reshape(2, 4, 2, 2, tile, half).transpose(3, 0, 1, 2, 4, 5)
-    other = swap(pick(split, 1 - core), CORE, CORE)
-    pair = pick(split, core).astype(jnp.float32) + other.astype(jnp.float32)
+    own, other = pick(split, core), swap(pick(split, 1 - core), CORE, CORE)
 
-    def column(i, j):
-        return lax.dynamic_slice(pair, (i, 0, j, 0, 0), (1, 4, 1, tile, half)).reshape(4, tile, half)
+    def part(value, i):
+        by_xy = lax.dynamic_slice(value, (i // 2, 0, i % 2, 0, 0), (1, 4, 1, tile, half))
+        by_z = lax.dynamic_slice(value, (0, i, 0, 0, 0), (2, 1, 2, tile, half))
+        return jnp.where(core == 0, by_xy.reshape(4, tile, half), by_z.reshape(4, tile, half))
 
-    x_first, y_first = 1 - core, core
-    sent = narrow(jnp.stack([column(x ^ x_first, y ^ y_first), column(1 - x, 1 - y)]))
-    got = widen(swap(sent, X, Y))
-    keep = column(x, y) + got[0]
-    send = column(x ^ y_first, y ^ x_first) + got[1]
-    quad = keep + widen(swap(narrow(send), Y, X))
+    def pair(i):
+        return part(own, i).astype(jnp.float32) + part(other, i).astype(jnp.float32)
 
-    total = pick(quad, z)
-    for step, flip in ((3, Z_FAR + Z_NEAR), (2, Z_FAR), (1, Z_NEAR)):
-        total = total + widen(swap(narrow(pick(quad, z ^ step)), flip, flip))
+    over_xy, over_z = (0, Y, X, X + Y), (0, Z_NEAR, Z_FAR, Z_NEAR + Z_FAR)
+    me = jnp.where(core == 0, 2 * x + y, z)
+    got = [swap(narrow(pair(me ^ d)), over_xy[d], over_z[d]) for d in (3, 2, 1)]
+    quarter = pair(me) + widen(got[0]) + widen(got[1]) + widen(got[2])
+    me = jnp.where(core == 0, z, 2 * x + y)
+    got = [swap(narrow(pick(quarter, me ^ d)), over_z[d], over_xy[d]) for d in (3, 2, 1)]
+    total = pick(quarter, me) + widen(got[0]) + widen(got[1]) + widen(got[2])
 
     by_core = total.reshape(2, tile // 2, half)
     own, other = pick(by_core, core), swap(pick(by_core, 1 - core), CORE, CORE)
@@ -72,8 +73,15 @@
 
 def gather_blocks(mine):
     row_block, col_block = mine.shape
-    whole = lax.all_gather(mine, "hst", axis=0, tiled=False)
-    return whole.transpose(1, 0, 2).reshape(row_block, 8 * col_block)
+    me = lax.axis_index("hst")
+    far = jnp.stack([mine, swap(mine, Z_FAR, Z_FAR)])
+    got = [(0, far)] + [(bits, swap(far, 4 * bits, 4 * bits)) for bits in (3, 2, 1)]
+    whole = jnp.zeros((row_block, 8 * col_block), mine.dtype)
+    for bits, blocks in got:
+        for i in (0, 1):
+            place = me ^ bits ^ (4 * i)
+            whole = lax.dynamic_update_slice_in_dim(whole, blocks[i], place * col_block, 1)
+    return whole
 
 
 def reduce_general(gradient):

time: 64.2 us -> 43.5 us (0.68)
  blocking collectives: 31 us -> 0 us
  waiting for transfers between devices: 17 us -> 22 us
  starting transfers between devices: 10.4 us -> 15.2 us
    all_gather x1 -> x0, blocking collectives: 31 us -> none  [gather_blocks(): whole = lax.all_gather(mine, 'hst', axis=0, tiled=False)]
    ppermute x7 -> x12, waiting for transfers between devices: 17 us -> 22 us  [swap(): return lax.ppermute(value, ('hst', 'local'), flip_pairs(flips))]
    ppermute x7 -> x12, starting transfers between devices: 10.4 us -> 15.2 us  [swap(): return lax.ppermute(value, ('hst', 'local'), flip_pairs(flips))]
    dynamic_update_slice x0 -> x1, other arithmetic: none -> 0.89 us  [gather_blocks(): lax.dynamic_update_slice_in_dim(whole, blocks[i], place * col_block, 1)]
    unnamed x1 -> x0, other arithmetic: 0.87 us -> none
    add x3 -> x2, other arithmetic: 1.41 us -> 1.31 us  [the longest x1 1.27 us: reduce_blocks(): quarter = pair(me) + widen(got[0]) + widen(got[1]) + widen(got[2])]
  transfers between devices with their start and end apart: 7 -> 12, of which waited for: 7 -> 11; matrix products, arithmetic and copies ran while one was open for 0% -> 1% of each run, Pallas kernels for 0% -> 0%
where the time goes in v5:
time: 43.5 us; the launch traced here: 43.3 us
  waiting for transfers between devices  22 us (51%)
  starting transfers between devices  15.2 us (35%)
  other arithmetic  2.78 us (6%)
  local copies, waits for them, and re-layouts  2.55 us (6%)
  between operations  0.81 us (2%)
    ppermute x12, waiting for transfers between devices, swap(): return lax.ppermute(value, ('hst', 'local'), flip_pairs(flips))  22 us
    ppermute x12, starting transfers between devices, swap(): return lax.ppermute(value, ('hst', 'local'), flip_pairs(flips))  15.2 us
    squeeze x2, local copies, waits for them, and re-layouts, pick(): return lax.dynamic_index_in_dim(value, index, 0, keepdims=False)  1.33 us
    add x1, other arithmetic, reduce_blocks(): quarter = pair(me) + widen(got[0]) + widen(got[1]) + widen(got[2])  1.27 us
    dynamic_update_slice x1, other arithmetic, gather_blocks(): lax.dynamic_update_slice_in_dim(whole, blocks[i], place * col_block, 1)  0.89 us
  transfers between devices with their start and end apart: 12, of which 11 were waited for; matrix products, arithmetic and copies ran while one was open for 1% of the time, Pallas kernels for 0%

profile of v5, /device:TPU:0, one launch (start us, length us, event | category | flops | bytes accessed | tf_op | source)
XLA Modules:
  0.0 43.3 jit_solution(18027255441761901323)
XLA Ops:
  0.7 1.3 %dynamic-slice_bitcast_fusion = bf16[2,4,2,8,3072]{4,3,2,1,0:T(8,128)(2,1)S(1)} fusion(bf16[2,4,2,2,8,3072]{5,4,3,2,1,0:T(8,128)(2,1)} %bitcast.98, s32[]{:T(128)S(6)} %select_n.251), kind=kLoop, calls=%fused_computation | loop fusion | bytes 1572868 | tf_op jit(solution)/shard_map/jit(dynamic_index_in_dim)/squeeze | solution.py:35
  2.0 0.5 %collective-permute-start = (bf16[2,4,2,8,3072]{4,3,2,1,0:T(8,128)(2,1)S(1)}, bf16[2,4,2,8,3072]{4,3,2,1,0:T(8,128)(2,1)S(1)}, u32[]{:S(2)}, u32[]{:S(2)}) collective-permute-start(bf16[2,4,2,8,3072]{4,3,2,1,0:T(8,128)(2,1)S(1)} %dynamic-slice_bitcast_fusion), channel_id=1, source_target_pairs={{0,1},{1,0},{2,3},{3,2},{4,5},{5,4},{6,7},{7,6},{8,9},{9,8},{10,11... | collective-permute-start | bytes 2359304 | tf_op jit(solution)/shard_map/ppermute | solution.py:23
  2.5 0.1 constant_dynamic-slice_fusion.7
  2.6 1.8 %collective-permute-done = bf16[2,4,2,8,3072]{4,3,2,1,0:T(8,128)(2,1)S(1)} collective-permute-done((bf16[2,4,2,8,3072]{4,3,2,1,0:T(8,128)(2,1)S(1)}, bf16[2,4,2,8,3072]{4,3,2,1,0:T(8,128)(2,1)S(1)}, u32[]{:S(2)}, u32[]{:S(2)}) %collective-permute-start) | collective-permute-done | bytes 786464 | tf_op jit(solution)/shard_map/ppermute | solution.py:23
  4.4 0.1 constant_dynamic-slice_fusion.6
  4.5 0.2 multiply_convert_fusion.1
  4.6 2.9 %collective-permute-start.2 = (f16[4,8,3072]{2,1,0:T(8,128)(2,1)S(1)}, f16[4,8,3072]{2,1,0:T(8,128)(2,1)S(1)}, u32[]{:S(2)}, u32[]{:S(2)}) collective-permute-start(f16[4,8,3072]{2,1,0:T(8,128)(2,1)S(1)} %multiply_convert_fusion.1), channel_id=1, source_target_pairs={{0,2},{1,17},{2,0},{3,19},{4,6},{5,21},{6,4},{7,23},{8,10},{9,25},... | collective-permute-start | bytes 589832 | tf_op jit(solution)/shard_map/ppermute | solution.py:23
  7.6 0.3 multiply_convert_fusion.2
  7.9 1.6 %collective-permute-start.1 = (f16[4,8,3072]{2,1,0:T(8,128)(2,1)S(1)}, f16[4,8,3072]{2,1,0:T(8,128)(2,1)}, u32[]{:S(2)}, u32[]{:S(2)}) collective-permute-start(f16[4,8,3072]{2,1,0:T(8,128)(2,1)S(1)} %get-tuple-element.11), channel_id=1, source_target_pairs={{0,6},{1,25},{2,4},{3,27},{4,2},{5,29},{6,0},{7,31},{8,14},{9,17},... | collective-permute-start | bytes 589832 | tf_op jit(solution)/shard_map/ppermute | solution.py:23
  9.4 0.1 collective-permute-start.3
  9.5 1.7 %collective-permute-done.2 = f16[4,8,3072]{2,1,0:T(8,128)(2,1)S(1)} collective-permute-done((f16[4,8,3072]{2,1,0:T(8,128)(2,1)S(1)}, f16[4,8,3072]{2,1,0:T(8,128)(2,1)S(1)}, u32[]{:S(2)}, u32[]{:S(2)}) %collective-permute-start.2) | collective-permute-done | bytes 196640 | tf_op jit(solution)/shard_map/ppermute | solution.py:23
  11.2 3.8 %collective-permute-done.1 = f16[4,8,3072]{2,1,0:T(8,128)(2,1)} collective-permute-done((f16[4,8,3072]{2,1,0:T(8,128)(2,1)S(1)}, f16[4,8,3072]{2,1,0:T(8,128)(2,1)}, u32[]{:S(2)}, u32[]{:S(2)}) %collective-permute-start.1) | collective-permute-done | bytes 196640 | tf_op jit(solution)/shard_map/ppermute | solution.py:23
  15.0 2.0 %collective-permute-done.3 = f16[4,8,3072]{2,1,0:T(8,128)(2,1)} collective-permute-done((f16[4,8,3072]{2,1,0:T(8,128)(2,1)S(1)}, f16[4,8,3072]{2,1,0:T(8,128)(2,1)}, u32[]{:S(2)}, u32[]{:S(2)}) %collective-permute-start.3) | collective-permute-done | bytes 196640 | tf_op jit(solution)/shard_map/ppermute | solution.py:23
  17.0 1.3 %multiply_add_fusion = f32[4,8,3072]{2,1,0:T(8,128)S(1)} fusion(f16[4,8,3072]{2,1,0:T(8,128)(2,1)} %collective-permute-done.3, f16[4,8,3072]{2,1,0:T(8,128)(2,1)S(1)} %collective-permute-done.2, f16[4,8,3072]{2,1,0:T(8,128)(2,1)} %collective-permute-done.1, bf16[2,1,2,8,3072]{4,3,2,1,0:T(8,128)(2,1)S(1)} %get-tuple-element.17, ...), kind=kLoop, calls=%fused_computation.1 | loop fusion | flops 1376256 | bytes 1769493 | tf_op jit(solution)/shard_map/add | solution.py:63
  18.4 3.7 %collective-permute-start.4 = (f16[8,3072]{1,0:T(8,128)(2,1)S(1)}, f16[8,3072]{1,0:T(8,128)(2,1)S(1)}, u32[]{:S(2)}, u32[]{:S(2)}) collective-permute-start(f16[8,3072]{1,0:T(8,128)(2,1)S(1)} %get-tuple-element.21), channel_id=1, source_target_pairs={{0,24},{1,7},{2,26},{3,5},{4,28},{5,3},{6,30},{7,1},{8,16},{9,15},... | collective-permute-start | bytes 147464 | tf_op jit(solution)/shard_map/ppermute | solution.py:23
  22.0 0.8 %collective-permute-start.6 = (f16[8,3072]{1,0:T(8,128)(2,1)S(1)}, f16[8,3072]{1,0:T(8,128)(2,1)S(1)}, u32[]{:S(2)}, u32[]{:S(2)}) collective-permute-start(f16[8,3072]{1,0:T(8,128)(2,1)S(1)} %get-tuple-element.22), channel_id=1, source_target_pairs={{0,8},{1,5},{2,10},{3,7},{4,12},{5,1},{6,14},{7,3},{8,0},{9,13},{1... | collective-permute-start | bytes 147464 | tf_op jit(solution)/shard_map/ppermute | solution.py:23
  22.8 1.5 %collective-permute-done.4 = f16[8,3072]{1,0:T(8,128)(2,1)S(1)} collective-permute-done((f16[8,3072]{1,0:T(8,128)(2,1)S(1)}, f16[8,3072]{1,0:T(8,128)(2,1)S(1)}, u32[]{:S(2)}, u32[]{:S(2)}) %collective-permute-start.4) | collective-permute-done | bytes 49184 | tf_op jit(solution)/shard_map/ppermute | solution.py:23
  24.3 2.7 %collective-permute-done.5 = f16[8,3072]{1,0:T(8,128)(2,1)S(1)} collective-permute-done((f16[8,3072]{1,0:T(8,128)(2,1)S(1)}, f16[8,3072]{1,0:T(8,128)(2,1)S(1)}, u32[]{:S(2)}, u32[]{:S(2)}) %collective-permute-start.5) | collective-permute-done | bytes 49184 | tf_op jit(solution)/shard_map/ppermute | solution.py:23
  27.1 0.1 collective-permute-start.7
  27.2 1.2 %collective-permute-done.7 = f32[4,3072]{1,0:T(4,128)S(1)} collective-permute-done((f32[4,3072]{1,0:T(4,128)S(1)}, f32[4,3072]{1,0:T(4,128)S(1)}, u32[]{:S(2)}, u32[]{:S(2)}) %collective-permute-start.7) | collective-permute-done | bytes 49184 | tf_op jit(solution)/shard_map/ppermute | solution.py:23
  28.4 0.1 broadcast_in_dim.3
  28.6 0.9 %constant_dynamic-update-slice_fusion.1 = (bf16[4,49152]{1,0:T(4,128)(2,1)S(1)}, bf16[4,6144]{1,0:T(4,128)(2,1)S(1)}, f32[4,6144]{1,0:T(4,128)}, f32[4,6144]{1,0...) fusion(bf16[4,49152]{1,0:T(4,128)(2,1)S(1)} %broadcast_in_dim.3, s32[]{:T(128)S(6)} %select_n.290, ...), kind=kLoop, calls=%fused_computation.44 | loop fusion | flops 417792 | bytes 884740 | tf_op jit(solution)/shard_map/dynamic_update_slice | solution.py:83
  29.5 2.0 %collective-permute-start.8 = (bf16[4,6144]{1,0:T(4,128)(2,1)S(1)}, bf16[4,6144]{1,0:T(4,128)(2,1)S(1)}, u32[]{:S(2)}, u32[]{:S(2)}) collective-permute-start(bf16[4,6144]{1,0:T(4,128)(2,1)S(1)} %get-tuple-element.6), channel_id=1, source_target_pairs={{0,16},{1,17},{2,18},{3,19},{4,20},{5,21},{6,22},{7,23},{8,24},{9,... | collective-permute-start | bytes 147464 | tf_op jit(solution)/shard_map/ppermute | solution.py:23
  31.5 3.3 %collective-permute-done.8 = bf16[4,6144]{1,0:T(4,128)(2,1)S(1)} collective-permute-done((bf16[4,6144]{1,0:T(4,128)(2,1)S(1)}, bf16[4,6144]{1,0:T(4,128)(2,1)S(1)}, u32[]{:S(2)}, u32[]{:S(2)}) %collective-permute-start.8) | collective-permute-done | bytes 49184 | tf_op jit(solution)/shard_map/ppermute | solution.py:23
  34.8 0.1 pad_maximum_fusion.1
  34.9 0.1 collective-permute-start.9
  35.0 2.2 %collective-permute-start.10 = (bf16[2,4,6144]{2,1,0:T(4,128)(2,1)S(1)}, bf16[2,4,6144]{2,1,0:T(4,128)(2,1)S(1)}, u32[]{:S(2)}, u32[]{:S(2)}) collective-permute-start(bf16[2,4,6144]{2,1,0:T(4,128)(2,1)S(1)} %pad_maximum_fusion.1), channel_id=1, source_target_pairs={{0,8},{1,9},{2,10},{3,11},{4,12},{5,13},{6,14},{7,15},{8,0},{9,1},... | collective-permute-start | bytes 294920 | tf_op jit(solution)/shard_map/ppermute | solution.py:23
  37.2 1.2 %collective-permute-start.11 = (bf16[2,4,6144]{2,1,0:T(4,128)(2,1)S(1)}, bf16[2,4,6144]{2,1,0:T(4,128)(2,1)S(1)}, u32[]{:S(2)}, u32[]{:S(2)}) collective-permute-start(bf16[2,4,6144]{2,1,0:T(4,128)(2,1)S(1)} %pad_maximum_fusion.1), channel_id=1, source_target_pairs={{0,4},{1,5},{2,6},{3,7},{4,0},{5,1},{6,2},{7,3},{8,12},{9,13},{10,... | collective-permute-start | bytes 294920 | tf_op jit(solution)/shard_map/ppermute | solution.py:23
  38.5 3.0 %collective-permute-done.9 = bf16[2,4,6144]{2,1,0:T(4,128)(2,1)S(1)} collective-permute-done((bf16[2,4,6144]{2,1,0:T(4,128)(2,1)S(1)}, bf16[2,4,6144]{2,1,0:T(4,128)(2,1)S(1)}, u32[]{:S(2)}, u32[]{:S(2)}) %collective-permute-start.9) | collective-permute-done | bytes 98336 | tf_op jit(solution)/shard_map/ppermute | solution.py:23
  41.5 0.3 collective-permute-done.10
  41.9 0.6 %collective-permute-done.11 = bf16[2,4,6144]{2,1,0:T(4,128)(2,1)S(1)} collective-permute-done((bf16[2,4,6144]{2,1,0:T(4,128)(2,1)S(1)}, bf16[2,4,6144]{2,1,0:T(4,128)(2,1)S(1)}, u32[]{:S(2)}, u32[]{:S(2)}) %collective-permute-start.11) | collective-permute-done | bytes 98336 | tf_op jit(solution)/shard_map/ppermute | solution.py:23
  42.6 0.7 %copy-done.1 = bf16[4,49152]{1,0:T(4,128)(2,1)} copy-done((bf16[4,49152]{1,0:T(4,128)(2,1)}, bf16[4,49152]{1,0:T(4,128)(2,1)S(1)}, u32[]{:S(2)}) %copy-start.1) | copy-done | bytes 393240
  (23 shorter events, 0.4 us)
Async XLA Ops:
  0.6 1.9 %copy-start = (bf16[1,1,16,49152]{3,2,1,0:T(8,128)(2,1)S(1)}, bf16[1,1,16,49152]{3,2,1,0:T(8,128)(2,1)}, u32[]{:S(2)}) copy-start(bf16[1,1,16,49152]{3,2,1,0:T(8,128)(2,1)} %param.4) | copy-start | bytes 4718596
  2.0 2.4 %collective-permute-start = (bf16[2,4,2,8,3072]{4,3,2,1,0:T(8,128)(2,1)S(1)}, bf16[2,4,2,8,3072]{4,3,2,1,0:T(8,128)(2,1)S(1)}, u32[]{:S(2)}, u32[]{:S(2)}) collective-permute-start(bf16[2,4,2,8,3072]{4,3,2,1,0:T(8,128)(2,1)S(1)} %dynamic-slice_bitcast_fusion), channel_id=1, source_target_pairs={{0,1},{1,0},{2,3},{3,2},{4,5},{5,4},{6,7},{7,6},{8,9},{9,8},{10,11... | collective-permute-start | bytes 2359304 | tf_op jit(solution)/shard_map/ppermute | solution.py:23
  4.6 6.6 %collective-permute-start.2 = (f16[4,8,3072]{2,1,0:T(8,128)(2,1)S(1)}, f16[4,8,3072]{2,1,0:T(8,128)(2,1)S(1)}, u32[]{:S(2)}, u32[]{:S(2)}) collective-permute-start(f16[4,8,3072]{2,1,0:T(8,128)(2,1)S(1)} %multiply_convert_fusion.1), channel_id=1, source_target_pairs={{0,2},{1,17},{2,0},{3,19},{4,6},{5,21},{6,4},{7,23},{8,10},{9,25},... | collective-permute-start | bytes 589832 | tf_op jit(solution)/shard_map/ppermute | solution.py:23
  7.9 7.1 %collective-permute-start.1 = (f16[4,8,3072]{2,1,0:T(8,128)(2,1)S(1)}, f16[4,8,3072]{2,1,0:T(8,128)(2,1)}, u32[]{:S(2)}, u32[]{:S(2)}) collective-permute-start(f16[4,8,3072]{2,1,0:T(8,128)(2,1)S(1)} %get-tuple-element.11), channel_id=1, source_target_pairs={{0,6},{1,25},{2,4},{3,27},{4,2},{5,29},{6,0},{7,31},{8,14},{9,17},... | collective-permute-start | bytes 589832 | tf_op jit(solution)/shard_map/ppermute | solution.py:23
  9.4 7.6 %collective-permute-start.3 = (f16[4,8,3072]{2,1,0:T(8,128)(2,1)S(1)}, f16[4,8,3072]{2,1,0:T(8,128)(2,1)}, u32[]{:S(2)}, u32[]{:S(2)}) collective-permute-start(f16[4,8,3072]{2,1,0:T(8,128)(2,1)S(1)} %get-tuple-element.12), channel_id=1, source_target_pairs={{0,4},{1,9},{2,6},{3,11},{4,0},{5,13},{6,2},{7,15},{8,12},{9,1},{1... | collective-permute-start | bytes 589832 | tf_op jit(solution)/shard_map/ppermute | solution.py:23
  17.0 11.5 %copy-start.2 = (f32[4,6144]{1,0:T(4,128)S(1)}, f32[4,6144]{1,0:T(4,128)}, u32[]{:S(2)}) copy-start(f32[4,6144]{1,0:T(4,128)} %param.5) | copy-start | bytes 294916
  17.0 11.5 %copy-start.3 = (f32[4,6144]{1,0:T(4,128)S(1)}, f32[4,6144]{1,0:T(4,128)}, u32[]{:S(2)}) copy-start(f32[4,6144]{1,0:T(4,128)} %param.6) | copy-start | bytes 294916
  18.3 10.3 %copy-start.4 = (f32[4,6144]{1,0:T(4,128)S(1)}, f32[4,6144]{1,0:T(4,128)}, u32[]{:S(2)}) copy-start(f32[4,6144]{1,0:T(4,128)} %param.7) | copy-start | bytes 294916
  18.4 6.0 %collective-permute-start.4 = (f16[8,3072]{1,0:T(8,128)(2,1)S(1)}, f16[8,3072]{1,0:T(8,128)(2,1)S(1)}, u32[]{:S(2)}, u32[]{:S(2)}) collective-permute-start(f16[8,3072]{1,0:T(8,128)(2,1)S(1)} %get-tuple-element.21), channel_id=1, source_target_pairs={{0,24},{1,7},{2,26},{3,5},{4,28},{5,3},{6,30},{7,1},{8,16},{9,15},... | collective-permute-start | bytes 147464 | tf_op jit(solution)/shard_map/ppermute | solution.py:23
  22.0 5.0 %collective-permute-start.5 = (f16[8,3072]{1,0:T(8,128)(2,1)S(1)}, f16[8,3072]{1,0:T(8,128)(2,1)S(1)}, u32[]{:S(2)}, u32[]{:S(2)}) collective-permute-start(f16[8,3072]{1,0:T(8,128)(2,1)S(1)} %get-tuple-element.23), channel_id=1, source_target_pairs={{0,16},{1,3},{2,18},{3,1},{4,20},{5,7},{6,22},{7,5},{8,24},{9,11},... | collective-permute-start | bytes 147464 | tf_op jit(solution)/shard_map/ppermute | solution.py:23
  22.0 5.0 %collective-permute-start.6 = (f16[8,3072]{1,0:T(8,128)(2,1)S(1)}, f16[8,3072]{1,0:T(8,128)(2,1)S(1)}, u32[]{:S(2)}, u32[]{:S(2)}) collective-permute-start(f16[8,3072]{1,0:T(8,128)(2,1)S(1)} %get-tuple-element.22), channel_id=1, source_target_pairs={{0,8},{1,5},{2,10},{3,7},{4,12},{5,1},{6,14},{7,3},{8,0},{9,13},{1... | collective-permute-start | bytes 147464 | tf_op jit(solution)/shard_map/ppermute | solution.py:23
  27.1 1.3 %collective-permute-start.7 = (f32[4,3072]{1,0:T(4,128)S(1)}, f32[4,3072]{1,0:T(4,128)S(1)}, u32[]{:S(2)}, u32[]{:S(2)}) collective-permute-start(f32[4,3072]{1,0:T(4,128)S(1)} %dynamic-slice_bitcast_fusion.1), channel_id=1, source_target_pairs={{0,1},{1,0},{2,3},{3,2},{4,5},{5,4},{6,7},{7,6},{8,9},{9,8},{10,11... | collective-permute-start | bytes 147464 | tf_op jit(solution)/shard_map/ppermute | solution.py:23
  29.5 5.3 %collective-permute-start.8 = (bf16[4,6144]{1,0:T(4,128)(2,1)S(1)}, bf16[4,6144]{1,0:T(4,128)(2,1)S(1)}, u32[]{:S(2)}, u32[]{:S(2)}) collective-permute-start(bf16[4,6144]{1,0:T(4,128)(2,1)S(1)} %get-tuple-element.6), channel_id=1, source_target_pairs={{0,16},{1,17},{2,18},{3,19},{4,20},{5,21},{6,22},{7,23},{8,24},{9,... | collective-permute-start | bytes 147464 | tf_op jit(solution)/shard_map/ppermute | solution.py:23
  34.9 6.6 %collective-permute-start.9 = (bf16[2,4,6144]{2,1,0:T(4,128)(2,1)S(1)}, bf16[2,4,6144]{2,1,0:T(4,128)(2,1)S(1)}, u32[]{:S(2)}, u32[]{:S(2)}) collective-permute-start(bf16[2,4,6144]{2,1,0:T(4,128)(2,1)S(1)} %pad_maximum_fusion.1), channel_id=1, source_target_pairs={{0,12},{1,13},{2,14},{3,15},{4,8},{5,9},{6,10},{7,11},{8,4},{9,5},... | collective-permute-start | bytes 294920 | tf_op jit(solution)/shard_map/ppermute | solution.py:23
  35.0 6.8 %collective-permute-start.10 = (bf16[2,4,6144]{2,1,0:T(4,128)(2,1)S(1)}, bf16[2,4,6144]{2,1,0:T(4,128)(2,1)S(1)}, u32[]{:S(2)}, u32[]{:S(2)}) collective-permute-start(bf16[2,4,6144]{2,1,0:T(4,128)(2,1)S(1)} %pad_maximum_fusion.1), channel_id=1, source_target_pairs={{0,8},{1,9},{2,10},{3,11},{4,12},{5,13},{6,14},{7,15},{8,0},{9,1},... | collective-permute-start | bytes 294920 | tf_op jit(solution)/shard_map/ppermute | solution.py:23
  37.2 5.3 %collective-permute-start.11 = (bf16[2,4,6144]{2,1,0:T(4,128)(2,1)S(1)}, bf16[2,4,6144]{2,1,0:T(4,128)(2,1)S(1)}, u32[]{:S(2)}, u32[]{:S(2)}) collective-permute-start(bf16[2,4,6144]{2,1,0:T(4,128)(2,1)S(1)} %pad_maximum_fusion.1), channel_id=1, source_target_pairs={{0,4},{1,5},{2,6},{3,7},{4,0},{5,1},{6,2},{7,3},{8,12},{9,13},{10,... | collective-permute-start | bytes 294920 | tf_op jit(solution)/shard_map/ppermute | solution.py:23
  42.6 0.7 %copy-start.1 = (bf16[4,49152]{1,0:T(4,128)(2,1)}, bf16[4,49152]{1,0:T(4,128)(2,1)S(1)}, u32[]{:S(2)}) copy-start(bf16[4,49152]{1,0:T(4,128)(2,1)S(1)} %fusion.6) | copy-start | bytes 1179652

commit v6 on v5

--- a/solution.py
+++ b/solution.py
@@ -45,22 +45,31 @@
     x, core = me_local // 2, me_local % 2
     z, y = me_host // 2, me_host % 2
 
-    split = gradient.reshape(2, tile, 16, half).transpose(0, 2, 1, 3)
-    split = split.reshape(2, 4, 2, 2, tile, half).transpose(3, 0, 1, 2, 4, 5)
-    own, other = pick(split, core), swap(pick(split, 1 - core), CORE, CORE)
-
-    def part(value, i):
+    def part(value, of_half, of_core, i):
+        value = value.reshape(2, tile, 16, half).transpose(0, 2, 1, 3)
+        value = pick(value.reshape(2, 4, 2, 2, tile, half).transpose(3, 0, 1, 2, 4, 5), of_half)
         by_xy = lax.dynamic_slice(value, (i // 2, 0, i % 2, 0, 0), (1, 4, 1, tile, half))
         by_z = lax.dynamic_slice(value, (0, i, 0, 0, 0), (2, 1, 2, tile, half))
-        return jnp.where(core == 0, by_xy.reshape(4, tile, half), by_z.reshape(4, tile, half))
-
-    def pair(i):
-        return part(own, i).astype(jnp.float32) + part(other, i).astype(jnp.float32)
+        return jnp.where(of_core == 0, by_xy.reshape(4, tile, half), by_z.reshape(4, tile, half))
 
     over_xy, over_z = (0, Y, X, X + Y), (0, Z_NEAR, Z_FAR, Z_NEAR + Z_FAR)
-    me = jnp.where(core == 0, 2 * x + y, z)
-    got = [swap(narrow(pair(me ^ d)), over_xy[d], over_z[d]) for d in (3, 2, 1)]
-    quarter = pair(me) + widen(got[0]) + widen(got[1]) + widen(got[2])
+    me, mate = jnp.where(core == 0, 2 * x + y, z), jnp.where(core == 0, z, 2 * x + y)
+
+    def give(d):
+        nonlocal gradient
+        sent = part(gradient, 1 - core, 1 - core, mate ^ d)
+        gradient, sent = lax.optimization_barrier((gradient, sent))
+        return swap(sent, CORE, CORE)
+
+    def pair(d, other):
+        return part(gradient, core, core, me ^ d).astype(jnp.float32) + other.astype(jnp.float32)
+
+    other = {d: give(d) for d in (3, 2, 1)}
+    sent = [narrow(pair(d, other[d])) for d in (3, 2, 1)]
+    got = [swap(v, over_xy[d], over_z[d]) for v, d in zip(sent, (3, 2, 1))]
+    gradient, got[0] = lax.optimization_barrier((gradient, got[0]))
+    quarter = lax.optimization_barrier(pair(0, give(0)) + widen(got[0]))
+    quarter = quarter + widen(got[1]) + widen(got[2])
     me = jnp.where(core == 0, z, 2 * x + y)
     got = [swap(narrow(pick(quarter, me ^ d)), over_z[d], over_xy[d]) for d in (3, 2, 1)]
     total = pick(quarter, me) + widen(got[0]) + widen(got[1]) + widen(got[2])
@@ -71,16 +80,18 @@
     return jnp.concatenate([left, right], axis=1)
 
 
-def gather_blocks(mine):
+def gather_blocks(first, mine):
     row_block, col_block = mine.shape
     me = lax.axis_index("hst")
-    far = jnp.stack([mine, swap(mine, Z_FAR, Z_FAR)])
-    got = [(0, far)] + [(bits, swap(far, 4 * bits, 4 * bits)) for bits in (3, 2, 1)]
+    far = swap(first, Z_FAR, Z_FAR)
+    pair = jnp.stack([mine, far])
+    both = swap(mine, Z_NEAR + Y, Z_NEAR + Y), swap(far, Z_NEAR + Y, Z_NEAR + Y)
+    near, side = swap(pair, Z_NEAR, Z_NEAR), swap(pair, Y, Y)
+    got = [(0, mine), (3, both[0]), (4, far)]
+    got += [(1, side[0]), (5, side[1]), (2, near[0]), (6, near[1]), (7, both[1])]
     whole = jnp.zeros((row_block, 8 * col_block), mine.dtype)
-    for bits, blocks in got:
-        for i in (0, 1):
-            place = me ^ bits ^ (4 * i)
-            whole = lax.dynamic_update_slice_in_dim(whole, blocks[i], place * col_block, 1)
+    for bits, block in got:
+        whole = lax.dynamic_update_slice_in_dim(whole, block, (me ^ bits) * col_block, 1)
     return whole
 
 
@@ -107,17 +118,24 @@
     return jnp.sum(arrived, axis=1)
 
 
+def adam(grad_total, master, moment_one, moment_two):
+    new_one = beta_one * moment_one + (1.0 - beta_one) * grad_total
+    new_two = beta_two * moment_two + (1.0 - beta_two) * grad_total * grad_total
+    update = new_one / correct_one / (jnp.sqrt(new_two / correct_two) + epsilon)
+    new_master = master - learn_rate * (update + decay_rate * master)
+    return new_master, new_one, new_two
+
+
 def local(grads, master, moment_one, moment_two):
     tuned = lax.axis_size("local") == 4 and lax.axis_size("hst") == 8
     gradient = grads[0, 0]
     grad_total = reduce_blocks(gradient) if tuned else reduce_general(gradient)
-    new_one = beta_one * moment_one + (1.0 - beta_one) * grad_total
-    new_two = beta_two * moment_two + (1.0 - beta_two) * grad_total * grad_total
-    update = new_one / correct_one / (jnp.sqrt(new_two / correct_two) + epsilon)
-    new_master = master - learn_rate * (update + decay_rate * master)
+    first = adam(grad_total, master, moment_one, moment_two)[0].astype(jnp.bfloat16)
+    grad_total, first = lax.optimization_barrier((grad_total, first))
+    new_master, new_one, new_two = adam(grad_total, master, moment_one, moment_two)
     mine = new_master.astype(jnp.bfloat16)
     if tuned:
-        secondary = gather_blocks(mine)
+        secondary = gather_blocks(first, mine)
     else:
         secondary = lax.all_gather(mine, "hst", axis=1, tiled=True)
     return (grad_total, new_master, new_one, new_two, secondary)

time: 43.5 us -> 41.3 us (0.949)
  waiting for transfers between devices: 22 us -> 15.4 us
  starting transfers between devices: 15.2 us -> 18.5 us
  local copies, waits for them, and re-layouts: 2.55 us -> 3.23 us
    ppermute x12 -> x16, waiting for transfers between devices: 22 us -> 15.4 us  [swap(): return lax.ppermute(value, ('hst', 'local'), flip_pairs(flips))]
    ppermute x12 -> x16, starting transfers between devices: 15.2 us -> 18.5 us  [swap(): return lax.ppermute(value, ('hst', 'local'), flip_pairs(flips))]
    dynamic_slice x2 -> x6, local copies, waits for them, and re-layouts: 0.11 us -> 2.1 us  [part(): by_z = lax.dynamic_slice(value, (0, i, 0, 0, 0), (2, 1, 2, tile, half))]
    squeeze x2 -> x1, local copies, waits for them, and re-layouts: 1.33 us -> 0.01 us  [pick(): return lax.dynamic_index_in_dim(value, index, 0, keepdims=False)]
    select_n x0 -> x4, other arithmetic: none -> 1.1 us  [part(): jnp.where(of_core == 0, by_xy.reshape(4, tile, half), by_z.reshape(4, til...]
    add x1 -> x2, other arithmetic: 1.27 us -> 0.2 us  [the longest x1 0.12 us: reduce_blocks(): quarter = lax.optimization_barrier(pair(0, give(0)) + widen(got[0]))]
  transfers between devices with their start and end apart: 12 -> 16, of which waited for: 11 -> 14; matrix products, arithmetic and copies ran while one was open for 1% -> 4% of each run, Pallas kernels for 0% -> 0%
where the time goes in v6:
time: 41.3 us; the launch traced here: 41.1 us
  starting transfers between devices  18.5 us (45%)
  waiting for transfers between devices  15.4 us (37%)
  local copies, waits for them, and re-layouts  3.23 us (8%)
  other arithmetic  2.84 us (7%)
  between operations  1.12 us (3%)
    ppermute x16, starting transfers between devices, swap(): return lax.ppermute(value, ('hst', 'local'), flip_pairs(flips))  18.5 us
    ppermute x16, waiting for transfers between devices, swap(): return lax.ppermute(value, ('hst', 'local'), flip_pairs(flips))  15.4 us
    dynamic_slice x6, local copies, waits for them, and re-layouts, part(): by_z = lax.dynamic_slice(value, (0, i, 0, 0, 0), (2, 1, 2, tile, half))  2.1 us
    select_n x4, other arithmetic, part(): jnp.where(of_core == 0, by_xy.reshape(4, tile, half), by_z.reshape(4, til...  1.1 us
    dynamic_update_slice x1, other arithmetic, gather_blocks(): lax.dynamic_update_slice_in_dim(whole, block, (me ^ bits) * col_block, 1)  0.87 us
  transfers between devices with their start and end apart: 16, of which 14 were waited for; matrix products, arithmetic and copies ran while one was open for 4% of the time, Pallas kernels for 0%

profile of v6, /device:TPU:0, one launch (start us, length us, event | category | flops | bytes accessed | tf_op | source)
XLA Modules:
  0.0 41.1 jit_solution(16835031336176879686)
XLA Ops:
  0.8 1.1 %constant_dynamic-slice_fusion.7 = bf16[2,1,2,1,8,3072]{5,4,3,2,1,0:T(8,128)(2,1)S(1)} fusion(bf16[2,4,2,2,8,3072]{5,4,3,2,1,0:T(8,128)(2,1)} %bitcast.106, s32[]{:T(128)S(6)} %select_n.317, s32[]{:T(128)S(6)} %select_n.315), kind=kLoop, calls=%fused_computation.57 | loop fusion | bytes 393224 | tf_op jit(solution)/shard_map/dynamic_slice | solution.py:52
  1.9 1.0 %bitcast_select_fusion.7 = bf16[4,8,3072]{2,1,0:T(8,128)(2,1)S(1)} fusion(bf16[2,1,2,1,8,3072]{5,4,3,2,1,0:T(8,128)(2,1)S(1)} %constant_dynamic-slice_fusion.7, bf16[2,4,2,2,8,3072]{5,4,3,2,1,0:T(8,128)(2,1)} %bitcast.107, s32[]{:T(128)S(6)} %select_n.310, s32[]{:T(128)S(6)} %select_n.313, s32[]{:T(128)S(6)} %select_n.315, pred[]{:T(512)S(6)} %eq.29), kind=kLoop, calls=%fused_computation.12 | loop fusion | flops 98304 | bytes 589837 | tf_op jit(solution)/shard_map/jit(_where)/select_n | solution.py:53
  2.9 1.0 %constant_dynamic-slice_fusion.6 = bf16[2,1,2,1,8,3072]{5,4,3,2,1,0:T(8,128)(2,1)S(1)} fusion(bf16[2,4,2,2,8,3072]{5,4,3,2,1,0:T(8,128)(2,1)} %bitcast.108, s32[]{:T(128)S(6)} %select_n.326, s32[]{:T(128)S(6)} %select_n.315), kind=kLoop, calls=%fused_computation.56 | loop fusion | bytes 393224 | tf_op jit(solution)/shard_map/dynamic_slice | solution.py:52
  4.0 0.5 %collective-permute-start.5 = (bf16[4,8,3072]{2,1,0:T(8,128)(2,1)S(1)}, bf16[4,8,3072]{2,1,0:T(8,128)(2,1)S(1)}, u32[]{:S(2)}, u32[]{:S(2)}) collective-permute-start(bf16[4,8,3072]{2,1,0:T(8,128)(2,1)S(1)} %bitcast_select_fusion.5), channel_id=1, source_target_pairs={{0,1},{1,0},{2,3},{3,2},{4,5},{5,4},{6,7},{7,6},{8,9},{9,8},{10,11... | collective-permute-start | bytes 589832 | tf_op jit(solution)/shard_map/ppermute | solution.py:23
  4.6 0.4 %collective-permute-start = (bf16[4,8,3072]{2,1,0:T(8,128)(2,1)S(1)}, bf16[4,8,3072]{2,1,0:T(8,128)(2,1)S(1)}, u32[]{:S(2)}, u32[]{:S(2)}) collective-permute-start(bf16[4,8,3072]{2,1,0:T(8,128)(2,1)S(1)} %bitcast_select_fusion.7), channel_id=1, source_target_pairs={{0,1},{1,0},{2,3},{3,2},{4,5},{5,4},{6,7},{7,6},{8,9},{9,8},{10,11... | collective-permute-start | bytes 589832 | tf_op jit(solution)/shard_map/ppermute | solution.py:23
  5.1 0.5 %collective-permute-done.5 = bf16[4,8,3072]{2,1,0:T(8,128)(2,1)S(1)} collective-permute-done((bf16[4,8,3072]{2,1,0:T(8,128)(2,1)S(1)}, bf16[4,8,3072]{2,1,0:T(8,128)(2,1)S(1)}, u32[]{:S(2)}, u32[]{:S(2)}) %collective-permute-start.5) | collective-permute-done | bytes 196640 | tf_op jit(solution)/shard_map/ppermute | solution.py:23
  5.6 0.4 collective-permute-done.3
  6.0 0.3 collective-permute-done
  6.2 0.3 multiply_convert_fusion.1
  6.6 3.8 %collective-permute-start.1 = (f16[4,8,3072]{2,1,0:T(8,128)(2,1)S(1)}, f16[4,8,3072]{2,1,0:T(8,128)(2,1)S(1)}, u32[]{:S(2)}, u32[]{:S(2)}) collective-permute-start(f16[4,8,3072]{2,1,0:T(8,128)(2,1)S(1)} %get-tuple-element.36), channel_id=1, source_target_pairs={{0,6},{1,25},{2,4},{3,27},{4,2},{5,29},{6,0},{7,31},{8,14},{9,17},... | collective-permute-start | bytes 589832 | tf_op jit(solution)/shard_map/ppermute | solution.py:23
  10.4 0.5 %collective-permute-start.4 = (f16[4,8,3072]{2,1,0:T(8,128)(2,1)S(1)}, f16[4,8,3072]{2,1,0:T(8,128)(2,1)S(1)}, u32[]{:S(2)}, u32[]{:S(2)}) collective-permute-start(f16[4,8,3072]{2,1,0:T(8,128)(2,1)S(1)} %get-tuple-element.34), channel_id=1, source_target_pairs={{0,2},{1,17},{2,0},{3,19},{4,6},{5,21},{6,4},{7,23},{8,10},{9,25},... | collective-permute-start | bytes 589832 | tf_op jit(solution)/shard_map/ppermute | solution.py:23
  10.9 0.2 collective-permute-start.6
  11.1 2.9 %collective-permute-done.1 = f16[4,8,3072]{2,1,0:T(8,128)(2,1)S(1)} collective-permute-done((f16[4,8,3072]{2,1,0:T(8,128)(2,1)S(1)}, f16[4,8,3072]{2,1,0:T(8,128)(2,1)S(1)}, u32[]{:S(2)}, u32[]{:S(2)}) %collective-permute-start.1) | collective-permute-done | bytes 196640 | tf_op jit(solution)/shard_map/ppermute | solution.py:23
  14.1 0.8 %collective-permute-start.2 = (bf16[4,8,3072]{2,1,0:T(8,128)(2,1)S(1)}, bf16[4,8,3072]{2,1,0:T(8,128)(2,1)S(1)}, u32[]{:S(2)}, u32[]{:S(2)}) collective-permute-start(bf16[4,8,3072]{2,1,0:T(8,128)(2,1)S(1)} %bitcast_select_fusion.3), channel_id=1, source_target_pairs={{0,1},{1,0},{2,3},{3,2},{4,5},{5,4},{6,7},{7,6},{8,9},{9,8},{10,11... | collective-permute-start | bytes 589832 | tf_op jit(solution)/shard_map/ppermute | solution.py:23
  14.9 1.0 %collective-permute-done.2 = bf16[4,8,3072]{2,1,0:T(8,128)(2,1)S(1)} collective-permute-done((bf16[4,8,3072]{2,1,0:T(8,128)(2,1)S(1)}, bf16[4,8,3072]{2,1,0:T(8,128)(2,1)S(1)}, u32[]{:S(2)}, u32[]{:S(2)}) %collective-permute-start.2) | collective-permute-done | bytes 196640 | tf_op jit(solution)/shard_map/ppermute | solution.py:23
  16.0 0.6 %collective-permute-done.4 = f16[4,8,3072]{2,1,0:T(8,128)(2,1)S(1)} collective-permute-done((f16[4,8,3072]{2,1,0:T(8,128)(2,1)S(1)}, f16[4,8,3072]{2,1,0:T(8,128)(2,1)S(1)}, u32[]{:S(2)}, u32[]{:S(2)}) %collective-permute-start.4) | collective-permute-done | bytes 196640 | tf_op jit(solution)/shard_map/ppermute | solution.py:23
  16.8 3.7 %collective-permute-start.7 = (f16[8,3072]{1,0:T(8,128)(2,1)S(1)}, f16[8,3072]{1,0:T(8,128)(2,1)S(1)}, u32[]{:S(2)}, u32[]{:S(2)}) collective-permute-start(f16[8,3072]{1,0:T(8,128)(2,1)S(1)} %get-tuple-element.40), channel_id=1, source_target_pairs={{0,24},{1,7},{2,26},{3,5},{4,28},{5,3},{6,30},{7,1},{8,16},{9,15},... | collective-permute-start | bytes 147464 | tf_op jit(solution)/shard_map/ppermute | solution.py:23
  20.4 1.0 %collective-permute-start.8 = (f16[8,3072]{1,0:T(8,128)(2,1)S(1)}, f16[8,3072]{1,0:T(8,128)(2,1)S(1)}, u32[]{:S(2)}, u32[]{:S(2)}) collective-permute-start(f16[8,3072]{1,0:T(8,128)(2,1)S(1)} %get-tuple-element.42), channel_id=1, source_target_pairs={{0,16},{1,3},{2,18},{3,1},{4,20},{5,7},{6,22},{7,5},{8,24},{9,11},... | collective-permute-start | bytes 147464 | tf_op jit(solution)/shard_map/ppermute | solution.py:23
  21.6 1.1 %collective-permute-done.7 = f16[8,3072]{1,0:T(8,128)(2,1)S(1)} collective-permute-done((f16[8,3072]{1,0:T(8,128)(2,1)S(1)}, f16[8,3072]{1,0:T(8,128)(2,1)S(1)}, u32[]{:S(2)}, u32[]{:S(2)}) %collective-permute-start.7) | collective-permute-done | bytes 49184 | tf_op jit(solution)/shard_map/ppermute | solution.py:23
  22.7 2.7 %collective-permute-done.8 = f16[8,3072]{1,0:T(8,128)(2,1)S(1)} collective-permute-done((f16[8,3072]{1,0:T(8,128)(2,1)S(1)}, f16[8,3072]{1,0:T(8,128)(2,1)S(1)}, u32[]{:S(2)}, u32[]{:S(2)}) %collective-permute-start.8) | collective-permute-done | bytes 49184 | tf_op jit(solution)/shard_map/ppermute | solution.py:23
  25.5 0.5 %collective-permute-done.9 = f16[8,3072]{1,0:T(8,128)(2,1)S(1)} collective-permute-done((f16[8,3072]{1,0:T(8,128)(2,1)S(1)}, f16[8,3072]{1,0:T(8,128)(2,1)S(1)}, u32[]{:S(2)}, u32[]{:S(2)}) %collective-permute-start.9) | collective-permute-done | bytes 49184 | tf_op jit(solution)/shard_map/ppermute | solution.py:23
  26.2 1.2 %collective-permute-done.10 = f32[4,3072]{1,0:T(4,128)S(1)} collective-permute-done((f32[4,3072]{1,0:T(4,128)S(1)}, f32[4,3072]{1,0:T(4,128)S(1)}, u32[]{:S(2)}, u32[]{:S(2)}) %collective-permute-start.10) | collective-permute-done | bytes 49184 | tf_op jit(solution)/shard_map/ppermute | solution.py:23
  27.6 1.6 %collective-permute-start.12 = (bf16[4,6144]{1,0:T(4,128)(2,1)S(1)}, bf16[4,6144]{1,0:T(4,128)(2,1)S(1)}, u32[]{:S(2)}, u32[]{:S(2)}) collective-permute-start(bf16[4,6144]{1,0:T(4,128)(2,1)S(1)} %get-tuple-element.28), channel_id=1, source_target_pairs={{0,16},{1,17},{2,18},{3,19},{4,20},{5,21},{6,22},{7,23},{8,24},{9,... | collective-permute-start | bytes 147464 | tf_op jit(solution)/shard_map/ppermute | solution.py:23
  29.3 0.9 %constant_dynamic-update-slice_fusion.3 = (bf16[4,49152]{1,0:T(4,128)(2,1)S(1)}, bf16[4,6144]{1,0:T(4,128)(2,1)S(1)}, f32[4,6144]{1,0:T(4,128)}, f32[4,6144]{1,0:T(4,128)}, f32[4,6144]{1,0:T(4,128)}) fusion(bf16[4,49152]{1,0:T(4,128)(2,1)S(1)} %broadcast_in_dim.3, s32[]{:T(128)S(6)} %select_n.387, f32[4,6144]{1,0:T(4,128)S(1)} %copy-done.2, ...), kind=kLoop, calls=%fused_computation.49 | loop fusion | flops 393216 | bytes 786436 | tf_op jit(solution)/shard_map/dynamic_update_slice | solution.py:94
  30.1 2.2 %collective-permute-start.11 = (bf16[4,6144]{1,0:T(4,128)(2,1)S(1)}, bf16[4,6144]{1,0:T(4,128)(2,1)S(1)}, u32[]{:S(2)}, u32[]{:S(2)}) collective-permute-start(bf16[4,6144]{1,0:T(4,128)(2,1)S(1)} %get-tuple-element.30), channel_id=1, source_target_pairs={{0,12},{1,13},{2,14},{3,15},{4,8},{5,9},{6,10},{7,11},{8,4},{9,5},... | collective-permute-start | bytes 147464 | tf_op jit(solution)/shard_map/ppermute | solution.py:23
  32.3 1.1 %collective-permute-done.12 = bf16[4,6144]{1,0:T(4,128)(2,1)S(1)} collective-permute-done((bf16[4,6144]{1,0:T(4,128)(2,1)S(1)}, bf16[4,6144]{1,0:T(4,128)(2,1)S(1)}, u32[]{:S(2)}, u32[]{:S(2)}) %collective-permute-start.12) | collective-permute-done | bytes 49184 | tf_op jit(solution)/shard_map/ppermute | solution.py:23
  33.5 1.6 %collective-permute-start.13 = (bf16[2,4,6144]{2,1,0:T(4,128)(2,1)S(1)}, bf16[2,4,6144]{2,1,0:T(4,128)(2,1)S(1)}, u32[]{:S(2)}, u32[]{:S(2)}) collective-permute-start(bf16[2,4,6144]{2,1,0:T(4,128)(2,1)S(1)} %pad_maximum_fusion.1), channel_id=1, source_target_pairs={{0,4},{1,5},{2,6},{3,7},{4,0},{5,1},{6,2},{7,3},{8,12},{9,13},{10,... | collective-permute-start | bytes 294920 | tf_op jit(solution)/shard_map/ppermute | solution.py:23
  35.1 1.9 %collective-permute-start.15 = (bf16[4,6144]{1,0:T(4,128)(2,1)S(1)}, bf16[4,6144]{1,0:T(4,128)(2,1)S(1)}, u32[]{:S(2)}, u32[]{:S(2)}) collective-permute-start(bf16[4,6144]{1,0:T(4,128)(2,1)S(1)} %collective-permute-done.12), channel_id=1, source_target_pairs={{0,12},{1,13},{2,14},{3,15},{4,8},{5,9},{6,10},{7,11},{8,4},{9,5},... | collective-permute-start | bytes 147464 | tf_op jit(solution)/shard_map/ppermute | solution.py:23
  37.1 1.1 %collective-permute-done.13 = bf16[2,4,6144]{2,1,0:T(4,128)(2,1)S(1)} collective-permute-done((bf16[2,4,6144]{2,1,0:T(4,128)(2,1)S(1)}, bf16[2,4,6144]{2,1,0:T(4,128)(2,1)S(1)}, u32[]{:S(2)}, u32[]{:S(2)}) %collective-permute-start.13) | collective-permute-done | bytes 98336 | tf_op jit(solution)/shard_map/ppermute | solution.py:23
  38.3 1.6 %collective-permute-done.14 = bf16[2,4,6144]{2,1,0:T(4,128)(2,1)S(1)} collective-permute-done((bf16[2,4,6144]{2,1,0:T(4,128)(2,1)S(1)}, bf16[2,4,6144]{2,1,0:T(4,128)(2,1)S(1)}, u32[]{:S(2)}, u32[]{:S(2)}) %collective-permute-start.14) | collective-permute-done | bytes 98336 | tf_op jit(solution)/shard_map/ppermute | solution.py:23
  39.9 0.5 %collective-permute-done.15 = bf16[4,6144]{1,0:T(4,128)(2,1)S(1)} collective-permute-done((bf16[4,6144]{1,0:T(4,128)(2,1)S(1)}, bf16[4,6144]{1,0:T(4,128)(2,1)S(1)}, u32[]{:S(2)}, u32[]{:S(2)}) %collective-permute-start.15) | collective-permute-done | bytes 49184 | tf_op jit(solution)/shard_map/ppermute | solution.py:23
  40.4 0.7 %copy-done.1 = bf16[4,49152]{1,0:T(4,128)(2,1)} copy-done((bf16[4,49152]{1,0:T(4,128)(2,1)}, bf16[4,49152]{1,0:T(4,128)(2,1)S(1)}, u32[]{:S(2)}) %copy-start.1) | copy-done | bytes 393240
  (41 shorter events, 1.4 us)
Async XLA Ops:
  0.6 3.2 %copy-start = (bf16[1,1,16,49152]{3,2,1,0:T(8,128)(2,1)S(1)}, bf16[1,1,16,49152]{3,2,1,0:T(8,128)(2,1)}, u32[]{:S(2)}) copy-start(bf16[1,1,16,49152]{3,2,1,0:T(8,128)(2,1)} %param.4) | copy-start | bytes 4718596
  4.0 1.6 %collective-permute-start.5 = (bf16[4,8,3072]{2,1,0:T(8,128)(2,1)S(1)}, bf16[4,8,3072]{2,1,0:T(8,128)(2,1)S(1)}, u32[]{:S(2)}, u32[]{:S(2)}) collective-permute-start(bf16[4,8,3072]{2,1,0:T(8,128)(2,1)S(1)} %bitcast_select_fusion.5), channel_id=1, source_target_pairs={{0,1},{1,0},{2,3},{3,2},{4,5},{5,4},{6,7},{7,6},{8,9},{9,8},{10,11... | collective-permute-start | bytes 589832 | tf_op jit(solution)/shard_map/ppermute | solution.py:23
  4.5 1.4 %collective-permute-start.3 = (bf16[4,8,3072]{2,1,0:T(8,128)(2,1)S(1)}, bf16[4,8,3072]{2,1,0:T(8,128)(2,1)S(1)}, u32[]{:S(2)}, u32[]{:S(2)}) collective-permute-start(bf16[4,8,3072]{2,1,0:T(8,128)(2,1)S(1)} %bitcast_select_fusion.6), channel_id=1, source_target_pairs={{0,1},{1,0},{2,3},{3,2},{4,5},{5,4},{6,7},{7,6},{8,9},{9,8},{10,11... | collective-permute-start | bytes 589832 | tf_op jit(solution)/shard_map/ppermute | solution.py:23
  4.6 1.6 %collective-permute-start = (bf16[4,8,3072]{2,1,0:T(8,128)(2,1)S(1)}, bf16[4,8,3072]{2,1,0:T(8,128)(2,1)S(1)}, u32[]{:S(2)}, u32[]{:S(2)}) collective-permute-start(bf16[4,8,3072]{2,1,0:T(8,128)(2,1)S(1)} %bitcast_select_fusion.7), channel_id=1, source_target_pairs={{0,1},{1,0},{2,3},{3,2},{4,5},{5,4},{6,7},{7,6},{8,9},{9,8},{10,11... | collective-permute-start | bytes 589832 | tf_op jit(solution)/shard_map/ppermute | solution.py:23
  6.6 7.4 %collective-permute-start.1 = (f16[4,8,3072]{2,1,0:T(8,128)(2,1)S(1)}, f16[4,8,3072]{2,1,0:T(8,128)(2,1)S(1)}, u32[]{:S(2)}, u32[]{:S(2)}) collective-permute-start(f16[4,8,3072]{2,1,0:T(8,128)(2,1)S(1)} %get-tuple-element.36), channel_id=1, source_target_pairs={{0,6},{1,25},{2,4},{3,27},{4,2},{5,29},{6,0},{7,31},{8,14},{9,17},... | collective-permute-start | bytes 589832 | tf_op jit(solution)/shard_map/ppermute | solution.py:23
  10.4 6.3 %collective-permute-start.4 = (f16[4,8,3072]{2,1,0:T(8,128)(2,1)S(1)}, f16[4,8,3072]{2,1,0:T(8,128)(2,1)S(1)}, u32[]{:S(2)}, u32[]{:S(2)}) collective-permute-start(f16[4,8,3072]{2,1,0:T(8,128)(2,1)S(1)} %get-tuple-element.34), channel_id=1, source_target_pairs={{0,2},{1,17},{2,0},{3,19},{4,6},{5,21},{6,4},{7,23},{8,10},{9,25},... | collective-permute-start | bytes 589832 | tf_op jit(solution)/shard_map/ppermute | solution.py:23
  10.9 5.8 %collective-permute-start.6 = (f16[4,8,3072]{2,1,0:T(8,128)(2,1)S(1)}, f16[4,8,3072]{2,1,0:T(8,128)(2,1)S(1)}, u32[]{:S(2)}, u32[]{:S(2)}) collective-permute-start(f16[4,8,3072]{2,1,0:T(8,128)(2,1)S(1)} %get-tuple-element.35), channel_id=1, source_target_pairs={{0,4},{1,9},{2,6},{3,11},{4,0},{5,13},{6,2},{7,15},{8,12},{9,1},{1... | collective-permute-start | bytes 589832 | tf_op jit(solution)/shard_map/ppermute | solution.py:23
  14.1 1.8 %collective-permute-start.2 = (bf16[4,8,3072]{2,1,0:T(8,128)(2,1)S(1)}, bf16[4,8,3072]{2,1,0:T(8,128)(2,1)S(1)}, u32[]{:S(2)}, u32[]{:S(2)}) collective-permute-start(bf16[4,8,3072]{2,1,0:T(8,128)(2,1)S(1)} %bitcast_select_fusion.3), channel_id=1, source_target_pairs={{0,1},{1,0},{2,3},{3,2},{4,5},{5,4},{6,7},{7,6},{8,9},{9,8},{10,11... | collective-permute-start | bytes 589832 | tf_op jit(solution)/shard_map/ppermute | solution.py:23
  14.8 12.5 %copy-start.2 = (f32[4,6144]{1,0:T(4,128)S(1)}, f32[4,6144]{1,0:T(4,128)}, u32[]{:S(2)}) copy-start(f32[4,6144]{1,0:T(4,128)} %param.5) | copy-start | bytes 294916
  14.9 12.5 %copy-start.3 = (f32[4,6144]{1,0:T(4,128)S(1)}, f32[4,6144]{1,0:T(4,128)}, u32[]{:S(2)}) copy-start(f32[4,6144]{1,0:T(4,128)} %param.7) | copy-start | bytes 294916
  14.9 12.5 %copy-start.4 = (f32[4,6144]{1,0:T(4,128)S(1)}, f32[4,6144]{1,0:T(4,128)}, u32[]{:S(2)}) copy-start(f32[4,6144]{1,0:T(4,128)} %param.6) | copy-start | bytes 294916
  16.8 6.0 %collective-permute-start.7 = (f16[8,3072]{1,0:T(8,128)(2,1)S(1)}, f16[8,3072]{1,0:T(8,128)(2,1)S(1)}, u32[]{:S(2)}, u32[]{:S(2)}) collective-permute-start(f16[8,3072]{1,0:T(8,128)(2,1)S(1)} %get-tuple-element.40), channel_id=1, source_target_pairs={{0,24},{1,7},{2,26},{3,5},{4,28},{5,3},{6,30},{7,1},{8,16},{9,15},... | collective-permute-start | bytes 147464 | tf_op jit(solution)/shard_map/ppermute | solution.py:23
  20.4 5.0 %collective-permute-start.8 = (f16[8,3072]{1,0:T(8,128)(2,1)S(1)}, f16[8,3072]{1,0:T(8,128)(2,1)S(1)}, u32[]{:S(2)}, u32[]{:S(2)}) collective-permute-start(f16[8,3072]{1,0:T(8,128)(2,1)S(1)} %get-tuple-element.42), channel_id=1, source_target_pairs={{0,16},{1,3},{2,18},{3,1},{4,20},{5,7},{6,22},{7,5},{8,24},{9,11},... | collective-permute-start | bytes 147464 | tf_op jit(solution)/shard_map/ppermute | solution.py:23
  21.5 4.5 %collective-permute-start.9 = (f16[8,3072]{1,0:T(8,128)(2,1)S(1)}, f16[8,3072]{1,0:T(8,128)(2,1)S(1)}, u32[]{:S(2)}, u32[]{:S(2)}) collective-permute-start(f16[8,3072]{1,0:T(8,128)(2,1)S(1)} %get-tuple-element.41), channel_id=1, source_target_pairs={{0,8},{1,5},{2,10},{3,7},{4,12},{5,1},{6,14},{7,3},{8,0},{9,13},{1... | collective-permute-start | bytes 147464 | tf_op jit(solution)/shard_map/ppermute | solution.py:23
  26.1 1.3 %collective-permute-start.10 = (f32[4,3072]{1,0:T(4,128)S(1)}, f32[4,3072]{1,0:T(4,128)S(1)}, u32[]{:S(2)}, u32[]{:S(2)}) collective-permute-start(f32[4,3072]{1,0:T(4,128)S(1)} %dynamic-slice_bitcast_fusion), channel_id=1, source_target_pairs={{0,1},{1,0},{2,3},{3,2},{4,5},{5,4},{6,7},{7,6},{8,9},{9,8},{10,11... | collective-permute-start | bytes 147464 | tf_op jit(solution)/shard_map/ppermute | solution.py:23
  27.6 12.8 %copy-start.5 = (f32[4,6144]{1,0:T(4,128)}, f32[4,6144]{1,0:T(4,128)S(1)}, u32[]{:S(2)}) copy-start(f32[4,6144]{1,0:T(4,128)S(1)} %get-tuple-element.12) | copy-start | bytes 294916
  27.6 5.8 %collective-permute-start.12 = (bf16[4,6144]{1,0:T(4,128)(2,1)S(1)}, bf16[4,6144]{1,0:T(4,128)(2,1)S(1)}, u32[]{:S(2)}, u32[]{:S(2)}) collective-permute-start(bf16[4,6144]{1,0:T(4,128)(2,1)S(1)} %get-tuple-element.28), channel_id=1, source_target_pairs={{0,16},{1,17},{2,18},{3,19},{4,20},{5,21},{6,22},{7,23},{8,24},{9,... | collective-permute-start | bytes 147464 | tf_op jit(solution)/shard_map/ppermute | solution.py:23
  30.1 6.9 %collective-permute-start.11 = (bf16[4,6144]{1,0:T(4,128)(2,1)S(1)}, bf16[4,6144]{1,0:T(4,128)(2,1)S(1)}, u32[]{:S(2)}, u32[]{:S(2)}) collective-permute-start(bf16[4,6144]{1,0:T(4,128)(2,1)S(1)} %get-tuple-element.30), channel_id=1, source_target_pairs={{0,12},{1,13},{2,14},{3,15},{4,8},{5,9},{6,10},{7,11},{8,4},{9,5},... | collective-permute-start | bytes 147464 | tf_op jit(solution)/shard_map/ppermute | solution.py:23
  33.5 4.7 %collective-permute-start.13 = (bf16[2,4,6144]{2,1,0:T(4,128)(2,1)S(1)}, bf16[2,4,6144]{2,1,0:T(4,128)(2,1)S(1)}, u32[]{:S(2)}, u32[]{:S(2)}) collective-permute-start(bf16[2,4,6144]{2,1,0:T(4,128)(2,1)S(1)} %pad_maximum_fusion.1), channel_id=1, source_target_pairs={{0,4},{1,5},{2,6},{3,7},{4,0},{5,1},{6,2},{7,3},{8,12},{9,13},{10,... | collective-permute-start | bytes 294920 | tf_op jit(solution)/shard_map/ppermute | solution.py:23
  35.1 4.7 %collective-permute-start.14 = (bf16[2,4,6144]{2,1,0:T(4,128)(2,1)S(1)}, bf16[2,4,6144]{2,1,0:T(4,128)(2,1)S(1)}, u32[]{:S(2)}, u32[]{:S(2)}) collective-permute-start(bf16[2,4,6144]{2,1,0:T(4,128)(2,1)S(1)} %pad_maximum_fusion.1), channel_id=1, source_target_pairs={{0,8},{1,9},{2,10},{3,11},{4,12},{5,13},{6,14},{7,15},{8,0},{9,1},... | collective-permute-start | bytes 294920 | tf_op jit(solution)/shard_map/ppermute | solution.py:23
  35.1 5.2 %collective-permute-start.15 = (bf16[4,6144]{1,0:T(4,128)(2,1)S(1)}, bf16[4,6144]{1,0:T(4,128)(2,1)S(1)}, u32[]{:S(2)}, u32[]{:S(2)}) collective-permute-start(bf16[4,6144]{1,0:T(4,128)(2,1)S(1)} %collective-permute-done.12), channel_id=1, source_target_pairs={{0,12},{1,13},{2,14},{3,15},{4,8},{5,9},{6,10},{7,11},{8,4},{9,5},... | collective-permute-start | bytes 147464 | tf_op jit(solution)/shard_map/ppermute | solution.py:23
  40.4 0.7 %copy-start.1 = (bf16[4,49152]{1,0:T(4,128)(2,1)}, bf16[4,49152]{1,0:T(4,128)(2,1)S(1)}, u32[]{:S(2)}) copy-start(bf16[4,49152]{1,0:T(4,128)(2,1)S(1)} %constant_dynamic-update-slice_fusion) | copy-start | bytes 1179652

commit v7 on v6

--- a/solution.py
+++ b/solution.py
@@ -56,19 +56,14 @@
     me, mate = jnp.where(core == 0, 2 * x + y, z), jnp.where(core == 0, z, 2 * x + y)
 
     def give(d):
-        nonlocal gradient
-        sent = part(gradient, 1 - core, 1 - core, mate ^ d)
-        gradient, sent = lax.optimization_barrier((gradient, sent))
-        return swap(sent, CORE, CORE)
+        return swap(part(gradient, 1 - core, 1 - core, mate ^ d), CORE, CORE)
 
     def pair(d, other):
         return part(gradient, core, core, me ^ d).astype(jnp.float32) + other.astype(jnp.float32)
 
-    other = {d: give(d) for d in (3, 2, 1)}
-    sent = [narrow(pair(d, other[d])) for d in (3, 2, 1)]
-    got = [swap(v, over_xy[d], over_z[d]) for v, d in zip(sent, (3, 2, 1))]
-    gradient, got[0] = lax.optimization_barrier((gradient, got[0]))
-    quarter = lax.optimization_barrier(pair(0, give(0)) + widen(got[0]))
+    other = {d: give(d) for d in (3, 2, 1, 0)}
+    got = [swap(narrow(pair(d, other[d])), over_xy[d], over_z[d]) for d in (3, 2, 1)]
+    quarter = lax.optimization_barrier(pair(0, other[0]) + widen(got[0]))
     quarter = quarter + widen(got[1]) + widen(got[2])
     me = jnp.where(core == 0, z, 2 * x + y)
     got = [swap(narrow(pick(quarter, me ^ d)), over_z[d], over_xy[d]) for d in (3, 2, 1)]

time: 41.3 us -> 41.1 us (level)
  waiting for transfers between devices: 15.4 us -> 17.1 us
  starting transfers between devices: 18.5 us -> 16.8 us
    ppermute x16, starting transfers between devices: 18.5 us -> 16.8 us  [swap(): return lax.ppermute(value, ('hst', 'local'), flip_pairs(flips))]
    ppermute x16, waiting for transfers between devices: 15.4 us -> 17.1 us  [swap(): return lax.ppermute(value, ('hst', 'local'), flip_pairs(flips))]
    convert_element_type x2, other arithmetic: 0.37 us -> 1.36 us  [narrow(): return (value * wire_scale).astype(jnp.float16)]
    select_n x4 -> x1, other arithmetic: 1.1 us -> 0.13 us  [part(): jnp.where(of_core == 0, by_xy.reshape(4, tile, half), by_z.reshape(4, til...]
    dynamic_slice x6 -> x1, local copies, waits for them, and re-layouts: 2.1 us -> 1.72 us  [part(): by_z = lax.dynamic_slice(value, (0, i, 0, 0, 0), (2, 1, 2, tile, half))]
  transfers between devices with their start and end apart: 16 -> 16, of which waited for: 14 -> 12; matrix products, arithmetic and copies ran while one was open for 4% -> 7% of each run, Pallas kernels for 0% -> 0%
where the time goes in v7:
time: 41.1 us; the launch traced here: 40.9 us
  waiting for transfers between devices  17.1 us (42%)
  starting transfers between devices  16.8 us (41%)
  local copies, waits for them, and re-layouts  3.09 us (8%)
  other arithmetic  2.86 us (7%)
  between operations  1.1 us (3%)
    ppermute x16, waiting for transfers between devices, swap(): return lax.ppermute(value, ('hst', 'local'), flip_pairs(flips))  17.1 us
    ppermute x16, starting transfers between devices, swap(): return lax.ppermute(value, ('hst', 'local'), flip_pairs(flips))  16.8 us
    dynamic_slice x1, local copies, waits for them, and re-layouts, part(): by_z = lax.dynamic_slice(value, (0, i, 0, 0, 0), (2, 1, 2, tile, half))  1.72 us
    convert_element_type x2, other arithmetic, narrow(): return (value * wire_scale).astype(jnp.float16)  1.36 us
    unnamed x12, local copies, waits for them, and re-layouts  1.01 us
    dynamic_update_slice x1, other arithmetic, gather_blocks(): lax.dynamic_update_slice_in_dim(whole, block, (me ^ bits) * col_block, 1)  0.87 us
  transfers between devices with their start and end apart: 16, of which 12 were waited for; matrix products, arithmetic and copies ran while one was open for 7% of the time, Pallas kernels for 0%

profile of v7, /device:TPU:0, one launch (start us, length us, event | category | flops | bytes accessed | tf_op | source)
XLA Modules:
  0.0 40.9 jit_solution(3469306546531910410)
XLA Ops:
  1.0 1.7 %constant_dynamic-slice_fusion.3 = (bf16[2,1,2,1,8,3072]{5,4,3,2,1,0:T(8,128)(2,1)S(1)}, bf16[2,1,2,1,8,3072]{5,4,3,2,1,0:T(8,128)(2,1)S(1)}, bf16[2,1,2,1,8,307...) fusion(bf16[2,4,2,2,8,3072]{5,4,3,2,1,0:T(8,128)(2,1)} %bitcast, ...), kind=kLoop, calls=%fused_computation.53 | loop fusion | bytes 3145768 | tf_op jit(solution)/shard_map/dynamic_slice | solution.py:52
  2.7 0.3 copy-done
  2.9 0.1 bitcast_select_fusion.2
  3.1 0.5 %collective-permute-start.1 = (bf16[4,8,3072]{2,1,0:T(8,128)(2,1)S(1)}, bf16[4,8,3072]{2,1,0:T(8,128)(2,1)S(1)}, u32[]{:S(2)}, u32[]{:S(2)}) collective-permute-start(bf16[4,8,3072]{2,1,0:T(8,128)(2,1)S(1)} %get-tuple-element.27), channel_id=1, source_target_pairs={{0,1},{1,0},{2,3},{3,2},{4,5},{5,4},{6,7},{7,6},{8,9},{9,8},{10,11... | collective-permute-start | bytes 589832 | tf_op jit(solution)/shard_map/ppermute | solution.py:23
  3.7 0.4 %collective-permute-start.5 = (bf16[4,8,3072]{2,1,0:T(8,128)(2,1)S(1)}, bf16[4,8,3072]{2,1,0:T(8,128)(2,1)}, u32[]{:S(2)}, u32[]{:S(2)}) collective-permute-start(bf16[4,8,3072]{2,1,0:T(8,128)(2,1)S(1)} %get-tuple-element.26), channel_id=1, source_target_pairs={{0,1},{1,0},{2,3},{3,2},{4,5},{5,4},{6,7},{7,6},{8,9},{9,8},{10,11... | collective-permute-start | bytes 589832 | tf_op jit(solution)/shard_map/ppermute | solution.py:23
  4.2 0.5 %collective-permute-done.1 = bf16[4,8,3072]{2,1,0:T(8,128)(2,1)S(1)} collective-permute-done((bf16[4,8,3072]{2,1,0:T(8,128)(2,1)S(1)}, bf16[4,8,3072]{2,1,0:T(8,128)(2,1)S(1)}, u32[]{:S(2)}, u32[]{:S(2)}) %collective-permute-start.1) | collective-permute-done | bytes 196640 | tf_op jit(solution)/shard_map/ppermute | solution.py:23
  4.7 0.5 %collective-permute-done.3 = bf16[4,8,3072]{2,1,0:T(8,128)(2,1)} collective-permute-done((bf16[4,8,3072]{2,1,0:T(8,128)(2,1)S(1)}, bf16[4,8,3072]{2,1,0:T(8,128)(2,1)}, u32[]{:S(2)}, u32[]{:S(2)}) %collective-permute-start.3) | collective-permute-done | bytes 196640 | tf_op jit(solution)/shard_map/ppermute | solution.py:23
  5.2 0.3 collective-permute-done.5
  5.4 1.3 %multiply_convert_fusion.1 = (f16[4,8,3072]{2,1,0:T(8,128)(2,1)S(1)}, f16[4,8,3072]{2,1,0:T(8,128)(2,1)S(1)}, f16[4,8,3072]{2,1,0:T(8,128)(2,1)S(1)}) fusion(bf16[4,8,3072]{2,1,0:T(8,128)(2,1)} %collective-permute-done.3, bf16[2,1,2,1,8,3072]{5,4,3,2,1,0:T(8,128)(2,1)S(1)} %get-tuple-element.17, bf16[2,4,2,2,8,3072]{5,4,3,2,1,0:T(8,128)(2,1)S(1)} %bitcast.82, ...), kind=kLoop, calls=%fused_computation.2 | loop fusion | flops 1769472 | bytes 2359325 | tf_op jit(solution)/shard_map/convert_element_type | solution.py:27
  6.8 3.8 %collective-permute-start.2 = (f16[4,8,3072]{2,1,0:T(8,128)(2,1)S(1)}, f16[4,8,3072]{2,1,0:T(8,128)(2,1)S(1)}, u32[]{:S(2)}, u32[]{:S(2)}) collective-permute-start(f16[4,8,3072]{2,1,0:T(8,128)(2,1)S(1)} %get-tuple-element.16), channel_id=1, source_target_pairs={{0,6},{1,25},{2,4},{3,27},{4,2},{5,29},{6,0},{7,31},{8,14},{9,17},... | collective-permute-start | bytes 589832 | tf_op jit(solution)/shard_map/ppermute | solution.py:23
  10.6 0.5 %collective-permute-start.4 = (f16[4,8,3072]{2,1,0:T(8,128)(2,1)S(1)}, f16[4,8,3072]{2,1,0:T(8,128)(2,1)S(1)}, u32[]{:S(2)}, u32[]{:S(2)}) collective-permute-start(f16[4,8,3072]{2,1,0:T(8,128)(2,1)S(1)} %get-tuple-element.14), channel_id=1, source_target_pairs={{0,2},{1,17},{2,0},{3,19},{4,6},{5,21},{6,4},{7,23},{8,10},{9,25},... | collective-permute-start | bytes 589832 | tf_op jit(solution)/shard_map/ppermute | solution.py:23
  11.1 0.2 collective-permute-start.6
  11.2 3.0 %collective-permute-done.2 = f16[4,8,3072]{2,1,0:T(8,128)(2,1)S(1)} collective-permute-done((f16[4,8,3072]{2,1,0:T(8,128)(2,1)S(1)}, f16[4,8,3072]{2,1,0:T(8,128)(2,1)S(1)}, u32[]{:S(2)}, u32[]{:S(2)}) %collective-permute-start.2) | collective-permute-done | bytes 196640 | tf_op jit(solution)/shard_map/ppermute | solution.py:23
  14.2 0.1 multiply_add_fusion.1
  14.3 2.5 %collective-permute-done.4 = f16[4,8,3072]{2,1,0:T(8,128)(2,1)S(1)} collective-permute-done((f16[4,8,3072]{2,1,0:T(8,128)(2,1)S(1)}, f16[4,8,3072]{2,1,0:T(8,128)(2,1)S(1)}, u32[]{:S(2)}, u32[]{:S(2)}) %collective-permute-start.4) | collective-permute-done | bytes 196640 | tf_op jit(solution)/shard_map/ppermute | solution.py:23
  17.0 3.7 %collective-permute-start.7 = (f16[8,3072]{1,0:T(8,128)(2,1)S(1)}, f16[8,3072]{1,0:T(8,128)(2,1)S(1)}, u32[]{:S(2)}, u32[]{:S(2)}) collective-permute-start(f16[8,3072]{1,0:T(8,128)(2,1)S(1)} %get-tuple-element.29), channel_id=1, source_target_pairs={{0,24},{1,7},{2,26},{3,5},{4,28},{5,3},{6,30},{7,1},{8,16},{9,15},... | collective-permute-start | bytes 147464 | tf_op jit(solution)/shard_map/ppermute | solution.py:23
  20.6 0.8 %collective-permute-start.9 = (f16[8,3072]{1,0:T(8,128)(2,1)S(1)}, f16[8,3072]{1,0:T(8,128)(2,1)S(1)}, u32[]{:S(2)}, u32[]{:S(2)}) collective-permute-start(f16[8,3072]{1,0:T(8,128)(2,1)S(1)} %get-tuple-element.30), channel_id=1, source_target_pairs={{0,8},{1,5},{2,10},{3,7},{4,12},{5,1},{6,14},{7,3},{8,0},{9,13},{1... | collective-permute-start | bytes 147464 | tf_op jit(solution)/shard_map/ppermute | solution.py:23
  21.4 1.5 %collective-permute-done.7 = f16[8,3072]{1,0:T(8,128)(2,1)S(1)} collective-permute-done((f16[8,3072]{1,0:T(8,128)(2,1)S(1)}, f16[8,3072]{1,0:T(8,128)(2,1)S(1)}, u32[]{:S(2)}, u32[]{:S(2)}) %collective-permute-start.7) | collective-permute-done | bytes 49184 | tf_op jit(solution)/shard_map/ppermute | solution.py:23
  22.9 2.7 %collective-permute-done.8 = f16[8,3072]{1,0:T(8,128)(2,1)S(1)} collective-permute-done((f16[8,3072]{1,0:T(8,128)(2,1)S(1)}, f16[8,3072]{1,0:T(8,128)(2,1)S(1)}, u32[]{:S(2)}, u32[]{:S(2)}) %collective-permute-start.8) | collective-permute-done | bytes 49184 | tf_op jit(solution)/shard_map/ppermute | solution.py:23
  25.7 0.2 collective-permute-start.10
  25.9 1.1 %collective-permute-done.10 = f32[4,3072]{1,0:T(4,128)S(1)} collective-permute-done((f32[4,3072]{1,0:T(4,128)S(1)}, f32[4,3072]{1,0:T(4,128)S(1)}, u32[]{:S(2)}, u32[]{:S(2)}) %collective-permute-start.10) | collective-permute-done | bytes 49184 | tf_op jit(solution)/shard_map/ppermute | solution.py:23
  27.1 0.2 subtract_convert_fusion
  27.3 2.1 %collective-permute-start.12 = (bf16[4,6144]{1,0:T(4,128)(2,1)S(1)}, bf16[4,6144]{1,0:T(4,128)(2,1)S(1)}, u32[]{:S(2)}, u32[]{:S(2)}) collective-permute-start(bf16[4,6144]{1,0:T(4,128)(2,1)S(1)} %get-tuple-element.8), channel_id=1, source_target_pairs={{0,16},{1,17},{2,18},{3,19},{4,20},{5,21},{6,22},{7,23},{8,24},{9,... | collective-permute-start | bytes 147464 | tf_op jit(solution)/shard_map/ppermute | solution.py:23
  29.5 0.9 %constant_dynamic-update-slice_fusion.3 = (bf16[4,49152]{1,0:T(4,128)(2,1)S(1)}, bf16[4,6144]{1,0:T(4,128)(2,1)S(1)}, f32[4,6144]{1,0:T(4,128)}, f32[4,6144]{1,0:T(4,128)}, f32[4,6144]{1,0:T(4,128)}) fusion(bf16[4,49152]{1,0:T(4,128)(2,1)S(1)} %broadcast_in_dim.3, s32[]{:T(128)S(6)} %select_n.387, f32[4,6144]{1,0:T(4,128)S(1)} %copy-done.2, ...), kind=kLoop, calls=%fused_computation.49 | loop fusion | flops 393216 | bytes 786436 | tf_op jit(solution)/shard_map/dynamic_update_slice | solution.py:89
  30.3 0.9 %collective-permute-start.11 = (bf16[4,6144]{1,0:T(4,128)(2,1)S(1)}, bf16[4,6144]{1,0:T(4,128)(2,1)S(1)}, u32[]{:S(2)}, u32[]{:S(2)}) collective-permute-start(bf16[4,6144]{1,0:T(4,128)(2,1)S(1)} %get-tuple-element.10), channel_id=1, source_target_pairs={{0,12},{1,13},{2,14},{3,15},{4,8},{5,9},{6,10},{7,11},{8,4},{9,5},... | collective-permute-start | bytes 147464 | tf_op jit(solution)/shard_map/ppermute | solution.py:23
  31.2 1.8 %collective-permute-done.12 = bf16[4,6144]{1,0:T(4,128)(2,1)S(1)} collective-permute-done((bf16[4,6144]{1,0:T(4,128)(2,1)S(1)}, bf16[4,6144]{1,0:T(4,128)(2,1)S(1)}, u32[]{:S(2)}, u32[]{:S(2)}) %collective-permute-start.12) | collective-permute-done | bytes 49184 | tf_op jit(solution)/shard_map/ppermute | solution.py:23
  33.1 1.1 %collective-permute-start.13 = (bf16[2,4,6144]{2,1,0:T(4,128)(2,1)S(1)}, bf16[2,4,6144]{2,1,0:T(4,128)(2,1)S(1)}, u32[]{:S(2)}, u32[]{:S(2)}) collective-permute-start(bf16[2,4,6144]{2,1,0:T(4,128)(2,1)S(1)} %pad_maximum_fusion.1), channel_id=1, source_target_pairs={{0,4},{1,5},{2,6},{3,7},{4,0},{5,1},{6,2},{7,3},{8,12},{9,13},{10,... | collective-permute-start | bytes 294920 | tf_op jit(solution)/shard_map/ppermute | solution.py:23
  34.3 2.4 %collective-permute-start.15 = (bf16[4,6144]{1,0:T(4,128)(2,1)S(1)}, bf16[4,6144]{1,0:T(4,128)(2,1)S(1)}, u32[]{:S(2)}, u32[]{:S(2)}) collective-permute-start(bf16[4,6144]{1,0:T(4,128)(2,1)S(1)} %collective-permute-done.12), channel_id=1, source_target_pairs={{0,12},{1,13},{2,14},{3,15},{4,8},{5,9},{6,10},{7,11},{8,4},{9,5},... | collective-permute-start | bytes 147464 | tf_op jit(solution)/shard_map/ppermute | solution.py:23
  36.8 1.2 %collective-permute-done.13 = bf16[2,4,6144]{2,1,0:T(4,128)(2,1)S(1)} collective-permute-done((bf16[2,4,6144]{2,1,0:T(4,128)(2,1)S(1)}, bf16[2,4,6144]{2,1,0:T(4,128)(2,1)S(1)}, u32[]{:S(2)}, u32[]{:S(2)}) %collective-permute-start.13) | collective-permute-done | bytes 98336 | tf_op jit(solution)/shard_map/ppermute | solution.py:23
  38.0 1.1 %collective-permute-done.14 = bf16[2,4,6144]{2,1,0:T(4,128)(2,1)S(1)} collective-permute-done((bf16[2,4,6144]{2,1,0:T(4,128)(2,1)S(1)}, bf16[2,4,6144]{2,1,0:T(4,128)(2,1)S(1)}, u32[]{:S(2)}, u32[]{:S(2)}) %collective-permute-start.14) | collective-permute-done | bytes 98336 | tf_op jit(solution)/shard_map/ppermute | solution.py:23
  39.1 1.0 %collective-permute-done.15 = bf16[4,6144]{1,0:T(4,128)(2,1)S(1)} collective-permute-done((bf16[4,6144]{1,0:T(4,128)(2,1)S(1)}, bf16[4,6144]{1,0:T(4,128)(2,1)S(1)}, u32[]{:S(2)}, u32[]{:S(2)}) %collective-permute-start.15) | collective-permute-done | bytes 49184 | tf_op jit(solution)/shard_map/ppermute | solution.py:23
  40.2 0.7 %copy-done.1 = bf16[4,49152]{1,0:T(4,128)(2,1)} copy-done((bf16[4,49152]{1,0:T(4,128)(2,1)}, bf16[4,49152]{1,0:T(4,128)(2,1)S(1)}, u32[]{:S(2)}) %copy-start.1) | copy-done | bytes 393240
  (33 shorter events, 0.8 us)
Async XLA Ops:
  0.9 2.0 %copy-start = (bf16[1,1,16,49152]{3,2,1,0:T(8,128)(2,1)S(1)}, bf16[1,1,16,49152]{3,2,1,0:T(8,128)(2,1)}, u32[]{:S(2)}) copy-start(bf16[1,1,16,49152]{3,2,1,0:T(8,128)(2,1)} %param.4) | copy-start | bytes 4718596
  3.1 1.6 %collective-permute-start.1 = (bf16[4,8,3072]{2,1,0:T(8,128)(2,1)S(1)}, bf16[4,8,3072]{2,1,0:T(8,128)(2,1)S(1)}, u32[]{:S(2)}, u32[]{:S(2)}) collective-permute-start(bf16[4,8,3072]{2,1,0:T(8,128)(2,1)S(1)} %get-tuple-element.27), channel_id=1, source_target_pairs={{0,1},{1,0},{2,3},{3,2},{4,5},{5,4},{6,7},{7,6},{8,9},{9,8},{10,11... | collective-permute-start | bytes 589832 | tf_op jit(solution)/shard_map/ppermute | solution.py:23
  3.6 1.6 %collective-permute-start.3 = (bf16[4,8,3072]{2,1,0:T(8,128)(2,1)S(1)}, bf16[4,8,3072]{2,1,0:T(8,128)(2,1)}, u32[]{:S(2)}, u32[]{:S(2)}) collective-permute-start(bf16[4,8,3072]{2,1,0:T(8,128)(2,1)S(1)} %get-tuple-element.25), channel_id=1, source_target_pairs={{0,1},{1,0},{2,3},{3,2},{4,5},{5,4},{6,7},{7,6},{8,9},{9,8},{10,11... | collective-permute-start | bytes 589832 | tf_op jit(solution)/shard_map/ppermute | solution.py:23
  3.7 1.8 %collective-permute-start.5 = (bf16[4,8,3072]{2,1,0:T(8,128)(2,1)S(1)}, bf16[4,8,3072]{2,1,0:T(8,128)(2,1)}, u32[]{:S(2)}, u32[]{:S(2)}) collective-permute-start(bf16[4,8,3072]{2,1,0:T(8,128)(2,1)S(1)} %get-tuple-element.26), channel_id=1, source_target_pairs={{0,1},{1,0},{2,3},{3,2},{4,5},{5,4},{6,7},{7,6},{8,9},{9,8},{10,11... | collective-permute-start | bytes 589832 | tf_op jit(solution)/shard_map/ppermute | solution.py:23
  4.1 7.1 %collective-permute-start = (bf16[4,8,3072]{2,1,0:T(8,128)(2,1)S(1)}, bf16[4,8,3072]{2,1,0:T(8,128)(2,1)S(1)}, u32[]{:S(2)}, u32[]{:S(2)}) collective-permute-start(bf16[4,8,3072]{2,1,0:T(8,128)(2,1)S(1)} %get-tuple-element.28), channel_id=1, source_target_pairs={{0,1},{1,0},{2,3},{3,2},{4,5},{5,4},{6,7},{7,6},{8,9},{9,8},{10,11... | collective-permute-start | bytes 589832 | tf_op jit(solution)/shard_map/ppermute | solution.py:23
  6.8 7.4 %collective-permute-start.2 = (f16[4,8,3072]{2,1,0:T(8,128)(2,1)S(1)}, f16[4,8,3072]{2,1,0:T(8,128)(2,1)S(1)}, u32[]{:S(2)}, u32[]{:S(2)}) collective-permute-start(f16[4,8,3072]{2,1,0:T(8,128)(2,1)S(1)} %get-tuple-element.16), channel_id=1, source_target_pairs={{0,6},{1,25},{2,4},{3,27},{4,2},{5,29},{6,0},{7,31},{8,14},{9,17},... | collective-permute-start | bytes 589832 | tf_op jit(solution)/shard_map/ppermute | solution.py:23
  10.6 6.3 %collective-permute-start.4 = (f16[4,8,3072]{2,1,0:T(8,128)(2,1)S(1)}, f16[4,8,3072]{2,1,0:T(8,128)(2,1)S(1)}, u32[]{:S(2)}, u32[]{:S(2)}) collective-permute-start(f16[4,8,3072]{2,1,0:T(8,128)(2,1)S(1)} %get-tuple-element.14), channel_id=1, source_target_pairs={{0,2},{1,17},{2,0},{3,19},{4,6},{5,21},{6,4},{7,23},{8,10},{9,25},... | collective-permute-start | bytes 589832 | tf_op jit(solution)/shard_map/ppermute | solution.py:23
  11.1 5.8 %collective-permute-start.6 = (f16[4,8,3072]{2,1,0:T(8,128)(2,1)S(1)}, f16[4,8,3072]{2,1,0:T(8,128)(2,1)S(1)}, u32[]{:S(2)}, u32[]{:S(2)}) collective-permute-start(f16[4,8,3072]{2,1,0:T(8,128)(2,1)S(1)} %get-tuple-element.15), channel_id=1, source_target_pairs={{0,4},{1,9},{2,6},{3,11},{4,0},{5,13},{6,2},{7,15},{8,12},{9,1},{1... | collective-permute-start | bytes 589832 | tf_op jit(solution)/shard_map/ppermute | solution.py:23
  14.2 12.8 %copy-start.2 = (f32[4,6144]{1,0:T(4,128)S(1)}, f32[4,6144]{1,0:T(4,128)}, u32[]{:S(2)}) copy-start(f32[4,6144]{1,0:T(4,128)} %param.5) | copy-start | bytes 294916
  14.2 12.9 %copy-start.3 = (f32[4,6144]{1,0:T(4,128)S(1)}, f32[4,6144]{1,0:T(4,128)}, u32[]{:S(2)}) copy-start(f32[4,6144]{1,0:T(4,128)} %param.7) | copy-start | bytes 294916
  14.2 12.9 %copy-start.4 = (f32[4,6144]{1,0:T(4,128)S(1)}, f32[4,6144]{1,0:T(4,128)}, u32[]{:S(2)}) copy-start(f32[4,6144]{1,0:T(4,128)} %param.6) | copy-start | bytes 294916
  17.0 6.0 %collective-permute-start.7 = (f16[8,3072]{1,0:T(8,128)(2,1)S(1)}, f16[8,3072]{1,0:T(8,128)(2,1)S(1)}, u32[]{:S(2)}, u32[]{:S(2)}) collective-permute-start(f16[8,3072]{1,0:T(8,128)(2,1)S(1)} %get-tuple-element.29), channel_id=1, source_target_pairs={{0,24},{1,7},{2,26},{3,5},{4,28},{5,3},{6,30},{7,1},{8,16},{9,15},... | collective-permute-start | bytes 147464 | tf_op jit(solution)/shard_map/ppermute | solution.py:23
  20.6 5.0 %collective-permute-start.8 = (f16[8,3072]{1,0:T(8,128)(2,1)S(1)}, f16[8,3072]{1,0:T(8,128)(2,1)S(1)}, u32[]{:S(2)}, u32[]{:S(2)}) collective-permute-start(f16[8,3072]{1,0:T(8,128)(2,1)S(1)} %get-tuple-element.31), channel_id=1, source_target_pairs={{0,16},{1,3},{2,18},{3,1},{4,20},{5,7},{6,22},{7,5},{8,24},{9,11},... | collective-permute-start | bytes 147464 | tf_op jit(solution)/shard_map/ppermute | solution.py:23
  20.6 5.0 %collective-permute-start.9 = (f16[8,3072]{1,0:T(8,128)(2,1)S(1)}, f16[8,3072]{1,0:T(8,128)(2,1)S(1)}, u32[]{:S(2)}, u32[]{:S(2)}) collective-permute-start(f16[8,3072]{1,0:T(8,128)(2,1)S(1)} %get-tuple-element.30), channel_id=1, source_target_pairs={{0,8},{1,5},{2,10},{3,7},{4,12},{5,1},{6,14},{7,3},{8,0},{9,13},{1... | collective-permute-start | bytes 147464 | tf_op jit(solution)/shard_map/ppermute | solution.py:23
  25.7 1.3 %collective-permute-start.10 = (f32[4,3072]{1,0:T(4,128)S(1)}, f32[4,3072]{1,0:T(4,128)S(1)}, u32[]{:S(2)}, u32[]{:S(2)}) collective-permute-start(f32[4,3072]{1,0:T(4,128)S(1)} %dynamic-slice_bitcast_fusion), channel_id=1, source_target_pairs={{0,1},{1,0},{2,3},{3,2},{4,5},{5,4},{6,7},{7,6},{8,9},{9,8},{10,11... | collective-permute-start | bytes 147464 | tf_op jit(solution)/shard_map/ppermute | solution.py:23
  27.3 12.9 %copy-start.5 = (f32[4,6144]{1,0:T(4,128)}, f32[4,6144]{1,0:T(4,128)S(1)}, u32[]{:S(2)}) copy-start(f32[4,6144]{1,0:T(4,128)S(1)} %get-tuple-element.2) | copy-start | bytes 294916
  27.3 5.8 %collective-permute-start.12 = (bf16[4,6144]{1,0:T(4,128)(2,1)S(1)}, bf16[4,6144]{1,0:T(4,128)(2,1)S(1)}, u32[]{:S(2)}, u32[]{:S(2)}) collective-permute-start(bf16[4,6144]{1,0:T(4,128)(2,1)S(1)} %get-tuple-element.8), channel_id=1, source_target_pairs={{0,16},{1,17},{2,18},{3,19},{4,20},{5,21},{6,22},{7,23},{8,24},{9,... | collective-permute-start | bytes 147464 | tf_op jit(solution)/shard_map/ppermute | solution.py:23
  30.3 6.4 %collective-permute-start.11 = (bf16[4,6144]{1,0:T(4,128)(2,1)S(1)}, bf16[4,6144]{1,0:T(4,128)(2,1)S(1)}, u32[]{:S(2)}, u32[]{:S(2)}) collective-permute-start(bf16[4,6144]{1,0:T(4,128)(2,1)S(1)} %get-tuple-element.10), channel_id=1, source_target_pairs={{0,12},{1,13},{2,14},{3,15},{4,8},{5,9},{6,10},{7,11},{8,4},{9,5},... | collective-permute-start | bytes 147464 | tf_op jit(solution)/shard_map/ppermute | solution.py:23
  33.1 4.8 %collective-permute-start.13 = (bf16[2,4,6144]{2,1,0:T(4,128)(2,1)S(1)}, bf16[2,4,6144]{2,1,0:T(4,128)(2,1)S(1)}, u32[]{:S(2)}, u32[]{:S(2)}) collective-permute-start(bf16[2,4,6144]{2,1,0:T(4,128)(2,1)S(1)} %pad_maximum_fusion.1), channel_id=1, source_target_pairs={{0,4},{1,5},{2,6},{3,7},{4,0},{5,1},{6,2},{7,3},{8,12},{9,13},{10,... | collective-permute-start | bytes 294920 | tf_op jit(solution)/shard_map/ppermute | solution.py:23
  34.3 4.8 %collective-permute-start.14 = (bf16[2,4,6144]{2,1,0:T(4,128)(2,1)S(1)}, bf16[2,4,6144]{2,1,0:T(4,128)(2,1)S(1)}, u32[]{:S(2)}, u32[]{:S(2)}) collective-permute-start(bf16[2,4,6144]{2,1,0:T(4,128)(2,1)S(1)} %pad_maximum_fusion.1), channel_id=1, source_target_pairs={{0,8},{1,9},{2,10},{3,11},{4,12},{5,13},{6,14},{7,15},{8,0},{9,1},... | collective-permute-start | bytes 294920 | tf_op jit(solution)/shard_map/ppermute | solution.py:23
  34.3 5.9 %collective-permute-start.15 = (bf16[4,6144]{1,0:T(4,128)(2,1)S(1)}, bf16[4,6144]{1,0:T(4,128)(2,1)S(1)}, u32[]{:S(2)}, u32[]{:S(2)}) collective-permute-start(bf16[4,6144]{1,0:T(4,128)(2,1)S(1)} %collective-permute-done.12), channel_id=1, source_target_pairs={{0,12},{1,13},{2,14},{3,15},{4,8},{5,9},{6,10},{7,11},{8,4},{9,5},... | collective-permute-start | bytes 147464 | tf_op jit(solution)/shard_map/ppermute | solution.py:23
  40.2 0.7 %copy-start.1 = (bf16[4,49152]{1,0:T(4,128)(2,1)}, bf16[4,49152]{1,0:T(4,128)(2,1)S(1)}, u32[]{:S(2)}) copy-start(bf16[4,49152]{1,0:T(4,128)(2,1)S(1)} %constant_dynamic-update-slice_fusion) | copy-start | bytes 1179652

commit v8 on v7

--- a/solution.py
+++ b/solution.py
@@ -45,25 +45,22 @@
     x, core = me_local // 2, me_local % 2
     z, y = me_host // 2, me_host % 2
 
-    def part(value, of_half, of_core, i):
-        value = value.reshape(2, tile, 16, half).transpose(0, 2, 1, 3)
-        value = pick(value.reshape(2, 4, 2, 2, tile, half).transpose(3, 0, 1, 2, 4, 5), of_half)
+    split = gradient.reshape(2, tile, 16, half).transpose(0, 2, 1, 3)
+    split = split.reshape(2, 4, 2, 2, tile, half).transpose(3, 0, 1, 2, 4, 5)
+    own, other = pick(split, core), swap(pick(split, 1 - core), CORE, CORE)
+
+    def part(value, i):
         by_xy = lax.dynamic_slice(value, (i // 2, 0, i % 2, 0, 0), (1, 4, 1, tile, half))
         by_z = lax.dynamic_slice(value, (0, i, 0, 0, 0), (2, 1, 2, tile, half))
-        return jnp.where(of_core == 0, by_xy.reshape(4, tile, half), by_z.reshape(4, tile, half))
+        return jnp.where(core == 0, by_xy.reshape(4, tile, half), by_z.reshape(4, tile, half))
+
+    def pair(i):
+        return part(own, i).astype(jnp.float32) + part(other, i).astype(jnp.float32)
 
     over_xy, over_z = (0, Y, X, X + Y), (0, Z_NEAR, Z_FAR, Z_NEAR + Z_FAR)
-    me, mate = jnp.where(core == 0, 2 * x + y, z), jnp.where(core == 0, z, 2 * x + y)
-
-    def give(d):
-        return swap(part(gradient, 1 - core, 1 - core, mate ^ d), CORE, CORE)
-
-    def pair(d, other):
-        return part(gradient, core, core, me ^ d).astype(jnp.float32) + other.astype(jnp.float32)
-
-    other = {d: give(d) for d in (3, 2, 1, 0)}
-    got = [swap(narrow(pair(d, other[d])), over_xy[d], over_z[d]) for d in (3, 2, 1)]
-    quarter = lax.optimization_barrier(pair(0, other[0]) + widen(got[0]))
+    me = jnp.where(core == 0, 2 * x + y, z)
+    got = [swap(narrow(pair(me ^ d)), over_xy[d], over_z[d]) for d in (3, 2, 1)]
+    quarter = lax.optimization_barrier(pair(me) + widen(got[0]))
     quarter = quarter + widen(got[1]) + widen(got[2])
     me = jnp.where(core == 0, z, 2 * x + y)
     got = [swap(narrow(pick(quarter, me ^ d)), over_z[d], over_xy[d]) for d in (3, 2, 1)]

time: 41.1 us -> 38.8 us (0.944)
  other arithmetic: 2.86 us -> 1.92 us
  starting transfers between devices: 16.8 us -> 15.9 us
  local copies, waits for them, and re-layouts: 3.09 us -> 2.56 us
    dynamic_slice x1 -> x2, local copies, waits for them, and re-layouts: 1.72 us -> 0.12 us  [part(): by_z = lax.dynamic_slice(value, (0, i, 0, 0, 0), (2, 1, 2, tile, half))]
    squeeze x1 -> x2, local copies, waits for them, and re-layouts: 0.01 us -> 1.33 us  [pick(): return lax.dynamic_index_in_dim(value, index, 0, keepdims=False)]
    ppermute x16 -> x13, starting transfers between devices: 16.8 us -> 15.9 us  [swap(): return lax.ppermute(value, ('hst', 'local'), flip_pairs(flips))]
    convert_element_type x2 -> x3, other arithmetic: 1.36 us -> 0.5 us  [narrow(): return (value * wire_scale).astype(jnp.float16)]
    ppermute x16 -> x13, waiting for transfers between devices: 17.1 us -> 17.4 us  [swap(): return lax.ppermute(value, ('hst', 'local'), flip_pairs(flips))]
  transfers between devices with their start and end apart: 16 -> 13, of which waited for: 12 -> 11; matrix products, arithmetic and copies ran while one was open for 7% -> 4% of each run, Pallas kernels for 0% -> 0%
where the time goes in v8:
time: 38.8 us; the launch traced here: 38.7 us
  waiting for transfers between devices  17.4 us (45%)
  starting transfers between devices  15.9 us (41%)
  local copies, waits for them, and re-layouts  2.56 us (7%)
  other arithmetic  1.92 us (5%)
  between operations  0.86 us (2%)
    ppermute x13, waiting for transfers between devices, swap(): return lax.ppermute(value, ('hst', 'local'), flip_pairs(flips))  17.4 us
    ppermute x13, starting transfers between devices, swap(): return lax.ppermute(value, ('hst', 'local'), flip_pairs(flips))  15.9 us
    squeeze x2, local copies, waits for them, and re-layouts, pick(): return lax.dynamic_index_in_dim(value, index, 0, keepdims=False)  1.33 us
    dynamic_update_slice x1, other arithmetic, gather_blocks(): lax.dynamic_update_slice_in_dim(whole, block, (me ^ bits) * col_block, 1)  0.87 us
  transfers between devices with their start and end apart: 13, of which 11 were waited for; matrix products, arithmetic and copies ran while one was open for 4% of the time, Pallas kernels for 0%

profile of v8, /device:TPU:0, one launch (start us, length us, event | category | flops | bytes accessed | tf_op | source)
XLA Modules:
  0.0 38.7 jit_solution(17845495920589752150)
XLA Ops:
  0.7 1.3 %dynamic-slice_bitcast_fusion = bf16[2,4,2,8,3072]{4,3,2,1,0:T(8,128)(2,1)S(1)} fusion(bf16[2,4,2,2,8,3072]{5,4,3,2,1,0:T(8,128)(2,1)} %bitcast.90, s32[]{:T(128)S(6)} %select_n.251), kind=kLoop, calls=%fused_computation | loop fusion | bytes 1572868 | tf_op jit(solution)/shard_map/jit(dynamic_index_in_dim)/squeeze | solution.py:35
  2.0 0.5 %collective-permute-start = (bf16[2,4,2,8,3072]{4,3,2,1,0:T(8,128)(2,1)S(1)}, bf16[2,4,2,8,3072]{4,3,2,1,0:T(8,128)(2,1)S(1)}, u32[]{:S(2)}, u32[]{:S(2)}) collective-permute-start(bf16[2,4,2,8,3072]{4,3,2,1,0:T(8,128)(2,1)S(1)} %dynamic-slice_bitcast_fusion), channel_id=1, source_target_pairs={{0,1},{1,0},{2,3},{3,2},{4,5},{5,4},{6,7},{7,6},{8,9},{9,8},{10,11... | collective-permute-start | bytes 2359304 | tf_op jit(solution)/shard_map/ppermute | solution.py:23
  2.6 1.9 %collective-permute-done = bf16[2,4,2,8,3072]{4,3,2,1,0:T(8,128)(2,1)S(1)} collective-permute-done((bf16[2,4,2,8,3072]{4,3,2,1,0:T(8,128)(2,1)S(1)}, bf16[2,4,2,8,3072]{4,3,2,1,0:T(8,128)(2,1)S(1)}, u32[]{:S(2)}, u32[]{:S(2)}) %collective-permute-start) | collective-permute-done | bytes 786464 | tf_op jit(solution)/shard_map/ppermute | solution.py:23
  4.4 0.1 constant_dynamic-slice_fusion.2
  4.5 0.2 multiply_convert_fusion.2
  4.7 3.9 %collective-permute-start.1 = (f16[4,8,3072]{2,1,0:T(8,128)(2,1)S(1)}, f16[4,8,3072]{2,1,0:T(8,128)(2,1)S(1)}, u32[]{:S(2)}, u32[]{:S(2)}) collective-permute-start(f16[4,8,3072]{2,1,0:T(8,128)(2,1)S(1)} %multiply_convert_fusion.2), channel_id=1, source_target_pairs={{0,6},{1,25},{2,4},{3,27},{4,2},{5,29},{6,0},{7,31},{8,14},{9,17},... | collective-permute-start | bytes 589832 | tf_op jit(solution)/shard_map/ppermute | solution.py:23
  8.5 0.3 multiply_convert_fusion.1
  8.8 0.6 %collective-permute-start.2 = (f16[4,8,3072]{2,1,0:T(8,128)(2,1)S(1)}, f16[4,8,3072]{2,1,0:T(8,128)(2,1)S(1)}, u32[]{:S(2)}, u32[]{:S(2)}) collective-permute-start(f16[4,8,3072]{2,1,0:T(8,128)(2,1)S(1)} %get-tuple-element.14), channel_id=1, source_target_pairs={{0,2},{1,17},{2,0},{3,19},{4,6},{5,21},{6,4},{7,23},{8,10},{9,25},... | collective-permute-start | bytes 589832 | tf_op jit(solution)/shard_map/ppermute | solution.py:23
  9.5 2.7 %collective-permute-done.1 = f16[4,8,3072]{2,1,0:T(8,128)(2,1)S(1)} collective-permute-done((f16[4,8,3072]{2,1,0:T(8,128)(2,1)S(1)}, f16[4,8,3072]{2,1,0:T(8,128)(2,1)S(1)}, u32[]{:S(2)}, u32[]{:S(2)}) %collective-permute-start.1) | collective-permute-done | bytes 196640 | tf_op jit(solution)/shard_map/ppermute | solution.py:23
  12.2 0.2 multiply_add_fusion.1
  12.4 2.4 %collective-permute-done.2 = f16[4,8,3072]{2,1,0:T(8,128)(2,1)S(1)} collective-permute-done((f16[4,8,3072]{2,1,0:T(8,128)(2,1)S(1)}, f16[4,8,3072]{2,1,0:T(8,128)(2,1)S(1)}, u32[]{:S(2)}, u32[]{:S(2)}) %collective-permute-start.2) | collective-permute-done | bytes 196640 | tf_op jit(solution)/shard_map/ppermute | solution.py:23
  14.8 0.3 collective-permute-done.3
  15.1 0.1 multiply_add_fusion
  15.3 3.7 %collective-permute-start.4 = (f16[8,3072]{1,0:T(8,128)(2,1)S(1)}, f16[8,3072]{1,0:T(8,128)(2,1)S(1)}, u32[]{:S(2)}, u32[]{:S(2)}) collective-permute-start(f16[8,3072]{1,0:T(8,128)(2,1)S(1)} %get-tuple-element.24), channel_id=1, source_target_pairs={{0,24},{1,7},{2,26},{3,5},{4,28},{5,3},{6,30},{7,1},{8,16},{9,15},... | collective-permute-start | bytes 147464 | tf_op jit(solution)/shard_map/ppermute | solution.py:23
  18.9 0.8 %collective-permute-start.6 = (f16[8,3072]{1,0:T(8,128)(2,1)S(1)}, f16[8,3072]{1,0:T(8,128)(2,1)S(1)}, u32[]{:S(2)}, u32[]{:S(2)}) collective-permute-start(f16[8,3072]{1,0:T(8,128)(2,1)S(1)} %get-tuple-element.25), channel_id=1, source_target_pairs={{0,8},{1,5},{2,10},{3,7},{4,12},{5,1},{6,14},{7,3},{8,0},{9,13},{1... | collective-permute-start | bytes 147464 | tf_op jit(solution)/shard_map/ppermute | solution.py:23
  19.7 1.5 %collective-permute-done.4 = f16[8,3072]{1,0:T(8,128)(2,1)S(1)} collective-permute-done((f16[8,3072]{1,0:T(8,128)(2,1)S(1)}, f16[8,3072]{1,0:T(8,128)(2,1)S(1)}, u32[]{:S(2)}, u32[]{:S(2)}) %collective-permute-start.4) | collective-permute-done | bytes 49184 | tf_op jit(solution)/shard_map/ppermute | solution.py:23
  21.2 2.7 %collective-permute-done.5 = f16[8,3072]{1,0:T(8,128)(2,1)S(1)} collective-permute-done((f16[8,3072]{1,0:T(8,128)(2,1)S(1)}, f16[8,3072]{1,0:T(8,128)(2,1)S(1)}, u32[]{:S(2)}, u32[]{:S(2)}) %collective-permute-start.5) | collective-permute-done | bytes 49184 | tf_op jit(solution)/shard_map/ppermute | solution.py:23
  24.0 0.1 collective-permute-start.7
  24.1 1.2 %collective-permute-done.7 = f32[4,3072]{1,0:T(4,128)S(1)} collective-permute-done((f32[4,3072]{1,0:T(4,128)S(1)}, f32[4,3072]{1,0:T(4,128)S(1)}, u32[]{:S(2)}, u32[]{:S(2)}) %collective-permute-start.7) | collective-permute-done | bytes 49184 | tf_op jit(solution)/shard_map/ppermute | solution.py:23
  25.4 0.2 subtract_convert_fusion
  25.6 2.1 %collective-permute-start.9 = (bf16[4,6144]{1,0:T(4,128)(2,1)S(1)}, bf16[4,6144]{1,0:T(4,128)(2,1)S(1)}, u32[]{:S(2)}, u32[]{:S(2)}) collective-permute-start(bf16[4,6144]{1,0:T(4,128)(2,1)S(1)} %get-tuple-element.8), channel_id=1, source_target_pairs={{0,16},{1,17},{2,18},{3,19},{4,20},{5,21},{6,22},{7,23},{8,24},{9,... | collective-permute-start | bytes 147464 | tf_op jit(solution)/shard_map/ppermute | solution.py:23
  27.6 0.1 broadcast_in_dim.3
  27.8 0.9 %constant_dynamic-update-slice_fusion.2 = (bf16[4,49152]{1,0:T(4,128)(2,1)S(1)}, bf16[4,6144]{1,0:T(4,128)(2,1)S(1)}, f32[4,6144]{1,0:T(4,128)}, f32[4,6144]{1,0:T(4,128)}, f32[4,6144]{1,0:T(4,128)}) fusion(bf16[4,49152]{1,0:T(4,128)(2,1)S(1)} %broadcast_in_dim.3, s32[]{:T(128)S(6)} %select_n.290, f32[4,6144]{1,0:T(4,128)S(1)} %copy-done.2, ...), kind=kLoop, calls=%fused_computation.49 | loop fusion | flops 393216 | bytes 786436 | tf_op jit(solution)/shard_map/dynamic_update_slice | solution.py:86
  28.6 0.6 %collective-permute-start.8 = (bf16[4,6144]{1,0:T(4,128)(2,1)S(1)}, bf16[4,6144]{1,0:T(4,128)(2,1)S(1)}, u32[]{:S(2)}, u32[]{:S(2)}) collective-permute-start(bf16[4,6144]{1,0:T(4,128)(2,1)S(1)} %get-tuple-element.10), channel_id=1, source_target_pairs={{0,12},{1,13},{2,14},{3,15},{4,8},{5,9},{6,10},{7,11},{8,4},{9,5},... | collective-permute-start | bytes 147464 | tf_op jit(solution)/shard_map/ppermute | solution.py:23
  29.2 1.7 %collective-permute-done.9 = bf16[4,6144]{1,0:T(4,128)(2,1)S(1)} collective-permute-done((bf16[4,6144]{1,0:T(4,128)(2,1)S(1)}, bf16[4,6144]{1,0:T(4,128)(2,1)S(1)}, u32[]{:S(2)}, u32[]{:S(2)}) %collective-permute-start.9) | collective-permute-done | bytes 49184 | tf_op jit(solution)/shard_map/ppermute | solution.py:23
  31.0 0.1 pad_maximum_fusion.1
  31.0 1.2 %collective-permute-start.10 = (bf16[2,4,6144]{2,1,0:T(4,128)(2,1)S(1)}, bf16[2,4,6144]{2,1,0:T(4,128)(2,1)S(1)}, u32[]{:S(2)}, u32[]{:S(2)}) collective-permute-start(bf16[2,4,6144]{2,1,0:T(4,128)(2,1)S(1)} %pad_maximum_fusion.1), channel_id=1, source_target_pairs={{0,4},{1,5},{2,6},{3,7},{4,0},{5,1},{6,2},{7,3},{8,12},{9,13},{10,... | collective-permute-start | bytes 294920 | tf_op jit(solution)/shard_map/ppermute | solution.py:23
  32.3 2.3 %collective-permute-start.12 = (bf16[4,6144]{1,0:T(4,128)(2,1)S(1)}, bf16[4,6144]{1,0:T(4,128)(2,1)S(1)}, u32[]{:S(2)}, u32[]{:S(2)}) collective-permute-start(bf16[4,6144]{1,0:T(4,128)(2,1)S(1)} %collective-permute-done.9), channel_id=1, source_target_pairs={{0,12},{1,13},{2,14},{3,15},{4,8},{5,9},{6,10},{7,11},{8,4},{9,5},... | collective-permute-start | bytes 147464 | tf_op jit(solution)/shard_map/ppermute | solution.py:23
  34.7 1.1 %collective-permute-done.10 = bf16[2,4,6144]{2,1,0:T(4,128)(2,1)S(1)} collective-permute-done((bf16[2,4,6144]{2,1,0:T(4,128)(2,1)S(1)}, bf16[2,4,6144]{2,1,0:T(4,128)(2,1)S(1)}, u32[]{:S(2)}, u32[]{:S(2)}) %collective-permute-start.10) | collective-permute-done | bytes 98336 | tf_op jit(solution)/shard_map/ppermute | solution.py:23
  35.8 1.3 %collective-permute-done.11 = bf16[2,4,6144]{2,1,0:T(4,128)(2,1)S(1)} collective-permute-done((bf16[2,4,6144]{2,1,0:T(4,128)(2,1)S(1)}, bf16[2,4,6144]{2,1,0:T(4,128)(2,1)S(1)}, u32[]{:S(2)}, u32[]{:S(2)}) %collective-permute-start.11) | collective-permute-done | bytes 98336 | tf_op jit(solution)/shard_map/ppermute | solution.py:23
  37.1 0.7 %collective-permute-done.12 = bf16[4,6144]{1,0:T(4,128)(2,1)S(1)} collective-permute-done((bf16[4,6144]{1,0:T(4,128)(2,1)S(1)}, bf16[4,6144]{1,0:T(4,128)(2,1)S(1)}, u32[]{:S(2)}, u32[]{:S(2)}) %collective-permute-start.12) | collective-permute-done | bytes 49184 | tf_op jit(solution)/shard_map/ppermute | solution.py:23
  37.9 0.7 %copy-done.1 = bf16[4,49152]{1,0:T(4,128)(2,1)} copy-done((bf16[4,49152]{1,0:T(4,128)(2,1)}, bf16[4,49152]{1,0:T(4,128)(2,1)S(1)}, u32[]{:S(2)}) %copy-start.1) | copy-done | bytes 393240
  (29 shorter events, 0.5 us)
Async XLA Ops:
  0.6 1.9 %copy-start = (bf16[1,1,16,49152]{3,2,1,0:T(8,128)(2,1)S(1)}, bf16[1,1,16,49152]{3,2,1,0:T(8,128)(2,1)}, u32[]{:S(2)}) copy-start(bf16[1,1,16,49152]{3,2,1,0:T(8,128)(2,1)} %param.4) | copy-start | bytes 4718596
  2.0 2.4 %collective-permute-start = (bf16[2,4,2,8,3072]{4,3,2,1,0:T(8,128)(2,1)S(1)}, bf16[2,4,2,8,3072]{4,3,2,1,0:T(8,128)(2,1)S(1)}, u32[]{:S(2)}, u32[]{:S(2)}) collective-permute-start(bf16[2,4,2,8,3072]{4,3,2,1,0:T(8,128)(2,1)S(1)} %dynamic-slice_bitcast_fusion), channel_id=1, source_target_pairs={{0,1},{1,0},{2,3},{3,2},{4,5},{5,4},{6,7},{7,6},{8,9},{9,8},{10,11... | collective-permute-start | bytes 2359304 | tf_op jit(solution)/shard_map/ppermute | solution.py:23
  4.7 7.5 %collective-permute-start.1 = (f16[4,8,3072]{2,1,0:T(8,128)(2,1)S(1)}, f16[4,8,3072]{2,1,0:T(8,128)(2,1)S(1)}, u32[]{:S(2)}, u32[]{:S(2)}) collective-permute-start(f16[4,8,3072]{2,1,0:T(8,128)(2,1)S(1)} %multiply_convert_fusion.2), channel_id=1, source_target_pairs={{0,6},{1,25},{2,4},{3,27},{4,2},{5,29},{6,0},{7,31},{8,14},{9,17},... | collective-permute-start | bytes 589832 | tf_op jit(solution)/shard_map/ppermute | solution.py:23
  8.8 6.0 %collective-permute-start.2 = (f16[4,8,3072]{2,1,0:T(8,128)(2,1)S(1)}, f16[4,8,3072]{2,1,0:T(8,128)(2,1)S(1)}, u32[]{:S(2)}, u32[]{:S(2)}) collective-permute-start(f16[4,8,3072]{2,1,0:T(8,128)(2,1)S(1)} %get-tuple-element.14), channel_id=1, source_target_pairs={{0,2},{1,17},{2,0},{3,19},{4,6},{5,21},{6,4},{7,23},{8,10},{9,25},... | collective-permute-start | bytes 589832 | tf_op jit(solution)/shard_map/ppermute | solution.py:23
  9.4 5.7 %collective-permute-start.3 = (f16[4,8,3072]{2,1,0:T(8,128)(2,1)S(1)}, f16[4,8,3072]{2,1,0:T(8,128)(2,1)S(1)}, u32[]{:S(2)}, u32[]{:S(2)}) collective-permute-start(f16[4,8,3072]{2,1,0:T(8,128)(2,1)S(1)} %get-tuple-element.15), channel_id=1, source_target_pairs={{0,4},{1,9},{2,6},{3,11},{4,0},{5,13},{6,2},{7,15},{8,12},{9,1},{1... | collective-permute-start | bytes 589832 | tf_op jit(solution)/shard_map/ppermute | solution.py:23
  12.3 13.0 %copy-start.2 = (f32[4,6144]{1,0:T(4,128)S(1)}, f32[4,6144]{1,0:T(4,128)}, u32[]{:S(2)}) copy-start(f32[4,6144]{1,0:T(4,128)} %param.5) | copy-start | bytes 294916
  12.4 13.0 %copy-start.3 = (f32[4,6144]{1,0:T(4,128)S(1)}, f32[4,6144]{1,0:T(4,128)}, u32[]{:S(2)}) copy-start(f32[4,6144]{1,0:T(4,128)} %param.7) | copy-start | bytes 294916
  12.4 13.0 %copy-start.4 = (f32[4,6144]{1,0:T(4,128)S(1)}, f32[4,6144]{1,0:T(4,128)}, u32[]{:S(2)}) copy-start(f32[4,6144]{1,0:T(4,128)} %param.6) | copy-start | bytes 294916
  15.3 6.0 %collective-permute-start.4 = (f16[8,3072]{1,0:T(8,128)(2,1)S(1)}, f16[8,3072]{1,0:T(8,128)(2,1)S(1)}, u32[]{:S(2)}, u32[]{:S(2)}) collective-permute-start(f16[8,3072]{1,0:T(8,128)(2,1)S(1)} %get-tuple-element.24), channel_id=1, source_target_pairs={{0,24},{1,7},{2,26},{3,5},{4,28},{5,3},{6,30},{7,1},{8,16},{9,15},... | collective-permute-start | bytes 147464 | tf_op jit(solution)/shard_map/ppermute | solution.py:23
  18.9 5.0 %collective-permute-start.5 = (f16[8,3072]{1,0:T(8,128)(2,1)S(1)}, f16[8,3072]{1,0:T(8,128)(2,1)S(1)}, u32[]{:S(2)}, u32[]{:S(2)}) collective-permute-start(f16[8,3072]{1,0:T(8,128)(2,1)S(1)} %get-tuple-element.26), channel_id=1, source_target_pairs={{0,16},{1,3},{2,18},{3,1},{4,20},{5,7},{6,22},{7,5},{8,24},{9,11},... | collective-permute-start | bytes 147464 | tf_op jit(solution)/shard_map/ppermute | solution.py:23
  18.9 5.0 %collective-permute-start.6 = (f16[8,3072]{1,0:T(8,128)(2,1)S(1)}, f16[8,3072]{1,0:T(8,128)(2,1)S(1)}, u32[]{:S(2)}, u32[]{:S(2)}) collective-permute-start(f16[8,3072]{1,0:T(8,128)(2,1)S(1)} %get-tuple-element.25), channel_id=1, source_target_pairs={{0,8},{1,5},{2,10},{3,7},{4,12},{5,1},{6,14},{7,3},{8,0},{9,13},{1... | collective-permute-start | bytes 147464 | tf_op jit(solution)/shard_map/ppermute | solution.py:23
  24.0 1.3 %collective-permute-start.7 = (f32[4,3072]{1,0:T(4,128)S(1)}, f32[4,3072]{1,0:T(4,128)S(1)}, u32[]{:S(2)}, u32[]{:S(2)}) collective-permute-start(f32[4,3072]{1,0:T(4,128)S(1)} %dynamic-slice_bitcast_fusion.1), channel_id=1, source_target_pairs={{0,1},{1,0},{2,3},{3,2},{4,5},{5,4},{6,7},{7,6},{8,9},{9,8},{10,11... | collective-permute-start | bytes 147464 | tf_op jit(solution)/shard_map/ppermute | solution.py:23
  25.5 12.4 %copy-start.5 = (f32[4,6144]{1,0:T(4,128)}, f32[4,6144]{1,0:T(4,128)S(1)}, u32[]{:S(2)}) copy-start(f32[4,6144]{1,0:T(4,128)S(1)} %get-tuple-element.2) | copy-start | bytes 294916
  25.6 5.4 %collective-permute-start.9 = (bf16[4,6144]{1,0:T(4,128)(2,1)S(1)}, bf16[4,6144]{1,0:T(4,128)(2,1)S(1)}, u32[]{:S(2)}, u32[]{:S(2)}) collective-permute-start(bf16[4,6144]{1,0:T(4,128)(2,1)S(1)} %get-tuple-element.8), channel_id=1, source_target_pairs={{0,16},{1,17},{2,18},{3,19},{4,20},{5,21},{6,22},{7,23},{8,24},{9,... | collective-permute-start | bytes 147464 | tf_op jit(solution)/shard_map/ppermute | solution.py:23
  28.6 6.0 %collective-permute-start.8 = (bf16[4,6144]{1,0:T(4,128)(2,1)S(1)}, bf16[4,6144]{1,0:T(4,128)(2,1)S(1)}, u32[]{:S(2)}, u32[]{:S(2)}) collective-permute-start(bf16[4,6144]{1,0:T(4,128)(2,1)S(1)} %get-tuple-element.10), channel_id=1, source_target_pairs={{0,12},{1,13},{2,14},{3,15},{4,8},{5,9},{6,10},{7,11},{8,4},{9,5},... | collective-permute-start | bytes 147464 | tf_op jit(solution)/shard_map/ppermute | solution.py:23
  31.0 4.7 %collective-permute-start.10 = (bf16[2,4,6144]{2,1,0:T(4,128)(2,1)S(1)}, bf16[2,4,6144]{2,1,0:T(4,128)(2,1)S(1)}, u32[]{:S(2)}, u32[]{:S(2)}) collective-permute-start(bf16[2,4,6144]{2,1,0:T(4,128)(2,1)S(1)} %pad_maximum_fusion.1), channel_id=1, source_target_pairs={{0,4},{1,5},{2,6},{3,7},{4,0},{5,1},{6,2},{7,3},{8,12},{9,13},{10,... | collective-permute-start | bytes 294920 | tf_op jit(solution)/shard_map/ppermute | solution.py:23
  32.3 4.8 %collective-permute-start.11 = (bf16[2,4,6144]{2,1,0:T(4,128)(2,1)S(1)}, bf16[2,4,6144]{2,1,0:T(4,128)(2,1)S(1)}, u32[]{:S(2)}, u32[]{:S(2)}) collective-permute-start(bf16[2,4,6144]{2,1,0:T(4,128)(2,1)S(1)} %pad_maximum_fusion.1), channel_id=1, source_target_pairs={{0,8},{1,9},{2,10},{3,11},{4,12},{5,13},{6,14},{7,15},{8,0},{9,1},... | collective-permute-start | bytes 294920 | tf_op jit(solution)/shard_map/ppermute | solution.py:23
  32.3 5.6 %collective-permute-start.12 = (bf16[4,6144]{1,0:T(4,128)(2,1)S(1)}, bf16[4,6144]{1,0:T(4,128)(2,1)S(1)}, u32[]{:S(2)}, u32[]{:S(2)}) collective-permute-start(bf16[4,6144]{1,0:T(4,128)(2,1)S(1)} %collective-permute-done.9), channel_id=1, source_target_pairs={{0,12},{1,13},{2,14},{3,15},{4,8},{5,9},{6,10},{7,11},{8,4},{9,5},... | collective-permute-start | bytes 147464 | tf_op jit(solution)/shard_map/ppermute | solution.py:23
  37.9 0.7 %copy-start.1 = (bf16[4,49152]{1,0:T(4,128)(2,1)}, bf16[4,49152]{1,0:T(4,128)(2,1)S(1)}, u32[]{:S(2)}) copy-start(bf16[4,49152]{1,0:T(4,128)(2,1)S(1)} %constant_dynamic-update-slice_fusion.3) | copy-start | bytes 1179652

commit v9 on v8

--- a/solution.py
+++ b/solution.py
@@ -76,11 +76,11 @@
     row_block, col_block = mine.shape
     me = lax.axis_index("hst")
     far = swap(first, Z_FAR, Z_FAR)
+    corner, far_corner = (swap(mine, f, f) for f in (Z_NEAR + Y, Z_FAR + Z_NEAR + Y))
     pair = jnp.stack([mine, far])
-    both = swap(mine, Z_NEAR + Y, Z_NEAR + Y), swap(far, Z_NEAR + Y, Z_NEAR + Y)
     near, side = swap(pair, Z_NEAR, Z_NEAR), swap(pair, Y, Y)
-    got = [(0, mine), (3, both[0]), (4, far)]
-    got += [(1, side[0]), (5, side[1]), (2, near[0]), (6, near[1]), (7, both[1])]
+    got = [(0, mine), (3, corner), (4, far), (7, far_corner)]
+    got += [(2, near[0]), (6, near[1]), (1, side[0]), (5, side[1])]
     whole = jnp.zeros((row_block, 8 * col_block), mine.dtype)
     for bits, block in got:
         whole = lax.dynamic_update_slice_in_dim(whole, block, (me ^ bits) * col_block, 1)

time: 38.8 us -> 38.2 us (0.985)
  waiting for transfers between devices: 17.4 us -> 16.4 us
  starting transfers between devices: 15.9 us -> 16.3 us
    ppermute x13, waiting for transfers between devices: 17.4 us -> 16.4 us  [swap(): return lax.ppermute(value, ('hst', 'local'), flip_pairs(flips))]
    ppermute x13, starting transfers between devices: 15.9 us -> 16.3 us  [swap(): return lax.ppermute(value, ('hst', 'local'), flip_pairs(flips))]
  transfers between devices with their start and end apart: 13 -> 13, of which waited for: 11 -> 10; matrix products, arithmetic and copies ran while one was open for 4% -> 4% of each run, Pallas kernels for 0% -> 0%
where the time goes in v9:
time: 38.2 us; the launch traced here: 38 us
  waiting for transfers between devices  16.4 us (43%)
  starting transfers between devices  16.3 us (43%)
  local copies, waits for them, and re-layouts  2.56 us (7%)
  other arithmetic  1.92 us (5%)
  between operations  0.87 us (2%)
    ppermute x13, waiting for transfers between devices, swap(): return lax.ppermute(value, ('hst', 'local'), flip_pairs(flips))  16.4 us
    ppermute x13, starting transfers between devices, swap(): return lax.ppermute(value, ('hst', 'local'), flip_pairs(flips))  16.3 us
    squeeze x2, local copies, waits for them, and re-layouts, pick(): return lax.dynamic_index_in_dim(value, index, 0, keepdims=False)  1.33 us
    dynamic_update_slice x1, other arithmetic, gather_blocks(): lax.dynamic_update_slice_in_dim(whole, block, (me ^ bits) * col_block, 1)  0.87 us
  transfers between devices with their start and end apart: 13, of which 10 were waited for; matrix products, arithmetic and copies ran while one was open for 4% of the time, Pallas kernels for 0%

profile of v9, /device:TPU:0, one launch (start us, length us, event | category | flops | bytes accessed | tf_op | source)
XLA Modules:
  0.0 38.0 jit_solution(7026715211711279717)
XLA Ops:
  0.7 1.3 %dynamic-slice_bitcast_fusion = bf16[2,4,2,8,3072]{4,3,2,1,0:T(8,128)(2,1)S(1)} fusion(bf16[2,4,2,2,8,3072]{5,4,3,2,1,0:T(8,128)(2,1)} %bitcast.90, s32[]{:T(128)S(6)} %select_n.251), kind=kLoop, calls=%fused_computation | loop fusion | bytes 1572868 | tf_op jit(solution)/shard_map/jit(dynamic_index_in_dim)/squeeze | solution.py:35
  2.0 0.5 %collective-permute-start = (bf16[2,4,2,8,3072]{4,3,2,1,0:T(8,128)(2,1)S(1)}, bf16[2,4,2,8,3072]{4,3,2,1,0:T(8,128)(2,1)S(1)}, u32[]{:S(2)}, u32[]{:S(2)}) collective-permute-start(bf16[2,4,2,8,3072]{4,3,2,1,0:T(8,128)(2,1)S(1)} %dynamic-slice_bitcast_fusion), channel_id=1, source_target_pairs={{0,1},{1,0},{2,3},{3,2},{4,5},{5,4},{6,7},{7,6},{8,9},{9,8},{10,11... | collective-permute-start | bytes 2359304 | tf_op jit(solution)/shard_map/ppermute | solution.py:23
  2.6 1.9 %collective-permute-done = bf16[2,4,2,8,3072]{4,3,2,1,0:T(8,128)(2,1)S(1)} collective-permute-done((bf16[2,4,2,8,3072]{4,3,2,1,0:T(8,128)(2,1)S(1)}, bf16[2,4,2,8,3072]{4,3,2,1,0:T(8,128)(2,1)S(1)}, u32[]{:S(2)}, u32[]{:S(2)}) %collective-permute-start) | collective-permute-done | bytes 786464 | tf_op jit(solution)/shard_map/ppermute | solution.py:23
  4.4 0.1 constant_dynamic-slice_fusion.2
  4.5 0.2 multiply_convert_fusion.2
  4.7 3.9 %collective-permute-start.1 = (f16[4,8,3072]{2,1,0:T(8,128)(2,1)S(1)}, f16[4,8,3072]{2,1,0:T(8,128)(2,1)S(1)}, u32[]{:S(2)}, u32[]{:S(2)}) collective-permute-start(f16[4,8,3072]{2,1,0:T(8,128)(2,1)S(1)} %multiply_convert_fusion.2), channel_id=1, source_target_pairs={{0,6},{1,25},{2,4},{3,27},{4,2},{5,29},{6,0},{7,31},{8,14},{9,17},... | collective-permute-start | bytes 589832 | tf_op jit(solution)/shard_map/ppermute | solution.py:23
  8.5 0.3 multiply_convert_fusion.1
  8.8 0.6 %collective-permute-start.2 = (f16[4,8,3072]{2,1,0:T(8,128)(2,1)S(1)}, f16[4,8,3072]{2,1,0:T(8,128)(2,1)S(1)}, u32[]{:S(2)}, u32[]{:S(2)}) collective-permute-start(f16[4,8,3072]{2,1,0:T(8,128)(2,1)S(1)} %get-tuple-element.14), channel_id=1, source_target_pairs={{0,2},{1,17},{2,0},{3,19},{4,6},{5,21},{6,4},{7,23},{8,10},{9,25},... | collective-permute-start | bytes 589832 | tf_op jit(solution)/shard_map/ppermute | solution.py:23
  9.5 2.7 %collective-permute-done.1 = f16[4,8,3072]{2,1,0:T(8,128)(2,1)S(1)} collective-permute-done((f16[4,8,3072]{2,1,0:T(8,128)(2,1)S(1)}, f16[4,8,3072]{2,1,0:T(8,128)(2,1)S(1)}, u32[]{:S(2)}, u32[]{:S(2)}) %collective-permute-start.1) | collective-permute-done | bytes 196640 | tf_op jit(solution)/shard_map/ppermute | solution.py:23
  12.2 0.2 multiply_add_fusion.1
  12.4 2.4 %collective-permute-done.2 = f16[4,8,3072]{2,1,0:T(8,128)(2,1)S(1)} collective-permute-done((f16[4,8,3072]{2,1,0:T(8,128)(2,1)S(1)}, f16[4,8,3072]{2,1,0:T(8,128)(2,1)S(1)}, u32[]{:S(2)}, u32[]{:S(2)}) %collective-permute-start.2) | collective-permute-done | bytes 196640 | tf_op jit(solution)/shard_map/ppermute | solution.py:23
  14.8 0.3 collective-permute-done.3
  15.1 0.1 multiply_add_fusion
  15.3 3.7 %collective-permute-start.4 = (f16[8,3072]{1,0:T(8,128)(2,1)S(1)}, f16[8,3072]{1,0:T(8,128)(2,1)S(1)}, u32[]{:S(2)}, u32[]{:S(2)}) collective-permute-start(f16[8,3072]{1,0:T(8,128)(2,1)S(1)} %get-tuple-element.24), channel_id=1, source_target_pairs={{0,24},{1,7},{2,26},{3,5},{4,28},{5,3},{6,30},{7,1},{8,16},{9,15},... | collective-permute-start | bytes 147464 | tf_op jit(solution)/shard_map/ppermute | solution.py:23
  18.9 0.8 %collective-permute-start.6 = (f16[8,3072]{1,0:T(8,128)(2,1)S(1)}, f16[8,3072]{1,0:T(8,128)(2,1)S(1)}, u32[]{:S(2)}, u32[]{:S(2)}) collective-permute-start(f16[8,3072]{1,0:T(8,128)(2,1)S(1)} %get-tuple-element.25), channel_id=1, source_target_pairs={{0,8},{1,5},{2,10},{3,7},{4,12},{5,1},{6,14},{7,3},{8,0},{9,13},{1... | collective-permute-start | bytes 147464 | tf_op jit(solution)/shard_map/ppermute | solution.py:23
  19.7 1.5 %collective-permute-done.4 = f16[8,3072]{1,0:T(8,128)(2,1)S(1)} collective-permute-done((f16[8,3072]{1,0:T(8,128)(2,1)S(1)}, f16[8,3072]{1,0:T(8,128)(2,1)S(1)}, u32[]{:S(2)}, u32[]{:S(2)}) %collective-permute-start.4) | collective-permute-done | bytes 49184 | tf_op jit(solution)/shard_map/ppermute | solution.py:23
  21.2 2.7 %collective-permute-done.5 = f16[8,3072]{1,0:T(8,128)(2,1)S(1)} collective-permute-done((f16[8,3072]{1,0:T(8,128)(2,1)S(1)}, f16[8,3072]{1,0:T(8,128)(2,1)S(1)}, u32[]{:S(2)}, u32[]{:S(2)}) %collective-permute-start.5) | collective-permute-done | bytes 49184 | tf_op jit(solution)/shard_map/ppermute | solution.py:23
  24.0 0.1 collective-permute-start.7
  24.1 1.2 %collective-permute-done.7 = f32[4,3072]{1,0:T(4,128)S(1)} collective-permute-done((f32[4,3072]{1,0:T(4,128)S(1)}, f32[4,3072]{1,0:T(4,128)S(1)}, u32[]{:S(2)}, u32[]{:S(2)}) %collective-permute-start.7) | collective-permute-done | bytes 49184 | tf_op jit(solution)/shard_map/ppermute | solution.py:23
  25.4 0.2 subtract_convert_fusion
  25.6 2.1 %collective-permute-start.9 = (bf16[4,6144]{1,0:T(4,128)(2,1)S(1)}, bf16[4,6144]{1,0:T(4,128)(2,1)S(1)}, u32[]{:S(2)}, u32[]{:S(2)}) collective-permute-start(bf16[4,6144]{1,0:T(4,128)(2,1)S(1)} %get-tuple-element.8), channel_id=1, source_target_pairs={{0,16},{1,17},{2,18},{3,19},{4,20},{5,21},{6,22},{7,23},{8,24},{9,... | collective-permute-start | bytes 147464 | tf_op jit(solution)/shard_map/ppermute | solution.py:23
  27.6 0.1 broadcast_in_dim.3
  27.8 0.9 %constant_dynamic-update-slice_fusion.3 = (bf16[4,49152]{1,0:T(4,128)(2,1)S(1)}, bf16[4,6144]{1,0:T(4,128)(2,1)S(1)}, f32[4,6144]{1,0:T(4,128)}, f32[4,6144]{1,0:T(4,128)}, f32[4,6144]{1,0:T(4,128)}) fusion(bf16[4,49152]{1,0:T(4,128)(2,1)S(1)} %broadcast_in_dim.3, s32[]{:T(128)S(6)} %select_n.290, f32[4,6144]{1,0:T(4,128)S(1)} %copy-done.2, ...), kind=kLoop, calls=%fused_computation.50 | loop fusion | flops 393216 | bytes 786436 | tf_op jit(solution)/shard_map/dynamic_update_slice | solution.py:86
  28.6 0.6 %collective-permute-start.8 = (bf16[4,6144]{1,0:T(4,128)(2,1)S(1)}, bf16[4,6144]{1,0:T(4,128)(2,1)S(1)}, u32[]{:S(2)}, u32[]{:S(2)}) collective-permute-start(bf16[4,6144]{1,0:T(4,128)(2,1)S(1)} %get-tuple-element.10), channel_id=1, source_target_pairs={{0,12},{1,13},{2,14},{3,15},{4,8},{5,9},{6,10},{7,11},{8,4},{9,5},... | collective-permute-start | bytes 147464 | tf_op jit(solution)/shard_map/ppermute | solution.py:23
  29.2 2.6 %collective-permute-start.10 = (bf16[4,6144]{1,0:T(4,128)(2,1)S(1)}, bf16[4,6144]{1,0:T(4,128)(2,1)S(1)}, u32[]{:S(2)}, u32[]{:S(2)}) collective-permute-start(bf16[4,6144]{1,0:T(4,128)(2,1)S(1)} %get-tuple-element.10), channel_id=1, source_target_pairs={{0,28},{1,29},{2,30},{3,31},{4,24},{5,25},{6,26},{7,27},{8,20},{9,... | collective-permute-start | bytes 147464 | tf_op jit(solution)/shard_map/ppermute | solution.py:23
  31.9 0.1 pad_maximum_fusion.1
  32.0 0.1 collective-permute-start.11
  32.0 1.2 %collective-permute-start.12 = (bf16[2,4,6144]{2,1,0:T(4,128)(2,1)S(1)}, bf16[2,4,6144]{2,1,0:T(4,128)(2,1)S(1)}, u32[]{:S(2)}, u32[]{:S(2)}) collective-permute-start(bf16[2,4,6144]{2,1,0:T(4,128)(2,1)S(1)} %pad_maximum_fusion.1), channel_id=1, source_target_pairs={{0,4},{1,5},{2,6},{3,7},{4,0},{5,1},{6,2},{7,3},{8,12},{9,13},{10,... | collective-permute-start | bytes 294920 | tf_op jit(solution)/shard_map/ppermute | solution.py:23
  33.3 0.3 collective-permute-done.8
  33.7 2.8 %collective-permute-done.10 = bf16[4,6144]{1,0:T(4,128)(2,1)S(1)} collective-permute-done((bf16[4,6144]{1,0:T(4,128)(2,1)S(1)}, bf16[4,6144]{1,0:T(4,128)(2,1)S(1)}, u32[]{:S(2)}, u32[]{:S(2)}) %collective-permute-start.10) | collective-permute-done | bytes 49184 | tf_op jit(solution)/shard_map/ppermute | solution.py:23
  36.5 0.6 %collective-permute-done.11 = bf16[2,4,6144]{2,1,0:T(4,128)(2,1)S(1)} collective-permute-done((bf16[2,4,6144]{2,1,0:T(4,128)(2,1)S(1)}, bf16[2,4,6144]{2,1,0:T(4,128)(2,1)S(1)}, u32[]{:S(2)}, u32[]{:S(2)}) %collective-permute-start.11) | collective-permute-done | bytes 98336 | tf_op jit(solution)/shard_map/ppermute | solution.py:23
  37.3 0.7 %copy-done.1 = bf16[4,49152]{1,0:T(4,128)(2,1)} copy-done((bf16[4,49152]{1,0:T(4,128)(2,1)}, bf16[4,49152]{1,0:T(4,128)(2,1)S(1)}, u32[]{:S(2)}) %copy-start.1) | copy-done | bytes 393240
  (29 shorter events, 0.5 us)
Async XLA Ops:
  0.6 1.9 %copy-start = (bf16[1,1,16,49152]{3,2,1,0:T(8,128)(2,1)S(1)}, bf16[1,1,16,49152]{3,2,1,0:T(8,128)(2,1)}, u32[]{:S(2)}) copy-start(bf16[1,1,16,49152]{3,2,1,0:T(8,128)(2,1)} %param.4) | copy-start | bytes 4718596
  2.0 2.4 %collective-permute-start = (bf16[2,4,2,8,3072]{4,3,2,1,0:T(8,128)(2,1)S(1)}, bf16[2,4,2,8,3072]{4,3,2,1,0:T(8,128)(2,1)S(1)}, u32[]{:S(2)}, u32[]{:S(2)}) collective-permute-start(bf16[2,4,2,8,3072]{4,3,2,1,0:T(8,128)(2,1)S(1)} %dynamic-slice_bitcast_fusion), channel_id=1, source_target_pairs={{0,1},{1,0},{2,3},{3,2},{4,5},{5,4},{6,7},{7,6},{8,9},{9,8},{10,11... | collective-permute-start | bytes 2359304 | tf_op jit(solution)/shard_map/ppermute | solution.py:23
  4.7 7.5 %collective-permute-start.1 = (f16[4,8,3072]{2,1,0:T(8,128)(2,1)S(1)}, f16[4,8,3072]{2,1,0:T(8,128)(2,1)S(1)}, u32[]{:S(2)}, u32[]{:S(2)}) collective-permute-start(f16[4,8,3072]{2,1,0:T(8,128)(2,1)S(1)} %multiply_convert_fusion.2), channel_id=1, source_target_pairs={{0,6},{1,25},{2,4},{3,27},{4,2},{5,29},{6,0},{7,31},{8,14},{9,17},... | collective-permute-start | bytes 589832 | tf_op jit(solution)/shard_map/ppermute | solution.py:23
  8.8 6.0 %collective-permute-start.2 = (f16[4,8,3072]{2,1,0:T(8,128)(2,1)S(1)}, f16[4,8,3072]{2,1,0:T(8,128)(2,1)S(1)}, u32[]{:S(2)}, u32[]{:S(2)}) collective-permute-start(f16[4,8,3072]{2,1,0:T(8,128)(2,1)S(1)} %get-tuple-element.14), channel_id=1, source_target_pairs={{0,2},{1,17},{2,0},{3,19},{4,6},{5,21},{6,4},{7,23},{8,10},{9,25},... | collective-permute-start | bytes 589832 | tf_op jit(solution)/shard_map/ppermute | solution.py:23
  9.4 5.7 %collective-permute-start.3 = (f16[4,8,3072]{2,1,0:T(8,128)(2,1)S(1)}, f16[4,8,3072]{2,1,0:T(8,128)(2,1)S(1)}, u32[]{:S(2)}, u32[]{:S(2)}) collective-permute-start(f16[4,8,3072]{2,1,0:T(8,128)(2,1)S(1)} %get-tuple-element.15), channel_id=1, source_target_pairs={{0,4},{1,9},{2,6},{3,11},{4,0},{5,13},{6,2},{7,15},{8,12},{9,1},{1... | collective-permute-start | bytes 589832 | tf_op jit(solution)/shard_map/ppermute | solution.py:23
  12.3 13.0 %copy-start.2 = (f32[4,6144]{1,0:T(4,128)S(1)}, f32[4,6144]{1,0:T(4,128)}, u32[]{:S(2)}) copy-start(f32[4,6144]{1,0:T(4,128)} %param.5) | copy-start | bytes 294916
  12.4 13.0 %copy-start.3 = (f32[4,6144]{1,0:T(4,128)S(1)}, f32[4,6144]{1,0:T(4,128)}, u32[]{:S(2)}) copy-start(f32[4,6144]{1,0:T(4,128)} %param.7) | copy-start | bytes 294916
  12.4 13.0 %copy-start.4 = (f32[4,6144]{1,0:T(4,128)S(1)}, f32[4,6144]{1,0:T(4,128)}, u32[]{:S(2)}) copy-start(f32[4,6144]{1,0:T(4,128)} %param.6) | copy-start | bytes 294916
  15.3 6.0 %collective-permute-start.4 = (f16[8,3072]{1,0:T(8,128)(2,1)S(1)}, f16[8,3072]{1,0:T(8,128)(2,1)S(1)}, u32[]{:S(2)}, u32[]{:S(2)}) collective-permute-start(f16[8,3072]{1,0:T(8,128)(2,1)S(1)} %get-tuple-element.24), channel_id=1, source_target_pairs={{0,24},{1,7},{2,26},{3,5},{4,28},{5,3},{6,30},{7,1},{8,16},{9,15},... | collective-permute-start | bytes 147464 | tf_op jit(solution)/shard_map/ppermute | solution.py:23
  18.9 5.0 %collective-permute-start.5 = (f16[8,3072]{1,0:T(8,128)(2,1)S(1)}, f16[8,3072]{1,0:T(8,128)(2,1)S(1)}, u32[]{:S(2)}, u32[]{:S(2)}) collective-permute-start(f16[8,3072]{1,0:T(8,128)(2,1)S(1)} %get-tuple-element.26), channel_id=1, source_target_pairs={{0,16},{1,3},{2,18},{3,1},{4,20},{5,7},{6,22},{7,5},{8,24},{9,11},... | collective-permute-start | bytes 147464 | tf_op jit(solution)/shard_map/ppermute | solution.py:23
  18.9 5.0 %collective-permute-start.6 = (f16[8,3072]{1,0:T(8,128)(2,1)S(1)}, f16[8,3072]{1,0:T(8,128)(2,1)S(1)}, u32[]{:S(2)}, u32[]{:S(2)}) collective-permute-start(f16[8,3072]{1,0:T(8,128)(2,1)S(1)} %get-tuple-element.25), channel_id=1, source_target_pairs={{0,8},{1,5},{2,10},{3,7},{4,12},{5,1},{6,14},{7,3},{8,0},{9,13},{1... | collective-permute-start | bytes 147464 | tf_op jit(solution)/shard_map/ppermute | solution.py:23
  24.0 1.3 %collective-permute-start.7 = (f32[4,3072]{1,0:T(4,128)S(1)}, f32[4,3072]{1,0:T(4,128)S(1)}, u32[]{:S(2)}, u32[]{:S(2)}) collective-permute-start(f32[4,3072]{1,0:T(4,128)S(1)} %dynamic-slice_bitcast_fusion.1), channel_id=1, source_target_pairs={{0,1},{1,0},{2,3},{3,2},{4,5},{5,4},{6,7},{7,6},{8,9},{9,8},{10,11... | collective-permute-start | bytes 147464 | tf_op jit(solution)/shard_map/ppermute | solution.py:23
  25.5 11.7 %copy-start.5 = (f32[4,6144]{1,0:T(4,128)}, f32[4,6144]{1,0:T(4,128)S(1)}, u32[]{:S(2)}) copy-start(f32[4,6144]{1,0:T(4,128)S(1)} %get-tuple-element.2) | copy-start | bytes 294916
  25.6 6.3 %collective-permute-start.9 = (bf16[4,6144]{1,0:T(4,128)(2,1)S(1)}, bf16[4,6144]{1,0:T(4,128)(2,1)S(1)}, u32[]{:S(2)}, u32[]{:S(2)}) collective-permute-start(bf16[4,6144]{1,0:T(4,128)(2,1)S(1)} %get-tuple-element.8), channel_id=1, source_target_pairs={{0,16},{1,17},{2,18},{3,19},{4,20},{5,21},{6,22},{7,23},{8,24},{9,... | collective-permute-start | bytes 147464 | tf_op jit(solution)/shard_map/ppermute | solution.py:23
  28.6 5.0 %collective-permute-start.8 = (bf16[4,6144]{1,0:T(4,128)(2,1)S(1)}, bf16[4,6144]{1,0:T(4,128)(2,1)S(1)}, u32[]{:S(2)}, u32[]{:S(2)}) collective-permute-start(bf16[4,6144]{1,0:T(4,128)(2,1)S(1)} %get-tuple-element.10), channel_id=1, source_target_pairs={{0,12},{1,13},{2,14},{3,15},{4,8},{5,9},{6,10},{7,11},{8,4},{9,5},... | collective-permute-start | bytes 147464 | tf_op jit(solution)/shard_map/ppermute | solution.py:23
  29.2 7.2 %collective-permute-start.10 = (bf16[4,6144]{1,0:T(4,128)(2,1)S(1)}, bf16[4,6144]{1,0:T(4,128)(2,1)S(1)}, u32[]{:S(2)}, u32[]{:S(2)}) collective-permute-start(bf16[4,6144]{1,0:T(4,128)(2,1)S(1)} %get-tuple-element.10), channel_id=1, source_target_pairs={{0,28},{1,29},{2,30},{3,31},{4,24},{5,25},{6,26},{7,27},{8,20},{9,... | collective-permute-start | bytes 147464 | tf_op jit(solution)/shard_map/ppermute | solution.py:23
  32.0 5.1 %collective-permute-start.11 = (bf16[2,4,6144]{2,1,0:T(4,128)(2,1)S(1)}, bf16[2,4,6144]{2,1,0:T(4,128)(2,1)S(1)}, u32[]{:S(2)}, u32[]{:S(2)}) collective-permute-start(bf16[2,4,6144]{2,1,0:T(4,128)(2,1)S(1)} %pad_maximum_fusion.1), channel_id=1, source_target_pairs={{0,8},{1,9},{2,10},{3,11},{4,12},{5,13},{6,14},{7,15},{8,0},{9,1},... | collective-permute-start | bytes 294920 | tf_op jit(solution)/shard_map/ppermute | solution.py:23
  32.0 5.1 %collective-permute-start.12 = (bf16[2,4,6144]{2,1,0:T(4,128)(2,1)S(1)}, bf16[2,4,6144]{2,1,0:T(4,128)(2,1)S(1)}, u32[]{:S(2)}, u32[]{:S(2)}) collective-permute-start(bf16[2,4,6144]{2,1,0:T(4,128)(2,1)S(1)} %pad_maximum_fusion.1), channel_id=1, source_target_pairs={{0,4},{1,5},{2,6},{3,7},{4,0},{5,1},{6,2},{7,3},{8,12},{9,13},{10,... | collective-permute-start | bytes 294920 | tf_op jit(solution)/shard_map/ppermute | solution.py:23
  37.3 0.7 %copy-start.1 = (bf16[4,49152]{1,0:T(4,128)(2,1)}, bf16[4,49152]{1,0:T(4,128)(2,1)S(1)}, u32[]{:S(2)}) copy-start(bf16[4,49152]{1,0:T(4,128)(2,1)S(1)} %fusion.11) | copy-start | bytes 1179652

commit v10 on v9

--- a/solution.py
+++ b/solution.py
@@ -1,6 +1,8 @@
 import jax
 import jax.numpy as jnp
 from jax import lax
+from jax.experimental import pallas as pl
+from jax.experimental.pallas import tpu as pltpu
 from jax.sharding import PartitionSpec as P
 
 beta_one = 0.9
@@ -38,6 +40,45 @@
 CORE, X, Y, Z_NEAR, Z_FAR = 1, 2, 4, 8, 16
 
 
+def split_rows_kernel(whole, own, theirs, landed, arrived):
+    blocks, tile, half = own.shape[1:]
+    core = lax.axis_index("local") % 2
+    parts = [pl.ds(2 * i * half, 2 * half) for i in range(blocks)]
+    copies = [
+        pltpu.make_async_copy(whole.at[:, part], landed.at[:, part], arrived.at[i])
+        for i, part in enumerate(parts)
+    ]
+    for copy in copies:
+        copy.start()
+    for i in range(blocks):
+        copies[i].wait()
+        block = landed[:, parts[i]].astype(jnp.float32)
+        for x in (0, 1):
+            left, right = block[x * tile : (x + 1) * tile, :half], block[x * tile : (x + 1) * tile, half:]
+            rows = [
+                jnp.concatenate([left[at : at + tile // 2], right[at : at + tile // 2]], axis=0).astype(own.dtype)
+                for at in (0, tile // 2)
+            ]
+            own[x, i] = jnp.where(core == 0, rows[0], rows[1])
+            theirs[x, i] = jnp.where(core == 0, rows[1], rows[0])
+
+
+def split_rows(gradient):
+    rows, cols = gradient.shape
+    tile, half = rows // 2, cols // 16
+    shape = pltpu.VMEM((2, 8, tile, half), gradient.dtype)
+    outs = pl.pallas_call(
+        split_rows_kernel,
+        in_specs=[pl.BlockSpec(memory_space=pltpu.HBM)],
+        out_specs=[pl.BlockSpec(memory_space=pltpu.VMEM)] * 2,
+        out_shape=[shape, shape],
+        scratch_shapes=[pltpu.VMEM(gradient.shape, gradient.dtype), pltpu.SemaphoreType.DMA((8,))],
+        compiler_params=pltpu.CompilerParams(vmem_limit_bytes=8 << 20),
+        cost_estimate=pl.CostEstimate(flops=rows * cols, bytes_accessed=4 * rows * cols, transcendentals=0),
+    )(pltpu.with_memory_space_constraint(gradient, pltpu.HBM))
+    return [out.reshape(2, 4, 2, tile, half) for out in outs]
+
+
 def reduce_blocks(gradient):
     rows, cols = gradient.shape
     tile, half = rows // 2, cols // 16
@@ -45,9 +86,8 @@
     x, core = me_local // 2, me_local % 2
     z, y = me_host // 2, me_host % 2
 
-    split = gradient.reshape(2, tile, 16, half).transpose(0, 2, 1, 3)
-    split = split.reshape(2, 4, 2, 2, tile, half).transpose(3, 0, 1, 2, 4, 5)
-    own, other = pick(split, core), swap(pick(split, 1 - core), CORE, CORE)
+    own, sent = split_rows(gradient)
+    other = swap(sent, CORE, CORE)
 
     def part(value, i):
         by_xy = lax.dynamic_slice(value, (i // 2, 0, i % 2, 0, 0), (1, 4, 1, tile, half))
@@ -66,10 +106,7 @@
     got = [swap(narrow(pick(quarter, me ^ d)), over_z[d], over_xy[d]) for d in (3, 2, 1)]
     total = pick(quarter, me) + widen(got[0]) + widen(got[1]) + widen(got[2])
 
-    by_core = total.reshape(2, tile // 2, half)
-    own, other = pick(by_core, core), swap(pick(by_core, 1 - core), CORE, CORE)
-    left, right = jnp.where(core == 0, own, other), jnp.where(core == 0, other, own)
-    return jnp.concatenate([left, right], axis=1)
+    return jnp.concatenate([total[: tile // 2], total[tile // 2 :]], axis=1)
 
 
 def gather_blocks(first, mine):

time: 38.2 us -> 37.2 us (0.974)
  Pallas kernels: 0 us -> 1.65 us
  waiting for transfers between devices: 16.4 us -> 15 us
  local copies, waits for them, and re-layouts: 2.56 us -> 1.2 us
    pallas_call x0 -> x1, Pallas kernels: none -> 1.65 us  [split_rows(): pl.pallas_call(split_rows_kernel, in_specs=[pl.BlockSpec(memory_space=plt...]
    ppermute x13 -> x12, waiting for transfers between devices: 16.4 us -> 15 us  [swap(): return lax.ppermute(value, ('hst', 'local'), flip_pairs(flips))]
    squeeze x2 -> x0, local copies, waits for them, and re-layouts: 1.33 us -> none  [pick(): return lax.dynamic_index_in_dim(value, index, 0, keepdims=False)]
    ppermute x13 -> x12, starting transfers between devices: 16.3 us -> 16.5 us  [swap(): return lax.ppermute(value, ('hst', 'local'), flip_pairs(flips))]
  transfers between devices with their start and end apart: 13 -> 12, of which waited for: 10 -> 7; matrix products, arithmetic and copies ran while one was open for 4% -> 4% of each run, Pallas kernels for 0% -> 0%
where the time goes in v10:
time: 37.2 us; the launch traced here: 37 us
  starting transfers between devices  16.5 us (44%)
  waiting for transfers between devices  15 us (40%)
  other arithmetic  1.91 us (5%)
  Pallas kernels  1.65 us (4%)
  local copies, waits for them, and re-layouts  1.2 us (3%)
  between operations  0.78 us (2%)
    ppermute x12, starting transfers between devices, swap(): return lax.ppermute(value, ('hst', 'local'), flip_pairs(flips))  16.5 us
    ppermute x12, waiting for transfers between devices, swap(): return lax.ppermute(value, ('hst', 'local'), flip_pairs(flips))  15 us
    pallas_call x1, Pallas kernels, split_rows(): pl.pallas_call(split_rows_kernel, in_specs=[pl.BlockSpec(memory_space=plt...  1.65 us
    dynamic_update_slice x1, other arithmetic, gather_blocks(): lax.dynamic_update_slice_in_dim(whole, block, (me ^ bits) * col_block, 1)  0.87 us
    unnamed x10, local copies, waits for them, and re-layouts  0.75 us
  transfers between devices with their start and end apart: 12, of which 7 were waited for; matrix products, arithmetic and copies ran while one was open for 4% of the time, Pallas kernels for 0%

profile of v10, /device:TPU:0, one launch (start us, length us, event | category | flops | bytes accessed | tf_op | source)
XLA Modules:
  0.0 37.0 jit_solution(2041852459774363479)
XLA Ops:
  0.6 1.7 %shard_map.83 = (bf16[2,8,8,3072]{3,2,1,0:T(8,128)(2,1)S(1)}, bf16[2,8,8,3072]{3,2,1,0:T(8,128)(2,1)S(1)}) custom-call(bf16[16,49152]{1,0:T(8,128)(2,1)} %bitcast.85), custom_call_target="tpu_custom_call" | custom-call | flops 786432 | bytes 3145728 | tf_op jit(solution)/shard_map/pallas_call | solution.py:70
  2.3 0.5 %collective-permute-start = (bf16[2,4,2,8,3072]{4,3,2,1,0:T(8,128)(2,1)S(1)}, bf16[2,4,2,8,3072]{4,3,2,1,0:T(8,128)(2,1)S(1)}, u32[]{:S(2)}, u32[]{:S(2)}) collective-permute-start(bf16[2,4,2,8,3072]{4,3,2,1,0:T(8,128)(2,1)S(1)} %bitcast.84), channel_id=1, source_target_pairs={{0,1},{1,0},{2,3},{3,2},{4,5},{5,4},{6,7},{7,6},{8,9},{9,8},{10,11... | collective-permute-start | bytes 2359304 | tf_op jit(solution)/shard_map/ppermute | solution.py:25
  2.8 0.1 constant_dynamic-slice_fusion.3
  2.9 1.9 %collective-permute-done = bf16[2,4,2,8,3072]{4,3,2,1,0:T(8,128)(2,1)S(1)} collective-permute-done((bf16[2,4,2,8,3072]{4,3,2,1,0:T(8,128)(2,1)S(1)}, bf16[2,4,2,8,3072]{4,3,2,1,0:T(8,128)(2,1)S(1)}, u32[]{:S(2)}, u32[]{:S(2)}) %collective-permute-start) | collective-permute-done | bytes 786464 | tf_op jit(solution)/shard_map/ppermute | solution.py:25
  4.7 0.1 constant_dynamic-slice_fusion.2
  4.8 0.5 %multiply_convert_fusion.1 = (f16[4,8,3072]{2,1,0:T(8,128)(2,1)S(1)}, f16[4,8,3072]{2,1,0:T(8,128)(2,1)S(1)}, f16[4,8,3072]{2,1,0:T(8,128)(2,1)S(1)}) fusion(bf16[2,1,2,8,3072]{4,3,2,1,0:T(8,128)(2,1)S(1)} %get-tuple-element.25, bf16[2,1,2,8,3072]{4,3,2,1,0:T(8,128)(2,1)S(1)} %get-tuple-element.21, bf16[2,4,2,8,3072]{4,3,2,1,0:T(8,128)(2,1)S(1)} %collective-permute-done, ...), kind=kLoop, calls=%fused_computation.2 | loop fusion | flops 2064384 | bytes 2949145 | tf_op jit(solution)/shard_map/convert_element_type | solution.py:29
  5.3 3.9 %collective-permute-start.1 = (f16[4,8,3072]{2,1,0:T(8,128)(2,1)S(1)}, f16[4,8,3072]{2,1,0:T(8,128)(2,1)S(1)}, u32[]{:S(2)}, u32[]{:S(2)}) collective-permute-start(f16[4,8,3072]{2,1,0:T(8,128)(2,1)S(1)} %get-tuple-element.20), channel_id=1, source_target_pairs={{0,6},{1,25},{2,4},{3,27},{4,2},{5,29},{6,0},{7,31},{8,14},{9,17},... | collective-permute-start | bytes 589832 | tf_op jit(solution)/shard_map/ppermute | solution.py:25
  9.1 0.5 %collective-permute-start.2 = (f16[4,8,3072]{2,1,0:T(8,128)(2,1)S(1)}, f16[4,8,3072]{2,1,0:T(8,128)(2,1)S(1)}, u32[]{:S(2)}, u32[]{:S(2)}) collective-permute-start(f16[4,8,3072]{2,1,0:T(8,128)(2,1)S(1)} %get-tuple-element.18), channel_id=1, source_target_pairs={{0,2},{1,17},{2,0},{3,19},{4,6},{5,21},{6,4},{7,23},{8,10},{9,25},... | collective-permute-start | bytes 589832 | tf_op jit(solution)/shard_map/ppermute | solution.py:25
  9.7 0.2 collective-permute-start.3
  9.8 2.9 %collective-permute-done.1 = f16[4,8,3072]{2,1,0:T(8,128)(2,1)S(1)} collective-permute-done((f16[4,8,3072]{2,1,0:T(8,128)(2,1)S(1)}, f16[4,8,3072]{2,1,0:T(8,128)(2,1)S(1)}, u32[]{:S(2)}, u32[]{:S(2)}) %collective-permute-start.1) | collective-permute-done | bytes 196640 | tf_op jit(solution)/shard_map/ppermute | solution.py:25
  12.8 0.2 multiply_add_fusion.1
  13.0 2.5 %collective-permute-done.2 = f16[4,8,3072]{2,1,0:T(8,128)(2,1)S(1)} collective-permute-done((f16[4,8,3072]{2,1,0:T(8,128)(2,1)S(1)}, f16[4,8,3072]{2,1,0:T(8,128)(2,1)S(1)}, u32[]{:S(2)}, u32[]{:S(2)}) %collective-permute-start.2) | collective-permute-done | bytes 196640 | tf_op jit(solution)/shard_map/ppermute | solution.py:25
  15.4 0.1 multiply_add_fusion
  15.6 3.7 %collective-permute-start.4 = (f16[8,3072]{1,0:T(8,128)(2,1)S(1)}, f16[8,3072]{1,0:T(8,128)(2,1)S(1)}, u32[]{:S(2)}, u32[]{:S(2)}) collective-permute-start(f16[8,3072]{1,0:T(8,128)(2,1)S(1)} %get-tuple-element.29), channel_id=1, source_target_pairs={{0,24},{1,7},{2,26},{3,5},{4,28},{5,3},{6,30},{7,1},{8,16},{9,15},... | collective-permute-start | bytes 147464 | tf_op jit(solution)/shard_map/ppermute | solution.py:25
  19.2 0.8 %collective-permute-start.6 = (f16[8,3072]{1,0:T(8,128)(2,1)S(1)}, f16[8,3072]{1,0:T(8,128)(2,1)S(1)}, u32[]{:S(2)}, u32[]{:S(2)}) collective-permute-start(f16[8,3072]{1,0:T(8,128)(2,1)S(1)} %get-tuple-element.30), channel_id=1, source_target_pairs={{0,8},{1,5},{2,10},{3,7},{4,12},{5,1},{6,14},{7,3},{8,0},{9,13},{1... | collective-permute-start | bytes 147464 | tf_op jit(solution)/shard_map/ppermute | solution.py:25
  20.0 1.5 %collective-permute-done.4 = f16[8,3072]{1,0:T(8,128)(2,1)S(1)} collective-permute-done((f16[8,3072]{1,0:T(8,128)(2,1)S(1)}, f16[8,3072]{1,0:T(8,128)(2,1)S(1)}, u32[]{:S(2)}, u32[]{:S(2)}) %collective-permute-start.4) | collective-permute-done | bytes 49184 | tf_op jit(solution)/shard_map/ppermute | solution.py:25
  21.5 2.7 %collective-permute-done.5 = f16[8,3072]{1,0:T(8,128)(2,1)S(1)} collective-permute-done((f16[8,3072]{1,0:T(8,128)(2,1)S(1)}, f16[8,3072]{1,0:T(8,128)(2,1)S(1)}, u32[]{:S(2)}, u32[]{:S(2)}) %collective-permute-start.5) | collective-permute-done | bytes 49184 | tf_op jit(solution)/shard_map/ppermute | solution.py:25
  24.3 0.2 subtract_convert_fusion
  24.5 2.1 %collective-permute-start.8 = (bf16[4,6144]{1,0:T(4,128)(2,1)S(1)}, bf16[4,6144]{1,0:T(4,128)(2,1)S(1)}, u32[]{:S(2)}, u32[]{:S(2)}) collective-permute-start(bf16[4,6144]{1,0:T(4,128)(2,1)S(1)} %get-tuple-element.12), channel_id=1, source_target_pairs={{0,16},{1,17},{2,18},{3,19},{4,20},{5,21},{6,22},{7,23},{8,24},{9,... | collective-permute-start | bytes 147464 | tf_op jit(solution)/shard_map/ppermute | solution.py:25
  26.6 0.1 broadcast_in_dim.3
  26.7 0.9 %constant_dynamic-update-slice_fusion.3 = (bf16[4,49152]{1,0:T(4,128)(2,1)S(1)}, bf16[4,6144]{1,0:T(4,128)(2,1)S(1)}, f32[4,6144]{1,0:T(4,128)}, f32[4,6144]{1,0:T(4,128)}, f32[4,6144]{1,0:T(4,128)}) fusion(bf16[4,49152]{1,0:T(4,128)(2,1)S(1)} %broadcast_in_dim.3, s32[]{:T(128)S(6)} %select_n.224, f32[4,6144]{1,0:T(4,128)S(1)} %copy-done.1, ...), kind=kLoop, calls=%fused_computation.46 | loop fusion | flops 393216 | bytes 786436 | tf_op jit(solution)/shard_map/dynamic_update_slice | solution.py:123
  27.6 0.9 %collective-permute-start.7 = (bf16[4,6144]{1,0:T(4,128)(2,1)S(1)}, bf16[4,6144]{1,0:T(4,128)(2,1)S(1)}, u32[]{:S(2)}, u32[]{:S(2)}) collective-permute-start(bf16[4,6144]{1,0:T(4,128)(2,1)S(1)} %get-tuple-element.14), channel_id=1, source_target_pairs={{0,12},{1,13},{2,14},{3,15},{4,8},{5,9},{6,10},{7,11},{8,4},{9,5},... | collective-permute-start | bytes 147464 | tf_op jit(solution)/shard_map/ppermute | solution.py:25
  28.5 2.4 %collective-permute-start.9 = (bf16[4,6144]{1,0:T(4,128)(2,1)S(1)}, bf16[4,6144]{1,0:T(4,128)(2,1)S(1)}, u32[]{:S(2)}, u32[]{:S(2)}) collective-permute-start(bf16[4,6144]{1,0:T(4,128)(2,1)S(1)} %get-tuple-element.14), channel_id=1, source_target_pairs={{0,28},{1,29},{2,30},{3,31},{4,24},{5,25},{6,26},{7,27},{8,20},{9,... | collective-permute-start | bytes 147464 | tf_op jit(solution)/shard_map/ppermute | solution.py:25
  30.9 0.1 pad_maximum_fusion.1
  30.9 0.1 collective-permute-start.10
  31.0 1.5 %collective-permute-start.11 = (bf16[2,4,6144]{2,1,0:T(4,128)(2,1)S(1)}, bf16[2,4,6144]{2,1,0:T(4,128)(2,1)S(1)}, u32[]{:S(2)}, u32[]{:S(2)}) collective-permute-start(bf16[2,4,6144]{2,1,0:T(4,128)(2,1)S(1)} %pad_maximum_fusion.1), channel_id=1, source_target_pairs={{0,4},{1,5},{2,6},{3,7},{4,0},{5,1},{6,2},{7,3},{8,12},{9,13},{10,... | collective-permute-start | bytes 294920 | tf_op jit(solution)/shard_map/ppermute | solution.py:25
  32.5 0.0 collective-permute-done.7
  32.6 2.9 %collective-permute-done.9 = bf16[4,6144]{1,0:T(4,128)(2,1)S(1)} collective-permute-done((bf16[4,6144]{1,0:T(4,128)(2,1)S(1)}, bf16[4,6144]{1,0:T(4,128)(2,1)S(1)}, u32[]{:S(2)}, u32[]{:S(2)}) %collective-permute-start.9) | collective-permute-done | bytes 49184 | tf_op jit(solution)/shard_map/ppermute | solution.py:25
  35.6 0.6 %collective-permute-done.10 = bf16[2,4,6144]{2,1,0:T(4,128)(2,1)S(1)} collective-permute-done((bf16[2,4,6144]{2,1,0:T(4,128)(2,1)S(1)}, bf16[2,4,6144]{2,1,0:T(4,128)(2,1)S(1)}, u32[]{:S(2)}, u32[]{:S(2)}) %collective-permute-start.10) | collective-permute-done | bytes 98336 | tf_op jit(solution)/shard_map/ppermute | solution.py:25
  36.2 0.0 collective-permute-done.11
  36.3 0.0 copy-start
  36.3 0.7 %copy-done = bf16[4,49152]{1,0:T(4,128)(2,1)} copy-done((bf16[4,49152]{1,0:T(4,128)(2,1)}, bf16[4,49152]{1,0:T(4,128)(2,1)S(1)}, u32[]{:S(2)}) %copy-start) | copy-done | bytes 393240
  (22 shorter events, 0.3 us)
Async XLA Ops:
  2.3 2.4 %collective-permute-start = (bf16[2,4,2,8,3072]{4,3,2,1,0:T(8,128)(2,1)S(1)}, bf16[2,4,2,8,3072]{4,3,2,1,0:T(8,128)(2,1)S(1)}, u32[]{:S(2)}, u32[]{:S(2)}) collective-permute-start(bf16[2,4,2,8,3072]{4,3,2,1,0:T(8,128)(2,1)S(1)} %bitcast.84), channel_id=1, source_target_pairs={{0,1},{1,0},{2,3},{3,2},{4,5},{5,4},{6,7},{7,6},{8,9},{9,8},{10,11... | collective-permute-start | bytes 2359304 | tf_op jit(solution)/shard_map/ppermute | solution.py:25
  5.3 7.5 %collective-permute-start.1 = (f16[4,8,3072]{2,1,0:T(8,128)(2,1)S(1)}, f16[4,8,3072]{2,1,0:T(8,128)(2,1)S(1)}, u32[]{:S(2)}, u32[]{:S(2)}) collective-permute-start(f16[4,8,3072]{2,1,0:T(8,128)(2,1)S(1)} %get-tuple-element.20), channel_id=1, source_target_pairs={{0,6},{1,25},{2,4},{3,27},{4,2},{5,29},{6,0},{7,31},{8,14},{9,17},... | collective-permute-start | bytes 589832 | tf_op jit(solution)/shard_map/ppermute | solution.py:25
  9.1 6.3 %collective-permute-start.2 = (f16[4,8,3072]{2,1,0:T(8,128)(2,1)S(1)}, f16[4,8,3072]{2,1,0:T(8,128)(2,1)S(1)}, u32[]{:S(2)}, u32[]{:S(2)}) collective-permute-start(f16[4,8,3072]{2,1,0:T(8,128)(2,1)S(1)} %get-tuple-element.18), channel_id=1, source_target_pairs={{0,2},{1,17},{2,0},{3,19},{4,6},{5,21},{6,4},{7,23},{8,10},{9,25},... | collective-permute-start | bytes 589832 | tf_op jit(solution)/shard_map/ppermute | solution.py:25
  9.7 5.8 %collective-permute-start.3 = (f16[4,8,3072]{2,1,0:T(8,128)(2,1)S(1)}, f16[4,8,3072]{2,1,0:T(8,128)(2,1)S(1)}, u32[]{:S(2)}, u32[]{:S(2)}) collective-permute-start(f16[4,8,3072]{2,1,0:T(8,128)(2,1)S(1)} %get-tuple-element.19), channel_id=1, source_target_pairs={{0,4},{1,9},{2,6},{3,11},{4,0},{5,13},{6,2},{7,15},{8,12},{9,1},{1... | collective-permute-start | bytes 589832 | tf_op jit(solution)/shard_map/ppermute | solution.py:25
  12.8 11.5 %copy-start.1 = (f32[4,6144]{1,0:T(4,128)S(1)}, f32[4,6144]{1,0:T(4,128)}, u32[]{:S(2)}) copy-start(f32[4,6144]{1,0:T(4,128)} %param.5) | copy-start | bytes 294916
  12.8 11.5 %copy-start.2 = (f32[4,6144]{1,0:T(4,128)S(1)}, f32[4,6144]{1,0:T(4,128)}, u32[]{:S(2)}) copy-start(f32[4,6144]{1,0:T(4,128)} %param.7) | copy-start | bytes 294916
  12.8 11.5 %copy-start.3 = (f32[4,6144]{1,0:T(4,128)S(1)}, f32[4,6144]{1,0:T(4,128)}, u32[]{:S(2)}) copy-start(f32[4,6144]{1,0:T(4,128)} %param.6) | copy-start | bytes 294916
  15.6 6.0 %collective-permute-start.4 = (f16[8,3072]{1,0:T(8,128)(2,1)S(1)}, f16[8,3072]{1,0:T(8,128)(2,1)S(1)}, u32[]{:S(2)}, u32[]{:S(2)}) collective-permute-start(f16[8,3072]{1,0:T(8,128)(2,1)S(1)} %get-tuple-element.29), channel_id=1, source_target_pairs={{0,24},{1,7},{2,26},{3,5},{4,28},{5,3},{6,30},{7,1},{8,16},{9,15},... | collective-permute-start | bytes 147464 | tf_op jit(solution)/shard_map/ppermute | solution.py:25
  19.2 5.0 %collective-permute-start.5 = (f16[8,3072]{1,0:T(8,128)(2,1)S(1)}, f16[8,3072]{1,0:T(8,128)(2,1)S(1)}, u32[]{:S(2)}, u32[]{:S(2)}) collective-permute-start(f16[8,3072]{1,0:T(8,128)(2,1)S(1)} %get-tuple-element.31), channel_id=1, source_target_pairs={{0,16},{1,3},{2,18},{3,1},{4,20},{5,7},{6,22},{7,5},{8,24},{9,11},... | collective-permute-start | bytes 147464 | tf_op jit(solution)/shard_map/ppermute | solution.py:25
  19.2 5.0 %collective-permute-start.6 = (f16[8,3072]{1,0:T(8,128)(2,1)S(1)}, f16[8,3072]{1,0:T(8,128)(2,1)S(1)}, u32[]{:S(2)}, u32[]{:S(2)}) collective-permute-start(f16[8,3072]{1,0:T(8,128)(2,1)S(1)} %get-tuple-element.30), channel_id=1, source_target_pairs={{0,8},{1,5},{2,10},{3,7},{4,12},{5,1},{6,14},{7,3},{8,0},{9,13},{1... | collective-permute-start | bytes 147464 | tf_op jit(solution)/shard_map/ppermute | solution.py:25
  24.5 11.8 %copy-start.4 = (f32[4,6144]{1,0:T(4,128)}, f32[4,6144]{1,0:T(4,128)S(1)}, u32[]{:S(2)}) copy-start(f32[4,6144]{1,0:T(4,128)S(1)} %get-tuple-element.4) | copy-start | bytes 294916
  24.5 6.3 %collective-permute-start.8 = (bf16[4,6144]{1,0:T(4,128)(2,1)S(1)}, bf16[4,6144]{1,0:T(4,128)(2,1)S(1)}, u32[]{:S(2)}, u32[]{:S(2)}) collective-permute-start(bf16[4,6144]{1,0:T(4,128)(2,1)S(1)} %get-tuple-element.12), channel_id=1, source_target_pairs={{0,16},{1,17},{2,18},{3,19},{4,20},{5,21},{6,22},{7,23},{8,24},{9,... | collective-permute-start | bytes 147464 | tf_op jit(solution)/shard_map/ppermute | solution.py:25
  27.6 5.0 %collective-permute-start.7 = (bf16[4,6144]{1,0:T(4,128)(2,1)S(1)}, bf16[4,6144]{1,0:T(4,128)(2,1)S(1)}, u32[]{:S(2)}, u32[]{:S(2)}) collective-permute-start(bf16[4,6144]{1,0:T(4,128)(2,1)S(1)} %get-tuple-element.14), channel_id=1, source_target_pairs={{0,12},{1,13},{2,14},{3,15},{4,8},{5,9},{6,10},{7,11},{8,4},{9,5},... | collective-permute-start | bytes 147464 | tf_op jit(solution)/shard_map/ppermute | solution.py:25
  28.5 7.1 %collective-permute-start.9 = (bf16[4,6144]{1,0:T(4,128)(2,1)S(1)}, bf16[4,6144]{1,0:T(4,128)(2,1)S(1)}, u32[]{:S(2)}, u32[]{:S(2)}) collective-permute-start(bf16[4,6144]{1,0:T(4,128)(2,1)S(1)} %get-tuple-element.14), channel_id=1, source_target_pairs={{0,28},{1,29},{2,30},{3,31},{4,24},{5,25},{6,26},{7,27},{8,20},{9,... | collective-permute-start | bytes 147464 | tf_op jit(solution)/shard_map/ppermute | solution.py:25
  30.9 5.2 %collective-permute-start.10 = (bf16[2,4,6144]{2,1,0:T(4,128)(2,1)S(1)}, bf16[2,4,6144]{2,1,0:T(4,128)(2,1)S(1)}, u32[]{:S(2)}, u32[]{:S(2)}) collective-permute-start(bf16[2,4,6144]{2,1,0:T(4,128)(2,1)S(1)} %pad_maximum_fusion.1), channel_id=1, source_target_pairs={{0,8},{1,9},{2,10},{3,11},{4,12},{5,13},{6,14},{7,15},{8,0},{9,1},... | collective-permute-start | bytes 294920 | tf_op jit(solution)/shard_map/ppermute | solution.py:25
  31.0 5.2 %collective-permute-start.11 = (bf16[2,4,6144]{2,1,0:T(4,128)(2,1)S(1)}, bf16[2,4,6144]{2,1,0:T(4,128)(2,1)S(1)}, u32[]{:S(2)}, u32[]{:S(2)}) collective-permute-start(bf16[2,4,6144]{2,1,0:T(4,128)(2,1)S(1)} %pad_maximum_fusion.1), channel_id=1, source_target_pairs={{0,4},{1,5},{2,6},{3,7},{4,0},{5,1},{6,2},{7,3},{8,12},{9,13},{10,... | collective-permute-start | bytes 294920 | tf_op jit(solution)/shard_map/ppermute | solution.py:25
  36.3 0.7 %copy-start = (bf16[4,49152]{1,0:T(4,128)(2,1)}, bf16[4,49152]{1,0:T(4,128)(2,1)S(1)}, u32[]{:S(2)}) copy-start(bf16[4,49152]{1,0:T(4,128)(2,1)S(1)} %fusion.11) | copy-start | bytes 1179652

commit v11 on v9

--- a/solution.py
+++ b/solution.py
@@ -1,6 +1,8 @@
 import jax
 import jax.numpy as jnp
 from jax import lax
+from jax.experimental import pallas as pl
+from jax.experimental.pallas import tpu as pltpu
 from jax.sharding import PartitionSpec as P
 
 beta_one = 0.9
@@ -38,38 +40,91 @@
 CORE, X, Y, Z_NEAR, Z_FAR = 1, 2, 4, 8, 16
 
 
+def place():
+    me_local, me_host = lax.axis_index("local"), lax.axis_index("hst")
+    return me_local // 2, me_host % 2, me_host // 2, me_local % 2
+
+
+def rows_of(core, block, out, i):
+    tile, half = out.shape[2:]
+    my_x, my_y, my_z, _ = place()
+    z, y = i // 2, i % 2
+    for x in (0, 1):
+        left, right = block[x * tile : (x + 1) * tile, :half], block[x * tile : (x + 1) * tile, half:]
+        rows = [
+            jnp.concatenate([left[at : at + tile // 2], right[at : at + tile // 2]], axis=0).astype(out.dtype)
+            for at in (0, tile // 2)
+        ]
+        step = jnp.where(core == 0, (2 * my_x + my_y) ^ (2 * x + y), my_z ^ z)
+        member = jnp.where(core == 0, z, 2 * x + y)
+        out[step, member] = jnp.where(core == 0, rows[0], rows[1])
+
+
+def theirs_kernel(whole, theirs, landed, arrived):
+    half = theirs.shape[3]
+    core = place()[3]
+    parts = [pl.ds(2 * i * half, 2 * half) for i in range(8)]
+    copies = [
+        pltpu.make_async_copy(whole.at[:, part], landed.at[:, part], arrived.at[i])
+        for i, part in enumerate(parts)
+    ]
+    for copy in copies:
+        copy.start()
+    for i in range(8):
+        copies[i].wait()
+        rows_of(1 - core, landed[:, parts[i]].astype(jnp.float32), theirs, i)
+
+
+def own_kernel(landed, own):
+    half = own.shape[3]
+    core = place()[3]
+    for i in range(8):
+        rows_of(core, landed[:, pl.ds(2 * i * half, 2 * half)].astype(jnp.float32), own, i)
+
+
+def call(kernel, operand, space, outs, scratch=()):
+    size = operand.size
+    return pl.pallas_call(
+        kernel,
+        in_specs=[pl.BlockSpec(memory_space=space)],
+        out_specs=[pl.BlockSpec(memory_space=pltpu.VMEM)] * len(outs),
+        out_shape=[pltpu.VMEM(shape, operand.dtype) for shape in outs],
+        scratch_shapes=scratch,
+        compiler_params=pltpu.CompilerParams(vmem_limit_bytes=8 << 20),
+        cost_estimate=pl.CostEstimate(flops=size, bytes_accessed=4 * size, transcendentals=0),
+    )(pltpu.with_memory_space_constraint(operand, space))
+
+
+def split_rows(gradient):
+    rows, cols = gradient.shape
+    shape = (4, 4, rows // 2, cols // 16)
+    theirs, landed = call(
+        theirs_kernel, gradient, pltpu.HBM, [shape, gradient.shape], [pltpu.SemaphoreType.DMA((8,))]
+    )
+    theirs, landed = lax.optimization_barrier((theirs, landed))
+    (own,) = call(own_kernel, landed, pltpu.VMEM, [shape])
+    return theirs, own
+
+
 def reduce_blocks(gradient):
-    rows, cols = gradient.shape
-    tile, half = rows // 2, cols // 16
-    me_local, me_host = lax.axis_index("local"), lax.axis_index("hst")
-    x, core = me_local // 2, me_local % 2
-    z, y = me_host // 2, me_host % 2
-
-    split = gradient.reshape(2, tile, 16, half).transpose(0, 2, 1, 3)
-    split = split.reshape(2, 4, 2, 2, tile, half).transpose(3, 0, 1, 2, 4, 5)
-    own, other = pick(split, core), swap(pick(split, 1 - core), CORE, CORE)
-
-    def part(value, i):
-        by_xy = lax.dynamic_slice(value, (i // 2, 0, i % 2, 0, 0), (1, 4, 1, tile, half))
-        by_z = lax.dynamic_slice(value, (0, i, 0, 0, 0), (2, 1, 2, tile, half))
-        return jnp.where(core == 0, by_xy.reshape(4, tile, half), by_z.reshape(4, tile, half))
-
-    def pair(i):
-        return part(own, i).astype(jnp.float32) + part(other, i).astype(jnp.float32)
+    tile = gradient.shape[0] // 2
+    x, y, z, core = place()
+
+    sent, own = split_rows(gradient)
+    other = swap(sent, CORE, CORE)
+
+    def pair(d):
+        return own[d].astype(jnp.float32) + other[d].astype(jnp.float32)
 
     over_xy, over_z = (0, Y, X, X + Y), (0, Z_NEAR, Z_FAR, Z_NEAR + Z_FAR)
-    me = jnp.where(core == 0, 2 * x + y, z)
-    got = [swap(narrow(pair(me ^ d)), over_xy[d], over_z[d]) for d in (3, 2, 1)]
-    quarter = lax.optimization_barrier(pair(me) + widen(got[0]))
+    got = [swap(narrow(pair(d)), over_xy[d], over_z[d]) for d in (3, 1, 2)]
+    quarter = lax.optimization_barrier(pair(0) + widen(got[0]))
     quarter = quarter + widen(got[1]) + widen(got[2])
     me = jnp.where(core == 0, z, 2 * x + y)
-    got = [swap(narrow(pick(quarter, me ^ d)), over_z[d], over_xy[d]) for d in (3, 2, 1)]
+    got = [swap(narrow(pick(quarter, me ^ d)), over_z[d], over_xy[d]) for d in (1, 2, 3)]
     total = pick(quarter, me) + widen(got[0]) + widen(got[1]) + widen(got[2])
 
-    by_core = total.reshape(2, tile // 2, half)
-    own, other = pick(by_core, core), swap(pick(by_core, 1 - core), CORE, CORE)
-    left, right = jnp.where(core == 0, own, other), jnp.where(core == 0, other, own)
-    return jnp.concatenate([left, right], axis=1)
+    return jnp.concatenate([total[: tile // 2], total[tile // 2 :]], axis=1)
 
 
 def gather_blocks(first, mine):
@@ -84,7 +139,7 @@
     whole = jnp.zeros((row_block, 8 * col_block), mine.dtype)
     for bits, block in got:
         whole = lax.dynamic_update_slice_in_dim(whole, block, (me ^ bits) * col_block, 1)
-    return whole
+    return whole, corner
 
 
 def reduce_general(gradient):
@@ -123,13 +178,14 @@
     gradient = grads[0, 0]
     grad_total = reduce_blocks(gradient) if tuned else reduce_general(gradient)
     first = adam(grad_total, master, moment_one, moment_two)[0].astype(jnp.bfloat16)
-    grad_total, first = lax.optimization_barrier((grad_total, first))
+    again, first = lax.optimization_barrier((grad_total, first))
+    mine = adam(again, master, moment_one, moment_two)[0].astype(jnp.bfloat16)
+    if tuned:
+        secondary, corner = gather_blocks(first, mine)
+    else:
+        secondary = corner = lax.all_gather(mine, "hst", axis=1, tiled=True)
+    grad_total, _ = lax.optimization_barrier((again, corner))
     new_master, new_one, new_two = adam(grad_total, master, moment_one, moment_two)
-    mine = new_master.astype(jnp.bfloat16)
-    if tuned:
-        secondary = gather_blocks(first, mine)
-    else:
-        secondary = lax.all_gather(mine, "hst", axis=1, tiled=True)
     return (grad_total, new_master, new_one, new_two, secondary)
 
 

time: 38.2 us -> 36.6 us (0.958)
  Pallas kernels: 0 us -> 2.1 us
  waiting for transfers between devices: 16.4 us -> 14.3 us
  local copies, waits for them, and re-layouts: 2.56 us -> 1.1 us
    ppermute x13 -> x12, waiting for transfers between devices: 16.4 us -> 14.3 us  [swap(): return lax.ppermute(value, ('hst', 'local'), flip_pairs(flips))]
    pallas_call x0 -> x2, Pallas kernels: none -> 2.1 us  [call(): pl.pallas_call(kernel, in_specs=[pl.BlockSpec(memory_space=space)], out_s...]
    squeeze x2 -> x0, local copies, waits for them, and re-layouts: 1.33 us -> none  [pick(): return lax.dynamic_index_in_dim(value, index, 0, keepdims=False)]
    sub x0 -> x1, other arithmetic: none -> 0.84 us  [adam(): new_master = master - learn_rate * (update + decay_rate * master)]
    dynamic_update_slice x1, other arithmetic: 0.87 us -> 0.2 us  [gather_blocks(): lax.dynamic_update_slice_in_dim(whole, block, (me ^ bits) * col_block, 1)]
    ppermute x13 -> x12, starting transfers between devices: 16.3 us -> 16.5 us  [swap(): return lax.ppermute(value, ('hst', 'local'), flip_pairs(flips))]
  transfers between devices with their start and end apart: 13 -> 12, of which waited for: 10 -> 8; matrix products, arithmetic and copies ran while one was open for 4% -> 4% of each run, Pallas kernels for 0% -> 1%
where the time goes in v11:
time: 36.6 us; the launch traced here: 36.5 us
  starting transfers between devices  16.5 us (45%)
  waiting for transfers between devices  14.3 us (39%)
  Pallas kernels  2.1 us (6%)
  other arithmetic  1.73 us (5%)
  local copies, waits for them, and re-layouts  1.1 us (3%)
  between operations  0.78 us (2%)
    ppermute x12, starting transfers between devices, swap(): return lax.ppermute(value, ('hst', 'local'), flip_pairs(flips))  16.5 us
    ppermute x12, waiting for transfers between devices, swap(): return lax.ppermute(value, ('hst', 'local'), flip_pairs(flips))  14.3 us
    pallas_call x2, Pallas kernels, call(): pl.pallas_call(kernel, in_specs=[pl.BlockSpec(memory_space=space)], out_s...  2.1 us
    sub x1, other arithmetic, adam(): new_master = master - learn_rate * (update + decay_rate * master)  0.84 us
    unnamed x10, local copies, waits for them, and re-layouts  0.75 us
  transfers between devices with their start and end apart: 12, of which 8 were waited for; matrix products, arithmetic and copies ran while one was open for 4% of the time, Pallas kernels for 1%

profile of v11, /device:TPU:0, one launch (start us, length us, event | category | flops | bytes accessed | tf_op | source)
XLA Modules:
  0.0 36.5 jit_solution(910870211916893147)
XLA Ops:
  0.6 1.6 %shard_map.83 = (bf16[4,4,8,3072]{3,2,1,0:T(8,128)(2,1)S(1)}, bf16[16,49152]{1,0:T(8,128)(2,1)S(1)}) custom-call(bf16[16,49152]{1,0:T(8,128)(2,1)} %bitcast.39), custom_call_target="tpu_custom_call" | custom-call | flops 786432 | bytes 3145728 | tf_op jit(solution)/shard_map/pallas_call | solution.py:87
  2.2 0.5 %collective-permute-start = (bf16[4,4,8,3072]{3,2,1,0:T(8,128)(2,1)S(1)}, bf16[4,4,8,3072]{3,2,1,0:T(8,128)(2,1)S(1)}, u32[]{:S(2)}, u32[]{:S(2)}) collective-permute-start(bf16[4,4,8,3072]{3,2,1,0:T(8,128)(2,1)S(1)} %get-tuple-element.11), channel_id=1, source_target_pairs={{0,1},{1,0},{2,3},{3,2},{4,5},{5,4},{6,7},{7,6},{8,9},{9,8},{10,11... | collective-permute-start | bytes 2359304 | tf_op jit(solution)/shard_map/ppermute | solution.py:25
  2.8 0.5 %shard_map.84 = bf16[4,4,8,3072]{3,2,1,0:T(8,128)(2,1)S(1)} custom-call(bf16[16,49152]{1,0:T(8,128)(2,1)S(1)} %get-tuple-element.10.landed), custom_call_target="tpu_custom_call" | custom-call | flops 786432 | bytes 3145728 | tf_op jit(solution)/shard_map/pallas_call | solution.py:87
  3.3 1.4 %collective-permute-done = bf16[4,4,8,3072]{3,2,1,0:T(8,128)(2,1)S(1)} collective-permute-done((bf16[4,4,8,3072]{3,2,1,0:T(8,128)(2,1)S(1)}, bf16[4,4,8,3072]{3,2,1,0:T(8,128)(2,1)S(1)}, u32[]{:S(2)}, u32[]{:S(2)}) %collective-permute-start) | collective-permute-done | bytes 786464 | tf_op jit(solution)/shard_map/ppermute | solution.py:25
  4.7 0.2 fusion.1
  4.9 3.9 %collective-permute-start.1 = (f16[4,8,3072]{2,1,0:T(8,128)(2,1)S(1)}, f16[4,8,3072]{2,1,0:T(8,128)(2,1)S(1)}, u32[]{:S(2)}, u32[]{:S(2)}) collective-permute-start(f16[4,8,3072]{2,1,0:T(8,128)(2,1)S(1)} %get-tuple-element.22), channel_id=1, source_target_pairs={{0,6},{1,25},{2,4},{3,27},{4,2},{5,29},{6,0},{7,31},{8,14},{9,17},... | collective-permute-start | bytes 589832 | tf_op jit(solution)/shard_map/ppermute | solution.py:25
  8.8 0.5 %collective-permute-start.3 = (f16[4,8,3072]{2,1,0:T(8,128)(2,1)S(1)}, f16[4,8,3072]{2,1,0:T(8,128)(2,1)S(1)}, u32[]{:S(2)}, u32[]{:S(2)}) collective-permute-start(f16[4,8,3072]{2,1,0:T(8,128)(2,1)S(1)} %get-tuple-element.21), channel_id=1, source_target_pairs={{0,2},{1,17},{2,0},{3,19},{4,6},{5,21},{6,4},{7,23},{8,10},{9,25},... | collective-permute-start | bytes 589832 | tf_op jit(solution)/shard_map/ppermute | solution.py:25
  9.3 0.2 collective-permute-start.2
  9.5 2.9 %collective-permute-done.1 = f16[4,8,3072]{2,1,0:T(8,128)(2,1)S(1)} collective-permute-done((f16[4,8,3072]{2,1,0:T(8,128)(2,1)S(1)}, f16[4,8,3072]{2,1,0:T(8,128)(2,1)S(1)}, u32[]{:S(2)}, u32[]{:S(2)}) %collective-permute-start.1) | collective-permute-done | bytes 196640 | tf_op jit(solution)/shard_map/ppermute | solution.py:25
  12.4 0.1 bitcast_add_fusion
  12.5 2.6 %collective-permute-done.3 = f16[4,8,3072]{2,1,0:T(8,128)(2,1)S(1)} collective-permute-done((f16[4,8,3072]{2,1,0:T(8,128)(2,1)S(1)}, f16[4,8,3072]{2,1,0:T(8,128)(2,1)S(1)}, u32[]{:S(2)}, u32[]{:S(2)}) %collective-permute-start.3) | collective-permute-done | bytes 196640 | tf_op jit(solution)/shard_map/ppermute | solution.py:25
  15.1 0.1 multiply_add_fusion
  15.2 3.7 %collective-permute-start.6 = (f16[8,3072]{1,0:T(8,128)(2,1)S(1)}, f16[8,3072]{1,0:T(8,128)(2,1)S(1)}, u32[]{:S(2)}, u32[]{:S(2)}) collective-permute-start(f16[8,3072]{1,0:T(8,128)(2,1)S(1)} %get-tuple-element.24), channel_id=1, source_target_pairs={{0,24},{1,7},{2,26},{3,5},{4,28},{5,3},{6,30},{7,1},{8,16},{9,15},... | collective-permute-start | bytes 147464 | tf_op jit(solution)/shard_map/ppermute | solution.py:25
  18.9 0.8 %collective-permute-start.4 = (f16[8,3072]{1,0:T(8,128)(2,1)S(1)}, f16[8,3072]{1,0:T(8,128)(2,1)S(1)}, u32[]{:S(2)}, u32[]{:S(2)}) collective-permute-start(f16[8,3072]{1,0:T(8,128)(2,1)S(1)} %get-tuple-element.23), channel_id=1, source_target_pairs={{0,8},{1,5},{2,10},{3,7},{4,12},{5,1},{6,14},{7,3},{8,0},{9,13},{1... | collective-permute-start | bytes 147464 | tf_op jit(solution)/shard_map/ppermute | solution.py:25
  19.7 1.5 %collective-permute-done.6 = f16[8,3072]{1,0:T(8,128)(2,1)S(1)} collective-permute-done((f16[8,3072]{1,0:T(8,128)(2,1)S(1)}, f16[8,3072]{1,0:T(8,128)(2,1)S(1)}, u32[]{:S(2)}, u32[]{:S(2)}) %collective-permute-start.6) | collective-permute-done | bytes 49184 | tf_op jit(solution)/shard_map/ppermute | solution.py:25
  21.2 2.7 %collective-permute-done.5 = f16[8,3072]{1,0:T(8,128)(2,1)S(1)} collective-permute-done((f16[8,3072]{1,0:T(8,128)(2,1)S(1)}, f16[8,3072]{1,0:T(8,128)(2,1)S(1)}, u32[]{:S(2)}, u32[]{:S(2)}) %collective-permute-start.5) | collective-permute-done | bytes 49184 | tf_op jit(solution)/shard_map/ppermute | solution.py:25
  24.0 0.2 subtract_convert_fusion.1
  24.1 0.0 copy-start.3
  24.1 2.1 %collective-permute-start.8 = (bf16[4,6144]{1,0:T(4,128)(2,1)S(1)}, bf16[4,6144]{1,0:T(4,128)(2,1)S(1)}, u32[]{:S(2)}, u32[]{:S(2)}) collective-permute-start(bf16[4,6144]{1,0:T(4,128)(2,1)S(1)} %get-tuple-element.14), channel_id=1, source_target_pairs={{0,16},{1,17},{2,18},{3,19},{4,20},{5,21},{6,22},{7,23},{8,24},{9,... | collective-permute-start | bytes 147464 | tf_op jit(solution)/shard_map/ppermute | solution.py:25
  26.2 0.1 broadcast_in_dim.3
  26.3 0.2 constant_dynamic-update-slice_fusion.3
  26.5 1.0 %collective-permute-start.7 = (bf16[4,6144]{1,0:T(4,128)(2,1)S(1)}, bf16[4,6144]{1,0:T(4,128)(2,1)S(1)}, u32[]{:S(2)}, u32[]{:S(2)}) collective-permute-start(bf16[4,6144]{1,0:T(4,128)(2,1)S(1)} %get-tuple-element.16), channel_id=1, source_target_pairs={{0,12},{1,13},{2,14},{3,15},{4,8},{5,9},{6,10},{7,11},{8,4},{9,5},... | collective-permute-start | bytes 147464 | tf_op jit(solution)/shard_map/ppermute | solution.py:25
  27.5 2.4 %collective-permute-start.9 = (bf16[4,6144]{1,0:T(4,128)(2,1)S(1)}, bf16[4,6144]{1,0:T(4,128)(2,1)S(1)}, u32[]{:S(2)}, u32[]{:S(2)}) collective-permute-start(bf16[4,6144]{1,0:T(4,128)(2,1)S(1)} %get-tuple-element.16), channel_id=1, source_target_pairs={{0,28},{1,29},{2,30},{3,31},{4,24},{5,25},{6,26},{7,27},{8,20},{9,... | collective-permute-start | bytes 147464 | tf_op jit(solution)/shard_map/ppermute | solution.py:25
  29.9 0.1 collective-permute-done.8
  29.9 0.1 pad_maximum_fusion.1
  30.0 0.1 collective-permute-start.10
  30.1 1.5 %collective-permute-start.11 = (bf16[2,4,6144]{2,1,0:T(4,128)(2,1)S(1)}, bf16[2,4,6144]{2,1,0:T(4,128)(2,1)S(1)}, u32[]{:S(2)}, u32[]{:S(2)}) collective-permute-start(bf16[2,4,6144]{2,1,0:T(4,128)(2,1)S(1)} %pad_maximum_fusion.1), channel_id=1, source_target_pairs={{0,4},{1,5},{2,6},{3,7},{4,0},{5,1},{6,2},{7,3},{8,12},{9,13},{10,... | collective-permute-start | bytes 294920 | tf_op jit(solution)/shard_map/ppermute | solution.py:25
  31.5 0.0 collective-permute-done.7
  31.6 0.8 %multiply_subtract_fusion = (f32[4,6144]{1,0:T(4,128)}, f32[4,6144]{1,0:T(4,128)}, f32[4,6144]{1,0:T(4,128)}) fusion(f32[4,6144]{1,0:T(4,128)S(1)} %copy-done, f32[4,6144]{1,0:T(4,128)S(1)} %get-tuple-element.5, f32[4,6144]{1,0:T(4,128)S(1)} %copy-done.2, f32[4,6144]{1,0:T(4,128)S(1)} %copy-done.1), kind=kLoop, calls=%fused_computation.27 | loop fusion | flops 368640 | bytes 688128 | tf_op jit(solution)/shard_map/sub | solution.py:172
  32.5 2.1 %collective-permute-done.9 = bf16[4,6144]{1,0:T(4,128)(2,1)S(1)} collective-permute-done((bf16[4,6144]{1,0:T(4,128)(2,1)S(1)}, bf16[4,6144]{1,0:T(4,128)(2,1)S(1)}, u32[]{:S(2)}, u32[]{:S(2)}) %collective-permute-start.9) | collective-permute-done | bytes 49184 | tf_op jit(solution)/shard_map/ppermute | solution.py:25
  34.6 1.0 %collective-permute-done.10 = bf16[2,4,6144]{2,1,0:T(4,128)(2,1)S(1)} collective-permute-done((bf16[2,4,6144]{2,1,0:T(4,128)(2,1)S(1)}, bf16[2,4,6144]{2,1,0:T(4,128)(2,1)S(1)}, u32[]{:S(2)}, u32[]{:S(2)}) %collective-permute-start.10) | collective-permute-done | bytes 98336 | tf_op jit(solution)/shard_map/ppermute | solution.py:25
  35.7 0.7 %copy-done.4 = bf16[4,49152]{1,0:T(4,128)(2,1)} copy-done((bf16[4,49152]{1,0:T(4,128)(2,1)}, bf16[4,49152]{1,0:T(4,128)(2,1)S(1)}, u32[]{:S(2)}) %copy-start.4) | copy-done | bytes 393240
  (22 shorter events, 0.3 us)
Async XLA Ops:
  2.2 2.4 %collective-permute-start = (bf16[4,4,8,3072]{3,2,1,0:T(8,128)(2,1)S(1)}, bf16[4,4,8,3072]{3,2,1,0:T(8,128)(2,1)S(1)}, u32[]{:S(2)}, u32[]{:S(2)}) collective-permute-start(bf16[4,4,8,3072]{3,2,1,0:T(8,128)(2,1)S(1)} %get-tuple-element.11), channel_id=1, source_target_pairs={{0,1},{1,0},{2,3},{3,2},{4,5},{5,4},{6,7},{7,6},{8,9},{9,8},{10,11... | collective-permute-start | bytes 2359304 | tf_op jit(solution)/shard_map/ppermute | solution.py:25
  4.9 7.5 %collective-permute-start.1 = (f16[4,8,3072]{2,1,0:T(8,128)(2,1)S(1)}, f16[4,8,3072]{2,1,0:T(8,128)(2,1)S(1)}, u32[]{:S(2)}, u32[]{:S(2)}) collective-permute-start(f16[4,8,3072]{2,1,0:T(8,128)(2,1)S(1)} %get-tuple-element.22), channel_id=1, source_target_pairs={{0,6},{1,25},{2,4},{3,27},{4,2},{5,29},{6,0},{7,31},{8,14},{9,17},... | collective-permute-start | bytes 589832 | tf_op jit(solution)/shard_map/ppermute | solution.py:25
  8.8 6.3 %collective-permute-start.3 = (f16[4,8,3072]{2,1,0:T(8,128)(2,1)S(1)}, f16[4,8,3072]{2,1,0:T(8,128)(2,1)S(1)}, u32[]{:S(2)}, u32[]{:S(2)}) collective-permute-start(f16[4,8,3072]{2,1,0:T(8,128)(2,1)S(1)} %get-tuple-element.21), channel_id=1, source_target_pairs={{0,2},{1,17},{2,0},{3,19},{4,6},{5,21},{6,4},{7,23},{8,10},{9,25},... | collective-permute-start | bytes 589832 | tf_op jit(solution)/shard_map/ppermute | solution.py:25
  9.3 14.6 %copy-start = (f32[4,6144]{1,0:T(4,128)S(1)}, f32[4,6144]{1,0:T(4,128)}, u32[]{:S(2)}) copy-start(f32[4,6144]{1,0:T(4,128)} %param.5) | copy-start | bytes 294916
  9.3 14.6 %copy-start.1 = (f32[4,6144]{1,0:T(4,128)S(1)}, f32[4,6144]{1,0:T(4,128)}, u32[]{:S(2)}) copy-start(f32[4,6144]{1,0:T(4,128)} %param.7) | copy-start | bytes 294916
  9.3 14.6 %copy-start.2 = (f32[4,6144]{1,0:T(4,128)S(1)}, f32[4,6144]{1,0:T(4,128)}, u32[]{:S(2)}) copy-start(f32[4,6144]{1,0:T(4,128)} %param.6) | copy-start | bytes 294916
  9.3 5.7 %collective-permute-start.2 = (f16[4,8,3072]{2,1,0:T(8,128)(2,1)S(1)}, f16[4,8,3072]{2,1,0:T(8,128)(2,1)S(1)}, u32[]{:S(2)}, u32[]{:S(2)}) collective-permute-start(f16[4,8,3072]{2,1,0:T(8,128)(2,1)S(1)} %get-tuple-element.20), channel_id=1, source_target_pairs={{0,4},{1,9},{2,6},{3,11},{4,0},{5,13},{6,2},{7,15},{8,12},{9,1},{1... | collective-permute-start | bytes 589832 | tf_op jit(solution)/shard_map/ppermute | solution.py:25
  15.2 6.0 %collective-permute-start.6 = (f16[8,3072]{1,0:T(8,128)(2,1)S(1)}, f16[8,3072]{1,0:T(8,128)(2,1)S(1)}, u32[]{:S(2)}, u32[]{:S(2)}) collective-permute-start(f16[8,3072]{1,0:T(8,128)(2,1)S(1)} %get-tuple-element.24), channel_id=1, source_target_pairs={{0,24},{1,7},{2,26},{3,5},{4,28},{5,3},{6,30},{7,1},{8,16},{9,15},... | collective-permute-start | bytes 147464 | tf_op jit(solution)/shard_map/ppermute | solution.py:25
  18.9 5.0 %collective-permute-start.5 = (f16[8,3072]{1,0:T(8,128)(2,1)S(1)}, f16[8,3072]{1,0:T(8,128)(2,1)S(1)}, u32[]{:S(2)}, u32[]{:S(2)}) collective-permute-start(f16[8,3072]{1,0:T(8,128)(2,1)S(1)} %get-tuple-element.25), channel_id=1, source_target_pairs={{0,16},{1,3},{2,18},{3,1},{4,20},{5,7},{6,22},{7,5},{8,24},{9,11},... | collective-permute-start | bytes 147464 | tf_op jit(solution)/shard_map/ppermute | solution.py:25
  18.9 5.0 %collective-permute-start.4 = (f16[8,3072]{1,0:T(8,128)(2,1)S(1)}, f16[8,3072]{1,0:T(8,128)(2,1)S(1)}, u32[]{:S(2)}, u32[]{:S(2)}) collective-permute-start(f16[8,3072]{1,0:T(8,128)(2,1)S(1)} %get-tuple-element.23), channel_id=1, source_target_pairs={{0,8},{1,5},{2,10},{3,7},{4,12},{5,1},{6,14},{7,3},{8,0},{9,13},{1... | collective-permute-start | bytes 147464 | tf_op jit(solution)/shard_map/ppermute | solution.py:25
  24.1 11.6 %copy-start.3 = (f32[4,6144]{1,0:T(4,128)}, f32[4,6144]{1,0:T(4,128)S(1)}, u32[]{:S(2)}) copy-start(f32[4,6144]{1,0:T(4,128)S(1)} %get-tuple-element.5) | copy-start | bytes 294916
  24.1 5.8 %collective-permute-start.8 = (bf16[4,6144]{1,0:T(4,128)(2,1)S(1)}, bf16[4,6144]{1,0:T(4,128)(2,1)S(1)}, u32[]{:S(2)}, u32[]{:S(2)}) collective-permute-start(bf16[4,6144]{1,0:T(4,128)(2,1)S(1)} %get-tuple-element.14), channel_id=1, source_target_pairs={{0,16},{1,17},{2,18},{3,19},{4,20},{5,21},{6,22},{7,23},{8,24},{9,... | collective-permute-start | bytes 147464 | tf_op jit(solution)/shard_map/ppermute | solution.py:25
  26.5 5.0 %collective-permute-start.7 = (bf16[4,6144]{1,0:T(4,128)(2,1)S(1)}, bf16[4,6144]{1,0:T(4,128)(2,1)S(1)}, u32[]{:S(2)}, u32[]{:S(2)}) collective-permute-start(bf16[4,6144]{1,0:T(4,128)(2,1)S(1)} %get-tuple-element.16), channel_id=1, source_target_pairs={{0,12},{1,13},{2,14},{3,15},{4,8},{5,9},{6,10},{7,11},{8,4},{9,5},... | collective-permute-start | bytes 147464 | tf_op jit(solution)/shard_map/ppermute | solution.py:25
  27.5 7.1 %collective-permute-start.9 = (bf16[4,6144]{1,0:T(4,128)(2,1)S(1)}, bf16[4,6144]{1,0:T(4,128)(2,1)S(1)}, u32[]{:S(2)}, u32[]{:S(2)}) collective-permute-start(bf16[4,6144]{1,0:T(4,128)(2,1)S(1)} %get-tuple-element.16), channel_id=1, source_target_pairs={{0,28},{1,29},{2,30},{3,31},{4,24},{5,25},{6,26},{7,27},{8,20},{9,... | collective-permute-start | bytes 147464 | tf_op jit(solution)/shard_map/ppermute | solution.py:25
  30.0 5.6 %collective-permute-start.10 = (bf16[2,4,6144]{2,1,0:T(4,128)(2,1)S(1)}, bf16[2,4,6144]{2,1,0:T(4,128)(2,1)S(1)}, u32[]{:S(2)}, u32[]{:S(2)}) collective-permute-start(bf16[2,4,6144]{2,1,0:T(4,128)(2,1)S(1)} %pad_maximum_fusion.1), channel_id=1, source_target_pairs={{0,8},{1,9},{2,10},{3,11},{4,12},{5,13},{6,14},{7,15},{8,0},{9,1},... | collective-permute-start | bytes 294920 | tf_op jit(solution)/shard_map/ppermute | solution.py:25
  30.1 5.6 %collective-permute-start.11 = (bf16[2,4,6144]{2,1,0:T(4,128)(2,1)S(1)}, bf16[2,4,6144]{2,1,0:T(4,128)(2,1)S(1)}, u32[]{:S(2)}, u32[]{:S(2)}) collective-permute-start(bf16[2,4,6144]{2,1,0:T(4,128)(2,1)S(1)} %pad_maximum_fusion.1), channel_id=1, source_target_pairs={{0,4},{1,5},{2,6},{3,7},{4,0},{5,1},{6,2},{7,3},{8,12},{9,13},{10,... | collective-permute-start | bytes 294920 | tf_op jit(solution)/shard_map/ppermute | solution.py:25
  35.7 0.7 %copy-start.4 = (bf16[4,49152]{1,0:T(4,128)(2,1)}, bf16[4,49152]{1,0:T(4,128)(2,1)S(1)}, u32[]{:S(2)}) copy-start(bf16[4,49152]{1,0:T(4,128)(2,1)S(1)} %fusion.19) | copy-start | bytes 1179652

commit v12 on v11

--- a/solution.py
+++ b/solution.py
@@ -45,41 +45,57 @@
     return me_local // 2, me_host % 2, me_host // 2, me_local % 2
 
 
-def rows_of(core, block, out, i):
-    tile, half = out.shape[2:]
+def rows_of(core, block, i, store):
+    tile, half = block.shape[0] // 2, block.shape[1] // 2
     my_x, my_y, my_z, _ = place()
     z, y = i // 2, i % 2
+    block = block.astype(jnp.float32)
     for x in (0, 1):
         left, right = block[x * tile : (x + 1) * tile, :half], block[x * tile : (x + 1) * tile, half:]
         rows = [
-            jnp.concatenate([left[at : at + tile // 2], right[at : at + tile // 2]], axis=0).astype(out.dtype)
+            jnp.concatenate([left[at : at + tile // 2], right[at : at + tile // 2]], axis=0).astype(jnp.bfloat16)
             for at in (0, tile // 2)
         ]
         step = jnp.where(core == 0, (2 * my_x + my_y) ^ (2 * x + y), my_z ^ z)
         member = jnp.where(core == 0, z, 2 * x + y)
-        out[step, member] = jnp.where(core == 0, rows[0], rows[1])
-
-
-def theirs_kernel(whole, theirs, landed, arrived):
-    half = theirs.shape[3]
+        store(step, member, jnp.where(core == 0, rows[0], rows[1]))
+
+
+def theirs_kernel(whole, first, others, landed, arrived):
+    half = first.shape[2]
     core = place()[3]
-    parts = [pl.ds(2 * i * half, 2 * half) for i in range(8)]
+    parts = [pl.ds(i * half, half) for i in range(16)]
     copies = [
         pltpu.make_async_copy(whole.at[:, part], landed.at[:, part], arrived.at[i])
         for i, part in enumerate(parts)
     ]
     for copy in copies:
         copy.start()
+
+    def store(step, member, rows):
+        @pl.when(step == 3)
+        def _():
+            first[member] = rows
+
+        @pl.when(step != 3)
+        def _():
+            others[step, member] = rows
+
     for i in range(8):
-        copies[i].wait()
-        rows_of(1 - core, landed[:, parts[i]].astype(jnp.float32), theirs, i)
+        copies[2 * i].wait()
+        copies[2 * i + 1].wait()
+        rows_of(1 - core, landed[:, pl.ds(2 * i * half, 2 * half)], i, store)
 
 
 def own_kernel(landed, own):
     half = own.shape[3]
     core = place()[3]
+
+    def store(step, member, rows):
+        own[step, member] = rows
+
     for i in range(8):
-        rows_of(core, landed[:, pl.ds(2 * i * half, 2 * half)].astype(jnp.float32), own, i)
+        rows_of(core, landed[:, pl.ds(2 * i * half, 2 * half)], i, store)
 
 
 def call(kernel, operand, space, outs, scratch=()):
@@ -97,27 +113,34 @@
 
 def split_rows(gradient):
     rows, cols = gradient.shape
-    shape = (4, 4, rows // 2, cols // 16)
-    theirs, landed = call(
-        theirs_kernel, gradient, pltpu.HBM, [shape, gradient.shape], [pltpu.SemaphoreType.DMA((8,))]
-    )
-    theirs, landed = lax.optimization_barrier((theirs, landed))
-    (own,) = call(own_kernel, landed, pltpu.VMEM, [shape])
-    return theirs, own
+    shape = (4, rows // 2, cols // 16)
+    first, others, landed = call(
+        theirs_kernel,
+        gradient,
+        pltpu.HBM,
+        [shape, (3, *shape), gradient.shape],
+        [pltpu.SemaphoreType.DMA((16,))],
+    )
+    first, others, landed = lax.optimization_barrier((first, others, landed))
+    (own,) = call(own_kernel, landed, pltpu.VMEM, [(4, *shape)])
+    return first, others, own
 
 
 def reduce_blocks(gradient):
     tile = gradient.shape[0] // 2
     x, y, z, core = place()
 
-    sent, own = split_rows(gradient)
-    other = swap(sent, CORE, CORE)
+    first, others, own = split_rows(gradient)
+    first, others = swap(first, CORE, CORE), swap(others, CORE, CORE)
 
     def pair(d):
-        return own[d].astype(jnp.float32) + other[d].astype(jnp.float32)
+        return own[d].astype(jnp.float32) + (first if d == 3 else others[d]).astype(jnp.float32)
 
     over_xy, over_z = (0, Y, X, X + Y), (0, Z_NEAR, Z_FAR, Z_NEAR + Z_FAR)
-    got = [swap(narrow(pair(d)), over_xy[d], over_z[d]) for d in (3, 1, 2)]
+    sent = {3: narrow(pair(3))}
+    own, sent[3] = lax.optimization_barrier((own, sent[3]))
+    sent.update({d: narrow(pair(d)) for d in (1, 2)})
+    got = [swap(sent[d], over_xy[d], over_z[d]) for d in (3, 1, 2)]
     quarter = lax.optimization_barrier(pair(0) + widen(got[0]))
     quarter = quarter + widen(got[1]) + widen(got[2])
     me = jnp.where(core == 0, z, 2 * x + y)

time: 36.6 us -> 35.8 us (0.978)
  waiting for transfers between devices: 14.3 us -> 12.6 us
  starting transfers between devices: 16.5 us -> 17.1 us
    ppermute x12 -> x13, waiting for transfers between devices: 14.3 us -> 12.6 us  [swap(): return lax.ppermute(value, ('hst', 'local'), flip_pairs(flips))]
    ppermute x12 -> x13, starting transfers between devices: 16.5 us -> 17.1 us  [swap(): return lax.ppermute(value, ('hst', 'local'), flip_pairs(flips))]
  transfers between devices with their start and end apart: 12 -> 13, of which waited for: 8 -> 9; matrix products, arithmetic and copies ran while one was open for 4% -> 5% of each run, Pallas kernels for 1% -> 1%
where the time goes in v12:
time: 35.8 us; the launch traced here: 35.7 us
  starting transfers between devices  17.1 us (48%)
  waiting for transfers between devices  12.6 us (35%)
  Pallas kernels  2.31 us (6%)
  other arithmetic  1.76 us (5%)
  local copies, waits for them, and re-layouts  1.1 us (3%)
  between operations  0.78 us (2%)
    ppermute x13, starting transfers between devices, swap(): return lax.ppermute(value, ('hst', 'local'), flip_pairs(flips))  17.1 us
    ppermute x13, waiting for transfers between devices, swap(): return lax.ppermute(value, ('hst', 'local'), flip_pairs(flips))  12.6 us
    pallas_call x2, Pallas kernels, call(): pl.pallas_call(kernel, in_specs=[pl.BlockSpec(memory_space=space)], out_s...  2.31 us
    sub x1, other arithmetic, adam(): new_master = master - learn_rate * (update + decay_rate * master)  0.84 us
    unnamed x10, local copies, waits for them, and re-layouts  0.75 us
  transfers between devices with their start and end apart: 13, of which 9 were waited for; matrix products, arithmetic and copies ran while one was open for 5% of the time, Pallas kernels for 1%

profile of v12, /device:TPU:0, one launch (start us, length us, event | category | flops | bytes accessed | tf_op | source)
XLA Modules:
  0.0 35.7 jit_solution(8330604351192894470)
XLA Ops:
  0.6 1.8 %shard_map.83 = (bf16[4,8,3072]{2,1,0:T(8,128)(2,1)S(1)}, bf16[3,4,8,3072]{3,2,1,0:T(8,128)(2,1)S(1)}, bf16[16,49152]{1,0:T(8,128)(2,1)S(1)}) custom-call(bf16[16,49152]{1,0:T(8,128)(2,1)} %bitcast.42), custom_call_target="tpu_custom_call" | custom-call | flops 786432 | bytes 3145728 | tf_op jit(solution)/shard_map/pallas_call | solution.py:103
  2.5 0.5 %collective-permute-start = (bf16[4,8,3072]{2,1,0:T(8,128)(2,1)S(1)}, bf16[4,8,3072]{2,1,0:T(8,128)(2,1)S(1)}, u32[]{:S(2)}, u32[]{:S(2)}) collective-permute-start(bf16[4,8,3072]{2,1,0:T(8,128)(2,1)S(1)} %get-tuple-element.14), channel_id=1, source_target_pairs={{0,1},{1,0},{2,3},{3,2},{4,5},{5,4},{6,7},{7,6},{8,9},{9,8},{10,11... | collective-permute-start | bytes 589832 | tf_op jit(solution)/shard_map/ppermute | solution.py:25
  3.0 0.1 collective-permute-start.1
  3.1 0.5 %shard_map.84 = bf16[4,4,8,3072]{3,2,1,0:T(8,128)(2,1)S(1)} custom-call(bf16[16,49152]{1,0:T(8,128)(2,1)S(1)} %get-tuple-element.13.landed), custom_call_target="tpu_custom_call" | custom-call | flops 786432 | bytes 3145728 | tf_op jit(solution)/shard_map/pallas_call | solution.py:103
  3.5 0.5 %collective-permute-done = bf16[4,8,3072]{2,1,0:T(8,128)(2,1)S(1)} collective-permute-done((bf16[4,8,3072]{2,1,0:T(8,128)(2,1)S(1)}, bf16[4,8,3072]{2,1,0:T(8,128)(2,1)S(1)}, u32[]{:S(2)}, u32[]{:S(2)}) %collective-permute-start) | collective-permute-done | bytes 196640 | tf_op jit(solution)/shard_map/ppermute | solution.py:25
  4.0 0.1 fusion.1
  4.1 3.9 %collective-permute-start.2 = (f16[4,8,3072]{2,1,0:T(8,128)(2,1)S(1)}, f16[4,8,3072]{2,1,0:T(8,128)(2,1)S(1)}, u32[]{:S(2)}, u32[]{:S(2)}) collective-permute-start(f16[4,8,3072]{2,1,0:T(8,128)(2,1)S(1)} %fusion.1), channel_id=1, source_target_pairs={{0,6},{1,25},{2,4},{3,27},{4,2},{5,29},{6,0},{7,31},{8,14},{9,17},... | collective-permute-start | bytes 589832 | tf_op jit(solution)/shard_map/ppermute | solution.py:25
  8.0 0.1 fusion.2
  8.2 0.6 %collective-permute-start.4 = (f16[4,8,3072]{2,1,0:T(8,128)(2,1)S(1)}, f16[4,8,3072]{2,1,0:T(8,128)(2,1)S(1)}, u32[]{:S(2)}, u32[]{:S(2)}) collective-permute-start(f16[4,8,3072]{2,1,0:T(8,128)(2,1)S(1)} %get-tuple-element.27), channel_id=1, source_target_pairs={{0,2},{1,17},{2,0},{3,19},{4,6},{5,21},{6,4},{7,23},{8,10},{9,25},... | collective-permute-start | bytes 589832 | tf_op jit(solution)/shard_map/ppermute | solution.py:25
  8.8 0.7 %collective-permute-start.3 = (f16[4,8,3072]{2,1,0:T(8,128)(2,1)S(1)}, f16[4,8,3072]{2,1,0:T(8,128)(2,1)S(1)}, u32[]{:S(2)}, u32[]{:S(2)}) collective-permute-start(f16[4,8,3072]{2,1,0:T(8,128)(2,1)S(1)} %get-tuple-element.26), channel_id=1, source_target_pairs={{0,4},{1,9},{2,6},{3,11},{4,0},{5,13},{6,2},{7,15},{8,12},{9,1},{1... | collective-permute-start | bytes 589832 | tf_op jit(solution)/shard_map/ppermute | solution.py:25
  9.5 2.2 %collective-permute-done.2 = f16[4,8,3072]{2,1,0:T(8,128)(2,1)S(1)} collective-permute-done((f16[4,8,3072]{2,1,0:T(8,128)(2,1)S(1)}, f16[4,8,3072]{2,1,0:T(8,128)(2,1)S(1)}, u32[]{:S(2)}, u32[]{:S(2)}) %collective-permute-start.2) | collective-permute-done | bytes 196640 | tf_op jit(solution)/shard_map/ppermute | solution.py:25
  11.7 0.1 bitcast_add_fusion
  11.7 2.6 %collective-permute-done.4 = f16[4,8,3072]{2,1,0:T(8,128)(2,1)S(1)} collective-permute-done((f16[4,8,3072]{2,1,0:T(8,128)(2,1)S(1)}, f16[4,8,3072]{2,1,0:T(8,128)(2,1)S(1)}, u32[]{:S(2)}, u32[]{:S(2)}) %collective-permute-start.4) | collective-permute-done | bytes 196640 | tf_op jit(solution)/shard_map/ppermute | solution.py:25
  14.3 0.1 collective-permute-done.3
  14.4 0.1 multiply_add_fusion
  14.6 3.7 %collective-permute-start.7 = (f16[8,3072]{1,0:T(8,128)(2,1)S(1)}, f16[8,3072]{1,0:T(8,128)(2,1)S(1)}, u32[]{:S(2)}, u32[]{:S(2)}) collective-permute-start(f16[8,3072]{1,0:T(8,128)(2,1)S(1)} %get-tuple-element.29), channel_id=1, source_target_pairs={{0,24},{1,7},{2,26},{3,5},{4,28},{5,3},{6,30},{7,1},{8,16},{9,15},... | collective-permute-start | bytes 147464 | tf_op jit(solution)/shard_map/ppermute | solution.py:25
  18.2 0.8 %collective-permute-start.5 = (f16[8,3072]{1,0:T(8,128)(2,1)S(1)}, f16[8,3072]{1,0:T(8,128)(2,1)S(1)}, u32[]{:S(2)}, u32[]{:S(2)}) collective-permute-start(f16[8,3072]{1,0:T(8,128)(2,1)S(1)} %get-tuple-element.28), channel_id=1, source_target_pairs={{0,8},{1,5},{2,10},{3,7},{4,12},{5,1},{6,14},{7,3},{8,0},{9,13},{1... | collective-permute-start | bytes 147464 | tf_op jit(solution)/shard_map/ppermute | solution.py:25
  19.0 1.5 %collective-permute-done.7 = f16[8,3072]{1,0:T(8,128)(2,1)S(1)} collective-permute-done((f16[8,3072]{1,0:T(8,128)(2,1)S(1)}, f16[8,3072]{1,0:T(8,128)(2,1)S(1)}, u32[]{:S(2)}, u32[]{:S(2)}) %collective-permute-start.7) | collective-permute-done | bytes 49184 | tf_op jit(solution)/shard_map/ppermute | solution.py:25
  20.5 2.7 %collective-permute-done.6 = f16[8,3072]{1,0:T(8,128)(2,1)S(1)} collective-permute-done((f16[8,3072]{1,0:T(8,128)(2,1)S(1)}, f16[8,3072]{1,0:T(8,128)(2,1)S(1)}, u32[]{:S(2)}, u32[]{:S(2)}) %collective-permute-start.6) | collective-permute-done | bytes 49184 | tf_op jit(solution)/shard_map/ppermute | solution.py:25
  23.3 0.2 subtract_convert_fusion.1
  23.5 2.1 %collective-permute-start.9 = (bf16[4,6144]{1,0:T(4,128)(2,1)S(1)}, bf16[4,6144]{1,0:T(4,128)(2,1)S(1)}, u32[]{:S(2)}, u32[]{:S(2)}) collective-permute-start(bf16[4,6144]{1,0:T(4,128)(2,1)S(1)} %get-tuple-element.20), channel_id=1, source_target_pairs={{0,16},{1,17},{2,18},{3,19},{4,20},{5,21},{6,22},{7,23},{8,24},{9,... | collective-permute-start | bytes 147464 | tf_op jit(solution)/shard_map/ppermute | solution.py:25
  25.6 0.1 broadcast_in_dim.3
  25.7 0.2 constant_dynamic-update-slice_fusion.3
  25.9 0.8 %collective-permute-start.8 = (bf16[4,6144]{1,0:T(4,128)(2,1)S(1)}, bf16[4,6144]{1,0:T(4,128)(2,1)S(1)}, u32[]{:S(2)}, u32[]{:S(2)}) collective-permute-start(bf16[4,6144]{1,0:T(4,128)(2,1)S(1)} %get-tuple-element.22), channel_id=1, source_target_pairs={{0,12},{1,13},{2,14},{3,15},{4,8},{5,9},{6,10},{7,11},{8,4},{9,5},... | collective-permute-start | bytes 147464 | tf_op jit(solution)/shard_map/ppermute | solution.py:25
  26.7 2.5 %collective-permute-start.10 = (bf16[4,6144]{1,0:T(4,128)(2,1)S(1)}, bf16[4,6144]{1,0:T(4,128)(2,1)S(1)}, u32[]{:S(2)}, u32[]{:S(2)}) collective-permute-start(bf16[4,6144]{1,0:T(4,128)(2,1)S(1)} %get-tuple-element.22), channel_id=1, source_target_pairs={{0,28},{1,29},{2,30},{3,31},{4,24},{5,25},{6,26},{7,27},{8,20},{9,... | collective-permute-start | bytes 147464 | tf_op jit(solution)/shard_map/ppermute | solution.py:25
  29.3 0.1 collective-permute-start.11
  29.4 1.4 %collective-permute-start.12 = (bf16[2,4,6144]{2,1,0:T(4,128)(2,1)S(1)}, bf16[2,4,6144]{2,1,0:T(4,128)(2,1)S(1)}, u32[]{:S(2)}, u32[]{:S(2)}) collective-permute-start(bf16[2,4,6144]{2,1,0:T(4,128)(2,1)S(1)} %pad_maximum_fusion.1), channel_id=1, source_target_pairs={{0,4},{1,5},{2,6},{3,7},{4,0},{5,1},{6,2},{7,3},{8,12},{9,13},{10,... | collective-permute-start | bytes 294920 | tf_op jit(solution)/shard_map/ppermute | solution.py:25
  30.8 0.2 collective-permute-done.8
  31.0 0.8 %multiply_subtract_fusion = (f32[4,6144]{1,0:T(4,128)}, f32[4,6144]{1,0:T(4,128)}, f32[4,6144]{1,0:T(4,128)}) fusion(f32[4,6144]{1,0:T(4,128)S(1)} %copy-done, f32[4,6144]{1,0:T(4,128)S(1)} %get-tuple-element.8, f32[4,6144]{1,0:T(4,128)S(1)} %copy-done.2, f32[4,6144]{1,0:T(4,128)S(1)} %copy-done.1), kind=kLoop, calls=%fused_computation.29 | loop fusion | flops 368640 | bytes 688128 | tf_op jit(solution)/shard_map/sub | solution.py:195
  31.9 1.9 %collective-permute-done.10 = bf16[4,6144]{1,0:T(4,128)(2,1)S(1)} collective-permute-done((bf16[4,6144]{1,0:T(4,128)(2,1)S(1)}, bf16[4,6144]{1,0:T(4,128)(2,1)S(1)}, u32[]{:S(2)}, u32[]{:S(2)}) %collective-permute-start.10) | collective-permute-done | bytes 49184 | tf_op jit(solution)/shard_map/ppermute | solution.py:25
  33.8 0.9 %collective-permute-done.11 = bf16[2,4,6144]{2,1,0:T(4,128)(2,1)S(1)} collective-permute-done((bf16[2,4,6144]{2,1,0:T(4,128)(2,1)S(1)}, bf16[2,4,6144]{2,1,0:T(4,128)(2,1)S(1)}, u32[]{:S(2)}, u32[]{:S(2)}) %collective-permute-start.11) | collective-permute-done | bytes 98336 | tf_op jit(solution)/shard_map/ppermute | solution.py:25
  35.0 0.7 %copy-done.4 = bf16[4,49152]{1,0:T(4,128)(2,1)} copy-done((bf16[4,49152]{1,0:T(4,128)(2,1)}, bf16[4,49152]{1,0:T(4,128)(2,1)S(1)}, u32[]{:S(2)}) %copy-start.4) | copy-done | bytes 393240
  (25 shorter events, 0.4 us)
Async XLA Ops:
  2.5 1.6 %collective-permute-start = (bf16[4,8,3072]{2,1,0:T(8,128)(2,1)S(1)}, bf16[4,8,3072]{2,1,0:T(8,128)(2,1)S(1)}, u32[]{:S(2)}, u32[]{:S(2)}) collective-permute-start(bf16[4,8,3072]{2,1,0:T(8,128)(2,1)S(1)} %get-tuple-element.14), channel_id=1, source_target_pairs={{0,1},{1,0},{2,3},{3,2},{4,5},{5,4},{6,7},{7,6},{8,9},{9,8},{10,11... | collective-permute-start | bytes 589832 | tf_op jit(solution)/shard_map/ppermute | solution.py:25
  3.0 5.0 %collective-permute-start.1 = (bf16[3,4,8,3072]{3,2,1,0:T(8,128)(2,1)S(1)}, bf16[3,4,8,3072]{3,2,1,0:T(8,128)(2,1)S(1)}, u32[]{:S(2)}, u32[]{:S(2)}) collective-permute-start(bf16[3,4,8,3072]{3,2,1,0:T(8,128)(2,1)S(1)} %get-tuple-element.16), channel_id=1, source_target_pairs={{0,1},{1,0},{2,3},{3,2},{4,5},{5,4},{6,7},{7,6},{8,9},{9,8},{10,11... | collective-permute-start | bytes 1769480 | tf_op jit(solution)/shard_map/ppermute | solution.py:25
  4.1 7.5 %collective-permute-start.2 = (f16[4,8,3072]{2,1,0:T(8,128)(2,1)S(1)}, f16[4,8,3072]{2,1,0:T(8,128)(2,1)S(1)}, u32[]{:S(2)}, u32[]{:S(2)}) collective-permute-start(f16[4,8,3072]{2,1,0:T(8,128)(2,1)S(1)} %fusion.1), channel_id=1, source_target_pairs={{0,6},{1,25},{2,4},{3,27},{4,2},{5,29},{6,0},{7,31},{8,14},{9,17},... | collective-permute-start | bytes 589832 | tf_op jit(solution)/shard_map/ppermute | solution.py:25
  8.2 6.1 %collective-permute-start.4 = (f16[4,8,3072]{2,1,0:T(8,128)(2,1)S(1)}, f16[4,8,3072]{2,1,0:T(8,128)(2,1)S(1)}, u32[]{:S(2)}, u32[]{:S(2)}) collective-permute-start(f16[4,8,3072]{2,1,0:T(8,128)(2,1)S(1)} %get-tuple-element.27), channel_id=1, source_target_pairs={{0,2},{1,17},{2,0},{3,19},{4,6},{5,21},{6,4},{7,23},{8,10},{9,25},... | collective-permute-start | bytes 589832 | tf_op jit(solution)/shard_map/ppermute | solution.py:25
  8.8 14.5 %copy-start = (f32[4,6144]{1,0:T(4,128)S(1)}, f32[4,6144]{1,0:T(4,128)}, u32[]{:S(2)}) copy-start(f32[4,6144]{1,0:T(4,128)} %param.5) | copy-start | bytes 294916
  8.8 14.6 %copy-start.1 = (f32[4,6144]{1,0:T(4,128)S(1)}, f32[4,6144]{1,0:T(4,128)}, u32[]{:S(2)}) copy-start(f32[4,6144]{1,0:T(4,128)} %param.7) | copy-start | bytes 294916
  8.8 14.6 %copy-start.2 = (f32[4,6144]{1,0:T(4,128)S(1)}, f32[4,6144]{1,0:T(4,128)}, u32[]{:S(2)}) copy-start(f32[4,6144]{1,0:T(4,128)} %param.6) | copy-start | bytes 294916
  8.8 5.7 %collective-permute-start.3 = (f16[4,8,3072]{2,1,0:T(8,128)(2,1)S(1)}, f16[4,8,3072]{2,1,0:T(8,128)(2,1)S(1)}, u32[]{:S(2)}, u32[]{:S(2)}) collective-permute-start(f16[4,8,3072]{2,1,0:T(8,128)(2,1)S(1)} %get-tuple-element.26), channel_id=1, source_target_pairs={{0,4},{1,9},{2,6},{3,11},{4,0},{5,13},{6,2},{7,15},{8,12},{9,1},{1... | collective-permute-start | bytes 589832 | tf_op jit(solution)/shard_map/ppermute | solution.py:25
  14.6 6.0 %collective-permute-start.7 = (f16[8,3072]{1,0:T(8,128)(2,1)S(1)}, f16[8,3072]{1,0:T(8,128)(2,1)S(1)}, u32[]{:S(2)}, u32[]{:S(2)}) collective-permute-start(f16[8,3072]{1,0:T(8,128)(2,1)S(1)} %get-tuple-element.29), channel_id=1, source_target_pairs={{0,24},{1,7},{2,26},{3,5},{4,28},{5,3},{6,30},{7,1},{8,16},{9,15},... | collective-permute-start | bytes 147464 | tf_op jit(solution)/shard_map/ppermute | solution.py:25
  18.2 5.0 %collective-permute-start.6 = (f16[8,3072]{1,0:T(8,128)(2,1)S(1)}, f16[8,3072]{1,0:T(8,128)(2,1)S(1)}, u32[]{:S(2)}, u32[]{:S(2)}) collective-permute-start(f16[8,3072]{1,0:T(8,128)(2,1)S(1)} %get-tuple-element.30), channel_id=1, source_target_pairs={{0,16},{1,3},{2,18},{3,1},{4,20},{5,7},{6,22},{7,5},{8,24},{9,11},... | collective-permute-start | bytes 147464 | tf_op jit(solution)/shard_map/ppermute | solution.py:25
  18.2 5.0 %collective-permute-start.5 = (f16[8,3072]{1,0:T(8,128)(2,1)S(1)}, f16[8,3072]{1,0:T(8,128)(2,1)S(1)}, u32[]{:S(2)}, u32[]{:S(2)}) collective-permute-start(f16[8,3072]{1,0:T(8,128)(2,1)S(1)} %get-tuple-element.28), channel_id=1, source_target_pairs={{0,8},{1,5},{2,10},{3,7},{4,12},{5,1},{6,14},{7,3},{8,0},{9,13},{1... | collective-permute-start | bytes 147464 | tf_op jit(solution)/shard_map/ppermute | solution.py:25
  23.5 11.4 %copy-start.3 = (f32[4,6144]{1,0:T(4,128)}, f32[4,6144]{1,0:T(4,128)S(1)}, u32[]{:S(2)}) copy-start(f32[4,6144]{1,0:T(4,128)S(1)} %get-tuple-element.8) | copy-start | bytes 294916
  23.5 5.7 %collective-permute-start.9 = (bf16[4,6144]{1,0:T(4,128)(2,1)S(1)}, bf16[4,6144]{1,0:T(4,128)(2,1)S(1)}, u32[]{:S(2)}, u32[]{:S(2)}) collective-permute-start(bf16[4,6144]{1,0:T(4,128)(2,1)S(1)} %get-tuple-element.20), channel_id=1, source_target_pairs={{0,16},{1,17},{2,18},{3,19},{4,20},{5,21},{6,22},{7,23},{8,24},{9,... | collective-permute-start | bytes 147464 | tf_op jit(solution)/shard_map/ppermute | solution.py:25
  25.9 5.0 %collective-permute-start.8 = (bf16[4,6144]{1,0:T(4,128)(2,1)S(1)}, bf16[4,6144]{1,0:T(4,128)(2,1)S(1)}, u32[]{:S(2)}, u32[]{:S(2)}) collective-permute-start(bf16[4,6144]{1,0:T(4,128)(2,1)S(1)} %get-tuple-element.22), channel_id=1, source_target_pairs={{0,12},{1,13},{2,14},{3,15},{4,8},{5,9},{6,10},{7,11},{8,4},{9,5},... | collective-permute-start | bytes 147464 | tf_op jit(solution)/shard_map/ppermute | solution.py:25
  26.7 7.1 %collective-permute-start.10 = (bf16[4,6144]{1,0:T(4,128)(2,1)S(1)}, bf16[4,6144]{1,0:T(4,128)(2,1)S(1)}, u32[]{:S(2)}, u32[]{:S(2)}) collective-permute-start(bf16[4,6144]{1,0:T(4,128)(2,1)S(1)} %get-tuple-element.22), channel_id=1, source_target_pairs={{0,28},{1,29},{2,30},{3,31},{4,24},{5,25},{6,26},{7,27},{8,20},{9,... | collective-permute-start | bytes 147464 | tf_op jit(solution)/shard_map/ppermute | solution.py:25
  29.3 5.5 %collective-permute-start.11 = (bf16[2,4,6144]{2,1,0:T(4,128)(2,1)S(1)}, bf16[2,4,6144]{2,1,0:T(4,128)(2,1)S(1)}, u32[]{:S(2)}, u32[]{:S(2)}) collective-permute-start(bf16[2,4,6144]{2,1,0:T(4,128)(2,1)S(1)} %pad_maximum_fusion.1), channel_id=1, source_target_pairs={{0,8},{1,9},{2,10},{3,11},{4,12},{5,13},{6,14},{7,15},{8,0},{9,1},... | collective-permute-start | bytes 294920 | tf_op jit(solution)/shard_map/ppermute | solution.py:25
  29.4 5.5 %collective-permute-start.12 = (bf16[2,4,6144]{2,1,0:T(4,128)(2,1)S(1)}, bf16[2,4,6144]{2,1,0:T(4,128)(2,1)S(1)}, u32[]{:S(2)}, u32[]{:S(2)}) collective-permute-start(bf16[2,4,6144]{2,1,0:T(4,128)(2,1)S(1)} %pad_maximum_fusion.1), channel_id=1, source_target_pairs={{0,4},{1,5},{2,6},{3,7},{4,0},{5,1},{6,2},{7,3},{8,12},{9,13},{10,... | collective-permute-start | bytes 294920 | tf_op jit(solution)/shard_map/ppermute | solution.py:25
  34.9 0.7 %copy-start.4 = (bf16[4,49152]{1,0:T(4,128)(2,1)}, bf16[4,49152]{1,0:T(4,128)(2,1)S(1)}, u32[]{:S(2)}) copy-start(bf16[4,49152]{1,0:T(4,128)(2,1)S(1)} %fusion.20) | copy-start | bytes 1179652

commit v13 on v12

--- a/solution.py
+++ b/solution.py
@@ -152,16 +152,18 @@
 
 def gather_blocks(first, mine):
     row_block, col_block = mine.shape
-    me = lax.axis_index("hst")
+    me, core = lax.axis_index("hst"), place()[3]
     far = swap(first, Z_FAR, Z_FAR)
-    corner, far_corner = (swap(mine, f, f) for f in (Z_NEAR + Y, Z_FAR + Z_NEAR + Y))
+    corner, cross = swap(mine, Z_NEAR + Y, Z_FAR + Z_NEAR + Y), swap(mine, Z_FAR + Z_NEAR + Y, Z_NEAR + Y)
     pair = jnp.stack([mine, far])
-    near, side = swap(pair, Z_NEAR, Z_NEAR), swap(pair, Y, Y)
-    got = [(0, mine), (3, corner), (4, far), (7, far_corner)]
-    got += [(2, near[0]), (6, near[1]), (1, side[0]), (5, side[1])]
+    side, other_side = swap(pair, Z_NEAR, Y), swap(pair, Y, Z_NEAR)
+    bits = lambda at_0, at_1: jnp.where(core == 0, at_0, at_1)
+    got = [(0, mine), (4, far), (bits(3, 7), corner), (bits(7, 3), cross)]
+    got += [(bits(2, 1) + 4 * i, side[i]) for i in (0, 1)]
+    got += [(bits(1, 2) + 4 * i, other_side[i]) for i in (0, 1)]
     whole = jnp.zeros((row_block, 8 * col_block), mine.dtype)
-    for bits, block in got:
-        whole = lax.dynamic_update_slice_in_dim(whole, block, (me ^ bits) * col_block, 1)
+    for away, block in got:
+        whole = lax.dynamic_update_slice_in_dim(whole, block, (me ^ away) * col_block, 1)
     return whole, corner
 
 

time: 35.8 us -> 36 us (level)
  waiting for transfers between devices: 12.6 us -> 13.2 us
  starting transfers between devices: 17.1 us -> 16.7 us
    ppermute x13, waiting for transfers between devices: 12.6 us -> 13.2 us  [swap(): return lax.ppermute(value, ('hst', 'local'), flip_pairs(flips))]
    ppermute x13, starting transfers between devices: 17.1 us -> 16.7 us  [swap(): return lax.ppermute(value, ('hst', 'local'), flip_pairs(flips))]
  transfers between devices with their start and end apart: 13 -> 13, of which waited for: 9 -> 10; matrix products, arithmetic and copies ran while one was open for 5% -> 5% of each run, Pallas kernels for 1% -> 1%
where the time goes in v13:
time: 36 us; the launch traced here: 35.9 us
  starting transfers between devices  16.7 us (46%)
  waiting for transfers between devices  13.2 us (37%)
  Pallas kernels  2.31 us (6%)
  other arithmetic  1.76 us (5%)
  local copies, waits for them, and re-layouts  1.1 us (3%)
  between operations  0.78 us (2%)
    ppermute x13, starting transfers between devices, swap(): return lax.ppermute(value, ('hst', 'local'), flip_pairs(flips))  16.7 us
    ppermute x13, waiting for transfers between devices, swap(): return lax.ppermute(value, ('hst', 'local'), flip_pairs(flips))  13.2 us
    pallas_call x2, Pallas kernels, call(): pl.pallas_call(kernel, in_specs=[pl.BlockSpec(memory_space=space)], out_s...  2.31 us
    sub x1, other arithmetic, adam(): new_master = master - learn_rate * (update + decay_rate * master)  0.84 us
    unnamed x10, local copies, waits for them, and re-layouts  0.75 us
  transfers between devices with their start and end apart: 13, of which 10 were waited for; matrix products, arithmetic and copies ran while one was open for 5% of the time, Pallas kernels for 1%

profile of v13, /device:TPU:0, one launch (start us, length us, event | category | flops | bytes accessed | tf_op | source)
XLA Modules:
  0.0 35.9 jit_solution(8588162332691623293)
XLA Ops:
  0.6 1.8 %shard_map.83 = (bf16[4,8,3072]{2,1,0:T(8,128)(2,1)S(1)}, bf16[3,4,8,3072]{3,2,1,0:T(8,128)(2,1)S(1)}, bf16[16,49152]{1,0:T(8,128)(2,1)S(1)}) custom-call(bf16[16,49152]{1,0:T(8,128)(2,1)} %bitcast.42), custom_call_target="tpu_custom_call" | custom-call | flops 786432 | bytes 3145728 | tf_op jit(solution)/shard_map/pallas_call | solution.py:103
  2.5 0.5 %collective-permute-start = (bf16[4,8,3072]{2,1,0:T(8,128)(2,1)S(1)}, bf16[4,8,3072]{2,1,0:T(8,128)(2,1)S(1)}, u32[]{:S(2)}, u32[]{:S(2)}) collective-permute-start(bf16[4,8,3072]{2,1,0:T(8,128)(2,1)S(1)} %get-tuple-element.14), channel_id=1, source_target_pairs={{0,1},{1,0},{2,3},{3,2},{4,5},{5,4},{6,7},{7,6},{8,9},{9,8},{10,11... | collective-permute-start | bytes 589832 | tf_op jit(solution)/shard_map/ppermute | solution.py:25
  3.0 0.1 collective-permute-start.1
  3.1 0.5 %shard_map.84 = bf16[4,4,8,3072]{3,2,1,0:T(8,128)(2,1)S(1)} custom-call(bf16[16,49152]{1,0:T(8,128)(2,1)S(1)} %get-tuple-element.13.landed), custom_call_target="tpu_custom_call" | custom-call | flops 786432 | bytes 3145728 | tf_op jit(solution)/shard_map/pallas_call | solution.py:103
  3.5 0.5 %collective-permute-done = bf16[4,8,3072]{2,1,0:T(8,128)(2,1)S(1)} collective-permute-done((bf16[4,8,3072]{2,1,0:T(8,128)(2,1)S(1)}, bf16[4,8,3072]{2,1,0:T(8,128)(2,1)S(1)}, u32[]{:S(2)}, u32[]{:S(2)}) %collective-permute-start) | collective-permute-done | bytes 196640 | tf_op jit(solution)/shard_map/ppermute | solution.py:25
  4.0 0.1 fusion.1
  4.1 3.9 %collective-permute-start.2 = (f16[4,8,3072]{2,1,0:T(8,128)(2,1)S(1)}, f16[4,8,3072]{2,1,0:T(8,128)(2,1)S(1)}, u32[]{:S(2)}, u32[]{:S(2)}) collective-permute-start(f16[4,8,3072]{2,1,0:T(8,128)(2,1)S(1)} %fusion.1), channel_id=1, source_target_pairs={{0,6},{1,25},{2,4},{3,27},{4,2},{5,29},{6,0},{7,31},{8,14},{9,17},... | collective-permute-start | bytes 589832 | tf_op jit(solution)/shard_map/ppermute | solution.py:25
  8.0 0.1 fusion.2
  8.2 0.6 %collective-permute-start.4 = (f16[4,8,3072]{2,1,0:T(8,128)(2,1)S(1)}, f16[4,8,3072]{2,1,0:T(8,128)(2,1)S(1)}, u32[]{:S(2)}, u32[]{:S(2)}) collective-permute-start(f16[4,8,3072]{2,1,0:T(8,128)(2,1)S(1)} %get-tuple-element.27), channel_id=1, source_target_pairs={{0,2},{1,17},{2,0},{3,19},{4,6},{5,21},{6,4},{7,23},{8,10},{9,25},... | collective-permute-start | bytes 589832 | tf_op jit(solution)/shard_map/ppermute | solution.py:25
  8.8 0.7 %collective-permute-start.3 = (f16[4,8,3072]{2,1,0:T(8,128)(2,1)S(1)}, f16[4,8,3072]{2,1,0:T(8,128)(2,1)S(1)}, u32[]{:S(2)}, u32[]{:S(2)}) collective-permute-start(f16[4,8,3072]{2,1,0:T(8,128)(2,1)S(1)} %get-tuple-element.26), channel_id=1, source_target_pairs={{0,4},{1,9},{2,6},{3,11},{4,0},{5,13},{6,2},{7,15},{8,12},{9,1},{1... | collective-permute-start | bytes 589832 | tf_op jit(solution)/shard_map/ppermute | solution.py:25
  9.5 2.2 %collective-permute-done.2 = f16[4,8,3072]{2,1,0:T(8,128)(2,1)S(1)} collective-permute-done((f16[4,8,3072]{2,1,0:T(8,128)(2,1)S(1)}, f16[4,8,3072]{2,1,0:T(8,128)(2,1)S(1)}, u32[]{:S(2)}, u32[]{:S(2)}) %collective-permute-start.2) | collective-permute-done | bytes 196640 | tf_op jit(solution)/shard_map/ppermute | solution.py:25
  11.7 0.1 bitcast_add_fusion
  11.7 2.6 %collective-permute-done.4 = f16[4,8,3072]{2,1,0:T(8,128)(2,1)S(1)} collective-permute-done((f16[4,8,3072]{2,1,0:T(8,128)(2,1)S(1)}, f16[4,8,3072]{2,1,0:T(8,128)(2,1)S(1)}, u32[]{:S(2)}, u32[]{:S(2)}) %collective-permute-start.4) | collective-permute-done | bytes 196640 | tf_op jit(solution)/shard_map/ppermute | solution.py:25
  14.3 0.1 collective-permute-done.3
  14.4 0.1 multiply_add_fusion
  14.6 3.7 %collective-permute-start.7 = (f16[8,3072]{1,0:T(8,128)(2,1)S(1)}, f16[8,3072]{1,0:T(8,128)(2,1)S(1)}, u32[]{:S(2)}, u32[]{:S(2)}) collective-permute-start(f16[8,3072]{1,0:T(8,128)(2,1)S(1)} %get-tuple-element.29), channel_id=1, source_target_pairs={{0,24},{1,7},{2,26},{3,5},{4,28},{5,3},{6,30},{7,1},{8,16},{9,15},... | collective-permute-start | bytes 147464 | tf_op jit(solution)/shard_map/ppermute | solution.py:25
  18.2 0.8 %collective-permute-start.5 = (f16[8,3072]{1,0:T(8,128)(2,1)S(1)}, f16[8,3072]{1,0:T(8,128)(2,1)S(1)}, u32[]{:S(2)}, u32[]{:S(2)}) collective-permute-start(f16[8,3072]{1,0:T(8,128)(2,1)S(1)} %get-tuple-element.28), channel_id=1, source_target_pairs={{0,8},{1,5},{2,10},{3,7},{4,12},{5,1},{6,14},{7,3},{8,0},{9,13},{1... | collective-permute-start | bytes 147464 | tf_op jit(solution)/shard_map/ppermute | solution.py:25
  19.0 1.5 %collective-permute-done.7 = f16[8,3072]{1,0:T(8,128)(2,1)S(1)} collective-permute-done((f16[8,3072]{1,0:T(8,128)(2,1)S(1)}, f16[8,3072]{1,0:T(8,128)(2,1)S(1)}, u32[]{:S(2)}, u32[]{:S(2)}) %collective-permute-start.7) | collective-permute-done | bytes 49184 | tf_op jit(solution)/shard_map/ppermute | solution.py:25
  20.5 2.7 %collective-permute-done.6 = f16[8,3072]{1,0:T(8,128)(2,1)S(1)} collective-permute-done((f16[8,3072]{1,0:T(8,128)(2,1)S(1)}, f16[8,3072]{1,0:T(8,128)(2,1)S(1)}, u32[]{:S(2)}, u32[]{:S(2)}) %collective-permute-start.6) | collective-permute-done | bytes 49184 | tf_op jit(solution)/shard_map/ppermute | solution.py:25
  23.3 0.2 subtract_convert_fusion.1
  23.5 2.1 %collective-permute-start.9 = (bf16[4,6144]{1,0:T(4,128)(2,1)S(1)}, bf16[4,6144]{1,0:T(4,128)(2,1)S(1)}, u32[]{:S(2)}, u32[]{:S(2)}) collective-permute-start(bf16[4,6144]{1,0:T(4,128)(2,1)S(1)} %get-tuple-element.20), channel_id=1, source_target_pairs={{0,16},{1,17},{2,18},{3,19},{4,20},{5,21},{6,22},{7,23},{8,24},{9,... | collective-permute-start | bytes 147464 | tf_op jit(solution)/shard_map/ppermute | solution.py:25
  25.6 0.1 broadcast_in_dim.3
  25.7 0.2 constant_dynamic-update-slice_fusion.3
  25.9 0.8 %collective-permute-start.8 = (bf16[4,6144]{1,0:T(4,128)(2,1)S(1)}, bf16[4,6144]{1,0:T(4,128)(2,1)S(1)}, u32[]{:S(2)}, u32[]{:S(2)}) collective-permute-start(bf16[4,6144]{1,0:T(4,128)(2,1)S(1)} %get-tuple-element.22), channel_id=1, source_target_pairs={{0,12},{1,29},{2,14},{3,31},{4,8},{5,25},{6,10},{7,27},{8,4},{9,21... | collective-permute-start | bytes 147464 | tf_op jit(solution)/shard_map/ppermute | solution.py:25
  26.7 2.5 %collective-permute-start.10 = (bf16[4,6144]{1,0:T(4,128)(2,1)S(1)}, bf16[4,6144]{1,0:T(4,128)(2,1)S(1)}, u32[]{:S(2)}, u32[]{:S(2)}) collective-permute-start(bf16[4,6144]{1,0:T(4,128)(2,1)S(1)} %get-tuple-element.22), channel_id=1, source_target_pairs={{0,28},{1,13},{2,30},{3,15},{4,24},{5,9},{6,26},{7,11},{8,20},{9,5... | collective-permute-start | bytes 147464 | tf_op jit(solution)/shard_map/ppermute | solution.py:25
  29.2 0.5 %collective-permute-done.9 = bf16[4,6144]{1,0:T(4,128)(2,1)S(1)} collective-permute-done((bf16[4,6144]{1,0:T(4,128)(2,1)S(1)}, bf16[4,6144]{1,0:T(4,128)(2,1)S(1)}, u32[]{:S(2)}, u32[]{:S(2)}) %collective-permute-start.9) | collective-permute-done | bytes 49184 | tf_op jit(solution)/shard_map/ppermute | solution.py:25
  29.9 1.0 %collective-permute-start.12 = (bf16[2,4,6144]{2,1,0:T(4,128)(2,1)S(1)}, bf16[2,4,6144]{2,1,0:T(4,128)(2,1)S(1)}, u32[]{:S(2)}, u32[]{:S(2)}) collective-permute-start(bf16[2,4,6144]{2,1,0:T(4,128)(2,1)S(1)} %pad_maximum_fusion.1), channel_id=1, source_target_pairs={{0,4},{1,9},{2,6},{3,11},{4,0},{5,13},{6,2},{7,15},{8,12},{9,1},{1... | collective-permute-start | bytes 294920 | tf_op jit(solution)/shard_map/ppermute | solution.py:25
  30.9 0.2 collective-permute-done.8
  31.1 0.8 %multiply_subtract_fusion = (f32[4,6144]{1,0:T(4,128)}, f32[4,6144]{1,0:T(4,128)}, f32[4,6144]{1,0:T(4,128)}) fusion(f32[4,6144]{1,0:T(4,128)S(1)} %copy-done, f32[4,6144]{1,0:T(4,128)S(1)} %get-tuple-element.8, f32[4,6144]{1,0:T(4,128)S(1)} %copy-done.2, f32[4,6144]{1,0:T(4,128)S(1)} %copy-done.1), kind=kLoop, calls=%fused_computation.29 | loop fusion | flops 368640 | bytes 688128 | tf_op jit(solution)/shard_map/sub | solution.py:197
  32.0 2.1 %collective-permute-done.10 = bf16[4,6144]{1,0:T(4,128)(2,1)S(1)} collective-permute-done((bf16[4,6144]{1,0:T(4,128)(2,1)S(1)}, bf16[4,6144]{1,0:T(4,128)(2,1)S(1)}, u32[]{:S(2)}, u32[]{:S(2)}) %collective-permute-start.10) | collective-permute-done | bytes 49184 | tf_op jit(solution)/shard_map/ppermute | solution.py:25
  34.1 0.9 %collective-permute-done.11 = bf16[2,4,6144]{2,1,0:T(4,128)(2,1)S(1)} collective-permute-done((bf16[2,4,6144]{2,1,0:T(4,128)(2,1)S(1)}, bf16[2,4,6144]{2,1,0:T(4,128)(2,1)S(1)}, u32[]{:S(2)}, u32[]{:S(2)}) %collective-permute-start.11) | collective-permute-done | bytes 98336 | tf_op jit(solution)/shard_map/ppermute | solution.py:25
  35.1 0.7 %copy-done.4 = bf16[4,49152]{1,0:T(4,128)(2,1)} copy-done((bf16[4,49152]{1,0:T(4,128)(2,1)}, bf16[4,49152]{1,0:T(4,128)(2,1)S(1)}, u32[]{:S(2)}) %copy-start.4) | copy-done | bytes 393240
  (25 shorter events, 0.5 us)
Async XLA Ops:
  2.5 1.6 %collective-permute-start = (bf16[4,8,3072]{2,1,0:T(8,128)(2,1)S(1)}, bf16[4,8,3072]{2,1,0:T(8,128)(2,1)S(1)}, u32[]{:S(2)}, u32[]{:S(2)}) collective-permute-start(bf16[4,8,3072]{2,1,0:T(8,128)(2,1)S(1)} %get-tuple-element.14), channel_id=1, source_target_pairs={{0,1},{1,0},{2,3},{3,2},{4,5},{5,4},{6,7},{7,6},{8,9},{9,8},{10,11... | collective-permute-start | bytes 589832 | tf_op jit(solution)/shard_map/ppermute | solution.py:25
  3.0 5.0 %collective-permute-start.1 = (bf16[3,4,8,3072]{3,2,1,0:T(8,128)(2,1)S(1)}, bf16[3,4,8,3072]{3,2,1,0:T(8,128)(2,1)S(1)}, u32[]{:S(2)}, u32[]{:S(2)}) collective-permute-start(bf16[3,4,8,3072]{3,2,1,0:T(8,128)(2,1)S(1)} %get-tuple-element.16), channel_id=1, source_target_pairs={{0,1},{1,0},{2,3},{3,2},{4,5},{5,4},{6,7},{7,6},{8,9},{9,8},{10,11... | collective-permute-start | bytes 1769480 | tf_op jit(solution)/shard_map/ppermute | solution.py:25
  4.1 7.5 %collective-permute-start.2 = (f16[4,8,3072]{2,1,0:T(8,128)(2,1)S(1)}, f16[4,8,3072]{2,1,0:T(8,128)(2,1)S(1)}, u32[]{:S(2)}, u32[]{:S(2)}) collective-permute-start(f16[4,8,3072]{2,1,0:T(8,128)(2,1)S(1)} %fusion.1), channel_id=1, source_target_pairs={{0,6},{1,25},{2,4},{3,27},{4,2},{5,29},{6,0},{7,31},{8,14},{9,17},... | collective-permute-start | bytes 589832 | tf_op jit(solution)/shard_map/ppermute | solution.py:25
  8.2 6.1 %collective-permute-start.4 = (f16[4,8,3072]{2,1,0:T(8,128)(2,1)S(1)}, f16[4,8,3072]{2,1,0:T(8,128)(2,1)S(1)}, u32[]{:S(2)}, u32[]{:S(2)}) collective-permute-start(f16[4,8,3072]{2,1,0:T(8,128)(2,1)S(1)} %get-tuple-element.27), channel_id=1, source_target_pairs={{0,2},{1,17},{2,0},{3,19},{4,6},{5,21},{6,4},{7,23},{8,10},{9,25},... | collective-permute-start | bytes 589832 | tf_op jit(solution)/shard_map/ppermute | solution.py:25
  8.8 14.5 %copy-start = (f32[4,6144]{1,0:T(4,128)S(1)}, f32[4,6144]{1,0:T(4,128)}, u32[]{:S(2)}) copy-start(f32[4,6144]{1,0:T(4,128)} %param.5) | copy-start | bytes 294916
  8.8 14.6 %copy-start.1 = (f32[4,6144]{1,0:T(4,128)S(1)}, f32[4,6144]{1,0:T(4,128)}, u32[]{:S(2)}) copy-start(f32[4,6144]{1,0:T(4,128)} %param.7) | copy-start | bytes 294916
  8.8 14.6 %copy-start.2 = (f32[4,6144]{1,0:T(4,128)S(1)}, f32[4,6144]{1,0:T(4,128)}, u32[]{:S(2)}) copy-start(f32[4,6144]{1,0:T(4,128)} %param.6) | copy-start | bytes 294916
  8.8 5.7 %collective-permute-start.3 = (f16[4,8,3072]{2,1,0:T(8,128)(2,1)S(1)}, f16[4,8,3072]{2,1,0:T(8,128)(2,1)S(1)}, u32[]{:S(2)}, u32[]{:S(2)}) collective-permute-start(f16[4,8,3072]{2,1,0:T(8,128)(2,1)S(1)} %get-tuple-element.26), channel_id=1, source_target_pairs={{0,4},{1,9},{2,6},{3,11},{4,0},{5,13},{6,2},{7,15},{8,12},{9,1},{1... | collective-permute-start | bytes 589832 | tf_op jit(solution)/shard_map/ppermute | solution.py:25
  14.6 6.0 %collective-permute-start.7 = (f16[8,3072]{1,0:T(8,128)(2,1)S(1)}, f16[8,3072]{1,0:T(8,128)(2,1)S(1)}, u32[]{:S(2)}, u32[]{:S(2)}) collective-permute-start(f16[8,3072]{1,0:T(8,128)(2,1)S(1)} %get-tuple-element.29), channel_id=1, source_target_pairs={{0,24},{1,7},{2,26},{3,5},{4,28},{5,3},{6,30},{7,1},{8,16},{9,15},... | collective-permute-start | bytes 147464 | tf_op jit(solution)/shard_map/ppermute | solution.py:25
  18.2 5.0 %collective-permute-start.6 = (f16[8,3072]{1,0:T(8,128)(2,1)S(1)}, f16[8,3072]{1,0:T(8,128)(2,1)S(1)}, u32[]{:S(2)}, u32[]{:S(2)}) collective-permute-start(f16[8,3072]{1,0:T(8,128)(2,1)S(1)} %get-tuple-element.30), channel_id=1, source_target_pairs={{0,16},{1,3},{2,18},{3,1},{4,20},{5,7},{6,22},{7,5},{8,24},{9,11},... | collective-permute-start | bytes 147464 | tf_op jit(solution)/shard_map/ppermute | solution.py:25
  18.2 5.0 %collective-permute-start.5 = (f16[8,3072]{1,0:T(8,128)(2,1)S(1)}, f16[8,3072]{1,0:T(8,128)(2,1)S(1)}, u32[]{:S(2)}, u32[]{:S(2)}) collective-permute-start(f16[8,3072]{1,0:T(8,128)(2,1)S(1)} %get-tuple-element.28), channel_id=1, source_target_pairs={{0,8},{1,5},{2,10},{3,7},{4,12},{5,1},{6,14},{7,3},{8,0},{9,13},{1... | collective-permute-start | bytes 147464 | tf_op jit(solution)/shard_map/ppermute | solution.py:25
  23.5 11.6 %copy-start.3 = (f32[4,6144]{1,0:T(4,128)}, f32[4,6144]{1,0:T(4,128)S(1)}, u32[]{:S(2)}) copy-start(f32[4,6144]{1,0:T(4,128)S(1)} %get-tuple-element.8) | copy-start | bytes 294916
  23.5 6.2 %collective-permute-start.9 = (bf16[4,6144]{1,0:T(4,128)(2,1)S(1)}, bf16[4,6144]{1,0:T(4,128)(2,1)S(1)}, u32[]{:S(2)}, u32[]{:S(2)}) collective-permute-start(bf16[4,6144]{1,0:T(4,128)(2,1)S(1)} %get-tuple-element.20), channel_id=1, source_target_pairs={{0,16},{1,17},{2,18},{3,19},{4,20},{5,21},{6,22},{7,23},{8,24},{9,... | collective-permute-start | bytes 147464 | tf_op jit(solution)/shard_map/ppermute | solution.py:25
  25.9 5.1 %collective-permute-start.8 = (bf16[4,6144]{1,0:T(4,128)(2,1)S(1)}, bf16[4,6144]{1,0:T(4,128)(2,1)S(1)}, u32[]{:S(2)}, u32[]{:S(2)}) collective-permute-start(bf16[4,6144]{1,0:T(4,128)(2,1)S(1)} %get-tuple-element.22), channel_id=1, source_target_pairs={{0,12},{1,29},{2,14},{3,31},{4,8},{5,25},{6,10},{7,27},{8,4},{9,21... | collective-permute-start | bytes 147464 | tf_op jit(solution)/shard_map/ppermute | solution.py:25
  26.7 7.3 %collective-permute-start.10 = (bf16[4,6144]{1,0:T(4,128)(2,1)S(1)}, bf16[4,6144]{1,0:T(4,128)(2,1)S(1)}, u32[]{:S(2)}, u32[]{:S(2)}) collective-permute-start(bf16[4,6144]{1,0:T(4,128)(2,1)S(1)} %get-tuple-element.22), channel_id=1, source_target_pairs={{0,28},{1,13},{2,30},{3,15},{4,24},{5,9},{6,26},{7,11},{8,20},{9,5... | collective-permute-start | bytes 147464 | tf_op jit(solution)/shard_map/ppermute | solution.py:25
  29.8 5.1 %collective-permute-start.11 = (bf16[2,4,6144]{2,1,0:T(4,128)(2,1)S(1)}, bf16[2,4,6144]{2,1,0:T(4,128)(2,1)S(1)}, u32[]{:S(2)}, u32[]{:S(2)}) collective-permute-start(bf16[2,4,6144]{2,1,0:T(4,128)(2,1)S(1)} %pad_maximum_fusion.1), channel_id=1, source_target_pairs={{0,8},{1,5},{2,10},{3,7},{4,12},{5,1},{6,14},{7,3},{8,0},{9,13},{1... | collective-permute-start | bytes 294920 | tf_op jit(solution)/shard_map/ppermute | solution.py:25
  29.9 5.1 %collective-permute-start.12 = (bf16[2,4,6144]{2,1,0:T(4,128)(2,1)S(1)}, bf16[2,4,6144]{2,1,0:T(4,128)(2,1)S(1)}, u32[]{:S(2)}, u32[]{:S(2)}) collective-permute-start(bf16[2,4,6144]{2,1,0:T(4,128)(2,1)S(1)} %pad_maximum_fusion.1), channel_id=1, source_target_pairs={{0,4},{1,9},{2,6},{3,11},{4,0},{5,13},{6,2},{7,15},{8,12},{9,1},{1... | collective-permute-start | bytes 294920 | tf_op jit(solution)/shard_map/ppermute | solution.py:25
  35.1 0.7 %copy-start.4 = (bf16[4,49152]{1,0:T(4,128)(2,1)}, bf16[4,49152]{1,0:T(4,128)(2,1)S(1)}, u32[]{:S(2)}) copy-start(bf16[4,49152]{1,0:T(4,128)(2,1)S(1)} %fusion.20) | copy-start | bytes 1179652

commit v14 on v13

--- a/solution.py
+++ b/solution.py
@@ -45,106 +45,132 @@
     return me_local // 2, me_host % 2, me_host // 2, me_local % 2
 
 
-def rows_of(core, block, i, store):
+def tiles_of(block):
     tile, half = block.shape[0] // 2, block.shape[1] // 2
-    my_x, my_y, my_z, _ = place()
-    z, y = i // 2, i % 2
     block = block.astype(jnp.float32)
+    found = []
     for x in (0, 1):
         left, right = block[x * tile : (x + 1) * tile, :half], block[x * tile : (x + 1) * tile, half:]
-        rows = [
-            jnp.concatenate([left[at : at + tile // 2], right[at : at + tile // 2]], axis=0).astype(jnp.bfloat16)
-            for at in (0, tile // 2)
-        ]
+        found.append(
+            [
+                jnp.concatenate([left[at : at + tile // 2], right[at : at + tile // 2]], axis=0).astype(jnp.bfloat16)
+                for at in (0, tile // 2)
+            ]
+        )
+    return found
+
+
+def order():
+    _, y, z, _ = place()
+    far_z, far_y = z ^ 3, 1 - y
+    return [(far_z, far_y), (far_z, y)] + [(far_z ^ k, at) for at in (far_y, y) for k in (1, 2, 3)]
+
+
+def fetch(whole, landed, arrived, blocks):
+    cols = landed.shape[2]
+    copies = []
+    for i, (z, y) in enumerate(blocks):
+        at = pl.multiple_of((2 * z + y) * cols, 128)
+        copies.append(pltpu.make_async_copy(whole.at[:, pl.ds(at, cols)], landed.at[i], arrived.at[i]))
+        copies[-1].start()
+    return copies
+
+
+def far_kernel(whole, theirs, own, landed, arrived):
+    my_x, _, _, core = place()
+    blocks = order()[:5]
+    copies = fetch(whole, landed, arrived, blocks)
+
+    def store(of_core, member, rows):
+        @pl.when(core == of_core)
+        def _():
+            own[member] = rows
+
+        @pl.when(core != of_core)
+        def _():
+            theirs[member] = rows
+
+    for i, (z, y) in enumerate(blocks):
+        copies[i].wait()
+        tiles = tiles_of(landed[i])
+        if i < 2:
+            for x in (0, 1):
+                store(1, 2 * x + y, tiles[x][1])
+        if i != 1:
+            store(0, z, jnp.where(my_x == 0, tiles[1][0], tiles[0][0]))
+
+
+def store_rest(core, block, z, y, out):
+    my_x, my_y, my_z, _ = place()
+    tiles = tiles_of(block)
+    for x in (0, 1):
         step = jnp.where(core == 0, (2 * my_x + my_y) ^ (2 * x + y), my_z ^ z)
         member = jnp.where(core == 0, z, 2 * x + y)
-        store(step, member, jnp.where(core == 0, rows[0], rows[1]))
-
-
-def theirs_kernel(whole, first, others, landed, arrived):
-    half = first.shape[2]
+
+        @pl.when(step != 3)
+        def _(x=x, step=step, member=member):
+            out[step, member] = jnp.where(core == 0, tiles[x][0], tiles[x][1])
+
+
+def theirs_kernel(whole, landed, out, landed_rest, arrived):
+    core, blocks = place()[3], order()
+    copies = fetch(whole, landed_rest, arrived, blocks[5:])
+    for i, (z, y) in enumerate(blocks):
+        if i >= 5:
+            copies[i - 5].wait()
+        store_rest(1 - core, landed[i] if i < 5 else landed_rest[i - 5], z, y, out)
+
+
+def own_kernel(landed, landed_rest, out):
     core = place()[3]
-    parts = [pl.ds(i * half, half) for i in range(16)]
-    copies = [
-        pltpu.make_async_copy(whole.at[:, part], landed.at[:, part], arrived.at[i])
-        for i, part in enumerate(parts)
-    ]
-    for copy in copies:
-        copy.start()
-
-    def store(step, member, rows):
-        @pl.when(step == 3)
-        def _():
-            first[member] = rows
-
-        @pl.when(step != 3)
-        def _():
-            others[step, member] = rows
-
-    for i in range(8):
-        copies[2 * i].wait()
-        copies[2 * i + 1].wait()
-        rows_of(1 - core, landed[:, pl.ds(2 * i * half, 2 * half)], i, store)
-
-
-def own_kernel(landed, own):
-    half = own.shape[3]
-    core = place()[3]
-
-    def store(step, member, rows):
-        own[step, member] = rows
-
-    for i in range(8):
-        rows_of(core, landed[:, pl.ds(2 * i * half, 2 * half)], i, store)
-
-
-def call(kernel, operand, space, outs, scratch=()):
-    size = operand.size
+    for i, (z, y) in enumerate(order()):
+        store_rest(core, landed[i] if i < 5 else landed_rest[i - 5], z, y, out)
+
+
+def call(kernel, operands, outs, copies=0):
+    spaces = [pltpu.HBM if copies and i == 0 else pltpu.VMEM for i in range(len(operands))]
+    size = operands[0].size
     return pl.pallas_call(
         kernel,
-        in_specs=[pl.BlockSpec(memory_space=space)],
+        in_specs=[pl.BlockSpec(memory_space=space) for space in spaces],
         out_specs=[pl.BlockSpec(memory_space=pltpu.VMEM)] * len(outs),
-        out_shape=[pltpu.VMEM(shape, operand.dtype) for shape in outs],
-        scratch_shapes=scratch,
+        out_shape=[pltpu.VMEM(shape, jnp.bfloat16) for shape in outs],
+        scratch_shapes=[pltpu.SemaphoreType.DMA((copies,))] if copies else [],
         compiler_params=pltpu.CompilerParams(vmem_limit_bytes=8 << 20),
         cost_estimate=pl.CostEstimate(flops=size, bytes_accessed=4 * size, transcendentals=0),
-    )(pltpu.with_memory_space_constraint(operand, space))
+    )(*[pltpu.with_memory_space_constraint(v, space) for v, space in zip(operands, spaces)])
 
 
 def split_rows(gradient):
     rows, cols = gradient.shape
-    shape = (4, rows // 2, cols // 16)
-    first, others, landed = call(
-        theirs_kernel,
-        gradient,
-        pltpu.HBM,
-        [shape, (3, *shape), gradient.shape],
-        [pltpu.SemaphoreType.DMA((16,))],
-    )
-    first, others, landed = lax.optimization_barrier((first, others, landed))
-    (own,) = call(own_kernel, landed, pltpu.VMEM, [(4, *shape)])
-    return first, others, own
+    shape, block = (4, rows // 2, cols // 16), (rows, cols // 8)
+    theirs, own, landed = call(far_kernel, [gradient], [shape, shape, (5, *block)], copies=5)
+    theirs, landed = lax.optimization_barrier((theirs, landed))
+    theirs_rest, landed_rest = call(theirs_kernel, [gradient, landed], [(3, *shape), (3, *block)], copies=3)
+    return theirs, own, theirs_rest, [landed, landed_rest]
 
 
 def reduce_blocks(gradient):
     tile = gradient.shape[0] // 2
     x, y, z, core = place()
 
-    first, others, own = split_rows(gradient)
-    first, others = swap(first, CORE, CORE), swap(others, CORE, CORE)
+    theirs, own, theirs_rest, landed = split_rows(gradient)
+    other, other_rest = swap(theirs, CORE, CORE), swap(theirs_rest, CORE, CORE)
+
+    over_xy, over_z = (0, Y, X, X + Y), (0, Z_NEAR, Z_FAR, Z_NEAR + Z_FAR)
+    sent = {3: narrow(own.astype(jnp.float32) + other.astype(jnp.float32))}
+    *landed, sent[3] = lax.optimization_barrier((*landed, sent[3]))
+    (own_rest,) = call(own_kernel, landed, [(3, *own.shape)])
 
     def pair(d):
-        return own[d].astype(jnp.float32) + (first if d == 3 else others[d]).astype(jnp.float32)
-
-    over_xy, over_z = (0, Y, X, X + Y), (0, Z_NEAR, Z_FAR, Z_NEAR + Z_FAR)
-    sent = {3: narrow(pair(3))}
-    own, sent[3] = lax.optimization_barrier((own, sent[3]))
+        return own_rest[d].astype(jnp.float32) + other_rest[d].astype(jnp.float32)
+
     sent.update({d: narrow(pair(d)) for d in (1, 2)})
-    got = [swap(sent[d], over_xy[d], over_z[d]) for d in (3, 1, 2)]
+    got = [swap(sent[d], over_xy[d], over_z[d]) for d in (3, 2, 1)]
     quarter = lax.optimization_barrier(pair(0) + widen(got[0]))
     quarter = quarter + widen(got[1]) + widen(got[2])
     me = jnp.where(core == 0, z, 2 * x + y)
-    got = [swap(narrow(pick(quarter, me ^ d)), over_z[d], over_xy[d]) for d in (1, 2, 3)]
+    got = [swap(narrow(pick(quarter, me ^ d)), over_z[d], over_xy[d]) for d in (3, 2, 1)]
     total = pick(quarter, me) + widen(got[0]) + widen(got[1]) + widen(got[2])
 
     return jnp.concatenate([total[: tile // 2], total[tile // 2 :]], axis=1)

time: 36 us -> 36.2 us (level)
  Pallas kernels: 2.31 us -> 3.31 us
  waiting for transfers between devices: 13.2 us -> 12.3 us
    pallas_call x2 -> x3, Pallas kernels: 2.31 us -> 3.31 us  [call(): pl.pallas_call(kernel, in_specs=[pl.BlockSpec(memory_space=space) for spa...]
    ppermute x13, waiting for transfers between devices: 13.2 us -> 12.3 us  [swap(): return lax.ppermute(value, ('hst', 'local'), flip_pairs(flips))]
  transfers between devices with their start and end apart: 13 -> 13, of which waited for: 10 -> 9; matrix products, arithmetic and copies ran while one was open for 5% -> 5% of each run, Pallas kernels for 1% -> 5%
where the time goes in v14:
time: 36.2 us; the launch traced here: 36 us
  starting transfers between devices  16.8 us (46%)
  waiting for transfers between devices  12.3 us (34%)
  Pallas kernels  3.31 us (9%)
  other arithmetic  1.76 us (5%)
  local copies, waits for them, and re-layouts  1.1 us (3%)
  between operations  0.83 us (2%)
    ppermute x13, starting transfers between devices, swap(): return lax.ppermute(value, ('hst', 'local'), flip_pairs(flips))  16.8 us
    ppermute x13, waiting for transfers between devices, swap(): return lax.ppermute(value, ('hst', 'local'), flip_pairs(flips))  12.3 us
    pallas_call x3, Pallas kernels, call(): pl.pallas_call(kernel, in_specs=[pl.BlockSpec(memory_space=space) for spa...  3.31 us
    sub x1, other arithmetic, adam(): new_master = master - learn_rate * (update + decay_rate * master)  0.84 us
    unnamed x10, local copies, waits for them, and re-layouts  0.75 us
  transfers between devices with their start and end apart: 13, of which 9 were waited for; matrix products, arithmetic and copies ran while one was open for 5% of the time, Pallas kernels for 5%

profile of v14, /device:TPU:0, one launch (start us, length us, event | category | flops | bytes accessed | tf_op | source)
XLA Modules:
  0.0 36.0 jit_solution(3255754815442862814)
XLA Ops:
  0.6 1.4 %shard_map.83 = (bf16[4,8,3072]{2,1,0:T(8,128)(2,1)S(1)}, bf16[4,8,3072]{2,1,0:T(8,128)(2,1)S(1)}, bf16[5,16,6144]{2,1,0:T(8,128)(2,1)S(1)}) custom-call(bf16[16,49152]{1,0:T(8,128)(2,1)} %bitcast.37), custom_call_target="tpu_custom_call" | custom-call | flops 786432 | bytes 3145728 | tf_op jit(solution)/shard_map/pallas_call | solution.py:133
  2.0 0.5 %collective-permute-start = (bf16[4,8,3072]{2,1,0:T(8,128)(2,1)S(1)}, bf16[4,8,3072]{2,1,0:T(8,128)(2,1)S(1)}, u32[]{:S(2)}, u32[]{:S(2)}) collective-permute-start(bf16[4,8,3072]{2,1,0:T(8,128)(2,1)S(1)} %get-tuple-element.23), channel_id=1, source_target_pairs={{0,1},{1,0},{2,3},{3,2},{4,5},{5,4},{6,7},{7,6},{8,9},{9,8},{10,11... | collective-permute-start | bytes 589832 | tf_op jit(solution)/shard_map/ppermute | solution.py:25
  2.5 1.2 %shard_map.84 = (bf16[3,4,8,3072]{3,2,1,0:T(8,128)(2,1)S(1)}, bf16[3,16,6144]{2,1,0:T(8,128)(2,1)S(1)}) custom-call(bf16[16,49152]{1,0:T(8,128)(2,1)} %bitcast.38, bf16[5,16,6144]{2,1,0:T(8,128)(2,1)S(1)} %get-tuple-element.24.landed), custom_call_target="tpu_custom_call" | custom-call | flops 786432 | bytes 3145728 | tf_op jit(solution)/shard_map/pallas_call | solution.py:133
  3.8 0.1 collective-permute-start.1
  4.0 0.1 multiply_convert_fusion.2
  4.0 3.9 %collective-permute-start.2 = (f16[4,8,3072]{2,1,0:T(8,128)(2,1)S(1)}, f16[4,8,3072]{2,1,0:T(8,128)(2,1)S(1)}, u32[]{:S(2)}, u32[]{:S(2)}) collective-permute-start(f16[4,8,3072]{2,1,0:T(8,128)(2,1)S(1)} %multiply_convert_fusion.2), channel_id=1, source_target_pairs={{0,6},{1,25},{2,4},{3,27},{4,2},{5,29},{6,0},{7,31},{8,14},{9,17},... | collective-permute-start | bytes 589832 | tf_op jit(solution)/shard_map/ppermute | solution.py:25
  8.0 0.7 %shard_map.85 = bf16[3,4,8,3072]{3,2,1,0:T(8,128)(2,1)S(1)} custom-call(bf16[5,16,6144]{2,1,0:T(8,128)(2,1)S(1)} %get-tuple-element.24.landed, bf16[3,16,6144]{2,1,0:T(8,128)(2,1)S(1)} %get-tuple-element.25.landed_rest), custom_call_target="tpu_custom_call" | custom-call | flops 491520 | bytes 1966080 | tf_op jit(solution)/shard_map/pallas_call | solution.py:133
  8.7 0.1 fusion
  8.8 0.6 %collective-permute-start.3 = (f16[4,8,3072]{2,1,0:T(8,128)(2,1)S(1)}, f16[4,8,3072]{2,1,0:T(8,128)(2,1)S(1)}, u32[]{:S(2)}, u32[]{:S(2)}) collective-permute-start(f16[4,8,3072]{2,1,0:T(8,128)(2,1)S(1)} %get-tuple-element.36), channel_id=1, source_target_pairs={{0,2},{1,17},{2,0},{3,19},{4,6},{5,21},{6,4},{7,23},{8,10},{9,25},... | collective-permute-start | bytes 589832 | tf_op jit(solution)/shard_map/ppermute | solution.py:25
  9.4 0.8 %collective-permute-start.4 = (f16[4,8,3072]{2,1,0:T(8,128)(2,1)S(1)}, f16[4,8,3072]{2,1,0:T(8,128)(2,1)S(1)}, u32[]{:S(2)}, u32[]{:S(2)}) collective-permute-start(f16[4,8,3072]{2,1,0:T(8,128)(2,1)S(1)} %get-tuple-element.37), channel_id=1, source_target_pairs={{0,4},{1,9},{2,6},{3,11},{4,0},{5,13},{6,2},{7,15},{8,12},{9,1},{1... | collective-permute-start | bytes 589832 | tf_op jit(solution)/shard_map/ppermute | solution.py:25
  10.2 1.4 %collective-permute-done.2 = f16[4,8,3072]{2,1,0:T(8,128)(2,1)S(1)} collective-permute-done((f16[4,8,3072]{2,1,0:T(8,128)(2,1)S(1)}, f16[4,8,3072]{2,1,0:T(8,128)(2,1)S(1)}, u32[]{:S(2)}, u32[]{:S(2)}) %collective-permute-start.2) | collective-permute-done | bytes 196640 | tf_op jit(solution)/shard_map/ppermute | solution.py:25
  11.6 0.1 bitcast_add_fusion
  11.7 2.8 %collective-permute-done.3 = f16[4,8,3072]{2,1,0:T(8,128)(2,1)S(1)} collective-permute-done((f16[4,8,3072]{2,1,0:T(8,128)(2,1)S(1)}, f16[4,8,3072]{2,1,0:T(8,128)(2,1)S(1)}, u32[]{:S(2)}, u32[]{:S(2)}) %collective-permute-start.3) | collective-permute-done | bytes 196640 | tf_op jit(solution)/shard_map/ppermute | solution.py:25
  14.6 0.5 %collective-permute-done.4 = f16[4,8,3072]{2,1,0:T(8,128)(2,1)S(1)} collective-permute-done((f16[4,8,3072]{2,1,0:T(8,128)(2,1)S(1)}, f16[4,8,3072]{2,1,0:T(8,128)(2,1)S(1)}, u32[]{:S(2)}, u32[]{:S(2)}) %collective-permute-start.4) | collective-permute-done | bytes 196640 | tf_op jit(solution)/shard_map/ppermute | solution.py:25
  15.1 0.1 multiply_add_fusion
  15.2 3.7 %collective-permute-start.5 = (f16[8,3072]{1,0:T(8,128)(2,1)S(1)}, f16[8,3072]{1,0:T(8,128)(2,1)S(1)}, u32[]{:S(2)}, u32[]{:S(2)}) collective-permute-start(f16[8,3072]{1,0:T(8,128)(2,1)S(1)} %get-tuple-element.38), channel_id=1, source_target_pairs={{0,24},{1,7},{2,26},{3,5},{4,28},{5,3},{6,30},{7,1},{8,16},{9,15},... | collective-permute-start | bytes 147464 | tf_op jit(solution)/shard_map/ppermute | solution.py:25
  18.9 0.8 %collective-permute-start.7 = (f16[8,3072]{1,0:T(8,128)(2,1)S(1)}, f16[8,3072]{1,0:T(8,128)(2,1)S(1)}, u32[]{:S(2)}, u32[]{:S(2)}) collective-permute-start(f16[8,3072]{1,0:T(8,128)(2,1)S(1)} %get-tuple-element.39), channel_id=1, source_target_pairs={{0,8},{1,5},{2,10},{3,7},{4,12},{5,1},{6,14},{7,3},{8,0},{9,13},{1... | collective-permute-start | bytes 147464 | tf_op jit(solution)/shard_map/ppermute | solution.py:25
  19.7 1.5 %collective-permute-done.5 = f16[8,3072]{1,0:T(8,128)(2,1)S(1)} collective-permute-done((f16[8,3072]{1,0:T(8,128)(2,1)S(1)}, f16[8,3072]{1,0:T(8,128)(2,1)S(1)}, u32[]{:S(2)}, u32[]{:S(2)}) %collective-permute-start.5) | collective-permute-done | bytes 49184 | tf_op jit(solution)/shard_map/ppermute | solution.py:25
  21.2 2.7 %collective-permute-done.6 = f16[8,3072]{1,0:T(8,128)(2,1)S(1)} collective-permute-done((f16[8,3072]{1,0:T(8,128)(2,1)S(1)}, f16[8,3072]{1,0:T(8,128)(2,1)S(1)}, u32[]{:S(2)}, u32[]{:S(2)}) %collective-permute-start.6) | collective-permute-done | bytes 49184 | tf_op jit(solution)/shard_map/ppermute | solution.py:25
  24.0 0.2 subtract_convert_fusion.1
  24.2 2.1 %collective-permute-start.9 = (bf16[4,6144]{1,0:T(4,128)(2,1)S(1)}, bf16[4,6144]{1,0:T(4,128)(2,1)S(1)}, u32[]{:S(2)}, u32[]{:S(2)}) collective-permute-start(bf16[4,6144]{1,0:T(4,128)(2,1)S(1)} %get-tuple-element.30), channel_id=1, source_target_pairs={{0,16},{1,17},{2,18},{3,19},{4,20},{5,21},{6,22},{7,23},{8,24},{9,... | collective-permute-start | bytes 147464 | tf_op jit(solution)/shard_map/ppermute | solution.py:25
  26.3 0.1 broadcast_in_dim.3
  26.4 0.2 constant_dynamic-update-slice_fusion.3
  26.6 0.3 collective-permute-start.8
  26.9 3.0 %collective-permute-start.10 = (bf16[4,6144]{1,0:T(4,128)(2,1)S(1)}, bf16[4,6144]{1,0:T(4,128)(2,1)S(1)}, u32[]{:S(2)}, u32[]{:S(2)}) collective-permute-start(bf16[4,6144]{1,0:T(4,128)(2,1)S(1)} %get-tuple-element.32), channel_id=1, source_target_pairs={{0,28},{1,13},{2,30},{3,15},{4,24},{5,9},{6,26},{7,11},{8,20},{9,5... | collective-permute-start | bytes 147464 | tf_op jit(solution)/shard_map/ppermute | solution.py:25
  29.9 0.5 %collective-permute-done.9 = bf16[4,6144]{1,0:T(4,128)(2,1)S(1)} collective-permute-done((bf16[4,6144]{1,0:T(4,128)(2,1)S(1)}, bf16[4,6144]{1,0:T(4,128)(2,1)S(1)}, u32[]{:S(2)}, u32[]{:S(2)}) %collective-permute-start.9) | collective-permute-done | bytes 49184 | tf_op jit(solution)/shard_map/ppermute | solution.py:25
  30.5 0.8 %collective-permute-start.12 = (bf16[2,4,6144]{2,1,0:T(4,128)(2,1)S(1)}, bf16[2,4,6144]{2,1,0:T(4,128)(2,1)S(1)}, u32[]{:S(2)}, u32[]{:S(2)}) collective-permute-start(bf16[2,4,6144]{2,1,0:T(4,128)(2,1)S(1)} %pad_maximum_fusion.1), channel_id=1, source_target_pairs={{0,4},{1,9},{2,6},{3,11},{4,0},{5,13},{6,2},{7,15},{8,12},{9,1},{1... | collective-permute-start | bytes 294920 | tf_op jit(solution)/shard_map/ppermute | solution.py:25
  31.4 0.3 collective-permute-done.8
  31.7 0.8 %multiply_subtract_fusion = (f32[4,6144]{1,0:T(4,128)}, f32[4,6144]{1,0:T(4,128)}, f32[4,6144]{1,0:T(4,128)}) fusion(f32[4,6144]{1,0:T(4,128)S(1)} %copy-done, f32[4,6144]{1,0:T(4,128)S(1)} %get-tuple-element.13, f32[4,6144]{1,0:T(4,128)S(1)} %copy-done.2, f32[4,6144]{1,0:T(4,128)S(1)} %copy-done.1), kind=kLoop, calls=%fused_computation.26 | loop fusion | flops 368640 | bytes 688128 | tf_op jit(solution)/shard_map/sub | solution.py:223
  32.6 1.2 %collective-permute-done.10 = bf16[4,6144]{1,0:T(4,128)(2,1)S(1)} collective-permute-done((bf16[4,6144]{1,0:T(4,128)(2,1)S(1)}, bf16[4,6144]{1,0:T(4,128)(2,1)S(1)}, u32[]{:S(2)}, u32[]{:S(2)}) %collective-permute-start.10) | collective-permute-done | bytes 49184 | tf_op jit(solution)/shard_map/ppermute | solution.py:25
  33.8 1.3 %collective-permute-done.11 = bf16[2,4,6144]{2,1,0:T(4,128)(2,1)S(1)} collective-permute-done((bf16[2,4,6144]{2,1,0:T(4,128)(2,1)S(1)}, bf16[2,4,6144]{2,1,0:T(4,128)(2,1)S(1)}, u32[]{:S(2)}, u32[]{:S(2)}) %collective-permute-start.11) | collective-permute-done | bytes 98336 | tf_op jit(solution)/shard_map/ppermute | solution.py:25
  35.3 0.7 %copy-done.4 = bf16[4,49152]{1,0:T(4,128)(2,1)} copy-done((bf16[4,49152]{1,0:T(4,128)(2,1)}, bf16[4,49152]{1,0:T(4,128)(2,1)S(1)}, u32[]{:S(2)}) %copy-start.4) | copy-done | bytes 393240
  (26 shorter events, 0.5 us)
Async XLA Ops:
  2.0 1.9 %collective-permute-start = (bf16[4,8,3072]{2,1,0:T(8,128)(2,1)S(1)}, bf16[4,8,3072]{2,1,0:T(8,128)(2,1)S(1)}, u32[]{:S(2)}, u32[]{:S(2)}) collective-permute-start(bf16[4,8,3072]{2,1,0:T(8,128)(2,1)S(1)} %get-tuple-element.23), channel_id=1, source_target_pairs={{0,1},{1,0},{2,3},{3,2},{4,5},{5,4},{6,7},{7,6},{8,9},{9,8},{10,11... | collective-permute-start | bytes 589832 | tf_op jit(solution)/shard_map/ppermute | solution.py:25
  3.8 4.8 %collective-permute-start.1 = (bf16[3,4,8,3072]{3,2,1,0:T(8,128)(2,1)S(1)}, bf16[3,4,8,3072]{3,2,1,0:T(8,128)(2,1)S(1)}, u32[]{:S(2)}, u32[]{:S(2)}) collective-permute-start(bf16[3,4,8,3072]{3,2,1,0:T(8,128)(2,1)S(1)} %get-tuple-element.26), channel_id=1, source_target_pairs={{0,1},{1,0},{2,3},{3,2},{4,5},{5,4},{6,7},{7,6},{8,9},{9,8},{10,11... | collective-permute-start | bytes 1769480 | tf_op jit(solution)/shard_map/ppermute | solution.py:25
  4.0 7.6 %collective-permute-start.2 = (f16[4,8,3072]{2,1,0:T(8,128)(2,1)S(1)}, f16[4,8,3072]{2,1,0:T(8,128)(2,1)S(1)}, u32[]{:S(2)}, u32[]{:S(2)}) collective-permute-start(f16[4,8,3072]{2,1,0:T(8,128)(2,1)S(1)} %multiply_convert_fusion.2), channel_id=1, source_target_pairs={{0,6},{1,25},{2,4},{3,27},{4,2},{5,29},{6,0},{7,31},{8,14},{9,17},... | collective-permute-start | bytes 589832 | tf_op jit(solution)/shard_map/ppermute | solution.py:25
  8.8 5.7 %collective-permute-start.3 = (f16[4,8,3072]{2,1,0:T(8,128)(2,1)S(1)}, f16[4,8,3072]{2,1,0:T(8,128)(2,1)S(1)}, u32[]{:S(2)}, u32[]{:S(2)}) collective-permute-start(f16[4,8,3072]{2,1,0:T(8,128)(2,1)S(1)} %get-tuple-element.36), channel_id=1, source_target_pairs={{0,2},{1,17},{2,0},{3,19},{4,6},{5,21},{6,4},{7,23},{8,10},{9,25},... | collective-permute-start | bytes 589832 | tf_op jit(solution)/shard_map/ppermute | solution.py:25
  9.4 14.5 %copy-start = (f32[4,6144]{1,0:T(4,128)S(1)}, f32[4,6144]{1,0:T(4,128)}, u32[]{:S(2)}) copy-start(f32[4,6144]{1,0:T(4,128)} %param.5) | copy-start | bytes 294916
  9.4 14.6 %copy-start.1 = (f32[4,6144]{1,0:T(4,128)S(1)}, f32[4,6144]{1,0:T(4,128)}, u32[]{:S(2)}) copy-start(f32[4,6144]{1,0:T(4,128)} %param.7) | copy-start | bytes 294916
  9.4 14.6 %copy-start.2 = (f32[4,6144]{1,0:T(4,128)S(1)}, f32[4,6144]{1,0:T(4,128)}, u32[]{:S(2)}) copy-start(f32[4,6144]{1,0:T(4,128)} %param.6) | copy-start | bytes 294916
  9.4 5.7 %collective-permute-start.4 = (f16[4,8,3072]{2,1,0:T(8,128)(2,1)S(1)}, f16[4,8,3072]{2,1,0:T(8,128)(2,1)S(1)}, u32[]{:S(2)}, u32[]{:S(2)}) collective-permute-start(f16[4,8,3072]{2,1,0:T(8,128)(2,1)S(1)} %get-tuple-element.37), channel_id=1, source_target_pairs={{0,4},{1,9},{2,6},{3,11},{4,0},{5,13},{6,2},{7,15},{8,12},{9,1},{1... | collective-permute-start | bytes 589832 | tf_op jit(solution)/shard_map/ppermute | solution.py:25
  15.2 6.0 %collective-permute-start.5 = (f16[8,3072]{1,0:T(8,128)(2,1)S(1)}, f16[8,3072]{1,0:T(8,128)(2,1)S(1)}, u32[]{:S(2)}, u32[]{:S(2)}) collective-permute-start(f16[8,3072]{1,0:T(8,128)(2,1)S(1)} %get-tuple-element.38), channel_id=1, source_target_pairs={{0,24},{1,7},{2,26},{3,5},{4,28},{5,3},{6,30},{7,1},{8,16},{9,15},... | collective-permute-start | bytes 147464 | tf_op jit(solution)/shard_map/ppermute | solution.py:25
  18.9 5.0 %collective-permute-start.6 = (f16[8,3072]{1,0:T(8,128)(2,1)S(1)}, f16[8,3072]{1,0:T(8,128)(2,1)S(1)}, u32[]{:S(2)}, u32[]{:S(2)}) collective-permute-start(f16[8,3072]{1,0:T(8,128)(2,1)S(1)} %get-tuple-element.40), channel_id=1, source_target_pairs={{0,16},{1,3},{2,18},{3,1},{4,20},{5,7},{6,22},{7,5},{8,24},{9,11},... | collective-permute-start | bytes 147464 | tf_op jit(solution)/shard_map/ppermute | solution.py:25
  18.9 5.0 %collective-permute-start.7 = (f16[8,3072]{1,0:T(8,128)(2,1)S(1)}, f16[8,3072]{1,0:T(8,128)(2,1)S(1)}, u32[]{:S(2)}, u32[]{:S(2)}) collective-permute-start(f16[8,3072]{1,0:T(8,128)(2,1)S(1)} %get-tuple-element.39), channel_id=1, source_target_pairs={{0,8},{1,5},{2,10},{3,7},{4,12},{5,1},{6,14},{7,3},{8,0},{9,13},{1... | collective-permute-start | bytes 147464 | tf_op jit(solution)/shard_map/ppermute | solution.py:25
  24.2 11.2 %copy-start.3 = (f32[4,6144]{1,0:T(4,128)}, f32[4,6144]{1,0:T(4,128)S(1)}, u32[]{:S(2)}) copy-start(f32[4,6144]{1,0:T(4,128)S(1)} %get-tuple-element.13) | copy-start | bytes 294916
  24.2 6.2 %collective-permute-start.9 = (bf16[4,6144]{1,0:T(4,128)(2,1)S(1)}, bf16[4,6144]{1,0:T(4,128)(2,1)S(1)}, u32[]{:S(2)}, u32[]{:S(2)}) collective-permute-start(bf16[4,6144]{1,0:T(4,128)(2,1)S(1)} %get-tuple-element.30), channel_id=1, source_target_pairs={{0,16},{1,17},{2,18},{3,19},{4,20},{5,21},{6,22},{7,23},{8,24},{9,... | collective-permute-start | bytes 147464 | tf_op jit(solution)/shard_map/ppermute | solution.py:25
  26.6 5.1 %collective-permute-start.8 = (bf16[4,6144]{1,0:T(4,128)(2,1)S(1)}, bf16[4,6144]{1,0:T(4,128)(2,1)S(1)}, u32[]{:S(2)}, u32[]{:S(2)}) collective-permute-start(bf16[4,6144]{1,0:T(4,128)(2,1)S(1)} %get-tuple-element.32), channel_id=1, source_target_pairs={{0,12},{1,29},{2,14},{3,31},{4,8},{5,25},{6,10},{7,27},{8,4},{9,21... | collective-permute-start | bytes 147464 | tf_op jit(solution)/shard_map/ppermute | solution.py:25
  26.9 6.9 %collective-permute-start.10 = (bf16[4,6144]{1,0:T(4,128)(2,1)S(1)}, bf16[4,6144]{1,0:T(4,128)(2,1)S(1)}, u32[]{:S(2)}, u32[]{:S(2)}) collective-permute-start(bf16[4,6144]{1,0:T(4,128)(2,1)S(1)} %get-tuple-element.32), channel_id=1, source_target_pairs={{0,28},{1,13},{2,30},{3,15},{4,24},{5,9},{6,26},{7,11},{8,20},{9,5... | collective-permute-start | bytes 147464 | tf_op jit(solution)/shard_map/ppermute | solution.py:25
  30.5 4.7 %collective-permute-start.11 = (bf16[2,4,6144]{2,1,0:T(4,128)(2,1)S(1)}, bf16[2,4,6144]{2,1,0:T(4,128)(2,1)S(1)}, u32[]{:S(2)}, u32[]{:S(2)}) collective-permute-start(bf16[2,4,6144]{2,1,0:T(4,128)(2,1)S(1)} %pad_maximum_fusion.1), channel_id=1, source_target_pairs={{0,8},{1,5},{2,10},{3,7},{4,12},{5,1},{6,14},{7,3},{8,0},{9,13},{1... | collective-permute-start | bytes 294920 | tf_op jit(solution)/shard_map/ppermute | solution.py:25
  30.5 4.7 %collective-permute-start.12 = (bf16[2,4,6144]{2,1,0:T(4,128)(2,1)S(1)}, bf16[2,4,6144]{2,1,0:T(4,128)(2,1)S(1)}, u32[]{:S(2)}, u32[]{:S(2)}) collective-permute-start(bf16[2,4,6144]{2,1,0:T(4,128)(2,1)S(1)} %pad_maximum_fusion.1), channel_id=1, source_target_pairs={{0,4},{1,9},{2,6},{3,11},{4,0},{5,13},{6,2},{7,15},{8,12},{9,1},{1... | collective-permute-start | bytes 294920 | tf_op jit(solution)/shard_map/ppermute | solution.py:25
  35.3 0.7 %copy-start.4 = (bf16[4,49152]{1,0:T(4,128)(2,1)}, bf16[4,49152]{1,0:T(4,128)(2,1)S(1)}, u32[]{:S(2)}) copy-start(bf16[4,49152]{1,0:T(4,128)(2,1)S(1)} %fusion.18) | copy-start | bytes 1179652

commit v15 on v13

--- a/solution.py
+++ b/solution.py
@@ -150,21 +150,18 @@
     return jnp.concatenate([total[: tile // 2], total[tile // 2 :]], axis=1)
 
 
-def gather_blocks(first, mine):
+def gather_blocks(mine):
     row_block, col_block = mine.shape
     me, core = lax.axis_index("hst"), place()[3]
-    far = swap(first, Z_FAR, Z_FAR)
-    corner, cross = swap(mine, Z_NEAR + Y, Z_FAR + Z_NEAR + Y), swap(mine, Z_FAR + Z_NEAR + Y, Z_NEAR + Y)
-    pair = jnp.stack([mine, far])
-    side, other_side = swap(pair, Z_NEAR, Y), swap(pair, Y, Z_NEAR)
-    bits = lambda at_0, at_1: jnp.where(core == 0, at_0, at_1)
-    got = [(0, mine), (4, far), (bits(3, 7), corner), (bits(7, 3), cross)]
-    got += [(bits(2, 1) + 4 * i, side[i]) for i in (0, 1)]
-    got += [(bits(1, 2) + 4 * i, other_side[i]) for i in (0, 1)]
+    pair = jnp.stack(lax.optimization_barrier([mine, swap(mine, Z_FAR, Z_FAR)]))
+    got = [pair] + [swap(pair, *f) for f in ((Z_NEAR + Y, Z_NEAR + Y), (Z_NEAR, Y), (Y, Z_NEAR))]
+    away = [0, 3, jnp.where(core == 0, 2, 1), jnp.where(core == 0, 1, 2)]
     whole = jnp.zeros((row_block, 8 * col_block), mine.dtype)
-    for away, block in got:
-        whole = lax.dynamic_update_slice_in_dim(whole, block, (me ^ away) * col_block, 1)
-    return whole, corner
+    for bits, blocks in zip(away, got):
+        for i in (0, 1):
+            place_at = (me ^ bits ^ (4 * i)) * col_block
+            whole = lax.dynamic_update_slice_in_dim(whole, blocks[i], place_at, 1)
+    return whole
 
 
 def reduce_general(gradient):
@@ -202,14 +199,12 @@
     tuned = lax.axis_size("local") == 4 and lax.axis_size("hst") == 8
     gradient = grads[0, 0]
     grad_total = reduce_blocks(gradient) if tuned else reduce_general(gradient)
-    first = adam(grad_total, master, moment_one, moment_two)[0].astype(jnp.bfloat16)
-    again, first = lax.optimization_barrier((grad_total, first))
-    mine = adam(again, master, moment_one, moment_two)[0].astype(jnp.bfloat16)
+    mine = adam(grad_total, master, moment_one, moment_two)[0].astype(jnp.bfloat16)
     if tuned:
-        secondary, corner = gather_blocks(first, mine)
+        secondary = gather_blocks(mine)
     else:
-        secondary = corner = lax.all_gather(mine, "hst", axis=1, tiled=True)
-    grad_total, _ = lax.optimization_barrier((again, corner))
+        secondary = lax.all_gather(mine, "hst", axis=1, tiled=True)
+    grad_total, _ = lax.optimization_barrier((grad_total, mine))
     new_master, new_one, new_two = adam(grad_total, master, moment_one, moment_two)
     return (grad_total, new_master, new_one, new_two, secondary)
 

time: 36 us -> 37.5 us (1.042)
  waiting for transfers between devices: 13.2 us -> 15.7 us
  starting transfers between devices: 16.7 us -> 15.9 us
    ppermute x13 -> x12, waiting for transfers between devices: 13.2 us -> 15.7 us  [swap(): return lax.ppermute(value, ('hst', 'local'), flip_pairs(flips))]
    ppermute x13 -> x12, starting transfers between devices: 16.7 us -> 15.9 us  [swap(): return lax.ppermute(value, ('hst', 'local'), flip_pairs(flips))]
  transfers between devices with their start and end apart: 13 -> 12, of which waited for: 10 -> 10; matrix products, arithmetic and copies ran while one was open for 5% -> 4% of each run, Pallas kernels for 1% -> 1%
where the time goes in v15:
time: 37.5 us; the launch traced here: 37.3 us
  starting transfers between devices  15.9 us (42%)
  waiting for transfers between devices  15.7 us (42%)
  Pallas kernels  2.31 us (6%)
  other arithmetic  1.56 us (4%)
  local copies, waits for them, and re-layouts  1.13 us (3%)
  between operations  0.77 us (2%)
    ppermute x12, starting transfers between devices, swap(): return lax.ppermute(value, ('hst', 'local'), flip_pairs(flips))  15.9 us
    ppermute x12, waiting for transfers between devices, swap(): return lax.ppermute(value, ('hst', 'local'), flip_pairs(flips))  15.7 us
    pallas_call x2, Pallas kernels, call(): pl.pallas_call(kernel, in_specs=[pl.BlockSpec(memory_space=space)], out_s...  2.31 us
    sub x1, other arithmetic, adam(): new_master = master - learn_rate * (update + decay_rate * master)  0.84 us
  transfers between devices with their start and end apart: 12, of which 10 were waited for; matrix products, arithmetic and copies ran while one was open for 4% of the time, Pallas kernels for 1%

profile of v15, /device:TPU:0, one launch (start us, length us, event | category | flops | bytes accessed | tf_op | source)
XLA Modules:
  0.0 37.3 jit_solution(1996069476051399913)
XLA Ops:
  0.6 1.8 %shard_map.83 = (bf16[4,8,3072]{2,1,0:T(8,128)(2,1)S(1)}, bf16[3,4,8,3072]{3,2,1,0:T(8,128)(2,1)S(1)}, bf16[16,49152]{1,0:T(8,128)(2,1)S(1)}) custom-call(bf16[16,49152]{1,0:T(8,128)(2,1)} %bitcast.50), custom_call_target="tpu_custom_call" | custom-call | flops 786432 | bytes 3145728 | tf_op jit(solution)/shard_map/pallas_call | solution.py:103
  2.5 0.5 %collective-permute-start = (bf16[4,8,3072]{2,1,0:T(8,128)(2,1)S(1)}, bf16[4,8,3072]{2,1,0:T(8,128)(2,1)S(1)}, u32[]{:S(2)}, u32[]{:S(2)}) collective-permute-start(bf16[4,8,3072]{2,1,0:T(8,128)(2,1)S(1)} %get-tuple-element.14), channel_id=1, source_target_pairs={{0,1},{1,0},{2,3},{3,2},{4,5},{5,4},{6,7},{7,6},{8,9},{9,8},{10,11... | collective-permute-start | bytes 589832 | tf_op jit(solution)/shard_map/ppermute | solution.py:25
  3.0 0.1 collective-permute-start.1
  3.1 0.5 %shard_map.84 = bf16[4,4,8,3072]{3,2,1,0:T(8,128)(2,1)S(1)} custom-call(bf16[16,49152]{1,0:T(8,128)(2,1)S(1)} %get-tuple-element.13.landed), custom_call_target="tpu_custom_call" | custom-call | flops 786432 | bytes 3145728 | tf_op jit(solution)/shard_map/pallas_call | solution.py:103
  3.5 0.5 %collective-permute-done = bf16[4,8,3072]{2,1,0:T(8,128)(2,1)S(1)} collective-permute-done((bf16[4,8,3072]{2,1,0:T(8,128)(2,1)S(1)}, bf16[4,8,3072]{2,1,0:T(8,128)(2,1)S(1)}, u32[]{:S(2)}, u32[]{:S(2)}) %collective-permute-start) | collective-permute-done | bytes 196640 | tf_op jit(solution)/shard_map/ppermute | solution.py:25
  4.0 0.1 fusion.1
  4.1 3.9 %collective-permute-start.2 = (f16[4,8,3072]{2,1,0:T(8,128)(2,1)S(1)}, f16[4,8,3072]{2,1,0:T(8,128)(2,1)S(1)}, u32[]{:S(2)}, u32[]{:S(2)}) collective-permute-start(f16[4,8,3072]{2,1,0:T(8,128)(2,1)S(1)} %fusion.1), channel_id=1, source_target_pairs={{0,6},{1,25},{2,4},{3,27},{4,2},{5,29},{6,0},{7,31},{8,14},{9,17},... | collective-permute-start | bytes 589832 | tf_op jit(solution)/shard_map/ppermute | solution.py:25
  8.0 0.1 fusion.2
  8.2 0.6 %collective-permute-start.4 = (f16[4,8,3072]{2,1,0:T(8,128)(2,1)S(1)}, f16[4,8,3072]{2,1,0:T(8,128)(2,1)S(1)}, u32[]{:S(2)}, u32[]{:S(2)}) collective-permute-start(f16[4,8,3072]{2,1,0:T(8,128)(2,1)S(1)} %get-tuple-element.25), channel_id=1, source_target_pairs={{0,2},{1,17},{2,0},{3,19},{4,6},{5,21},{6,4},{7,23},{8,10},{9,25},... | collective-permute-start | bytes 589832 | tf_op jit(solution)/shard_map/ppermute | solution.py:25
  8.8 0.7 %collective-permute-start.3 = (f16[4,8,3072]{2,1,0:T(8,128)(2,1)S(1)}, f16[4,8,3072]{2,1,0:T(8,128)(2,1)S(1)}, u32[]{:S(2)}, u32[]{:S(2)}) collective-permute-start(f16[4,8,3072]{2,1,0:T(8,128)(2,1)S(1)} %get-tuple-element.24), channel_id=1, source_target_pairs={{0,4},{1,9},{2,6},{3,11},{4,0},{5,13},{6,2},{7,15},{8,12},{9,1},{1... | collective-permute-start | bytes 589832 | tf_op jit(solution)/shard_map/ppermute | solution.py:25
  9.5 2.2 %collective-permute-done.2 = f16[4,8,3072]{2,1,0:T(8,128)(2,1)S(1)} collective-permute-done((f16[4,8,3072]{2,1,0:T(8,128)(2,1)S(1)}, f16[4,8,3072]{2,1,0:T(8,128)(2,1)S(1)}, u32[]{:S(2)}, u32[]{:S(2)}) %collective-permute-start.2) | collective-permute-done | bytes 196640 | tf_op jit(solution)/shard_map/ppermute | solution.py:25
  11.7 0.1 bitcast_add_fusion
  11.7 2.6 %collective-permute-done.4 = f16[4,8,3072]{2,1,0:T(8,128)(2,1)S(1)} collective-permute-done((f16[4,8,3072]{2,1,0:T(8,128)(2,1)S(1)}, f16[4,8,3072]{2,1,0:T(8,128)(2,1)S(1)}, u32[]{:S(2)}, u32[]{:S(2)}) %collective-permute-start.4) | collective-permute-done | bytes 196640 | tf_op jit(solution)/shard_map/ppermute | solution.py:25
  14.3 0.1 collective-permute-done.3
  14.4 0.1 multiply_add_fusion
  14.6 3.7 %collective-permute-start.7 = (f16[8,3072]{1,0:T(8,128)(2,1)S(1)}, f16[8,3072]{1,0:T(8,128)(2,1)S(1)}, u32[]{:S(2)}, u32[]{:S(2)}) collective-permute-start(f16[8,3072]{1,0:T(8,128)(2,1)S(1)} %get-tuple-element.27), channel_id=1, source_target_pairs={{0,24},{1,7},{2,26},{3,5},{4,28},{5,3},{6,30},{7,1},{8,16},{9,15},... | collective-permute-start | bytes 147464 | tf_op jit(solution)/shard_map/ppermute | solution.py:25
  18.2 0.8 %collective-permute-start.5 = (f16[8,3072]{1,0:T(8,128)(2,1)S(1)}, f16[8,3072]{1,0:T(8,128)(2,1)S(1)}, u32[]{:S(2)}, u32[]{:S(2)}) collective-permute-start(f16[8,3072]{1,0:T(8,128)(2,1)S(1)} %get-tuple-element.26), channel_id=1, source_target_pairs={{0,8},{1,5},{2,10},{3,7},{4,12},{5,1},{6,14},{7,3},{8,0},{9,13},{1... | collective-permute-start | bytes 147464 | tf_op jit(solution)/shard_map/ppermute | solution.py:25
  19.0 1.5 %collective-permute-done.7 = f16[8,3072]{1,0:T(8,128)(2,1)S(1)} collective-permute-done((f16[8,3072]{1,0:T(8,128)(2,1)S(1)}, f16[8,3072]{1,0:T(8,128)(2,1)S(1)}, u32[]{:S(2)}, u32[]{:S(2)}) %collective-permute-start.7) | collective-permute-done | bytes 49184 | tf_op jit(solution)/shard_map/ppermute | solution.py:25
  20.5 2.7 %collective-permute-done.6 = f16[8,3072]{1,0:T(8,128)(2,1)S(1)} collective-permute-done((f16[8,3072]{1,0:T(8,128)(2,1)S(1)}, f16[8,3072]{1,0:T(8,128)(2,1)S(1)}, u32[]{:S(2)}, u32[]{:S(2)}) %collective-permute-start.6) | collective-permute-done | bytes 49184 | tf_op jit(solution)/shard_map/ppermute | solution.py:25
  23.3 0.2 subtract_convert_fusion
  23.5 2.1 %collective-permute-start.8 = (bf16[4,6144]{1,0:T(4,128)(2,1)S(1)}, bf16[4,6144]{1,0:T(4,128)(2,1)S(1)}, u32[]{:S(2)}, u32[]{:S(2)}) collective-permute-start(bf16[4,6144]{1,0:T(4,128)(2,1)S(1)} %get-tuple-element.19), channel_id=1, source_target_pairs={{0,16},{1,17},{2,18},{3,19},{4,20},{5,21},{6,22},{7,23},{8,24},{9,... | collective-permute-start | bytes 147464 | tf_op jit(solution)/shard_map/ppermute | solution.py:25
  25.6 0.8 %multiply_subtract_fusion = (f32[4,6144]{1,0:T(4,128)}, f32[4,6144]{1,0:T(4,128)}, f32[4,6144]{1,0:T(4,128)}) fusion(f32[4,6144]{1,0:T(4,128)S(1)} %copy-done.1, f32[4,6144]{1,0:T(4,128)S(1)} %get-tuple-element.8, f32[4,6144]{1,0:T(4,128)S(1)} %copy-done.3, f32[4,6144]{1,0:T(4,128)S(1)} %copy-done.2), kind=kLoop, calls=%fused_computation.23 | loop fusion | flops 368640 | bytes 688128 | tf_op jit(solution)/shard_map/sub | solution.py:194
  26.5 2.6 %collective-permute-done.8 = bf16[4,6144]{1,0:T(4,128)(2,1)S(1)} collective-permute-done((bf16[4,6144]{1,0:T(4,128)(2,1)S(1)}, bf16[4,6144]{1,0:T(4,128)(2,1)S(1)}, u32[]{:S(2)}, u32[]{:S(2)}) %collective-permute-start.8) | collective-permute-done | bytes 49184 | tf_op jit(solution)/shard_map/ppermute | solution.py:25
  29.1 0.1 pad_maximum_fusion.1
  29.1 0.5 %collective-permute-start.9 = (bf16[2,4,6144]{2,1,0:T(4,128)(2,1)S(1)}, bf16[2,4,6144]{2,1,0:T(4,128)(2,1)S(1)}, u32[]{:S(2)}, u32[]{:S(2)}) collective-permute-start(bf16[2,4,6144]{2,1,0:T(4,128)(2,1)S(1)} %pad_maximum_fusion.1), channel_id=1, source_target_pairs={{0,12},{1,13},{2,14},{3,15},{4,8},{5,9},{6,10},{7,11},{8,4},{9,5},... | collective-permute-start | bytes 294920 | tf_op jit(solution)/shard_map/ppermute | solution.py:25
  29.6 2.0 %collective-permute-start.10 = (bf16[2,4,6144]{2,1,0:T(4,128)(2,1)S(1)}, bf16[2,4,6144]{2,1,0:T(4,128)(2,1)S(1)}, u32[]{:S(2)}, u32[]{:S(2)}) collective-permute-start(bf16[2,4,6144]{2,1,0:T(4,128)(2,1)S(1)} %pad_maximum_fusion.1), channel_id=1, source_target_pairs={{0,8},{1,5},{2,10},{3,7},{4,12},{5,1},{6,14},{7,3},{8,0},{9,13},{1... | collective-permute-start | bytes 294920 | tf_op jit(solution)/shard_map/ppermute | solution.py:25
  31.6 1.1 %collective-permute-start.11 = (bf16[2,4,6144]{2,1,0:T(4,128)(2,1)S(1)}, bf16[2,4,6144]{2,1,0:T(4,128)(2,1)S(1)}, u32[]{:S(2)}, u32[]{:S(2)}) collective-permute-start(bf16[2,4,6144]{2,1,0:T(4,128)(2,1)S(1)} %pad_maximum_fusion.1), channel_id=1, source_target_pairs={{0,4},{1,9},{2,6},{3,11},{4,0},{5,13},{6,2},{7,15},{8,12},{9,1},{1... | collective-permute-start | bytes 294920 | tf_op jit(solution)/shard_map/ppermute | solution.py:25
  32.7 0.1 broadcast_in_dim.3
  32.9 2.9 %collective-permute-done.9 = bf16[2,4,6144]{2,1,0:T(4,128)(2,1)S(1)} collective-permute-done((bf16[2,4,6144]{2,1,0:T(4,128)(2,1)S(1)}, bf16[2,4,6144]{2,1,0:T(4,128)(2,1)S(1)}, u32[]{:S(2)}, u32[]{:S(2)}) %collective-permute-start.9) | collective-permute-done | bytes 98336 | tf_op jit(solution)/shard_map/ppermute | solution.py:25
  35.8 0.3 collective-permute-done.10
  36.2 0.4 collective-permute-done.11
  36.6 0.7 %copy-done = bf16[4,49152]{1,0:T(4,128)(2,1)} copy-done((bf16[4,49152]{1,0:T(4,128)(2,1)}, bf16[4,49152]{1,0:T(4,128)(2,1)S(1)}, u32[]{:S(2)}) %copy-start) | copy-done | bytes 393240
  (23 shorter events, 0.4 us)
Async XLA Ops:
  2.5 1.6 %collective-permute-start = (bf16[4,8,3072]{2,1,0:T(8,128)(2,1)S(1)}, bf16[4,8,3072]{2,1,0:T(8,128)(2,1)S(1)}, u32[]{:S(2)}, u32[]{:S(2)}) collective-permute-start(bf16[4,8,3072]{2,1,0:T(8,128)(2,1)S(1)} %get-tuple-element.14), channel_id=1, source_target_pairs={{0,1},{1,0},{2,3},{3,2},{4,5},{5,4},{6,7},{7,6},{8,9},{9,8},{10,11... | collective-permute-start | bytes 589832 | tf_op jit(solution)/shard_map/ppermute | solution.py:25
  3.0 5.0 %collective-permute-start.1 = (bf16[3,4,8,3072]{3,2,1,0:T(8,128)(2,1)S(1)}, bf16[3,4,8,3072]{3,2,1,0:T(8,128)(2,1)S(1)}, u32[]{:S(2)}, u32[]{:S(2)}) collective-permute-start(bf16[3,4,8,3072]{3,2,1,0:T(8,128)(2,1)S(1)} %get-tuple-element.16), channel_id=1, source_target_pairs={{0,1},{1,0},{2,3},{3,2},{4,5},{5,4},{6,7},{7,6},{8,9},{9,8},{10,11... | collective-permute-start | bytes 1769480 | tf_op jit(solution)/shard_map/ppermute | solution.py:25
  4.1 7.5 %collective-permute-start.2 = (f16[4,8,3072]{2,1,0:T(8,128)(2,1)S(1)}, f16[4,8,3072]{2,1,0:T(8,128)(2,1)S(1)}, u32[]{:S(2)}, u32[]{:S(2)}) collective-permute-start(f16[4,8,3072]{2,1,0:T(8,128)(2,1)S(1)} %fusion.1), channel_id=1, source_target_pairs={{0,6},{1,25},{2,4},{3,27},{4,2},{5,29},{6,0},{7,31},{8,14},{9,17},... | collective-permute-start | bytes 589832 | tf_op jit(solution)/shard_map/ppermute | solution.py:25
  8.2 6.1 %collective-permute-start.4 = (f16[4,8,3072]{2,1,0:T(8,128)(2,1)S(1)}, f16[4,8,3072]{2,1,0:T(8,128)(2,1)S(1)}, u32[]{:S(2)}, u32[]{:S(2)}) collective-permute-start(f16[4,8,3072]{2,1,0:T(8,128)(2,1)S(1)} %get-tuple-element.25), channel_id=1, source_target_pairs={{0,2},{1,17},{2,0},{3,19},{4,6},{5,21},{6,4},{7,23},{8,10},{9,25},... | collective-permute-start | bytes 589832 | tf_op jit(solution)/shard_map/ppermute | solution.py:25
  8.8 14.5 %copy-start.1 = (f32[4,6144]{1,0:T(4,128)S(1)}, f32[4,6144]{1,0:T(4,128)}, u32[]{:S(2)}) copy-start(f32[4,6144]{1,0:T(4,128)} %param.5) | copy-start | bytes 294916
  8.8 14.6 %copy-start.2 = (f32[4,6144]{1,0:T(4,128)S(1)}, f32[4,6144]{1,0:T(4,128)}, u32[]{:S(2)}) copy-start(f32[4,6144]{1,0:T(4,128)} %param.7) | copy-start | bytes 294916
  8.8 14.6 %copy-start.3 = (f32[4,6144]{1,0:T(4,128)S(1)}, f32[4,6144]{1,0:T(4,128)}, u32[]{:S(2)}) copy-start(f32[4,6144]{1,0:T(4,128)} %param.6) | copy-start | bytes 294916
  8.8 5.7 %collective-permute-start.3 = (f16[4,8,3072]{2,1,0:T(8,128)(2,1)S(1)}, f16[4,8,3072]{2,1,0:T(8,128)(2,1)S(1)}, u32[]{:S(2)}, u32[]{:S(2)}) collective-permute-start(f16[4,8,3072]{2,1,0:T(8,128)(2,1)S(1)} %get-tuple-element.24), channel_id=1, source_target_pairs={{0,4},{1,9},{2,6},{3,11},{4,0},{5,13},{6,2},{7,15},{8,12},{9,1},{1... | collective-permute-start | bytes 589832 | tf_op jit(solution)/shard_map/ppermute | solution.py:25
  14.6 6.0 %collective-permute-start.7 = (f16[8,3072]{1,0:T(8,128)(2,1)S(1)}, f16[8,3072]{1,0:T(8,128)(2,1)S(1)}, u32[]{:S(2)}, u32[]{:S(2)}) collective-permute-start(f16[8,3072]{1,0:T(8,128)(2,1)S(1)} %get-tuple-element.27), channel_id=1, source_target_pairs={{0,24},{1,7},{2,26},{3,5},{4,28},{5,3},{6,30},{7,1},{8,16},{9,15},... | collective-permute-start | bytes 147464 | tf_op jit(solution)/shard_map/ppermute | solution.py:25
  18.2 5.0 %collective-permute-start.6 = (f16[8,3072]{1,0:T(8,128)(2,1)S(1)}, f16[8,3072]{1,0:T(8,128)(2,1)S(1)}, u32[]{:S(2)}, u32[]{:S(2)}) collective-permute-start(f16[8,3072]{1,0:T(8,128)(2,1)S(1)} %get-tuple-element.28), channel_id=1, source_target_pairs={{0,16},{1,3},{2,18},{3,1},{4,20},{5,7},{6,22},{7,5},{8,24},{9,11},... | collective-permute-start | bytes 147464 | tf_op jit(solution)/shard_map/ppermute | solution.py:25
  18.2 5.0 %collective-permute-start.5 = (f16[8,3072]{1,0:T(8,128)(2,1)S(1)}, f16[8,3072]{1,0:T(8,128)(2,1)S(1)}, u32[]{:S(2)}, u32[]{:S(2)}) collective-permute-start(f16[8,3072]{1,0:T(8,128)(2,1)S(1)} %get-tuple-element.26), channel_id=1, source_target_pairs={{0,8},{1,5},{2,10},{3,7},{4,12},{5,1},{6,14},{7,3},{8,0},{9,13},{1... | collective-permute-start | bytes 147464 | tf_op jit(solution)/shard_map/ppermute | solution.py:25
  23.5 13.1 %copy-start.4 = (f32[4,6144]{1,0:T(4,128)}, f32[4,6144]{1,0:T(4,128)S(1)}, u32[]{:S(2)}) copy-start(f32[4,6144]{1,0:T(4,128)S(1)} %get-tuple-element.8) | copy-start | bytes 294916
  23.5 5.5 %collective-permute-start.8 = (bf16[4,6144]{1,0:T(4,128)(2,1)S(1)}, bf16[4,6144]{1,0:T(4,128)(2,1)S(1)}, u32[]{:S(2)}, u32[]{:S(2)}) collective-permute-start(bf16[4,6144]{1,0:T(4,128)(2,1)S(1)} %get-tuple-element.19), channel_id=1, source_target_pairs={{0,16},{1,17},{2,18},{3,19},{4,20},{5,21},{6,22},{7,23},{8,24},{9,... | collective-permute-start | bytes 147464 | tf_op jit(solution)/shard_map/ppermute | solution.py:25
  29.1 6.6 %collective-permute-start.9 = (bf16[2,4,6144]{2,1,0:T(4,128)(2,1)S(1)}, bf16[2,4,6144]{2,1,0:T(4,128)(2,1)S(1)}, u32[]{:S(2)}, u32[]{:S(2)}) collective-permute-start(bf16[2,4,6144]{2,1,0:T(4,128)(2,1)S(1)} %pad_maximum_fusion.1), channel_id=1, source_target_pairs={{0,12},{1,13},{2,14},{3,15},{4,8},{5,9},{6,10},{7,11},{8,4},{9,5},... | collective-permute-start | bytes 294920 | tf_op jit(solution)/shard_map/ppermute | solution.py:25
  29.6 6.5 %collective-permute-start.10 = (bf16[2,4,6144]{2,1,0:T(4,128)(2,1)S(1)}, bf16[2,4,6144]{2,1,0:T(4,128)(2,1)S(1)}, u32[]{:S(2)}, u32[]{:S(2)}) collective-permute-start(bf16[2,4,6144]{2,1,0:T(4,128)(2,1)S(1)} %pad_maximum_fusion.1), channel_id=1, source_target_pairs={{0,8},{1,5},{2,10},{3,7},{4,12},{5,1},{6,14},{7,3},{8,0},{9,13},{1... | collective-permute-start | bytes 294920 | tf_op jit(solution)/shard_map/ppermute | solution.py:25
  31.6 4.9 %collective-permute-start.11 = (bf16[2,4,6144]{2,1,0:T(4,128)(2,1)S(1)}, bf16[2,4,6144]{2,1,0:T(4,128)(2,1)S(1)}, u32[]{:S(2)}, u32[]{:S(2)}) collective-permute-start(bf16[2,4,6144]{2,1,0:T(4,128)(2,1)S(1)} %pad_maximum_fusion.1), channel_id=1, source_target_pairs={{0,4},{1,9},{2,6},{3,11},{4,0},{5,13},{6,2},{7,15},{8,12},{9,1},{1... | collective-permute-start | bytes 294920 | tf_op jit(solution)/shard_map/ppermute | solution.py:25
  36.6 0.7 %copy-start = (bf16[4,49152]{1,0:T(4,128)(2,1)}, bf16[4,49152]{1,0:T(4,128)(2,1)S(1)}, u32[]{:S(2)}) copy-start(bf16[4,49152]{1,0:T(4,128)(2,1)S(1)} %fusion.15) | copy-start | bytes 1179652

commit v16 on v13

--- a/solution.py
+++ b/solution.py
@@ -64,7 +64,7 @@
 def theirs_kernel(whole, first, others, landed, arrived):
     half = first.shape[2]
     core = place()[3]
-    parts = [pl.ds(i * half, half) for i in range(16)]
+    parts = [pl.ds(2 * i * half, 2 * half) for i in range(8)]
     copies = [
         pltpu.make_async_copy(whole.at[:, part], landed.at[:, part], arrived.at[i])
         for i, part in enumerate(parts)
@@ -82,9 +82,8 @@
             others[step, member] = rows
 
     for i in range(8):
-        copies[2 * i].wait()
-        copies[2 * i + 1].wait()
-        rows_of(1 - core, landed[:, pl.ds(2 * i * half, 2 * half)], i, store)
+        copies[i].wait()
+        rows_of(1 - core, landed[:, parts[i]], i, store)
 
 
 def own_kernel(landed, own):
@@ -119,7 +118,7 @@
         gradient,
         pltpu.HBM,
         [shape, (3, *shape), gradient.shape],
-        [pltpu.SemaphoreType.DMA((16,))],
+        [pltpu.SemaphoreType.DMA((8,))],
     )
     first, others, landed = lax.optimization_barrier((first, others, landed))
     (own,) = call(own_kernel, landed, pltpu.VMEM, [(4, *shape)])
@@ -150,20 +149,37 @@
     return jnp.concatenate([total[: tile // 2], total[tile // 2 :]], axis=1)
 
 
+def join_kernel(mine, far, corner, cross, side, other_side, whole, left):
+    cols = mine.shape[1]
+    me, core = lax.axis_index("hst"), place()[3]
+    bits = lambda at_0, at_1: jnp.where(core == 0, at_0, at_1)
+    pieces = [(0, mine), (4, far), (bits(3, 7), corner), (bits(7, 3), cross)]
+    pieces += [(bits(2, 1) + 4 * i, side.at[i]) for i in (0, 1)]
+    pieces += [(bits(1, 2) + 4 * i, other_side.at[i]) for i in (0, 1)]
+    copies = []
+    for i, (away, block) in enumerate(pieces):
+        at = pl.multiple_of((me ^ away) * cols, 128)
+        copies.append(pltpu.make_async_copy(block, whole.at[:, pl.ds(at, cols)], left.at[i]))
+        copies[-1].start()
+    for copy in copies:
+        copy.wait()
+
+
 def gather_blocks(first, mine):
     row_block, col_block = mine.shape
-    me, core = lax.axis_index("hst"), place()[3]
     far = swap(first, Z_FAR, Z_FAR)
     corner, cross = swap(mine, Z_NEAR + Y, Z_FAR + Z_NEAR + Y), swap(mine, Z_FAR + Z_NEAR + Y, Z_NEAR + Y)
     pair = jnp.stack([mine, far])
     side, other_side = swap(pair, Z_NEAR, Y), swap(pair, Y, Z_NEAR)
-    bits = lambda at_0, at_1: jnp.where(core == 0, at_0, at_1)
-    got = [(0, mine), (4, far), (bits(3, 7), corner), (bits(7, 3), cross)]
-    got += [(bits(2, 1) + 4 * i, side[i]) for i in (0, 1)]
-    got += [(bits(1, 2) + 4 * i, other_side[i]) for i in (0, 1)]
-    whole = jnp.zeros((row_block, 8 * col_block), mine.dtype)
-    for away, block in got:
-        whole = lax.dynamic_update_slice_in_dim(whole, block, (me ^ away) * col_block, 1)
+    whole = pl.pallas_call(
+        join_kernel,
+        in_specs=[pl.BlockSpec(memory_space=pl.ANY)] * 6,
+        out_specs=pl.BlockSpec(memory_space=pl.ANY),
+        out_shape=jax.ShapeDtypeStruct((row_block, 8 * col_block), mine.dtype),
+        scratch_shapes=[pltpu.SemaphoreType.DMA((8,))],
+        compiler_params=pltpu.CompilerParams(vmem_limit_bytes=8 << 20),
+        cost_estimate=pl.CostEstimate(flops=0, bytes_accessed=4 * 8 * mine.size, transcendentals=0),
+    )(mine, far, corner, cross, side, other_side)
     return whole, corner
 
 

time: 36 us -> 35.8 us (level)
  local copies, waits for them, and re-layouts: 1.1 us -> 0.04 us
  Pallas kernels: 2.31 us -> 3.03 us
    pallas_call x0 -> x1, Pallas kernels: none -> 0.8 us  [gather_blocks(): pl.pallas_call(join_kernel, in_specs=[pl.BlockSpec(memory_space=pl.ANY)]...]
    unnamed x10 -> x8, local copies, waits for them, and re-layouts: 0.75 us -> 0.02 us
  transfers between devices with their start and end apart: 13 -> 13, of which waited for: 10 -> 10; matrix products, arithmetic and copies ran while one was open for 5% -> 4% of each run, Pallas kernels for 1% -> 1%
where the time goes in v16:
time: 35.8 us; the launch traced here: 35.6 us
  starting transfers between devices  16.8 us (47%)
  waiting for transfers between devices  13.3 us (37%)
  Pallas kernels  3.03 us (8%)
  other arithmetic  1.73 us (5%)
  between operations  0.75 us (2%)
    ppermute x13, starting transfers between devices, swap(): return lax.ppermute(value, ('hst', 'local'), flip_pairs(flips))  16.8 us
    ppermute x13, waiting for transfers between devices, swap(): return lax.ppermute(value, ('hst', 'local'), flip_pairs(flips))  13.3 us
    pallas_call x2, Pallas kernels, call(): pl.pallas_call(kernel, in_specs=[pl.BlockSpec(memory_space=space)], out_s...  2.23 us
    sub x1, other arithmetic, adam(): new_master = master - learn_rate * (update + decay_rate * master)  0.84 us
    pallas_call x1, Pallas kernels, gather_blocks(): pl.pallas_call(join_kernel, in_specs=[pl.BlockSpec(memory_space=pl.ANY)]...  0.8 us
  transfers between devices with their start and end apart: 13, of which 10 were waited for; matrix products, arithmetic and copies ran while one was open for 4% of the time, Pallas kernels for 1%

profile of v16, /device:TPU:0, one launch (start us, length us, event | category | flops | bytes accessed | tf_op | source)
XLA Modules:
  0.0 35.6 jit_solution(10850318800913082465)
XLA Ops:
  0.6 1.7 %shard_map.83 = (bf16[4,8,3072]{2,1,0:T(8,128)(2,1)S(1)}, bf16[3,4,8,3072]{3,2,1,0:T(8,128)(2,1)S(1)}, bf16[16,49152]{1,0:T(8,128)(2,1)S(1)}) custom-call(bf16[16,49152]{1,0:T(8,128)(2,1)} %bitcast.28), custom_call_target="tpu_custom_call" | custom-call | flops 786432 | bytes 3145728 | tf_op jit(solution)/shard_map/pallas_call | solution.py:102
  2.4 0.5 %collective-permute-start = (bf16[4,8,3072]{2,1,0:T(8,128)(2,1)S(1)}, bf16[4,8,3072]{2,1,0:T(8,128)(2,1)S(1)}, u32[]{:S(2)}, u32[]{:S(2)}) collective-permute-start(bf16[4,8,3072]{2,1,0:T(8,128)(2,1)S(1)} %get-tuple-element.14), channel_id=1, source_target_pairs={{0,1},{1,0},{2,3},{3,2},{4,5},{5,4},{6,7},{7,6},{8,9},{9,8},{10,11... | collective-permute-start | bytes 589832 | tf_op jit(solution)/shard_map/ppermute | solution.py:25
  2.9 0.1 collective-permute-start.1
  3.0 0.5 %shard_map.84 = bf16[4,4,8,3072]{3,2,1,0:T(8,128)(2,1)S(1)} custom-call(bf16[16,49152]{1,0:T(8,128)(2,1)S(1)} %get-tuple-element.13.landed), custom_call_target="tpu_custom_call" | custom-call | flops 786432 | bytes 3145728 | tf_op jit(solution)/shard_map/pallas_call | solution.py:102
  3.5 0.5 %collective-permute-done = bf16[4,8,3072]{2,1,0:T(8,128)(2,1)S(1)} collective-permute-done((bf16[4,8,3072]{2,1,0:T(8,128)(2,1)S(1)}, bf16[4,8,3072]{2,1,0:T(8,128)(2,1)S(1)}, u32[]{:S(2)}, u32[]{:S(2)}) %collective-permute-start) | collective-permute-done | bytes 196640 | tf_op jit(solution)/shard_map/ppermute | solution.py:25
  4.0 0.1 fusion.1
  4.0 3.9 %collective-permute-start.2 = (f16[4,8,3072]{2,1,0:T(8,128)(2,1)S(1)}, f16[4,8,3072]{2,1,0:T(8,128)(2,1)S(1)}, u32[]{:S(2)}, u32[]{:S(2)}) collective-permute-start(f16[4,8,3072]{2,1,0:T(8,128)(2,1)S(1)} %fusion.1), channel_id=1, source_target_pairs={{0,6},{1,25},{2,4},{3,27},{4,2},{5,29},{6,0},{7,31},{8,14},{9,17},... | collective-permute-start | bytes 589832 | tf_op jit(solution)/shard_map/ppermute | solution.py:25
  7.9 0.1 fusion.2
  8.1 0.6 %collective-permute-start.4 = (f16[4,8,3072]{2,1,0:T(8,128)(2,1)S(1)}, f16[4,8,3072]{2,1,0:T(8,128)(2,1)S(1)}, u32[]{:S(2)}, u32[]{:S(2)}) collective-permute-start(f16[4,8,3072]{2,1,0:T(8,128)(2,1)S(1)} %get-tuple-element.25), channel_id=1, source_target_pairs={{0,2},{1,17},{2,0},{3,19},{4,6},{5,21},{6,4},{7,23},{8,10},{9,25},... | collective-permute-start | bytes 589832 | tf_op jit(solution)/shard_map/ppermute | solution.py:25
  8.7 0.7 %collective-permute-start.3 = (f16[4,8,3072]{2,1,0:T(8,128)(2,1)S(1)}, f16[4,8,3072]{2,1,0:T(8,128)(2,1)S(1)}, u32[]{:S(2)}, u32[]{:S(2)}) collective-permute-start(f16[4,8,3072]{2,1,0:T(8,128)(2,1)S(1)} %get-tuple-element.24), channel_id=1, source_target_pairs={{0,4},{1,9},{2,6},{3,11},{4,0},{5,13},{6,2},{7,15},{8,12},{9,1},{1... | collective-permute-start | bytes 589832 | tf_op jit(solution)/shard_map/ppermute | solution.py:25
  9.4 2.2 %collective-permute-done.2 = f16[4,8,3072]{2,1,0:T(8,128)(2,1)S(1)} collective-permute-done((f16[4,8,3072]{2,1,0:T(8,128)(2,1)S(1)}, f16[4,8,3072]{2,1,0:T(8,128)(2,1)S(1)}, u32[]{:S(2)}, u32[]{:S(2)}) %collective-permute-start.2) | collective-permute-done | bytes 196640 | tf_op jit(solution)/shard_map/ppermute | solution.py:25
  11.6 0.1 bitcast_add_fusion
  11.7 2.6 %collective-permute-done.4 = f16[4,8,3072]{2,1,0:T(8,128)(2,1)S(1)} collective-permute-done((f16[4,8,3072]{2,1,0:T(8,128)(2,1)S(1)}, f16[4,8,3072]{2,1,0:T(8,128)(2,1)S(1)}, u32[]{:S(2)}, u32[]{:S(2)}) %collective-permute-start.4) | collective-permute-done | bytes 196640 | tf_op jit(solution)/shard_map/ppermute | solution.py:25
  14.2 0.1 collective-permute-done.3
  14.4 0.1 multiply_add_fusion
  14.5 3.7 %collective-permute-start.7 = (f16[8,3072]{1,0:T(8,128)(2,1)S(1)}, f16[8,3072]{1,0:T(8,128)(2,1)S(1)}, u32[]{:S(2)}, u32[]{:S(2)}) collective-permute-start(f16[8,3072]{1,0:T(8,128)(2,1)S(1)} %get-tuple-element.27), channel_id=1, source_target_pairs={{0,24},{1,7},{2,26},{3,5},{4,28},{5,3},{6,30},{7,1},{8,16},{9,15},... | collective-permute-start | bytes 147464 | tf_op jit(solution)/shard_map/ppermute | solution.py:25
  18.2 0.8 %collective-permute-start.5 = (f16[8,3072]{1,0:T(8,128)(2,1)S(1)}, f16[8,3072]{1,0:T(8,128)(2,1)S(1)}, u32[]{:S(2)}, u32[]{:S(2)}) collective-permute-start(f16[8,3072]{1,0:T(8,128)(2,1)S(1)} %get-tuple-element.26), channel_id=1, source_target_pairs={{0,8},{1,5},{2,10},{3,7},{4,12},{5,1},{6,14},{7,3},{8,0},{9,13},{1... | collective-permute-start | bytes 147464 | tf_op jit(solution)/shard_map/ppermute | solution.py:25
  19.0 1.5 %collective-permute-done.7 = f16[8,3072]{1,0:T(8,128)(2,1)S(1)} collective-permute-done((f16[8,3072]{1,0:T(8,128)(2,1)S(1)}, f16[8,3072]{1,0:T(8,128)(2,1)S(1)}, u32[]{:S(2)}, u32[]{:S(2)}) %collective-permute-start.7) | collective-permute-done | bytes 49184 | tf_op jit(solution)/shard_map/ppermute | solution.py:25
  20.5 2.7 %collective-permute-done.6 = f16[8,3072]{1,0:T(8,128)(2,1)S(1)} collective-permute-done((f16[8,3072]{1,0:T(8,128)(2,1)S(1)}, f16[8,3072]{1,0:T(8,128)(2,1)S(1)}, u32[]{:S(2)}, u32[]{:S(2)}) %collective-permute-start.6) | collective-permute-done | bytes 49184 | tf_op jit(solution)/shard_map/ppermute | solution.py:25
  23.2 0.2 subtract_convert_fusion.1
  23.4 2.1 %collective-permute-start.9 = (bf16[4,6144]{1,0:T(4,128)(2,1)S(1)}, bf16[4,6144]{1,0:T(4,128)(2,1)S(1)}, u32[]{:S(2)}, u32[]{:S(2)}) collective-permute-start(bf16[4,6144]{1,0:T(4,128)(2,1)S(1)} %get-tuple-element.20), channel_id=1, source_target_pairs={{0,16},{1,17},{2,18},{3,19},{4,20},{5,21},{6,22},{7,23},{8,24},{9,... | collective-permute-start | bytes 147464 | tf_op jit(solution)/shard_map/ppermute | solution.py:25
  25.5 0.2 subtract_convert_fusion.mine
  25.7 0.8 %collective-permute-start.8 = (bf16[4,6144]{1,0:T(4,128)(2,1)S(1)}, bf16[4,6144]{1,0:T(4,128)(2,1)S(1)}, u32[]{:S(2)}, u32[]{:S(2)}) collective-permute-start(bf16[4,6144]{1,0:T(4,128)(2,1)S(1)} %subtract_convert_fusion.mine), channel_id=1, source_target_pairs={{0,12},{1,29},{2,14},{3,31},{4,8},{5,25},{6,10},{7,27},{8,4},{9,21... | collective-permute-start | bytes 147464 | tf_op jit(solution)/shard_map/ppermute | solution.py:25
  26.5 2.5 %collective-permute-start.10 = (bf16[4,6144]{1,0:T(4,128)(2,1)S(1)}, bf16[4,6144]{1,0:T(4,128)(2,1)S(1)}, u32[]{:S(2)}, u32[]{:S(2)}) collective-permute-start(bf16[4,6144]{1,0:T(4,128)(2,1)S(1)} %subtract_convert_fusion.mine), channel_id=1, source_target_pairs={{0,28},{1,13},{2,30},{3,15},{4,24},{5,9},{6,26},{7,11},{8,20},{9,5... | collective-permute-start | bytes 147464 | tf_op jit(solution)/shard_map/ppermute | solution.py:25
  29.0 0.6 %collective-permute-done.9.far = bf16[4,6144]{1,0:T(4,128)(2,1)S(1)} collective-permute-done((bf16[4,6144]{1,0:T(4,128)(2,1)S(1)}, bf16[4,6144]{1,0:T(4,128)(2,1)S(1)}, u32[]{:S(2)}, u32[]{:S(2)}) %collective-permute-start.9) | collective-permute-done | bytes 49184 | tf_op jit(solution)/shard_map/ppermute | solution.py:25
  29.7 0.1 collective-permute-start.11
  29.8 1.1 %collective-permute-start.12 = (bf16[2,4,6144]{2,1,0:T(4,128)(2,1)S(1)}, bf16[2,4,6144]{2,1,0:T(4,128)(2,1)S(1)}, u32[]{:S(2)}, u32[]{:S(2)}) collective-permute-start(bf16[2,4,6144]{2,1,0:T(4,128)(2,1)S(1)} %pad_maximum_fusion.1), channel_id=1, source_target_pairs={{0,4},{1,9},{2,6},{3,11},{4,0},{5,13},{6,2},{7,15},{8,12},{9,1},{1... | collective-permute-start | bytes 294920 | tf_op jit(solution)/shard_map/ppermute | solution.py:25
  30.9 0.1 collective-permute-done.8.corner
  31.0 0.8 %multiply_subtract_fusion = (f32[4,6144]{1,0:T(4,128)}, f32[4,6144]{1,0:T(4,128)}, f32[4,6144]{1,0:T(4,128)}) fusion(f32[4,6144]{1,0:T(4,128)S(1)} %copy-done, f32[4,6144]{1,0:T(4,128)S(1)} %get-tuple-element.8, f32[4,6144]{1,0:T(4,128)S(1)} %copy-done.2, f32[4,6144]{1,0:T(4,128)S(1)} %copy-done.1), kind=kLoop, calls=%fused_computation.29 | loop fusion | flops 368640 | bytes 688128 | tf_op jit(solution)/shard_map/sub | solution.py:213
  31.8 2.0 %collective-permute-done.10.cross = bf16[4,6144]{1,0:T(4,128)(2,1)S(1)} collective-permute-done((bf16[4,6144]{1,0:T(4,128)(2,1)S(1)}, bf16[4,6144]{1,0:T(4,128)(2,1)S(1)}, u32[]{:S(2)}, u32[]{:S(2)}) %collective-permute-start.10) | collective-permute-done | bytes 49184 | tf_op jit(solution)/shard_map/ppermute | solution.py:25
  33.8 0.9 %collective-permute-done.11.side = bf16[2,4,6144]{2,1,0:T(4,128)(2,1)S(1)} collective-permute-done((bf16[2,4,6144]{2,1,0:T(4,128)(2,1)S(1)}, bf16[2,4,6144]{2,1,0:T(4,128)(2,1)S(1)}, u32[]{:S(2)}, u32[]{:S(2)}) %collective-permute-start.11) | collective-permute-done | bytes 98336 | tf_op jit(solution)/shard_map/ppermute | solution.py:25
  34.8 0.8 %shard_map.85 = bf16[4,49152]{1,0:T(4,128)(2,1)} custom-call(bf16[4,6144]{1,0:T(4,128)(2,1)S(1)} %subtract_convert_fusion.mine, bf16[4,6144]{1,0:T(4,128)(2,1)S(1)} %collective-permute-done.9.far, bf16[4,6144]{1,0:T(4,128)(2,1)S(1)} %collective-permute-done.8.corner, bf16[4,6144]{1,0:T(4,128)(2,1)S(1)} %collective-permute-done.10.cross, ...), custom_call_target="tpu_custom_call" | custom-call | bytes 786432 | tf_op jit(solution)/shard_map/pallas_call | solution.py:174
  (16 shorter events, 0.2 us)
Async XLA Ops:
  2.4 1.6 %collective-permute-start = (bf16[4,8,3072]{2,1,0:T(8,128)(2,1)S(1)}, bf16[4,8,3072]{2,1,0:T(8,128)(2,1)S(1)}, u32[]{:S(2)}, u32[]{:S(2)}) collective-permute-start(bf16[4,8,3072]{2,1,0:T(8,128)(2,1)S(1)} %get-tuple-element.14), channel_id=1, source_target_pairs={{0,1},{1,0},{2,3},{3,2},{4,5},{5,4},{6,7},{7,6},{8,9},{9,8},{10,11... | collective-permute-start | bytes 589832 | tf_op jit(solution)/shard_map/ppermute | solution.py:25
  2.9 5.0 %collective-permute-start.1 = (bf16[3,4,8,3072]{3,2,1,0:T(8,128)(2,1)S(1)}, bf16[3,4,8,3072]{3,2,1,0:T(8,128)(2,1)S(1)}, u32[]{:S(2)}, u32[]{:S(2)}) collective-permute-start(bf16[3,4,8,3072]{3,2,1,0:T(8,128)(2,1)S(1)} %get-tuple-element.16), channel_id=1, source_target_pairs={{0,1},{1,0},{2,3},{3,2},{4,5},{5,4},{6,7},{7,6},{8,9},{9,8},{10,11... | collective-permute-start | bytes 1769480 | tf_op jit(solution)/shard_map/ppermute | solution.py:25
  4.0 7.5 %collective-permute-start.2 = (f16[4,8,3072]{2,1,0:T(8,128)(2,1)S(1)}, f16[4,8,3072]{2,1,0:T(8,128)(2,1)S(1)}, u32[]{:S(2)}, u32[]{:S(2)}) collective-permute-start(f16[4,8,3072]{2,1,0:T(8,128)(2,1)S(1)} %fusion.1), channel_id=1, source_target_pairs={{0,6},{1,25},{2,4},{3,27},{4,2},{5,29},{6,0},{7,31},{8,14},{9,17},... | collective-permute-start | bytes 589832 | tf_op jit(solution)/shard_map/ppermute | solution.py:25
  8.1 6.1 %collective-permute-start.4 = (f16[4,8,3072]{2,1,0:T(8,128)(2,1)S(1)}, f16[4,8,3072]{2,1,0:T(8,128)(2,1)S(1)}, u32[]{:S(2)}, u32[]{:S(2)}) collective-permute-start(f16[4,8,3072]{2,1,0:T(8,128)(2,1)S(1)} %get-tuple-element.25), channel_id=1, source_target_pairs={{0,2},{1,17},{2,0},{3,19},{4,6},{5,21},{6,4},{7,23},{8,10},{9,25},... | collective-permute-start | bytes 589832 | tf_op jit(solution)/shard_map/ppermute | solution.py:25
  8.7 14.5 %copy-start = (f32[4,6144]{1,0:T(4,128)S(1)}, f32[4,6144]{1,0:T(4,128)}, u32[]{:S(2)}) copy-start(f32[4,6144]{1,0:T(4,128)} %param.5) | copy-start | bytes 294916
  8.7 14.5 %copy-start.1 = (f32[4,6144]{1,0:T(4,128)S(1)}, f32[4,6144]{1,0:T(4,128)}, u32[]{:S(2)}) copy-start(f32[4,6144]{1,0:T(4,128)} %param.7) | copy-start | bytes 294916
  8.7 14.6 %copy-start.2 = (f32[4,6144]{1,0:T(4,128)S(1)}, f32[4,6144]{1,0:T(4,128)}, u32[]{:S(2)}) copy-start(f32[4,6144]{1,0:T(4,128)} %param.6) | copy-start | bytes 294916
  8.7 5.7 %collective-permute-start.3 = (f16[4,8,3072]{2,1,0:T(8,128)(2,1)S(1)}, f16[4,8,3072]{2,1,0:T(8,128)(2,1)S(1)}, u32[]{:S(2)}, u32[]{:S(2)}) collective-permute-start(f16[4,8,3072]{2,1,0:T(8,128)(2,1)S(1)} %get-tuple-element.24), channel_id=1, source_target_pairs={{0,4},{1,9},{2,6},{3,11},{4,0},{5,13},{6,2},{7,15},{8,12},{9,1},{1... | collective-permute-start | bytes 589832 | tf_op jit(solution)/shard_map/ppermute | solution.py:25
  14.5 6.0 %collective-permute-start.7 = (f16[8,3072]{1,0:T(8,128)(2,1)S(1)}, f16[8,3072]{1,0:T(8,128)(2,1)S(1)}, u32[]{:S(2)}, u32[]{:S(2)}) collective-permute-start(f16[8,3072]{1,0:T(8,128)(2,1)S(1)} %get-tuple-element.27), channel_id=1, source_target_pairs={{0,24},{1,7},{2,26},{3,5},{4,28},{5,3},{6,30},{7,1},{8,16},{9,15},... | collective-permute-start | bytes 147464 | tf_op jit(solution)/shard_map/ppermute | solution.py:25
  18.2 5.0 %collective-permute-start.6 = (f16[8,3072]{1,0:T(8,128)(2,1)S(1)}, f16[8,3072]{1,0:T(8,128)(2,1)S(1)}, u32[]{:S(2)}, u32[]{:S(2)}) collective-permute-start(f16[8,3072]{1,0:T(8,128)(2,1)S(1)} %get-tuple-element.28), channel_id=1, source_target_pairs={{0,16},{1,3},{2,18},{3,1},{4,20},{5,7},{6,22},{7,5},{8,24},{9,11},... | collective-permute-start | bytes 147464 | tf_op jit(solution)/shard_map/ppermute | solution.py:25
  18.2 5.0 %collective-permute-start.5 = (f16[8,3072]{1,0:T(8,128)(2,1)S(1)}, f16[8,3072]{1,0:T(8,128)(2,1)S(1)}, u32[]{:S(2)}, u32[]{:S(2)}) collective-permute-start(f16[8,3072]{1,0:T(8,128)(2,1)S(1)} %get-tuple-element.26), channel_id=1, source_target_pairs={{0,8},{1,5},{2,10},{3,7},{4,12},{5,1},{6,14},{7,3},{8,0},{9,13},{1... | collective-permute-start | bytes 147464 | tf_op jit(solution)/shard_map/ppermute | solution.py:25
  23.4 12.2 %copy-start.3 = (f32[4,6144]{1,0:T(4,128)}, f32[4,6144]{1,0:T(4,128)S(1)}, u32[]{:S(2)}) copy-start(f32[4,6144]{1,0:T(4,128)S(1)} %get-tuple-element.8) | copy-start | bytes 294916
  23.4 6.2 %collective-permute-start.9 = (bf16[4,6144]{1,0:T(4,128)(2,1)S(1)}, bf16[4,6144]{1,0:T(4,128)(2,1)S(1)}, u32[]{:S(2)}, u32[]{:S(2)}) collective-permute-start(bf16[4,6144]{1,0:T(4,128)(2,1)S(1)} %get-tuple-element.20), channel_id=1, source_target_pairs={{0,16},{1,17},{2,18},{3,19},{4,20},{5,21},{6,22},{7,23},{8,24},{9,... | collective-permute-start | bytes 147464 | tf_op jit(solution)/shard_map/ppermute | solution.py:25
  25.7 5.3 %collective-permute-start.8 = (bf16[4,6144]{1,0:T(4,128)(2,1)S(1)}, bf16[4,6144]{1,0:T(4,128)(2,1)S(1)}, u32[]{:S(2)}, u32[]{:S(2)}) collective-permute-start(bf16[4,6144]{1,0:T(4,128)(2,1)S(1)} %subtract_convert_fusion.mine), channel_id=1, source_target_pairs={{0,12},{1,29},{2,14},{3,31},{4,8},{5,25},{6,10},{7,27},{8,4},{9,21... | collective-permute-start | bytes 147464 | tf_op jit(solution)/shard_map/ppermute | solution.py:25
  26.5 7.3 %collective-permute-start.10 = (bf16[4,6144]{1,0:T(4,128)(2,1)S(1)}, bf16[4,6144]{1,0:T(4,128)(2,1)S(1)}, u32[]{:S(2)}, u32[]{:S(2)}) collective-permute-start(bf16[4,6144]{1,0:T(4,128)(2,1)S(1)} %subtract_convert_fusion.mine), channel_id=1, source_target_pairs={{0,28},{1,13},{2,30},{3,15},{4,24},{5,9},{6,26},{7,11},{8,20},{9,5... | collective-permute-start | bytes 147464 | tf_op jit(solution)/shard_map/ppermute | solution.py:25
  29.7 5.0 %collective-permute-start.11 = (bf16[2,4,6144]{2,1,0:T(4,128)(2,1)S(1)}, bf16[2,4,6144]{2,1,0:T(4,128)(2,1)S(1)}, u32[]{:S(2)}, u32[]{:S(2)}) collective-permute-start(bf16[2,4,6144]{2,1,0:T(4,128)(2,1)S(1)} %pad_maximum_fusion.1), channel_id=1, source_target_pairs={{0,8},{1,5},{2,10},{3,7},{4,12},{5,1},{6,14},{7,3},{8,0},{9,13},{1... | collective-permute-start | bytes 294920 | tf_op jit(solution)/shard_map/ppermute | solution.py:25
  29.8 5.0 %collective-permute-start.12 = (bf16[2,4,6144]{2,1,0:T(4,128)(2,1)S(1)}, bf16[2,4,6144]{2,1,0:T(4,128)(2,1)S(1)}, u32[]{:S(2)}, u32[]{:S(2)}) collective-permute-start(bf16[2,4,6144]{2,1,0:T(4,128)(2,1)S(1)} %pad_maximum_fusion.1), channel_id=1, source_target_pairs={{0,4},{1,9},{2,6},{3,11},{4,0},{5,13},{6,2},{7,15},{8,12},{9,1},{1... | collective-permute-start | bytes 294920 | tf_op jit(solution)/shard_map/ppermute | solution.py:25

commit v17 on v16

--- a/solution.py
+++ b/solution.py
@@ -73,13 +73,13 @@
         copy.start()
 
     def store(step, member, rows):
-        @pl.when(step == 3)
+        @pl.when(step == 2)
         def _():
             first[member] = rows
 
-        @pl.when(step != 3)
+        @pl.when(step != 2)
         def _():
-            others[step, member] = rows
+            others[jnp.minimum(step, 2), member] = rows
 
     for i in range(8):
         copies[i].wait()
@@ -133,13 +133,13 @@
     first, others = swap(first, CORE, CORE), swap(others, CORE, CORE)
 
     def pair(d):
-        return own[d].astype(jnp.float32) + (first if d == 3 else others[d]).astype(jnp.float32)
+        return own[d].astype(jnp.float32) + (first if d == 2 else others[min(d, 2)]).astype(jnp.float32)
 
     over_xy, over_z = (0, Y, X, X + Y), (0, Z_NEAR, Z_FAR, Z_NEAR + Z_FAR)
-    sent = {3: narrow(pair(3))}
-    own, sent[3] = lax.optimization_barrier((own, sent[3]))
-    sent.update({d: narrow(pair(d)) for d in (1, 2)})
-    got = [swap(sent[d], over_xy[d], over_z[d]) for d in (3, 1, 2)]
+    sent = {2: narrow(pair(2))}
+    own, sent[2] = lax.optimization_barrier((own, sent[2]))
+    sent.update({d: narrow(pair(d)) for d in (1, 3)})
+    got = [swap(sent[d], over_xy[d], over_z[d]) for d in (2, 3, 1)]
     quarter = lax.optimization_barrier(pair(0) + widen(got[0]))
     quarter = quarter + widen(got[1]) + widen(got[2])
     me = jnp.where(core == 0, z, 2 * x + y)

time: 35.8 us -> 36.3 us (1.014)
  no operation moved by 1% of the time
where the time goes in v17:
time: 36.3 us; the launch traced here: 36.1 us
  starting transfers between devices  17 us (47%)
  waiting for transfers between devices  13.6 us (37%)
  Pallas kernels  3.04 us (8%)
  other arithmetic  1.73 us (5%)
  between operations  0.75 us (2%)
    ppermute x13, starting transfers between devices, swap(): return lax.ppermute(value, ('hst', 'local'), flip_pairs(flips))  17 us
    ppermute x13, waiting for transfers between devices, swap(): return lax.ppermute(value, ('hst', 'local'), flip_pairs(flips))  13.6 us
    pallas_call x2, Pallas kernels, call(): pl.pallas_call(kernel, in_specs=[pl.BlockSpec(memory_space=space)], out_s...  2.24 us
    sub x1, other arithmetic, adam(): new_master = master - learn_rate * (update + decay_rate * master)  0.84 us
    pallas_call x1, Pallas kernels, gather_blocks(): pl.pallas_call(join_kernel, in_specs=[pl.BlockSpec(memory_space=pl.ANY)]...  0.8 us
  transfers between devices with their start and end apart: 13, of which 10 were waited for; matrix products, arithmetic and copies ran while one was open for 4% of the time, Pallas kernels for 1%

profile of v17, /device:TPU:0, one launch (start us, length us, event | category | flops | bytes accessed | tf_op | source)
XLA Modules:
  0.0 36.1 jit_solution(9832539823451156767)
XLA Ops:
  0.6 1.8 %shard_map.83 = (bf16[4,8,3072]{2,1,0:T(8,128)(2,1)S(1)}, bf16[3,4,8,3072]{3,2,1,0:T(8,128)(2,1)S(1)}, bf16[16,49152]{1,0:T(8,128)(2,1)S(1)}) custom-call(bf16[16,49152]{1,0:T(8,128)(2,1)} %bitcast.28), custom_call_target="tpu_custom_call" | custom-call | flops 786432 | bytes 3145728 | tf_op jit(solution)/shard_map/pallas_call | solution.py:102
  2.4 0.5 %collective-permute-start = (bf16[4,8,3072]{2,1,0:T(8,128)(2,1)S(1)}, bf16[4,8,3072]{2,1,0:T(8,128)(2,1)S(1)}, u32[]{:S(2)}, u32[]{:S(2)}) collective-permute-start(bf16[4,8,3072]{2,1,0:T(8,128)(2,1)S(1)} %get-tuple-element.14), channel_id=1, source_target_pairs={{0,1},{1,0},{2,3},{3,2},{4,5},{5,4},{6,7},{7,6},{8,9},{9,8},{10,11... | collective-permute-start | bytes 589832 | tf_op jit(solution)/shard_map/ppermute | solution.py:25
  2.9 0.1 collective-permute-start.1
  3.0 0.5 %shard_map.84 = bf16[4,4,8,3072]{3,2,1,0:T(8,128)(2,1)S(1)} custom-call(bf16[16,49152]{1,0:T(8,128)(2,1)S(1)} %get-tuple-element.13.landed), custom_call_target="tpu_custom_call" | custom-call | flops 786432 | bytes 3145728 | tf_op jit(solution)/shard_map/pallas_call | solution.py:102
  3.5 0.5 %collective-permute-done = bf16[4,8,3072]{2,1,0:T(8,128)(2,1)S(1)} collective-permute-done((bf16[4,8,3072]{2,1,0:T(8,128)(2,1)S(1)}, bf16[4,8,3072]{2,1,0:T(8,128)(2,1)S(1)}, u32[]{:S(2)}, u32[]{:S(2)}) %collective-permute-start) | collective-permute-done | bytes 196640 | tf_op jit(solution)/shard_map/ppermute | solution.py:25
  4.0 0.1 fusion.1
  4.1 2.9 %collective-permute-start.2 = (f16[4,8,3072]{2,1,0:T(8,128)(2,1)S(1)}, f16[4,8,3072]{2,1,0:T(8,128)(2,1)S(1)}, u32[]{:S(2)}, u32[]{:S(2)}) collective-permute-start(f16[4,8,3072]{2,1,0:T(8,128)(2,1)S(1)} %fusion.1), channel_id=1, source_target_pairs={{0,2},{1,17},{2,0},{3,19},{4,6},{5,21},{6,4},{7,23},{8,10},{9,25},... | collective-permute-start | bytes 589832 | tf_op jit(solution)/shard_map/ppermute | solution.py:25
  7.0 0.1 fusion.2
  7.1 1.6 %collective-permute-start.4 = (f16[4,8,3072]{2,1,0:T(8,128)(2,1)S(1)}, f16[4,8,3072]{2,1,0:T(8,128)(2,1)S(1)}, u32[]{:S(2)}, u32[]{:S(2)}) collective-permute-start(f16[4,8,3072]{2,1,0:T(8,128)(2,1)S(1)} %get-tuple-element.25), channel_id=1, source_target_pairs={{0,4},{1,9},{2,6},{3,11},{4,0},{5,13},{6,2},{7,15},{8,12},{9,1},{1... | collective-permute-start | bytes 589832 | tf_op jit(solution)/shard_map/ppermute | solution.py:25
  8.7 0.6 %collective-permute-start.3 = (f16[4,8,3072]{2,1,0:T(8,128)(2,1)S(1)}, f16[4,8,3072]{2,1,0:T(8,128)(2,1)S(1)}, u32[]{:S(2)}, u32[]{:S(2)}) collective-permute-start(f16[4,8,3072]{2,1,0:T(8,128)(2,1)S(1)} %get-tuple-element.24), channel_id=1, source_target_pairs={{0,6},{1,25},{2,4},{3,27},{4,2},{5,29},{6,0},{7,31},{8,14},{9,17},... | collective-permute-start | bytes 589832 | tf_op jit(solution)/shard_map/ppermute | solution.py:25
  9.4 1.3 %collective-permute-done.2 = f16[4,8,3072]{2,1,0:T(8,128)(2,1)S(1)} collective-permute-done((f16[4,8,3072]{2,1,0:T(8,128)(2,1)S(1)}, f16[4,8,3072]{2,1,0:T(8,128)(2,1)S(1)}, u32[]{:S(2)}, u32[]{:S(2)}) %collective-permute-start.2) | collective-permute-done | bytes 196640 | tf_op jit(solution)/shard_map/ppermute | solution.py:25
  10.6 0.1 bitcast_add_fusion
  10.7 3.3 %collective-permute-done.4 = f16[4,8,3072]{2,1,0:T(8,128)(2,1)S(1)} collective-permute-done((f16[4,8,3072]{2,1,0:T(8,128)(2,1)S(1)}, f16[4,8,3072]{2,1,0:T(8,128)(2,1)S(1)}, u32[]{:S(2)}, u32[]{:S(2)}) %collective-permute-start.4) | collective-permute-done | bytes 196640 | tf_op jit(solution)/shard_map/ppermute | solution.py:25
  14.0 1.2 %collective-permute-done.3 = f16[4,8,3072]{2,1,0:T(8,128)(2,1)S(1)} collective-permute-done((f16[4,8,3072]{2,1,0:T(8,128)(2,1)S(1)}, f16[4,8,3072]{2,1,0:T(8,128)(2,1)S(1)}, u32[]{:S(2)}, u32[]{:S(2)}) %collective-permute-start.3) | collective-permute-done | bytes 196640 | tf_op jit(solution)/shard_map/ppermute | solution.py:25
  15.3 0.1 multiply_add_fusion
  15.4 3.7 %collective-permute-start.7 = (f16[8,3072]{1,0:T(8,128)(2,1)S(1)}, f16[8,3072]{1,0:T(8,128)(2,1)S(1)}, u32[]{:S(2)}, u32[]{:S(2)}) collective-permute-start(f16[8,3072]{1,0:T(8,128)(2,1)S(1)} %get-tuple-element.27), channel_id=1, source_target_pairs={{0,24},{1,7},{2,26},{3,5},{4,28},{5,3},{6,30},{7,1},{8,16},{9,15},... | collective-permute-start | bytes 147464 | tf_op jit(solution)/shard_map/ppermute | solution.py:25
  19.1 0.8 %collective-permute-start.5 = (f16[8,3072]{1,0:T(8,128)(2,1)S(1)}, f16[8,3072]{1,0:T(8,128)(2,1)S(1)}, u32[]{:S(2)}, u32[]{:S(2)}) collective-permute-start(f16[8,3072]{1,0:T(8,128)(2,1)S(1)} %get-tuple-element.26), channel_id=1, source_target_pairs={{0,8},{1,5},{2,10},{3,7},{4,12},{5,1},{6,14},{7,3},{8,0},{9,13},{1... | collective-permute-start | bytes 147464 | tf_op jit(solution)/shard_map/ppermute | solution.py:25
  19.9 1.5 %collective-permute-done.7 = f16[8,3072]{1,0:T(8,128)(2,1)S(1)} collective-permute-done((f16[8,3072]{1,0:T(8,128)(2,1)S(1)}, f16[8,3072]{1,0:T(8,128)(2,1)S(1)}, u32[]{:S(2)}, u32[]{:S(2)}) %collective-permute-start.7) | collective-permute-done | bytes 49184 | tf_op jit(solution)/shard_map/ppermute | solution.py:25
  21.4 2.7 %collective-permute-done.6 = f16[8,3072]{1,0:T(8,128)(2,1)S(1)} collective-permute-done((f16[8,3072]{1,0:T(8,128)(2,1)S(1)}, f16[8,3072]{1,0:T(8,128)(2,1)S(1)}, u32[]{:S(2)}, u32[]{:S(2)}) %collective-permute-start.6) | collective-permute-done | bytes 49184 | tf_op jit(solution)/shard_map/ppermute | solution.py:25
  24.2 0.2 subtract_convert_fusion.1
  24.4 2.1 %collective-permute-start.9 = (bf16[4,6144]{1,0:T(4,128)(2,1)S(1)}, bf16[4,6144]{1,0:T(4,128)(2,1)S(1)}, u32[]{:S(2)}, u32[]{:S(2)}) collective-permute-start(bf16[4,6144]{1,0:T(4,128)(2,1)S(1)} %get-tuple-element.20), channel_id=1, source_target_pairs={{0,16},{1,17},{2,18},{3,19},{4,20},{5,21},{6,22},{7,23},{8,24},{9,... | collective-permute-start | bytes 147464 | tf_op jit(solution)/shard_map/ppermute | solution.py:25
  26.5 0.2 subtract_convert_fusion.mine
  26.7 0.7 %collective-permute-start.8 = (bf16[4,6144]{1,0:T(4,128)(2,1)S(1)}, bf16[4,6144]{1,0:T(4,128)(2,1)S(1)}, u32[]{:S(2)}, u32[]{:S(2)}) collective-permute-start(bf16[4,6144]{1,0:T(4,128)(2,1)S(1)} %subtract_convert_fusion.mine), channel_id=1, source_target_pairs={{0,12},{1,29},{2,14},{3,31},{4,8},{5,25},{6,10},{7,27},{8,4},{9,21... | collective-permute-start | bytes 147464 | tf_op jit(solution)/shard_map/ppermute | solution.py:25
  27.4 2.6 %collective-permute-start.10 = (bf16[4,6144]{1,0:T(4,128)(2,1)S(1)}, bf16[4,6144]{1,0:T(4,128)(2,1)S(1)}, u32[]{:S(2)}, u32[]{:S(2)}) collective-permute-start(bf16[4,6144]{1,0:T(4,128)(2,1)S(1)} %subtract_convert_fusion.mine), channel_id=1, source_target_pairs={{0,28},{1,13},{2,30},{3,15},{4,24},{5,9},{6,26},{7,11},{8,20},{9,5... | collective-permute-start | bytes 147464 | tf_op jit(solution)/shard_map/ppermute | solution.py:25
  30.1 0.1 collective-permute-start.11
  30.1 1.3 %collective-permute-start.12 = (bf16[2,4,6144]{2,1,0:T(4,128)(2,1)S(1)}, bf16[2,4,6144]{2,1,0:T(4,128)(2,1)S(1)}, u32[]{:S(2)}, u32[]{:S(2)}) collective-permute-start(bf16[2,4,6144]{2,1,0:T(4,128)(2,1)S(1)} %pad_maximum_fusion.1), channel_id=1, source_target_pairs={{0,4},{1,9},{2,6},{3,11},{4,0},{5,13},{6,2},{7,15},{8,12},{9,1},{1... | collective-permute-start | bytes 294920 | tf_op jit(solution)/shard_map/ppermute | solution.py:25
  31.4 1.1 %collective-permute-done.8.corner = bf16[4,6144]{1,0:T(4,128)(2,1)S(1)} collective-permute-done((bf16[4,6144]{1,0:T(4,128)(2,1)S(1)}, bf16[4,6144]{1,0:T(4,128)(2,1)S(1)}, u32[]{:S(2)}, u32[]{:S(2)}) %collective-permute-start.8) | collective-permute-done | bytes 49184 | tf_op jit(solution)/shard_map/ppermute | solution.py:25
  32.5 0.8 %multiply_subtract_fusion = (f32[4,6144]{1,0:T(4,128)}, f32[4,6144]{1,0:T(4,128)}, f32[4,6144]{1,0:T(4,128)}) fusion(f32[4,6144]{1,0:T(4,128)S(1)} %copy-done, f32[4,6144]{1,0:T(4,128)S(1)} %get-tuple-element.8, f32[4,6144]{1,0:T(4,128)S(1)} %copy-done.2, f32[4,6144]{1,0:T(4,128)S(1)} %copy-done.1), kind=kLoop, calls=%fused_computation.29 | loop fusion | flops 368640 | bytes 688128 | tf_op jit(solution)/shard_map/sub | solution.py:213
  33.3 1.0 %collective-permute-done.10.cross = bf16[4,6144]{1,0:T(4,128)(2,1)S(1)} collective-permute-done((bf16[4,6144]{1,0:T(4,128)(2,1)S(1)}, bf16[4,6144]{1,0:T(4,128)(2,1)S(1)}, u32[]{:S(2)}, u32[]{:S(2)}) %collective-permute-start.10) | collective-permute-done | bytes 49184 | tf_op jit(solution)/shard_map/ppermute | solution.py:25
  34.3 0.5 %collective-permute-done.11.side = bf16[2,4,6144]{2,1,0:T(4,128)(2,1)S(1)} collective-permute-done((bf16[2,4,6144]{2,1,0:T(4,128)(2,1)S(1)}, bf16[2,4,6144]{2,1,0:T(4,128)(2,1)S(1)}, u32[]{:S(2)}, u32[]{:S(2)}) %collective-permute-start.11) | collective-permute-done | bytes 98336 | tf_op jit(solution)/shard_map/ppermute | solution.py:25
  34.8 0.5 %collective-permute-done.12.other_side = bf16[2,4,6144]{2,1,0:T(4,128)(2,1)S(1)} collective-permute-done((bf16[2,4,6144]{2,1,0:T(4,128)(2,1)S(1)}, bf16[2,4,6144]{2,1,0:T(4,128)(2,1)S(1)}, u32[]{:S(2)}, u32[]{:S(2)}) %collective-permute-start.12) | collective-permute-done | bytes 98336 | tf_op jit(solution)/shard_map/ppermute | solution.py:25
  35.3 0.8 %shard_map.85 = bf16[4,49152]{1,0:T(4,128)(2,1)} custom-call(bf16[4,6144]{1,0:T(4,128)(2,1)S(1)} %subtract_convert_fusion.mine, bf16[4,6144]{1,0:T(4,128)(2,1)S(1)} %collective-permute-done.9.far, bf16[4,6144]{1,0:T(4,128)(2,1)S(1)} %collective-permute-done.8.corner, bf16[4,6144]{1,0:T(4,128)(2,1)S(1)} %collective-permute-done.10.cross, ...), custom_call_target="tpu_custom_call" | custom-call | bytes 786432 | tf_op jit(solution)/shard_map/pallas_call | solution.py:174
  (16 shorter events, 0.2 us)
Async XLA Ops:
  2.4 1.6 %collective-permute-start = (bf16[4,8,3072]{2,1,0:T(8,128)(2,1)S(1)}, bf16[4,8,3072]{2,1,0:T(8,128)(2,1)S(1)}, u32[]{:S(2)}, u32[]{:S(2)}) collective-permute-start(bf16[4,8,3072]{2,1,0:T(8,128)(2,1)S(1)} %get-tuple-element.14), channel_id=1, source_target_pairs={{0,1},{1,0},{2,3},{3,2},{4,5},{5,4},{6,7},{7,6},{8,9},{9,8},{10,11... | collective-permute-start | bytes 589832 | tf_op jit(solution)/shard_map/ppermute | solution.py:25
  2.9 4.1 %collective-permute-start.1 = (bf16[3,4,8,3072]{3,2,1,0:T(8,128)(2,1)S(1)}, bf16[3,4,8,3072]{3,2,1,0:T(8,128)(2,1)S(1)}, u32[]{:S(2)}, u32[]{:S(2)}) collective-permute-start(bf16[3,4,8,3072]{3,2,1,0:T(8,128)(2,1)S(1)} %get-tuple-element.16), channel_id=1, source_target_pairs={{0,1},{1,0},{2,3},{3,2},{4,5},{5,4},{6,7},{7,6},{8,9},{9,8},{10,11... | collective-permute-start | bytes 1769480 | tf_op jit(solution)/shard_map/ppermute | solution.py:25
  4.1 6.6 %collective-permute-start.2 = (f16[4,8,3072]{2,1,0:T(8,128)(2,1)S(1)}, f16[4,8,3072]{2,1,0:T(8,128)(2,1)S(1)}, u32[]{:S(2)}, u32[]{:S(2)}) collective-permute-start(f16[4,8,3072]{2,1,0:T(8,128)(2,1)S(1)} %fusion.1), channel_id=1, source_target_pairs={{0,2},{1,17},{2,0},{3,19},{4,6},{5,21},{6,4},{7,23},{8,10},{9,25},... | collective-permute-start | bytes 589832 | tf_op jit(solution)/shard_map/ppermute | solution.py:25
  7.1 6.9 %collective-permute-start.4 = (f16[4,8,3072]{2,1,0:T(8,128)(2,1)S(1)}, f16[4,8,3072]{2,1,0:T(8,128)(2,1)S(1)}, u32[]{:S(2)}, u32[]{:S(2)}) collective-permute-start(f16[4,8,3072]{2,1,0:T(8,128)(2,1)S(1)} %get-tuple-element.25), channel_id=1, source_target_pairs={{0,4},{1,9},{2,6},{3,11},{4,0},{5,13},{6,2},{7,15},{8,12},{9,1},{1... | collective-permute-start | bytes 589832 | tf_op jit(solution)/shard_map/ppermute | solution.py:25
  8.7 15.4 %copy-start = (f32[4,6144]{1,0:T(4,128)S(1)}, f32[4,6144]{1,0:T(4,128)}, u32[]{:S(2)}) copy-start(f32[4,6144]{1,0:T(4,128)} %param.5) | copy-start | bytes 294916
  8.7 15.5 %copy-start.1 = (f32[4,6144]{1,0:T(4,128)S(1)}, f32[4,6144]{1,0:T(4,128)}, u32[]{:S(2)}) copy-start(f32[4,6144]{1,0:T(4,128)} %param.7) | copy-start | bytes 294916
  8.7 15.5 %copy-start.2 = (f32[4,6144]{1,0:T(4,128)S(1)}, f32[4,6144]{1,0:T(4,128)}, u32[]{:S(2)}) copy-start(f32[4,6144]{1,0:T(4,128)} %param.6) | copy-start | bytes 294916
  8.7 6.6 %collective-permute-start.3 = (f16[4,8,3072]{2,1,0:T(8,128)(2,1)S(1)}, f16[4,8,3072]{2,1,0:T(8,128)(2,1)S(1)}, u32[]{:S(2)}, u32[]{:S(2)}) collective-permute-start(f16[4,8,3072]{2,1,0:T(8,128)(2,1)S(1)} %get-tuple-element.24), channel_id=1, source_target_pairs={{0,6},{1,25},{2,4},{3,27},{4,2},{5,29},{6,0},{7,31},{8,14},{9,17},... | collective-permute-start | bytes 589832 | tf_op jit(solution)/shard_map/ppermute | solution.py:25
  15.4 6.0 %collective-permute-start.7 = (f16[8,3072]{1,0:T(8,128)(2,1)S(1)}, f16[8,3072]{1,0:T(8,128)(2,1)S(1)}, u32[]{:S(2)}, u32[]{:S(2)}) collective-permute-start(f16[8,3072]{1,0:T(8,128)(2,1)S(1)} %get-tuple-element.27), channel_id=1, source_target_pairs={{0,24},{1,7},{2,26},{3,5},{4,28},{5,3},{6,30},{7,1},{8,16},{9,15},... | collective-permute-start | bytes 147464 | tf_op jit(solution)/shard_map/ppermute | solution.py:25
  19.1 5.0 %collective-permute-start.6 = (f16[8,3072]{1,0:T(8,128)(2,1)S(1)}, f16[8,3072]{1,0:T(8,128)(2,1)S(1)}, u32[]{:S(2)}, u32[]{:S(2)}) collective-permute-start(f16[8,3072]{1,0:T(8,128)(2,1)S(1)} %get-tuple-element.28), channel_id=1, source_target_pairs={{0,16},{1,3},{2,18},{3,1},{4,20},{5,7},{6,22},{7,5},{8,24},{9,11},... | collective-permute-start | bytes 147464 | tf_op jit(solution)/shard_map/ppermute | solution.py:25
  19.1 5.0 %collective-permute-start.5 = (f16[8,3072]{1,0:T(8,128)(2,1)S(1)}, f16[8,3072]{1,0:T(8,128)(2,1)S(1)}, u32[]{:S(2)}, u32[]{:S(2)}) collective-permute-start(f16[8,3072]{1,0:T(8,128)(2,1)S(1)} %get-tuple-element.26), channel_id=1, source_target_pairs={{0,8},{1,5},{2,10},{3,7},{4,12},{5,1},{6,14},{7,3},{8,0},{9,13},{1... | collective-permute-start | bytes 147464 | tf_op jit(solution)/shard_map/ppermute | solution.py:25
  24.4 11.7 %copy-start.3 = (f32[4,6144]{1,0:T(4,128)}, f32[4,6144]{1,0:T(4,128)S(1)}, u32[]{:S(2)}) copy-start(f32[4,6144]{1,0:T(4,128)S(1)} %get-tuple-element.8) | copy-start | bytes 294916
  24.4 5.6 %collective-permute-start.9 = (bf16[4,6144]{1,0:T(4,128)(2,1)S(1)}, bf16[4,6144]{1,0:T(4,128)(2,1)S(1)}, u32[]{:S(2)}, u32[]{:S(2)}) collective-permute-start(bf16[4,6144]{1,0:T(4,128)(2,1)S(1)} %get-tuple-element.20), channel_id=1, source_target_pairs={{0,16},{1,17},{2,18},{3,19},{4,20},{5,21},{6,22},{7,23},{8,24},{9,... | collective-permute-start | bytes 147464 | tf_op jit(solution)/shard_map/ppermute | solution.py:25
  26.7 5.8 %collective-permute-start.8 = (bf16[4,6144]{1,0:T(4,128)(2,1)S(1)}, bf16[4,6144]{1,0:T(4,128)(2,1)S(1)}, u32[]{:S(2)}, u32[]{:S(2)}) collective-permute-start(bf16[4,6144]{1,0:T(4,128)(2,1)S(1)} %subtract_convert_fusion.mine), channel_id=1, source_target_pairs={{0,12},{1,29},{2,14},{3,31},{4,8},{5,25},{6,10},{7,27},{8,4},{9,21... | collective-permute-start | bytes 147464 | tf_op jit(solution)/shard_map/ppermute | solution.py:25
  27.4 6.9 %collective-permute-start.10 = (bf16[4,6144]{1,0:T(4,128)(2,1)S(1)}, bf16[4,6144]{1,0:T(4,128)(2,1)S(1)}, u32[]{:S(2)}, u32[]{:S(2)}) collective-permute-start(bf16[4,6144]{1,0:T(4,128)(2,1)S(1)} %subtract_convert_fusion.mine), channel_id=1, source_target_pairs={{0,28},{1,13},{2,30},{3,15},{4,24},{5,9},{6,26},{7,11},{8,20},{9,5... | collective-permute-start | bytes 147464 | tf_op jit(solution)/shard_map/ppermute | solution.py:25
  30.1 4.8 %collective-permute-start.11 = (bf16[2,4,6144]{2,1,0:T(4,128)(2,1)S(1)}, bf16[2,4,6144]{2,1,0:T(4,128)(2,1)S(1)}, u32[]{:S(2)}, u32[]{:S(2)}) collective-permute-start(bf16[2,4,6144]{2,1,0:T(4,128)(2,1)S(1)} %pad_maximum_fusion.1), channel_id=1, source_target_pairs={{0,8},{1,5},{2,10},{3,7},{4,12},{5,1},{6,14},{7,3},{8,0},{9,13},{1... | collective-permute-start | bytes 294920 | tf_op jit(solution)/shard_map/ppermute | solution.py:25
  30.1 5.2 %collective-permute-start.12 = (bf16[2,4,6144]{2,1,0:T(4,128)(2,1)S(1)}, bf16[2,4,6144]{2,1,0:T(4,128)(2,1)S(1)}, u32[]{:S(2)}, u32[]{:S(2)}) collective-permute-start(bf16[2,4,6144]{2,1,0:T(4,128)(2,1)S(1)} %pad_maximum_fusion.1), channel_id=1, source_target_pairs={{0,4},{1,9},{2,6},{3,11},{4,0},{5,13},{6,2},{7,15},{8,12},{9,1},{1... | collective-permute-start | bytes 294920 | tf_op jit(solution)/shard_map/ppermute | solution.py:25

commit v18 on v16

--- a/solution.py
+++ b/solution.py
@@ -56,7 +56,8 @@
             jnp.concatenate([left[at : at + tile // 2], right[at : at + tile // 2]], axis=0).astype(jnp.bfloat16)
             for at in (0, tile // 2)
         ]
-        step = jnp.where(core == 0, (2 * my_x + my_y) ^ (2 * x + y), my_z ^ z)
+        over_z = my_z ^ z
+        step = jnp.where(core == 0, (2 * my_x + my_y) ^ (2 * x + y), over_z ^ (over_z // 2))
         member = jnp.where(core == 0, z, 2 * x + y)
         store(step, member, jnp.where(core == 0, rows[0], rows[1]))
 
@@ -139,7 +140,7 @@
     sent = {3: narrow(pair(3))}
     own, sent[3] = lax.optimization_barrier((own, sent[3]))
     sent.update({d: narrow(pair(d)) for d in (1, 2)})
-    got = [swap(sent[d], over_xy[d], over_z[d]) for d in (3, 1, 2)]
+    got = [swap(sent[d], over_xy[d], over_z[d ^ (d // 2)]) for d in (3, 1, 2)]
     quarter = lax.optimization_barrier(pair(0) + widen(got[0]))
     quarter = quarter + widen(got[1]) + widen(got[2])
     me = jnp.where(core == 0, z, 2 * x + y)

time: 35.8 us -> 35.5 us (level)
  no operation moved by 1% of the time
where the time goes in v18:
time: 35.5 us; the launch traced here: 35.3 us
  starting transfers between devices  16.7 us (47%)
  waiting for transfers between devices  13 us (37%)
  Pallas kernels  3.03 us (9%)
  other arithmetic  1.73 us (5%)
  between operations  0.75 us (2%)
    ppermute x13, starting transfers between devices, swap(): return lax.ppermute(value, ('hst', 'local'), flip_pairs(flips))  16.7 us
    ppermute x13, waiting for transfers between devices, swap(): return lax.ppermute(value, ('hst', 'local'), flip_pairs(flips))  13 us
    pallas_call x2, Pallas kernels, call(): pl.pallas_call(kernel, in_specs=[pl.BlockSpec(memory_space=space)], out_s...  2.23 us
    sub x1, other arithmetic, adam(): new_master = master - learn_rate * (update + decay_rate * master)  0.84 us
    pallas_call x1, Pallas kernels, gather_blocks(): pl.pallas_call(join_kernel, in_specs=[pl.BlockSpec(memory_space=pl.ANY)]...  0.8 us
  transfers between devices with their start and end apart: 13, of which 10 were waited for; matrix products, arithmetic and copies ran while one was open for 4% of the time, Pallas kernels for 1%

profile of v18, /device:TPU:0, one launch (start us, length us, event | category | flops | bytes accessed | tf_op | source)
XLA Modules:
  0.0 35.3 jit_solution(10567082736873093217)
XLA Ops:
  0.6 1.7 %shard_map.83 = (bf16[4,8,3072]{2,1,0:T(8,128)(2,1)S(1)}, bf16[3,4,8,3072]{3,2,1,0:T(8,128)(2,1)S(1)}, bf16[16,49152]{1,0:T(8,128)(2,1)S(1)}) custom-call(bf16[16,49152]{1,0:T(8,128)(2,1)} %bitcast.28), custom_call_target="tpu_custom_call" | custom-call | flops 786432 | bytes 3145728 | tf_op jit(solution)/shard_map/pallas_call | solution.py:103
  2.4 0.5 %collective-permute-start = (bf16[4,8,3072]{2,1,0:T(8,128)(2,1)S(1)}, bf16[4,8,3072]{2,1,0:T(8,128)(2,1)S(1)}, u32[]{:S(2)}, u32[]{:S(2)}) collective-permute-start(bf16[4,8,3072]{2,1,0:T(8,128)(2,1)S(1)} %get-tuple-element.14), channel_id=1, source_target_pairs={{0,1},{1,0},{2,3},{3,2},{4,5},{5,4},{6,7},{7,6},{8,9},{9,8},{10,11... | collective-permute-start | bytes 589832 | tf_op jit(solution)/shard_map/ppermute | solution.py:25
  2.9 0.1 collective-permute-start.1
  3.0 0.5 %shard_map.84 = bf16[4,4,8,3072]{3,2,1,0:T(8,128)(2,1)S(1)} custom-call(bf16[16,49152]{1,0:T(8,128)(2,1)S(1)} %get-tuple-element.13.landed), custom_call_target="tpu_custom_call" | custom-call | flops 786432 | bytes 3145728 | tf_op jit(solution)/shard_map/pallas_call | solution.py:103
  3.5 0.5 %collective-permute-done = bf16[4,8,3072]{2,1,0:T(8,128)(2,1)S(1)} collective-permute-done((bf16[4,8,3072]{2,1,0:T(8,128)(2,1)S(1)}, bf16[4,8,3072]{2,1,0:T(8,128)(2,1)S(1)}, u32[]{:S(2)}, u32[]{:S(2)}) %collective-permute-start) | collective-permute-done | bytes 196640 | tf_op jit(solution)/shard_map/ppermute | solution.py:25
  4.0 0.1 fusion.1
  4.0 3.9 %collective-permute-start.2 = (f16[4,8,3072]{2,1,0:T(8,128)(2,1)S(1)}, f16[4,8,3072]{2,1,0:T(8,128)(2,1)S(1)}, u32[]{:S(2)}, u32[]{:S(2)}) collective-permute-start(f16[4,8,3072]{2,1,0:T(8,128)(2,1)S(1)} %fusion.1), channel_id=1, source_target_pairs={{0,6},{1,17},{2,4},{3,19},{4,2},{5,21},{6,0},{7,23},{8,14},{9,25},... | collective-permute-start | bytes 589832 | tf_op jit(solution)/shard_map/ppermute | solution.py:25
  7.9 0.1 fusion.2
  8.1 0.6 %collective-permute-start.4 = (f16[4,8,3072]{2,1,0:T(8,128)(2,1)S(1)}, f16[4,8,3072]{2,1,0:T(8,128)(2,1)S(1)}, u32[]{:S(2)}, u32[]{:S(2)}) collective-permute-start(f16[4,8,3072]{2,1,0:T(8,128)(2,1)S(1)} %get-tuple-element.25), channel_id=1, source_target_pairs={{0,2},{1,25},{2,0},{3,27},{4,6},{5,29},{6,4},{7,31},{8,10},{9,17},... | collective-permute-start | bytes 589832 | tf_op jit(solution)/shard_map/ppermute | solution.py:25
  8.7 0.7 %collective-permute-start.3 = (f16[4,8,3072]{2,1,0:T(8,128)(2,1)S(1)}, f16[4,8,3072]{2,1,0:T(8,128)(2,1)S(1)}, u32[]{:S(2)}, u32[]{:S(2)}) collective-permute-start(f16[4,8,3072]{2,1,0:T(8,128)(2,1)S(1)} %get-tuple-element.24), channel_id=1, source_target_pairs={{0,4},{1,9},{2,6},{3,11},{4,0},{5,13},{6,2},{7,15},{8,12},{9,1},{1... | collective-permute-start | bytes 589832 | tf_op jit(solution)/shard_map/ppermute | solution.py:25
  9.4 2.2 %collective-permute-done.2 = f16[4,8,3072]{2,1,0:T(8,128)(2,1)S(1)} collective-permute-done((f16[4,8,3072]{2,1,0:T(8,128)(2,1)S(1)}, f16[4,8,3072]{2,1,0:T(8,128)(2,1)S(1)}, u32[]{:S(2)}, u32[]{:S(2)}) %collective-permute-start.2) | collective-permute-done | bytes 196640 | tf_op jit(solution)/shard_map/ppermute | solution.py:25
  11.6 0.1 bitcast_add_fusion
  11.7 2.6 %collective-permute-done.4 = f16[4,8,3072]{2,1,0:T(8,128)(2,1)S(1)} collective-permute-done((f16[4,8,3072]{2,1,0:T(8,128)(2,1)S(1)}, f16[4,8,3072]{2,1,0:T(8,128)(2,1)S(1)}, u32[]{:S(2)}, u32[]{:S(2)}) %collective-permute-start.4) | collective-permute-done | bytes 196640 | tf_op jit(solution)/shard_map/ppermute | solution.py:25
  14.2 0.1 collective-permute-done.3
  14.4 0.1 multiply_add_fusion
  14.5 3.7 %collective-permute-start.7 = (f16[8,3072]{1,0:T(8,128)(2,1)S(1)}, f16[8,3072]{1,0:T(8,128)(2,1)S(1)}, u32[]{:S(2)}, u32[]{:S(2)}) collective-permute-start(f16[8,3072]{1,0:T(8,128)(2,1)S(1)} %get-tuple-element.27), channel_id=1, source_target_pairs={{0,24},{1,7},{2,26},{3,5},{4,28},{5,3},{6,30},{7,1},{8,16},{9,15},... | collective-permute-start | bytes 147464 | tf_op jit(solution)/shard_map/ppermute | solution.py:25
  18.2 0.8 %collective-permute-start.5 = (f16[8,3072]{1,0:T(8,128)(2,1)S(1)}, f16[8,3072]{1,0:T(8,128)(2,1)S(1)}, u32[]{:S(2)}, u32[]{:S(2)}) collective-permute-start(f16[8,3072]{1,0:T(8,128)(2,1)S(1)} %get-tuple-element.26), channel_id=1, source_target_pairs={{0,8},{1,5},{2,10},{3,7},{4,12},{5,1},{6,14},{7,3},{8,0},{9,13},{1... | collective-permute-start | bytes 147464 | tf_op jit(solution)/shard_map/ppermute | solution.py:25
  19.0 1.5 %collective-permute-done.7 = f16[8,3072]{1,0:T(8,128)(2,1)S(1)} collective-permute-done((f16[8,3072]{1,0:T(8,128)(2,1)S(1)}, f16[8,3072]{1,0:T(8,128)(2,1)S(1)}, u32[]{:S(2)}, u32[]{:S(2)}) %collective-permute-start.7) | collective-permute-done | bytes 49184 | tf_op jit(solution)/shard_map/ppermute | solution.py:25
  20.5 2.7 %collective-permute-done.6 = f16[8,3072]{1,0:T(8,128)(2,1)S(1)} collective-permute-done((f16[8,3072]{1,0:T(8,128)(2,1)S(1)}, f16[8,3072]{1,0:T(8,128)(2,1)S(1)}, u32[]{:S(2)}, u32[]{:S(2)}) %collective-permute-start.6) | collective-permute-done | bytes 49184 | tf_op jit(solution)/shard_map/ppermute | solution.py:25
  23.3 0.2 subtract_convert_fusion.1
  23.4 2.1 %collective-permute-start.9 = (bf16[4,6144]{1,0:T(4,128)(2,1)S(1)}, bf16[4,6144]{1,0:T(4,128)(2,1)S(1)}, u32[]{:S(2)}, u32[]{:S(2)}) collective-permute-start(bf16[4,6144]{1,0:T(4,128)(2,1)S(1)} %get-tuple-element.20), channel_id=1, source_target_pairs={{0,16},{1,17},{2,18},{3,19},{4,20},{5,21},{6,22},{7,23},{8,24},{9,... | collective-permute-start | bytes 147464 | tf_op jit(solution)/shard_map/ppermute | solution.py:25
  25.6 0.2 subtract_convert_fusion.mine
  25.7 0.8 %collective-permute-start.8 = (bf16[4,6144]{1,0:T(4,128)(2,1)S(1)}, bf16[4,6144]{1,0:T(4,128)(2,1)S(1)}, u32[]{:S(2)}, u32[]{:S(2)}) collective-permute-start(bf16[4,6144]{1,0:T(4,128)(2,1)S(1)} %subtract_convert_fusion.mine), channel_id=1, source_target_pairs={{0,12},{1,29},{2,14},{3,31},{4,8},{5,25},{6,10},{7,27},{8,4},{9,21... | collective-permute-start | bytes 147464 | tf_op jit(solution)/shard_map/ppermute | solution.py:25
  26.5 2.5 %collective-permute-start.10 = (bf16[4,6144]{1,0:T(4,128)(2,1)S(1)}, bf16[4,6144]{1,0:T(4,128)(2,1)S(1)}, u32[]{:S(2)}, u32[]{:S(2)}) collective-permute-start(bf16[4,6144]{1,0:T(4,128)(2,1)S(1)} %subtract_convert_fusion.mine), channel_id=1, source_target_pairs={{0,28},{1,13},{2,30},{3,15},{4,24},{5,9},{6,26},{7,11},{8,20},{9,5... | collective-permute-start | bytes 147464 | tf_op jit(solution)/shard_map/ppermute | solution.py:25
  29.0 0.4 %collective-permute-done.9.far = bf16[4,6144]{1,0:T(4,128)(2,1)S(1)} collective-permute-done((bf16[4,6144]{1,0:T(4,128)(2,1)S(1)}, bf16[4,6144]{1,0:T(4,128)(2,1)S(1)}, u32[]{:S(2)}, u32[]{:S(2)}) %collective-permute-start.9) | collective-permute-done | bytes 49184 | tf_op jit(solution)/shard_map/ppermute | solution.py:25
  29.5 0.1 collective-permute-start.11
  29.6 1.0 %collective-permute-start.12 = (bf16[2,4,6144]{2,1,0:T(4,128)(2,1)S(1)}, bf16[2,4,6144]{2,1,0:T(4,128)(2,1)S(1)}, u32[]{:S(2)}, u32[]{:S(2)}) collective-permute-start(bf16[2,4,6144]{2,1,0:T(4,128)(2,1)S(1)} %pad_maximum_fusion.1), channel_id=1, source_target_pairs={{0,4},{1,9},{2,6},{3,11},{4,0},{5,13},{6,2},{7,15},{8,12},{9,1},{1... | collective-permute-start | bytes 294920 | tf_op jit(solution)/shard_map/ppermute | solution.py:25
  30.6 0.5 %collective-permute-done.8.corner = bf16[4,6144]{1,0:T(4,128)(2,1)S(1)} collective-permute-done((bf16[4,6144]{1,0:T(4,128)(2,1)S(1)}, bf16[4,6144]{1,0:T(4,128)(2,1)S(1)}, u32[]{:S(2)}, u32[]{:S(2)}) %collective-permute-start.8) | collective-permute-done | bytes 49184 | tf_op jit(solution)/shard_map/ppermute | solution.py:25
  31.1 0.8 %multiply_subtract_fusion = (f32[4,6144]{1,0:T(4,128)}, f32[4,6144]{1,0:T(4,128)}, f32[4,6144]{1,0:T(4,128)}) fusion(f32[4,6144]{1,0:T(4,128)S(1)} %copy-done, f32[4,6144]{1,0:T(4,128)S(1)} %get-tuple-element.8, f32[4,6144]{1,0:T(4,128)S(1)} %copy-done.2, f32[4,6144]{1,0:T(4,128)S(1)} %copy-done.1), kind=kLoop, calls=%fused_computation.29 | loop fusion | flops 368640 | bytes 688128 | tf_op jit(solution)/shard_map/sub | solution.py:214
  32.0 1.5 %collective-permute-done.10.cross = bf16[4,6144]{1,0:T(4,128)(2,1)S(1)} collective-permute-done((bf16[4,6144]{1,0:T(4,128)(2,1)S(1)}, bf16[4,6144]{1,0:T(4,128)(2,1)S(1)}, u32[]{:S(2)}, u32[]{:S(2)}) %collective-permute-start.10) | collective-permute-done | bytes 49184 | tf_op jit(solution)/shard_map/ppermute | solution.py:25
  33.5 1.0 %collective-permute-done.11.side = bf16[2,4,6144]{2,1,0:T(4,128)(2,1)S(1)} collective-permute-done((bf16[2,4,6144]{2,1,0:T(4,128)(2,1)S(1)}, bf16[2,4,6144]{2,1,0:T(4,128)(2,1)S(1)}, u32[]{:S(2)}, u32[]{:S(2)}) %collective-permute-start.11) | collective-permute-done | bytes 98336 | tf_op jit(solution)/shard_map/ppermute | solution.py:25
  34.5 0.8 %shard_map.85 = bf16[4,49152]{1,0:T(4,128)(2,1)} custom-call(bf16[4,6144]{1,0:T(4,128)(2,1)S(1)} %subtract_convert_fusion.mine, bf16[4,6144]{1,0:T(4,128)(2,1)S(1)} %collective-permute-done.9.far, bf16[4,6144]{1,0:T(4,128)(2,1)S(1)} %collective-permute-done.8.corner, bf16[4,6144]{1,0:T(4,128)(2,1)S(1)} %collective-permute-done.10.cross, ...), custom_call_target="tpu_custom_call" | custom-call | bytes 786432 | tf_op jit(solution)/shard_map/pallas_call | solution.py:175
  (16 shorter events, 0.2 us)
Async XLA Ops:
  2.4 1.6 %collective-permute-start = (bf16[4,8,3072]{2,1,0:T(8,128)(2,1)S(1)}, bf16[4,8,3072]{2,1,0:T(8,128)(2,1)S(1)}, u32[]{:S(2)}, u32[]{:S(2)}) collective-permute-start(bf16[4,8,3072]{2,1,0:T(8,128)(2,1)S(1)} %get-tuple-element.14), channel_id=1, source_target_pairs={{0,1},{1,0},{2,3},{3,2},{4,5},{5,4},{6,7},{7,6},{8,9},{9,8},{10,11... | collective-permute-start | bytes 589832 | tf_op jit(solution)/shard_map/ppermute | solution.py:25
  2.9 5.0 %collective-permute-start.1 = (bf16[3,4,8,3072]{3,2,1,0:T(8,128)(2,1)S(1)}, bf16[3,4,8,3072]{3,2,1,0:T(8,128)(2,1)S(1)}, u32[]{:S(2)}, u32[]{:S(2)}) collective-permute-start(bf16[3,4,8,3072]{3,2,1,0:T(8,128)(2,1)S(1)} %get-tuple-element.16), channel_id=1, source_target_pairs={{0,1},{1,0},{2,3},{3,2},{4,5},{5,4},{6,7},{7,6},{8,9},{9,8},{10,11... | collective-permute-start | bytes 1769480 | tf_op jit(solution)/shard_map/ppermute | solution.py:25
  4.0 7.5 %collective-permute-start.2 = (f16[4,8,3072]{2,1,0:T(8,128)(2,1)S(1)}, f16[4,8,3072]{2,1,0:T(8,128)(2,1)S(1)}, u32[]{:S(2)}, u32[]{:S(2)}) collective-permute-start(f16[4,8,3072]{2,1,0:T(8,128)(2,1)S(1)} %fusion.1), channel_id=1, source_target_pairs={{0,6},{1,17},{2,4},{3,19},{4,2},{5,21},{6,0},{7,23},{8,14},{9,25},... | collective-permute-start | bytes 589832 | tf_op jit(solution)/shard_map/ppermute | solution.py:25
  8.1 6.1 %collective-permute-start.4 = (f16[4,8,3072]{2,1,0:T(8,128)(2,1)S(1)}, f16[4,8,3072]{2,1,0:T(8,128)(2,1)S(1)}, u32[]{:S(2)}, u32[]{:S(2)}) collective-permute-start(f16[4,8,3072]{2,1,0:T(8,128)(2,1)S(1)} %get-tuple-element.25), channel_id=1, source_target_pairs={{0,2},{1,25},{2,0},{3,27},{4,6},{5,29},{6,4},{7,31},{8,10},{9,17},... | collective-permute-start | bytes 589832 | tf_op jit(solution)/shard_map/ppermute | solution.py:25
  8.7 14.5 %copy-start = (f32[4,6144]{1,0:T(4,128)S(1)}, f32[4,6144]{1,0:T(4,128)}, u32[]{:S(2)}) copy-start(f32[4,6144]{1,0:T(4,128)} %param.5) | copy-start | bytes 294916
  8.7 14.6 %copy-start.1 = (f32[4,6144]{1,0:T(4,128)S(1)}, f32[4,6144]{1,0:T(4,128)}, u32[]{:S(2)}) copy-start(f32[4,6144]{1,0:T(4,128)} %param.7) | copy-start | bytes 294916
  8.7 14.6 %copy-start.2 = (f32[4,6144]{1,0:T(4,128)S(1)}, f32[4,6144]{1,0:T(4,128)}, u32[]{:S(2)}) copy-start(f32[4,6144]{1,0:T(4,128)} %param.6) | copy-start | bytes 294916
  8.7 5.7 %collective-permute-start.3 = (f16[4,8,3072]{2,1,0:T(8,128)(2,1)S(1)}, f16[4,8,3072]{2,1,0:T(8,128)(2,1)S(1)}, u32[]{:S(2)}, u32[]{:S(2)}) collective-permute-start(f16[4,8,3072]{2,1,0:T(8,128)(2,1)S(1)} %get-tuple-element.24), channel_id=1, source_target_pairs={{0,4},{1,9},{2,6},{3,11},{4,0},{5,13},{6,2},{7,15},{8,12},{9,1},{1... | collective-permute-start | bytes 589832 | tf_op jit(solution)/shard_map/ppermute | solution.py:25
  14.5 6.0 %collective-permute-start.7 = (f16[8,3072]{1,0:T(8,128)(2,1)S(1)}, f16[8,3072]{1,0:T(8,128)(2,1)S(1)}, u32[]{:S(2)}, u32[]{:S(2)}) collective-permute-start(f16[8,3072]{1,0:T(8,128)(2,1)S(1)} %get-tuple-element.27), channel_id=1, source_target_pairs={{0,24},{1,7},{2,26},{3,5},{4,28},{5,3},{6,30},{7,1},{8,16},{9,15},... | collective-permute-start | bytes 147464 | tf_op jit(solution)/shard_map/ppermute | solution.py:25
  18.2 5.0 %collective-permute-start.6 = (f16[8,3072]{1,0:T(8,128)(2,1)S(1)}, f16[8,3072]{1,0:T(8,128)(2,1)S(1)}, u32[]{:S(2)}, u32[]{:S(2)}) collective-permute-start(f16[8,3072]{1,0:T(8,128)(2,1)S(1)} %get-tuple-element.28), channel_id=1, source_target_pairs={{0,16},{1,3},{2,18},{3,1},{4,20},{5,7},{6,22},{7,5},{8,24},{9,11},... | collective-permute-start | bytes 147464 | tf_op jit(solution)/shard_map/ppermute | solution.py:25
  18.2 5.0 %collective-permute-start.5 = (f16[8,3072]{1,0:T(8,128)(2,1)S(1)}, f16[8,3072]{1,0:T(8,128)(2,1)S(1)}, u32[]{:S(2)}, u32[]{:S(2)}) collective-permute-start(f16[8,3072]{1,0:T(8,128)(2,1)S(1)} %get-tuple-element.26), channel_id=1, source_target_pairs={{0,8},{1,5},{2,10},{3,7},{4,12},{5,1},{6,14},{7,3},{8,0},{9,13},{1... | collective-permute-start | bytes 147464 | tf_op jit(solution)/shard_map/ppermute | solution.py:25
  23.4 11.9 %copy-start.3 = (f32[4,6144]{1,0:T(4,128)}, f32[4,6144]{1,0:T(4,128)S(1)}, u32[]{:S(2)}) copy-start(f32[4,6144]{1,0:T(4,128)S(1)} %get-tuple-element.8) | copy-start | bytes 294916
  23.4 6.0 %collective-permute-start.9 = (bf16[4,6144]{1,0:T(4,128)(2,1)S(1)}, bf16[4,6144]{1,0:T(4,128)(2,1)S(1)}, u32[]{:S(2)}, u32[]{:S(2)}) collective-permute-start(bf16[4,6144]{1,0:T(4,128)(2,1)S(1)} %get-tuple-element.20), channel_id=1, source_target_pairs={{0,16},{1,17},{2,18},{3,19},{4,20},{5,21},{6,22},{7,23},{8,24},{9,... | collective-permute-start | bytes 147464 | tf_op jit(solution)/shard_map/ppermute | solution.py:25
  25.7 5.4 %collective-permute-start.8 = (bf16[4,6144]{1,0:T(4,128)(2,1)S(1)}, bf16[4,6144]{1,0:T(4,128)(2,1)S(1)}, u32[]{:S(2)}, u32[]{:S(2)}) collective-permute-start(bf16[4,6144]{1,0:T(4,128)(2,1)S(1)} %subtract_convert_fusion.mine), channel_id=1, source_target_pairs={{0,12},{1,29},{2,14},{3,31},{4,8},{5,25},{6,10},{7,27},{8,4},{9,21... | collective-permute-start | bytes 147464 | tf_op jit(solution)/shard_map/ppermute | solution.py:25
  26.5 6.9 %collective-permute-start.10 = (bf16[4,6144]{1,0:T(4,128)(2,1)S(1)}, bf16[4,6144]{1,0:T(4,128)(2,1)S(1)}, u32[]{:S(2)}, u32[]{:S(2)}) collective-permute-start(bf16[4,6144]{1,0:T(4,128)(2,1)S(1)} %subtract_convert_fusion.mine), channel_id=1, source_target_pairs={{0,28},{1,13},{2,30},{3,15},{4,24},{5,9},{6,26},{7,11},{8,20},{9,5... | collective-permute-start | bytes 147464 | tf_op jit(solution)/shard_map/ppermute | solution.py:25
  29.5 5.0 %collective-permute-start.11 = (bf16[2,4,6144]{2,1,0:T(4,128)(2,1)S(1)}, bf16[2,4,6144]{2,1,0:T(4,128)(2,1)S(1)}, u32[]{:S(2)}, u32[]{:S(2)}) collective-permute-start(bf16[2,4,6144]{2,1,0:T(4,128)(2,1)S(1)} %pad_maximum_fusion.1), channel_id=1, source_target_pairs={{0,8},{1,5},{2,10},{3,7},{4,12},{5,1},{6,14},{7,3},{8,0},{9,13},{1... | collective-permute-start | bytes 294920 | tf_op jit(solution)/shard_map/ppermute | solution.py:25
  29.6 4.9 %collective-permute-start.12 = (bf16[2,4,6144]{2,1,0:T(4,128)(2,1)S(1)}, bf16[2,4,6144]{2,1,0:T(4,128)(2,1)S(1)}, u32[]{:S(2)}, u32[]{:S(2)}) collective-permute-start(bf16[2,4,6144]{2,1,0:T(4,128)(2,1)S(1)} %pad_maximum_fusion.1), channel_id=1, source_target_pairs={{0,4},{1,9},{2,6},{3,11},{4,0},{5,13},{6,2},{7,15},{8,12},{9,1},{1... | collective-permute-start | bytes 294920 | tf_op jit(solution)/shard_map/ppermute | solution.py:25

commit v19 on v18

--- a/solution.py
+++ b/solution.py
@@ -80,7 +80,7 @@
 
         @pl.when(step != 3)
         def _():
-            others[step, member] = rows
+            others[jnp.minimum(step, 2), member] = rows
 
     for i in range(8):
         copies[i].wait()
@@ -166,9 +166,9 @@
         copy.wait()
 
 
-def gather_blocks(first, mine):
+def gather_blocks(mine):
     row_block, col_block = mine.shape
-    far = swap(first, Z_FAR, Z_FAR)
+    far = swap(mine, Z_FAR, Z_FAR)
     corner, cross = swap(mine, Z_NEAR + Y, Z_FAR + Z_NEAR + Y), swap(mine, Z_FAR + Z_NEAR + Y, Z_NEAR + Y)
     pair = jnp.stack([mine, far])
     side, other_side = swap(pair, Z_NEAR, Y), swap(pair, Y, Z_NEAR)
@@ -219,14 +219,12 @@
     tuned = lax.axis_size("local") == 4 and lax.axis_size("hst") == 8
     gradient = grads[0, 0]
     grad_total = reduce_blocks(gradient) if tuned else reduce_general(gradient)
-    first = adam(grad_total, master, moment_one, moment_two)[0].astype(jnp.bfloat16)
-    again, first = lax.optimization_barrier((grad_total, first))
-    mine = adam(again, master, moment_one, moment_two)[0].astype(jnp.bfloat16)
+    mine = adam(grad_total, master, moment_one, moment_two)[0].astype(jnp.bfloat16)
     if tuned:
-        secondary, corner = gather_blocks(first, mine)
+        secondary, corner = gather_blocks(mine)
     else:
         secondary = corner = lax.all_gather(mine, "hst", axis=1, tiled=True)
-    grad_total, _ = lax.optimization_barrier((again, corner))
+    grad_total, _ = lax.optimization_barrier((grad_total, corner))
     new_master, new_one, new_two = adam(grad_total, master, moment_one, moment_two)
     return (grad_total, new_master, new_one, new_two, secondary)
 

time: 35.5 us -> 35.5 us (level)
  waiting for transfers between devices: 13 us -> 13.5 us
    ppermute x13, waiting for transfers between devices: 13 us -> 13.5 us  [swap(): return lax.ppermute(value, ('hst', 'local'), flip_pairs(flips))]
  transfers between devices with their start and end apart: 13 -> 13, of which waited for: 10 -> 10; matrix products, arithmetic and copies ran while one was open for 4% -> 3% of each run, Pallas kernels for 1% -> 1%
where the time goes in v19:
time: 35.5 us; the launch traced here: 35.3 us
  starting transfers between devices  16.4 us (46%)
  waiting for transfers between devices  13.5 us (38%)
  Pallas kernels  3.04 us (9%)
  other arithmetic  1.56 us (4%)
  between operations  0.75 us (2%)
    ppermute x13, starting transfers between devices, swap(): return lax.ppermute(value, ('hst', 'local'), flip_pairs(flips))  16.4 us
    ppermute x13, waiting for transfers between devices, swap(): return lax.ppermute(value, ('hst', 'local'), flip_pairs(flips))  13.5 us
    pallas_call x2, Pallas kernels, call(): pl.pallas_call(kernel, in_specs=[pl.BlockSpec(memory_space=space)], out_s...  2.24 us
    sub x1, other arithmetic, adam(): new_master = master - learn_rate * (update + decay_rate * master)  0.84 us
    pallas_call x1, Pallas kernels, gather_blocks(): pl.pallas_call(join_kernel, in_specs=[pl.BlockSpec(memory_space=pl.ANY)]...  0.8 us
  transfers between devices with their start and end apart: 13, of which 10 were waited for; matrix products, arithmetic and copies ran while one was open for 3% of the time, Pallas kernels for 1%

profile of v19, /device:TPU:0, one launch (start us, length us, event | category | flops | bytes accessed | tf_op | source)
XLA Modules:
  0.0 35.3 jit_solution(6133337453015024815)
XLA Ops:
  0.6 1.8 %shard_map.83 = (bf16[4,8,3072]{2,1,0:T(8,128)(2,1)S(1)}, bf16[3,4,8,3072]{3,2,1,0:T(8,128)(2,1)S(1)}, bf16[16,49152]{1,0:T(8,128)(2,1)S(1)}) custom-call(bf16[16,49152]{1,0:T(8,128)(2,1)} %bitcast.28), custom_call_target="tpu_custom_call" | custom-call | flops 786432 | bytes 3145728 | tf_op jit(solution)/shard_map/pallas_call | solution.py:103
  2.4 0.5 %collective-permute-start = (bf16[4,8,3072]{2,1,0:T(8,128)(2,1)S(1)}, bf16[4,8,3072]{2,1,0:T(8,128)(2,1)S(1)}, u32[]{:S(2)}, u32[]{:S(2)}) collective-permute-start(bf16[4,8,3072]{2,1,0:T(8,128)(2,1)S(1)} %get-tuple-element.12), channel_id=1, source_target_pairs={{0,1},{1,0},{2,3},{3,2},{4,5},{5,4},{6,7},{7,6},{8,9},{9,8},{10,11... | collective-permute-start | bytes 589832 | tf_op jit(solution)/shard_map/ppermute | solution.py:25
  2.9 0.1 collective-permute-start.1
  3.0 0.5 %shard_map.84 = bf16[4,4,8,3072]{3,2,1,0:T(8,128)(2,1)S(1)} custom-call(bf16[16,49152]{1,0:T(8,128)(2,1)S(1)} %get-tuple-element.11.landed), custom_call_target="tpu_custom_call" | custom-call | flops 786432 | bytes 3145728 | tf_op jit(solution)/shard_map/pallas_call | solution.py:103
  3.5 0.5 %collective-permute-done = bf16[4,8,3072]{2,1,0:T(8,128)(2,1)S(1)} collective-permute-done((bf16[4,8,3072]{2,1,0:T(8,128)(2,1)S(1)}, bf16[4,8,3072]{2,1,0:T(8,128)(2,1)S(1)}, u32[]{:S(2)}, u32[]{:S(2)}) %collective-permute-start) | collective-permute-done | bytes 196640 | tf_op jit(solution)/shard_map/ppermute | solution.py:25
  4.0 0.1 fusion.1
  4.1 3.9 %collective-permute-start.2 = (f16[4,8,3072]{2,1,0:T(8,128)(2,1)S(1)}, f16[4,8,3072]{2,1,0:T(8,128)(2,1)S(1)}, u32[]{:S(2)}, u32[]{:S(2)}) collective-permute-start(f16[4,8,3072]{2,1,0:T(8,128)(2,1)S(1)} %fusion.1), channel_id=1, source_target_pairs={{0,6},{1,17},{2,4},{3,19},{4,2},{5,21},{6,0},{7,23},{8,14},{9,25},... | collective-permute-start | bytes 589832 | tf_op jit(solution)/shard_map/ppermute | solution.py:25
  7.9 0.1 fusion.2
  8.1 0.6 %collective-permute-start.4 = (f16[4,8,3072]{2,1,0:T(8,128)(2,1)S(1)}, f16[4,8,3072]{2,1,0:T(8,128)(2,1)S(1)}, u32[]{:S(2)}, u32[]{:S(2)}) collective-permute-start(f16[4,8,3072]{2,1,0:T(8,128)(2,1)S(1)} %get-tuple-element.21), channel_id=1, source_target_pairs={{0,2},{1,25},{2,0},{3,27},{4,6},{5,29},{6,4},{7,31},{8,10},{9,17},... | collective-permute-start | bytes 589832 | tf_op jit(solution)/shard_map/ppermute | solution.py:25
  8.7 0.7 %collective-permute-start.3 = (f16[4,8,3072]{2,1,0:T(8,128)(2,1)S(1)}, f16[4,8,3072]{2,1,0:T(8,128)(2,1)S(1)}, u32[]{:S(2)}, u32[]{:S(2)}) collective-permute-start(f16[4,8,3072]{2,1,0:T(8,128)(2,1)S(1)} %get-tuple-element.20), channel_id=1, source_target_pairs={{0,4},{1,9},{2,6},{3,11},{4,0},{5,13},{6,2},{7,15},{8,12},{9,1},{1... | collective-permute-start | bytes 589832 | tf_op jit(solution)/shard_map/ppermute | solution.py:25
  9.4 2.2 %collective-permute-done.2 = f16[4,8,3072]{2,1,0:T(8,128)(2,1)S(1)} collective-permute-done((f16[4,8,3072]{2,1,0:T(8,128)(2,1)S(1)}, f16[4,8,3072]{2,1,0:T(8,128)(2,1)S(1)}, u32[]{:S(2)}, u32[]{:S(2)}) %collective-permute-start.2) | collective-permute-done | bytes 196640 | tf_op jit(solution)/shard_map/ppermute | solution.py:25
  11.6 0.1 bitcast_add_fusion
  11.7 2.6 %collective-permute-done.4 = f16[4,8,3072]{2,1,0:T(8,128)(2,1)S(1)} collective-permute-done((f16[4,8,3072]{2,1,0:T(8,128)(2,1)S(1)}, f16[4,8,3072]{2,1,0:T(8,128)(2,1)S(1)}, u32[]{:S(2)}, u32[]{:S(2)}) %collective-permute-start.4) | collective-permute-done | bytes 196640 | tf_op jit(solution)/shard_map/ppermute | solution.py:25
  14.2 0.1 collective-permute-done.3
  14.4 0.1 multiply_add_fusion
  14.5 3.7 %collective-permute-start.7 = (f16[8,3072]{1,0:T(8,128)(2,1)S(1)}, f16[8,3072]{1,0:T(8,128)(2,1)S(1)}, u32[]{:S(2)}, u32[]{:S(2)}) collective-permute-start(f16[8,3072]{1,0:T(8,128)(2,1)S(1)} %get-tuple-element.23), channel_id=1, source_target_pairs={{0,24},{1,7},{2,26},{3,5},{4,28},{5,3},{6,30},{7,1},{8,16},{9,15},... | collective-permute-start | bytes 147464 | tf_op jit(solution)/shard_map/ppermute | solution.py:25
  18.2 0.8 %collective-permute-start.5 = (f16[8,3072]{1,0:T(8,128)(2,1)S(1)}, f16[8,3072]{1,0:T(8,128)(2,1)S(1)}, u32[]{:S(2)}, u32[]{:S(2)}) collective-permute-start(f16[8,3072]{1,0:T(8,128)(2,1)S(1)} %get-tuple-element.22), channel_id=1, source_target_pairs={{0,8},{1,5},{2,10},{3,7},{4,12},{5,1},{6,14},{7,3},{8,0},{9,13},{1... | collective-permute-start | bytes 147464 | tf_op jit(solution)/shard_map/ppermute | solution.py:25
  19.0 1.5 %collective-permute-done.7 = f16[8,3072]{1,0:T(8,128)(2,1)S(1)} collective-permute-done((f16[8,3072]{1,0:T(8,128)(2,1)S(1)}, f16[8,3072]{1,0:T(8,128)(2,1)S(1)}, u32[]{:S(2)}, u32[]{:S(2)}) %collective-permute-start.7) | collective-permute-done | bytes 49184 | tf_op jit(solution)/shard_map/ppermute | solution.py:25
  20.5 2.7 %collective-permute-done.6 = f16[8,3072]{1,0:T(8,128)(2,1)S(1)} collective-permute-done((f16[8,3072]{1,0:T(8,128)(2,1)S(1)}, f16[8,3072]{1,0:T(8,128)(2,1)S(1)}, u32[]{:S(2)}, u32[]{:S(2)}) %collective-permute-start.6) | collective-permute-done | bytes 49184 | tf_op jit(solution)/shard_map/ppermute | solution.py:25
  23.3 0.2 subtract_convert_fusion
  23.5 2.1 %collective-permute-start.9 = (bf16[4,6144]{1,0:T(4,128)(2,1)S(1)}, bf16[4,6144]{1,0:T(4,128)(2,1)S(1)}, u32[]{:S(2)}, u32[]{:S(2)}) collective-permute-start(bf16[4,6144]{1,0:T(4,128)(2,1)S(1)} %get-tuple-element.25.mine), channel_id=1, source_target_pairs={{0,16},{1,17},{2,18},{3,19},{4,20},{5,21},{6,22},{7,23},{8,24},{9,... | collective-permute-start | bytes 147464 | tf_op jit(solution)/shard_map/ppermute | solution.py:25
  25.6 0.7 %collective-permute-start.8 = (bf16[4,6144]{1,0:T(4,128)(2,1)S(1)}, bf16[4,6144]{1,0:T(4,128)(2,1)S(1)}, u32[]{:S(2)}, u32[]{:S(2)}) collective-permute-start(bf16[4,6144]{1,0:T(4,128)(2,1)S(1)} %get-tuple-element.25.mine), channel_id=1, source_target_pairs={{0,12},{1,29},{2,14},{3,31},{4,8},{5,25},{6,10},{7,27},{8,4},{9,21... | collective-permute-start | bytes 147464 | tf_op jit(solution)/shard_map/ppermute | solution.py:25
  26.3 2.5 %collective-permute-start.10 = (bf16[4,6144]{1,0:T(4,128)(2,1)S(1)}, bf16[4,6144]{1,0:T(4,128)(2,1)S(1)}, u32[]{:S(2)}, u32[]{:S(2)}) collective-permute-start(bf16[4,6144]{1,0:T(4,128)(2,1)S(1)} %get-tuple-element.25.mine), channel_id=1, source_target_pairs={{0,28},{1,13},{2,30},{3,15},{4,24},{5,9},{6,26},{7,11},{8,20},{9,5... | collective-permute-start | bytes 147464 | tf_op jit(solution)/shard_map/ppermute | solution.py:25
  28.8 0.6 %collective-permute-done.9.far = bf16[4,6144]{1,0:T(4,128)(2,1)S(1)} collective-permute-done((bf16[4,6144]{1,0:T(4,128)(2,1)S(1)}, bf16[4,6144]{1,0:T(4,128)(2,1)S(1)}, u32[]{:S(2)}, u32[]{:S(2)}) %collective-permute-start.9) | collective-permute-done | bytes 49184 | tf_op jit(solution)/shard_map/ppermute | solution.py:25
  29.4 0.1 pad_maximum_fusion.1
  29.5 0.1 collective-permute-start.11
  29.6 0.8 %collective-permute-start.12 = (bf16[2,4,6144]{2,1,0:T(4,128)(2,1)S(1)}, bf16[2,4,6144]{2,1,0:T(4,128)(2,1)S(1)}, u32[]{:S(2)}, u32[]{:S(2)}) collective-permute-start(bf16[2,4,6144]{2,1,0:T(4,128)(2,1)S(1)} %pad_maximum_fusion.1), channel_id=1, source_target_pairs={{0,4},{1,9},{2,6},{3,11},{4,0},{5,13},{6,2},{7,15},{8,12},{9,1},{1... | collective-permute-start | bytes 294920 | tf_op jit(solution)/shard_map/ppermute | solution.py:25
  30.4 0.5 %collective-permute-done.8.corner = bf16[4,6144]{1,0:T(4,128)(2,1)S(1)} collective-permute-done((bf16[4,6144]{1,0:T(4,128)(2,1)S(1)}, bf16[4,6144]{1,0:T(4,128)(2,1)S(1)}, u32[]{:S(2)}, u32[]{:S(2)}) %collective-permute-start.8) | collective-permute-done | bytes 49184 | tf_op jit(solution)/shard_map/ppermute | solution.py:25
  30.9 0.8 %multiply_subtract_fusion = (f32[4,6144]{1,0:T(4,128)}, f32[4,6144]{1,0:T(4,128)}, f32[4,6144]{1,0:T(4,128)}) fusion(f32[4,6144]{1,0:T(4,128)S(1)} %copy-done, f32[4,6144]{1,0:T(4,128)S(1)} %get-tuple-element.6, f32[4,6144]{1,0:T(4,128)S(1)} %copy-done.2, f32[4,6144]{1,0:T(4,128)S(1)} %copy-done.1), kind=kLoop, calls=%fused_computation.23 | loop fusion | flops 368640 | bytes 688128 | tf_op jit(solution)/shard_map/sub | solution.py:214
  31.7 1.5 %collective-permute-done.10.cross = bf16[4,6144]{1,0:T(4,128)(2,1)S(1)} collective-permute-done((bf16[4,6144]{1,0:T(4,128)(2,1)S(1)}, bf16[4,6144]{1,0:T(4,128)(2,1)S(1)}, u32[]{:S(2)}, u32[]{:S(2)}) %collective-permute-start.10) | collective-permute-done | bytes 49184 | tf_op jit(solution)/shard_map/ppermute | solution.py:25
  33.3 1.2 %collective-permute-done.11.side = bf16[2,4,6144]{2,1,0:T(4,128)(2,1)S(1)} collective-permute-done((bf16[2,4,6144]{2,1,0:T(4,128)(2,1)S(1)}, bf16[2,4,6144]{2,1,0:T(4,128)(2,1)S(1)}, u32[]{:S(2)}, u32[]{:S(2)}) %collective-permute-start.11) | collective-permute-done | bytes 98336 | tf_op jit(solution)/shard_map/ppermute | solution.py:25
  34.5 0.8 %shard_map.85 = bf16[4,49152]{1,0:T(4,128)(2,1)} custom-call(bf16[4,6144]{1,0:T(4,128)(2,1)S(1)} %get-tuple-element.25.mine, bf16[4,6144]{1,0:T(4,128)(2,1)S(1)} %collective-permute-done.9.far, bf16[4,6144]{1,0:T(4,128)(2,1)S(1)} %collective-permute-done.8.corner, bf16[4,6144]{1,0:T(4,128)(2,1)S(1)} %collective-permute-done.10.cross, ...), custom_call_target="tpu_custom_call" | custom-call | bytes 786432 | tf_op jit(solution)/shard_map/pallas_call | solution.py:175
  (15 shorter events, 0.1 us)
Async XLA Ops:
  2.4 1.6 %collective-permute-start = (bf16[4,8,3072]{2,1,0:T(8,128)(2,1)S(1)}, bf16[4,8,3072]{2,1,0:T(8,128)(2,1)S(1)}, u32[]{:S(2)}, u32[]{:S(2)}) collective-permute-start(bf16[4,8,3072]{2,1,0:T(8,128)(2,1)S(1)} %get-tuple-element.12), channel_id=1, source_target_pairs={{0,1},{1,0},{2,3},{3,2},{4,5},{5,4},{6,7},{7,6},{8,9},{9,8},{10,11... | collective-permute-start | bytes 589832 | tf_op jit(solution)/shard_map/ppermute | solution.py:25
  2.9 5.0 %collective-permute-start.1 = (bf16[3,4,8,3072]{3,2,1,0:T(8,128)(2,1)S(1)}, bf16[3,4,8,3072]{3,2,1,0:T(8,128)(2,1)S(1)}, u32[]{:S(2)}, u32[]{:S(2)}) collective-permute-start(bf16[3,4,8,3072]{3,2,1,0:T(8,128)(2,1)S(1)} %get-tuple-element.14), channel_id=1, source_target_pairs={{0,1},{1,0},{2,3},{3,2},{4,5},{5,4},{6,7},{7,6},{8,9},{9,8},{10,11... | collective-permute-start | bytes 1769480 | tf_op jit(solution)/shard_map/ppermute | solution.py:25
  4.1 7.5 %collective-permute-start.2 = (f16[4,8,3072]{2,1,0:T(8,128)(2,1)S(1)}, f16[4,8,3072]{2,1,0:T(8,128)(2,1)S(1)}, u32[]{:S(2)}, u32[]{:S(2)}) collective-permute-start(f16[4,8,3072]{2,1,0:T(8,128)(2,1)S(1)} %fusion.1), channel_id=1, source_target_pairs={{0,6},{1,17},{2,4},{3,19},{4,2},{5,21},{6,0},{7,23},{8,14},{9,25},... | collective-permute-start | bytes 589832 | tf_op jit(solution)/shard_map/ppermute | solution.py:25
  8.1 6.1 %collective-permute-start.4 = (f16[4,8,3072]{2,1,0:T(8,128)(2,1)S(1)}, f16[4,8,3072]{2,1,0:T(8,128)(2,1)S(1)}, u32[]{:S(2)}, u32[]{:S(2)}) collective-permute-start(f16[4,8,3072]{2,1,0:T(8,128)(2,1)S(1)} %get-tuple-element.21), channel_id=1, source_target_pairs={{0,2},{1,25},{2,0},{3,27},{4,6},{5,29},{6,4},{7,31},{8,10},{9,17},... | collective-permute-start | bytes 589832 | tf_op jit(solution)/shard_map/ppermute | solution.py:25
  8.7 14.5 %copy-start = (f32[4,6144]{1,0:T(4,128)S(1)}, f32[4,6144]{1,0:T(4,128)}, u32[]{:S(2)}) copy-start(f32[4,6144]{1,0:T(4,128)} %param.5) | copy-start | bytes 294916
  8.7 14.6 %copy-start.1 = (f32[4,6144]{1,0:T(4,128)S(1)}, f32[4,6144]{1,0:T(4,128)}, u32[]{:S(2)}) copy-start(f32[4,6144]{1,0:T(4,128)} %param.7) | copy-start | bytes 294916
  8.7 14.6 %copy-start.2 = (f32[4,6144]{1,0:T(4,128)S(1)}, f32[4,6144]{1,0:T(4,128)}, u32[]{:S(2)}) copy-start(f32[4,6144]{1,0:T(4,128)} %param.6) | copy-start | bytes 294916
  8.7 5.7 %collective-permute-start.3 = (f16[4,8,3072]{2,1,0:T(8,128)(2,1)S(1)}, f16[4,8,3072]{2,1,0:T(8,128)(2,1)S(1)}, u32[]{:S(2)}, u32[]{:S(2)}) collective-permute-start(f16[4,8,3072]{2,1,0:T(8,128)(2,1)S(1)} %get-tuple-element.20), channel_id=1, source_target_pairs={{0,4},{1,9},{2,6},{3,11},{4,0},{5,13},{6,2},{7,15},{8,12},{9,1},{1... | collective-permute-start | bytes 589832 | tf_op jit(solution)/shard_map/ppermute | solution.py:25
  14.5 6.0 %collective-permute-start.7 = (f16[8,3072]{1,0:T(8,128)(2,1)S(1)}, f16[8,3072]{1,0:T(8,128)(2,1)S(1)}, u32[]{:S(2)}, u32[]{:S(2)}) collective-permute-start(f16[8,3072]{1,0:T(8,128)(2,1)S(1)} %get-tuple-element.23), channel_id=1, source_target_pairs={{0,24},{1,7},{2,26},{3,5},{4,28},{5,3},{6,30},{7,1},{8,16},{9,15},... | collective-permute-start | bytes 147464 | tf_op jit(solution)/shard_map/ppermute | solution.py:25
  18.2 5.0 %collective-permute-start.6 = (f16[8,3072]{1,0:T(8,128)(2,1)S(1)}, f16[8,3072]{1,0:T(8,128)(2,1)S(1)}, u32[]{:S(2)}, u32[]{:S(2)}) collective-permute-start(f16[8,3072]{1,0:T(8,128)(2,1)S(1)} %get-tuple-element.24), channel_id=1, source_target_pairs={{0,16},{1,3},{2,18},{3,1},{4,20},{5,7},{6,22},{7,5},{8,24},{9,11},... | collective-permute-start | bytes 147464 | tf_op jit(solution)/shard_map/ppermute | solution.py:25
  18.2 5.0 %collective-permute-start.5 = (f16[8,3072]{1,0:T(8,128)(2,1)S(1)}, f16[8,3072]{1,0:T(8,128)(2,1)S(1)}, u32[]{:S(2)}, u32[]{:S(2)}) collective-permute-start(f16[8,3072]{1,0:T(8,128)(2,1)S(1)} %get-tuple-element.22), channel_id=1, source_target_pairs={{0,8},{1,5},{2,10},{3,7},{4,12},{5,1},{6,14},{7,3},{8,0},{9,13},{1... | collective-permute-start | bytes 147464 | tf_op jit(solution)/shard_map/ppermute | solution.py:25
  23.5 11.8 %copy-start.3 = (f32[4,6144]{1,0:T(4,128)}, f32[4,6144]{1,0:T(4,128)S(1)}, u32[]{:S(2)}) copy-start(f32[4,6144]{1,0:T(4,128)S(1)} %get-tuple-element.6) | copy-start | bytes 294916
  23.5 6.0 %collective-permute-start.9 = (bf16[4,6144]{1,0:T(4,128)(2,1)S(1)}, bf16[4,6144]{1,0:T(4,128)(2,1)S(1)}, u32[]{:S(2)}, u32[]{:S(2)}) collective-permute-start(bf16[4,6144]{1,0:T(4,128)(2,1)S(1)} %get-tuple-element.25.mine), channel_id=1, source_target_pairs={{0,16},{1,17},{2,18},{3,19},{4,20},{5,21},{6,22},{7,23},{8,24},{9,... | collective-permute-start | bytes 147464 | tf_op jit(solution)/shard_map/ppermute | solution.py:25
  25.6 5.3 %collective-permute-start.8 = (bf16[4,6144]{1,0:T(4,128)(2,1)S(1)}, bf16[4,6144]{1,0:T(4,128)(2,1)S(1)}, u32[]{:S(2)}, u32[]{:S(2)}) collective-permute-start(bf16[4,6144]{1,0:T(4,128)(2,1)S(1)} %get-tuple-element.25.mine), channel_id=1, source_target_pairs={{0,12},{1,29},{2,14},{3,31},{4,8},{5,25},{6,10},{7,27},{8,4},{9,21... | collective-permute-start | bytes 147464 | tf_op jit(solution)/shard_map/ppermute | solution.py:25
  26.3 6.9 %collective-permute-start.10 = (bf16[4,6144]{1,0:T(4,128)(2,1)S(1)}, bf16[4,6144]{1,0:T(4,128)(2,1)S(1)}, u32[]{:S(2)}, u32[]{:S(2)}) collective-permute-start(bf16[4,6144]{1,0:T(4,128)(2,1)S(1)} %get-tuple-element.25.mine), channel_id=1, source_target_pairs={{0,28},{1,13},{2,30},{3,15},{4,24},{5,9},{6,26},{7,11},{8,20},{9,5... | collective-permute-start | bytes 147464 | tf_op jit(solution)/shard_map/ppermute | solution.py:25
  29.5 5.0 %collective-permute-start.11 = (bf16[2,4,6144]{2,1,0:T(4,128)(2,1)S(1)}, bf16[2,4,6144]{2,1,0:T(4,128)(2,1)S(1)}, u32[]{:S(2)}, u32[]{:S(2)}) collective-permute-start(bf16[2,4,6144]{2,1,0:T(4,128)(2,1)S(1)} %pad_maximum_fusion.1), channel_id=1, source_target_pairs={{0,8},{1,5},{2,10},{3,7},{4,12},{5,1},{6,14},{7,3},{8,0},{9,13},{1... | collective-permute-start | bytes 294920 | tf_op jit(solution)/shard_map/ppermute | solution.py:25
  29.6 4.9 %collective-permute-start.12 = (bf16[2,4,6144]{2,1,0:T(4,128)(2,1)S(1)}, bf16[2,4,6144]{2,1,0:T(4,128)(2,1)S(1)}, u32[]{:S(2)}, u32[]{:S(2)}) collective-permute-start(bf16[2,4,6144]{2,1,0:T(4,128)(2,1)S(1)} %pad_maximum_fusion.1), channel_id=1, source_target_pairs={{0,4},{1,9},{2,6},{3,11},{4,0},{5,13},{6,2},{7,15},{8,12},{9,1},{1... | collective-permute-start | bytes 294920 | tf_op jit(solution)/shard_map/ppermute | solution.py:25

commit v20 on v19

--- a/solution.py
+++ b/solution.py
@@ -154,7 +154,7 @@
     cols = mine.shape[1]
     me, core = lax.axis_index("hst"), place()[3]
     bits = lambda at_0, at_1: jnp.where(core == 0, at_0, at_1)
-    pieces = [(0, mine), (4, far), (bits(3, 7), corner), (bits(7, 3), cross)]
+    pieces = [(0, mine), (4, far), (3, corner), (7, cross)]
     pieces += [(bits(2, 1) + 4 * i, side.at[i]) for i in (0, 1)]
     pieces += [(bits(1, 2) + 4 * i, other_side.at[i]) for i in (0, 1)]
     copies = []
@@ -169,7 +169,7 @@
 def gather_blocks(mine):
     row_block, col_block = mine.shape
     far = swap(mine, Z_FAR, Z_FAR)
-    corner, cross = swap(mine, Z_NEAR + Y, Z_FAR + Z_NEAR + Y), swap(mine, Z_FAR + Z_NEAR + Y, Z_NEAR + Y)
+    corner, cross = [swap(mine, to, to) for to in (Z_NEAR + Y, Z_FAR + Z_NEAR + Y)]
     pair = jnp.stack([mine, far])
     side, other_side = swap(pair, Z_NEAR, Y), swap(pair, Y, Z_NEAR)
     whole = pl.pallas_call(

time: 35.5 us -> 35.8 us (level)
  no operation moved by 1% of the time
where the time goes in v20:
time: 35.8 us; the launch traced here: 35.6 us
  starting transfers between devices  16.6 us (46%)
  waiting for transfers between devices  13.7 us (38%)
  Pallas kernels  3.04 us (8%)
  other arithmetic  1.56 us (4%)
  between operations  0.75 us (2%)
    ppermute x13, starting transfers between devices, swap(): return lax.ppermute(value, ('hst', 'local'), flip_pairs(flips))  16.6 us
    ppermute x13, waiting for transfers between devices, swap(): return lax.ppermute(value, ('hst', 'local'), flip_pairs(flips))  13.7 us
    pallas_call x2, Pallas kernels, call(): pl.pallas_call(kernel, in_specs=[pl.BlockSpec(memory_space=space)], out_s...  2.24 us
    sub x1, other arithmetic, adam(): new_master = master - learn_rate * (update + decay_rate * master)  0.84 us
    pallas_call x1, Pallas kernels, gather_blocks(): pl.pallas_call(join_kernel, in_specs=[pl.BlockSpec(memory_space=pl.ANY)]...  0.8 us
  transfers between devices with their start and end apart: 13, of which 10 were waited for; matrix products, arithmetic and copies ran while one was open for 3% of the time, Pallas kernels for 1%

profile of v20, /device:TPU:0, one launch (start us, length us, event | category | flops | bytes accessed | tf_op | source)
XLA Modules:
  0.0 35.6 jit_solution(1657715329284769047)
XLA Ops:
  0.6 1.8 %shard_map.83 = (bf16[4,8,3072]{2,1,0:T(8,128)(2,1)S(1)}, bf16[3,4,8,3072]{3,2,1,0:T(8,128)(2,1)S(1)}, bf16[16,49152]{1,0:T(8,128)(2,1)S(1)}) custom-call(bf16[16,49152]{1,0:T(8,128)(2,1)} %bitcast.28), custom_call_target="tpu_custom_call" | custom-call | flops 786432 | bytes 3145728 | tf_op jit(solution)/shard_map/pallas_call | solution.py:103
  2.4 0.5 %collective-permute-start = (bf16[4,8,3072]{2,1,0:T(8,128)(2,1)S(1)}, bf16[4,8,3072]{2,1,0:T(8,128)(2,1)S(1)}, u32[]{:S(2)}, u32[]{:S(2)}) collective-permute-start(bf16[4,8,3072]{2,1,0:T(8,128)(2,1)S(1)} %get-tuple-element.12), channel_id=1, source_target_pairs={{0,1},{1,0},{2,3},{3,2},{4,5},{5,4},{6,7},{7,6},{8,9},{9,8},{10,11... | collective-permute-start | bytes 589832 | tf_op jit(solution)/shard_map/ppermute | solution.py:25
  2.9 0.1 collective-permute-start.1
  3.0 0.5 %shard_map.84 = bf16[4,4,8,3072]{3,2,1,0:T(8,128)(2,1)S(1)} custom-call(bf16[16,49152]{1,0:T(8,128)(2,1)S(1)} %get-tuple-element.11.landed), custom_call_target="tpu_custom_call" | custom-call | flops 786432 | bytes 3145728 | tf_op jit(solution)/shard_map/pallas_call | solution.py:103
  3.5 0.5 %collective-permute-done = bf16[4,8,3072]{2,1,0:T(8,128)(2,1)S(1)} collective-permute-done((bf16[4,8,3072]{2,1,0:T(8,128)(2,1)S(1)}, bf16[4,8,3072]{2,1,0:T(8,128)(2,1)S(1)}, u32[]{:S(2)}, u32[]{:S(2)}) %collective-permute-start) | collective-permute-done | bytes 196640 | tf_op jit(solution)/shard_map/ppermute | solution.py:25
  4.0 0.1 fusion.1
  4.1 3.9 %collective-permute-start.2 = (f16[4,8,3072]{2,1,0:T(8,128)(2,1)S(1)}, f16[4,8,3072]{2,1,0:T(8,128)(2,1)S(1)}, u32[]{:S(2)}, u32[]{:S(2)}) collective-permute-start(f16[4,8,3072]{2,1,0:T(8,128)(2,1)S(1)} %fusion.1), channel_id=1, source_target_pairs={{0,6},{1,17},{2,4},{3,19},{4,2},{5,21},{6,0},{7,23},{8,14},{9,25},... | collective-permute-start | bytes 589832 | tf_op jit(solution)/shard_map/ppermute | solution.py:25
  7.9 0.1 fusion.2
  8.1 0.6 %collective-permute-start.4 = (f16[4,8,3072]{2,1,0:T(8,128)(2,1)S(1)}, f16[4,8,3072]{2,1,0:T(8,128)(2,1)S(1)}, u32[]{:S(2)}, u32[]{:S(2)}) collective-permute-start(f16[4,8,3072]{2,1,0:T(8,128)(2,1)S(1)} %get-tuple-element.21), channel_id=1, source_target_pairs={{0,2},{1,25},{2,0},{3,27},{4,6},{5,29},{6,4},{7,31},{8,10},{9,17},... | collective-permute-start | bytes 589832 | tf_op jit(solution)/shard_map/ppermute | solution.py:25
  8.7 0.7 %collective-permute-start.3 = (f16[4,8,3072]{2,1,0:T(8,128)(2,1)S(1)}, f16[4,8,3072]{2,1,0:T(8,128)(2,1)S(1)}, u32[]{:S(2)}, u32[]{:S(2)}) collective-permute-start(f16[4,8,3072]{2,1,0:T(8,128)(2,1)S(1)} %get-tuple-element.20), channel_id=1, source_target_pairs={{0,4},{1,9},{2,6},{3,11},{4,0},{5,13},{6,2},{7,15},{8,12},{9,1},{1... | collective-permute-start | bytes 589832 | tf_op jit(solution)/shard_map/ppermute | solution.py:25
  9.4 2.2 %collective-permute-done.2 = f16[4,8,3072]{2,1,0:T(8,128)(2,1)S(1)} collective-permute-done((f16[4,8,3072]{2,1,0:T(8,128)(2,1)S(1)}, f16[4,8,3072]{2,1,0:T(8,128)(2,1)S(1)}, u32[]{:S(2)}, u32[]{:S(2)}) %collective-permute-start.2) | collective-permute-done | bytes 196640 | tf_op jit(solution)/shard_map/ppermute | solution.py:25
  11.6 0.1 bitcast_add_fusion
  11.7 2.6 %collective-permute-done.4 = f16[4,8,3072]{2,1,0:T(8,128)(2,1)S(1)} collective-permute-done((f16[4,8,3072]{2,1,0:T(8,128)(2,1)S(1)}, f16[4,8,3072]{2,1,0:T(8,128)(2,1)S(1)}, u32[]{:S(2)}, u32[]{:S(2)}) %collective-permute-start.4) | collective-permute-done | bytes 196640 | tf_op jit(solution)/shard_map/ppermute | solution.py:25
  14.2 0.1 collective-permute-done.3
  14.4 0.1 multiply_add_fusion
  14.5 3.7 %collective-permute-start.7 = (f16[8,3072]{1,0:T(8,128)(2,1)S(1)}, f16[8,3072]{1,0:T(8,128)(2,1)S(1)}, u32[]{:S(2)}, u32[]{:S(2)}) collective-permute-start(f16[8,3072]{1,0:T(8,128)(2,1)S(1)} %get-tuple-element.23), channel_id=1, source_target_pairs={{0,24},{1,7},{2,26},{3,5},{4,28},{5,3},{6,30},{7,1},{8,16},{9,15},... | collective-permute-start | bytes 147464 | tf_op jit(solution)/shard_map/ppermute | solution.py:25
  18.2 0.8 %collective-permute-start.5 = (f16[8,3072]{1,0:T(8,128)(2,1)S(1)}, f16[8,3072]{1,0:T(8,128)(2,1)S(1)}, u32[]{:S(2)}, u32[]{:S(2)}) collective-permute-start(f16[8,3072]{1,0:T(8,128)(2,1)S(1)} %get-tuple-element.22), channel_id=1, source_target_pairs={{0,8},{1,5},{2,10},{3,7},{4,12},{5,1},{6,14},{7,3},{8,0},{9,13},{1... | collective-permute-start | bytes 147464 | tf_op jit(solution)/shard_map/ppermute | solution.py:25
  19.0 1.5 %collective-permute-done.7 = f16[8,3072]{1,0:T(8,128)(2,1)S(1)} collective-permute-done((f16[8,3072]{1,0:T(8,128)(2,1)S(1)}, f16[8,3072]{1,0:T(8,128)(2,1)S(1)}, u32[]{:S(2)}, u32[]{:S(2)}) %collective-permute-start.7) | collective-permute-done | bytes 49184 | tf_op jit(solution)/shard_map/ppermute | solution.py:25
  20.5 2.7 %collective-permute-done.6 = f16[8,3072]{1,0:T(8,128)(2,1)S(1)} collective-permute-done((f16[8,3072]{1,0:T(8,128)(2,1)S(1)}, f16[8,3072]{1,0:T(8,128)(2,1)S(1)}, u32[]{:S(2)}, u32[]{:S(2)}) %collective-permute-start.6) | collective-permute-done | bytes 49184 | tf_op jit(solution)/shard_map/ppermute | solution.py:25
  23.3 0.2 subtract_convert_fusion
  23.5 2.1 %collective-permute-start.9 = (bf16[4,6144]{1,0:T(4,128)(2,1)S(1)}, bf16[4,6144]{1,0:T(4,128)(2,1)S(1)}, u32[]{:S(2)}, u32[]{:S(2)}) collective-permute-start(bf16[4,6144]{1,0:T(4,128)(2,1)S(1)} %get-tuple-element.25.mine), channel_id=1, source_target_pairs={{0,16},{1,17},{2,18},{3,19},{4,20},{5,21},{6,22},{7,23},{8,24},{9,... | collective-permute-start | bytes 147464 | tf_op jit(solution)/shard_map/ppermute | solution.py:25
  25.6 0.7 %collective-permute-start.8 = (bf16[4,6144]{1,0:T(4,128)(2,1)S(1)}, bf16[4,6144]{1,0:T(4,128)(2,1)S(1)}, u32[]{:S(2)}, u32[]{:S(2)}) collective-permute-start(bf16[4,6144]{1,0:T(4,128)(2,1)S(1)} %get-tuple-element.25.mine), channel_id=1, source_target_pairs={{0,12},{1,13},{2,14},{3,15},{4,8},{5,9},{6,10},{7,11},{8,4},{9,5},... | collective-permute-start | bytes 147464 | tf_op jit(solution)/shard_map/ppermute | solution.py:25
  26.3 2.5 %collective-permute-start.10 = (bf16[4,6144]{1,0:T(4,128)(2,1)S(1)}, bf16[4,6144]{1,0:T(4,128)(2,1)S(1)}, u32[]{:S(2)}, u32[]{:S(2)}) collective-permute-start(bf16[4,6144]{1,0:T(4,128)(2,1)S(1)} %get-tuple-element.25.mine), channel_id=1, source_target_pairs={{0,28},{1,29},{2,30},{3,31},{4,24},{5,25},{6,26},{7,27},{8,20},{9,... | collective-permute-start | bytes 147464 | tf_op jit(solution)/shard_map/ppermute | solution.py:25
  28.8 0.4 %collective-permute-done.9.far = bf16[4,6144]{1,0:T(4,128)(2,1)S(1)} collective-permute-done((bf16[4,6144]{1,0:T(4,128)(2,1)S(1)}, bf16[4,6144]{1,0:T(4,128)(2,1)S(1)}, u32[]{:S(2)}, u32[]{:S(2)}) %collective-permute-start.9) | collective-permute-done | bytes 49184 | tf_op jit(solution)/shard_map/ppermute | solution.py:25
  29.3 0.1 pad_maximum_fusion.1
  29.3 0.1 collective-permute-start.11
  29.4 0.9 %collective-permute-start.12 = (bf16[2,4,6144]{2,1,0:T(4,128)(2,1)S(1)}, bf16[2,4,6144]{2,1,0:T(4,128)(2,1)S(1)}, u32[]{:S(2)}, u32[]{:S(2)}) collective-permute-start(bf16[2,4,6144]{2,1,0:T(4,128)(2,1)S(1)} %pad_maximum_fusion.1), channel_id=1, source_target_pairs={{0,4},{1,9},{2,6},{3,11},{4,0},{5,13},{6,2},{7,15},{8,12},{9,1},{1... | collective-permute-start | bytes 294920 | tf_op jit(solution)/shard_map/ppermute | solution.py:25
  30.4 0.2 collective-permute-done.8.corner
  30.6 0.8 %multiply_subtract_fusion = (f32[4,6144]{1,0:T(4,128)}, f32[4,6144]{1,0:T(4,128)}, f32[4,6144]{1,0:T(4,128)}) fusion(f32[4,6144]{1,0:T(4,128)S(1)} %copy-done, f32[4,6144]{1,0:T(4,128)S(1)} %get-tuple-element.6, f32[4,6144]{1,0:T(4,128)S(1)} %copy-done.2, f32[4,6144]{1,0:T(4,128)S(1)} %copy-done.1), kind=kLoop, calls=%fused_computation.23 | loop fusion | flops 368640 | bytes 688128 | tf_op jit(solution)/shard_map/sub | solution.py:214
  31.4 1.8 %collective-permute-done.10.cross = bf16[4,6144]{1,0:T(4,128)(2,1)S(1)} collective-permute-done((bf16[4,6144]{1,0:T(4,128)(2,1)S(1)}, bf16[4,6144]{1,0:T(4,128)(2,1)S(1)}, u32[]{:S(2)}, u32[]{:S(2)}) %collective-permute-start.10) | collective-permute-done | bytes 49184 | tf_op jit(solution)/shard_map/ppermute | solution.py:25
  33.3 1.6 %collective-permute-done.11.side = bf16[2,4,6144]{2,1,0:T(4,128)(2,1)S(1)} collective-permute-done((bf16[2,4,6144]{2,1,0:T(4,128)(2,1)S(1)}, bf16[2,4,6144]{2,1,0:T(4,128)(2,1)S(1)}, u32[]{:S(2)}, u32[]{:S(2)}) %collective-permute-start.11) | collective-permute-done | bytes 98336 | tf_op jit(solution)/shard_map/ppermute | solution.py:25
  34.8 0.8 %shard_map.85 = bf16[4,49152]{1,0:T(4,128)(2,1)} custom-call(bf16[4,6144]{1,0:T(4,128)(2,1)S(1)} %get-tuple-element.25.mine, bf16[4,6144]{1,0:T(4,128)(2,1)S(1)} %collective-permute-done.9.far, bf16[4,6144]{1,0:T(4,128)(2,1)S(1)} %collective-permute-done.8.corner, bf16[4,6144]{1,0:T(4,128)(2,1)S(1)} %collective-permute-done.10.cross, ...), custom_call_target="tpu_custom_call" | custom-call | bytes 786432 | tf_op jit(solution)/shard_map/pallas_call | solution.py:175
  (15 shorter events, 0.1 us)
Async XLA Ops:
  2.4 1.6 %collective-permute-start = (bf16[4,8,3072]{2,1,0:T(8,128)(2,1)S(1)}, bf16[4,8,3072]{2,1,0:T(8,128)(2,1)S(1)}, u32[]{:S(2)}, u32[]{:S(2)}) collective-permute-start(bf16[4,8,3072]{2,1,0:T(8,128)(2,1)S(1)} %get-tuple-element.12), channel_id=1, source_target_pairs={{0,1},{1,0},{2,3},{3,2},{4,5},{5,4},{6,7},{7,6},{8,9},{9,8},{10,11... | collective-permute-start | bytes 589832 | tf_op jit(solution)/shard_map/ppermute | solution.py:25
  2.9 5.0 %collective-permute-start.1 = (bf16[3,4,8,3072]{3,2,1,0:T(8,128)(2,1)S(1)}, bf16[3,4,8,3072]{3,2,1,0:T(8,128)(2,1)S(1)}, u32[]{:S(2)}, u32[]{:S(2)}) collective-permute-start(bf16[3,4,8,3072]{3,2,1,0:T(8,128)(2,1)S(1)} %get-tuple-element.14), channel_id=1, source_target_pairs={{0,1},{1,0},{2,3},{3,2},{4,5},{5,4},{6,7},{7,6},{8,9},{9,8},{10,11... | collective-permute-start | bytes 1769480 | tf_op jit(solution)/shard_map/ppermute | solution.py:25
  4.1 7.5 %collective-permute-start.2 = (f16[4,8,3072]{2,1,0:T(8,128)(2,1)S(1)}, f16[4,8,3072]{2,1,0:T(8,128)(2,1)S(1)}, u32[]{:S(2)}, u32[]{:S(2)}) collective-permute-start(f16[4,8,3072]{2,1,0:T(8,128)(2,1)S(1)} %fusion.1), channel_id=1, source_target_pairs={{0,6},{1,17},{2,4},{3,19},{4,2},{5,21},{6,0},{7,23},{8,14},{9,25},... | collective-permute-start | bytes 589832 | tf_op jit(solution)/shard_map/ppermute | solution.py:25
  8.1 6.1 %collective-permute-start.4 = (f16[4,8,3072]{2,1,0:T(8,128)(2,1)S(1)}, f16[4,8,3072]{2,1,0:T(8,128)(2,1)S(1)}, u32[]{:S(2)}, u32[]{:S(2)}) collective-permute-start(f16[4,8,3072]{2,1,0:T(8,128)(2,1)S(1)} %get-tuple-element.21), channel_id=1, source_target_pairs={{0,2},{1,25},{2,0},{3,27},{4,6},{5,29},{6,4},{7,31},{8,10},{9,17},... | collective-permute-start | bytes 589832 | tf_op jit(solution)/shard_map/ppermute | solution.py:25
  8.7 14.5 %copy-start = (f32[4,6144]{1,0:T(4,128)S(1)}, f32[4,6144]{1,0:T(4,128)}, u32[]{:S(2)}) copy-start(f32[4,6144]{1,0:T(4,128)} %param.5) | copy-start | bytes 294916
  8.7 14.6 %copy-start.1 = (f32[4,6144]{1,0:T(4,128)S(1)}, f32[4,6144]{1,0:T(4,128)}, u32[]{:S(2)}) copy-start(f32[4,6144]{1,0:T(4,128)} %param.7) | copy-start | bytes 294916
  8.7 14.6 %copy-start.2 = (f32[4,6144]{1,0:T(4,128)S(1)}, f32[4,6144]{1,0:T(4,128)}, u32[]{:S(2)}) copy-start(f32[4,6144]{1,0:T(4,128)} %param.6) | copy-start | bytes 294916
  8.7 5.7 %collective-permute-start.3 = (f16[4,8,3072]{2,1,0:T(8,128)(2,1)S(1)}, f16[4,8,3072]{2,1,0:T(8,128)(2,1)S(1)}, u32[]{:S(2)}, u32[]{:S(2)}) collective-permute-start(f16[4,8,3072]{2,1,0:T(8,128)(2,1)S(1)} %get-tuple-element.20), channel_id=1, source_target_pairs={{0,4},{1,9},{2,6},{3,11},{4,0},{5,13},{6,2},{7,15},{8,12},{9,1},{1... | collective-permute-start | bytes 589832 | tf_op jit(solution)/shard_map/ppermute | solution.py:25
  14.5 6.0 %collective-permute-start.7 = (f16[8,3072]{1,0:T(8,128)(2,1)S(1)}, f16[8,3072]{1,0:T(8,128)(2,1)S(1)}, u32[]{:S(2)}, u32[]{:S(2)}) collective-permute-start(f16[8,3072]{1,0:T(8,128)(2,1)S(1)} %get-tuple-element.23), channel_id=1, source_target_pairs={{0,24},{1,7},{2,26},{3,5},{4,28},{5,3},{6,30},{7,1},{8,16},{9,15},... | collective-permute-start | bytes 147464 | tf_op jit(solution)/shard_map/ppermute | solution.py:25
  18.2 5.0 %collective-permute-start.6 = (f16[8,3072]{1,0:T(8,128)(2,1)S(1)}, f16[8,3072]{1,0:T(8,128)(2,1)S(1)}, u32[]{:S(2)}, u32[]{:S(2)}) collective-permute-start(f16[8,3072]{1,0:T(8,128)(2,1)S(1)} %get-tuple-element.24), channel_id=1, source_target_pairs={{0,16},{1,3},{2,18},{3,1},{4,20},{5,7},{6,22},{7,5},{8,24},{9,11},... | collective-permute-start | bytes 147464 | tf_op jit(solution)/shard_map/ppermute | solution.py:25
  18.2 5.0 %collective-permute-start.5 = (f16[8,3072]{1,0:T(8,128)(2,1)S(1)}, f16[8,3072]{1,0:T(8,128)(2,1)S(1)}, u32[]{:S(2)}, u32[]{:S(2)}) collective-permute-start(f16[8,3072]{1,0:T(8,128)(2,1)S(1)} %get-tuple-element.22), channel_id=1, source_target_pairs={{0,8},{1,5},{2,10},{3,7},{4,12},{5,1},{6,14},{7,3},{8,0},{9,13},{1... | collective-permute-start | bytes 147464 | tf_op jit(solution)/shard_map/ppermute | solution.py:25
  23.5 12.2 %copy-start.3 = (f32[4,6144]{1,0:T(4,128)}, f32[4,6144]{1,0:T(4,128)S(1)}, u32[]{:S(2)}) copy-start(f32[4,6144]{1,0:T(4,128)S(1)} %get-tuple-element.6) | copy-start | bytes 294916
  23.5 5.8 %collective-permute-start.9 = (bf16[4,6144]{1,0:T(4,128)(2,1)S(1)}, bf16[4,6144]{1,0:T(4,128)(2,1)S(1)}, u32[]{:S(2)}, u32[]{:S(2)}) collective-permute-start(bf16[4,6144]{1,0:T(4,128)(2,1)S(1)} %get-tuple-element.25.mine), channel_id=1, source_target_pairs={{0,16},{1,17},{2,18},{3,19},{4,20},{5,21},{6,22},{7,23},{8,24},{9,... | collective-permute-start | bytes 147464 | tf_op jit(solution)/shard_map/ppermute | solution.py:25
  25.6 5.0 %collective-permute-start.8 = (bf16[4,6144]{1,0:T(4,128)(2,1)S(1)}, bf16[4,6144]{1,0:T(4,128)(2,1)S(1)}, u32[]{:S(2)}, u32[]{:S(2)}) collective-permute-start(bf16[4,6144]{1,0:T(4,128)(2,1)S(1)} %get-tuple-element.25.mine), channel_id=1, source_target_pairs={{0,12},{1,13},{2,14},{3,15},{4,8},{5,9},{6,10},{7,11},{8,4},{9,5},... | collective-permute-start | bytes 147464 | tf_op jit(solution)/shard_map/ppermute | solution.py:25
  26.3 6.9 %collective-permute-start.10 = (bf16[4,6144]{1,0:T(4,128)(2,1)S(1)}, bf16[4,6144]{1,0:T(4,128)(2,1)S(1)}, u32[]{:S(2)}, u32[]{:S(2)}) collective-permute-start(bf16[4,6144]{1,0:T(4,128)(2,1)S(1)} %get-tuple-element.25.mine), channel_id=1, source_target_pairs={{0,28},{1,29},{2,30},{3,31},{4,24},{5,25},{6,26},{7,27},{8,20},{9,... | collective-permute-start | bytes 147464 | tf_op jit(solution)/shard_map/ppermute | solution.py:25
  29.3 5.5 %collective-permute-start.11 = (bf16[2,4,6144]{2,1,0:T(4,128)(2,1)S(1)}, bf16[2,4,6144]{2,1,0:T(4,128)(2,1)S(1)}, u32[]{:S(2)}, u32[]{:S(2)}) collective-permute-start(bf16[2,4,6144]{2,1,0:T(4,128)(2,1)S(1)} %pad_maximum_fusion.1), channel_id=1, source_target_pairs={{0,8},{1,5},{2,10},{3,7},{4,12},{5,1},{6,14},{7,3},{8,0},{9,13},{1... | collective-permute-start | bytes 294920 | tf_op jit(solution)/shard_map/ppermute | solution.py:25
  29.4 5.4 %collective-permute-start.12 = (bf16[2,4,6144]{2,1,0:T(4,128)(2,1)S(1)}, bf16[2,4,6144]{2,1,0:T(4,128)(2,1)S(1)}, u32[]{:S(2)}, u32[]{:S(2)}) collective-permute-start(bf16[2,4,6144]{2,1,0:T(4,128)(2,1)S(1)} %pad_maximum_fusion.1), channel_id=1, source_target_pairs={{0,4},{1,9},{2,6},{3,11},{4,0},{5,13},{6,2},{7,15},{8,12},{9,1},{1... | collective-permute-start | bytes 294920 | tf_op jit(solution)/shard_map/ppermute | solution.py:25

commit v21 on v20

--- a/solution.py
+++ b/solution.py
@@ -150,13 +150,12 @@
     return jnp.concatenate([total[: tile // 2], total[tile // 2 :]], axis=1)
 
 
-def join_kernel(mine, far, corner, cross, side, other_side, whole, left):
+def join_kernel(mine, far, beside, cross, three, small, whole, left):
     cols = mine.shape[1]
     me, core = lax.axis_index("hst"), place()[3]
     bits = lambda at_0, at_1: jnp.where(core == 0, at_0, at_1)
-    pieces = [(0, mine), (4, far), (3, corner), (7, cross)]
-    pieces += [(bits(2, 1) + 4 * i, side.at[i]) for i in (0, 1)]
-    pieces += [(bits(1, 2) + 4 * i, other_side.at[i]) for i in (0, 1)]
+    pieces = [(0, mine), (4, far), (bits(2, 1), beside), (7, cross)]
+    pieces += [(bits(1, 2), three.at[0]), (bits(5, 6), three.at[1]), (3, three.at[2]), (bits(6, 5), small)]
     copies = []
     for i, (away, block) in enumerate(pieces):
         at = pl.multiple_of((me ^ away) * cols, 128)
@@ -169,9 +168,10 @@
 def gather_blocks(mine):
     row_block, col_block = mine.shape
     far = swap(mine, Z_FAR, Z_FAR)
-    corner, cross = [swap(mine, to, to) for to in (Z_NEAR + Y, Z_FAR + Z_NEAR + Y)]
-    pair = jnp.stack([mine, far])
-    side, other_side = swap(pair, Z_NEAR, Y), swap(pair, Y, Z_NEAR)
+    beside = swap(mine, Z_NEAR, Y)
+    cross = swap(mine, Z_FAR + Z_NEAR + Y, Z_FAR + Z_NEAR + Y)
+    three = swap(jnp.stack([mine, far, beside]), Y, Z_NEAR)
+    small = swap(far, Z_NEAR, Y)
     whole = pl.pallas_call(
         join_kernel,
         in_specs=[pl.BlockSpec(memory_space=pl.ANY)] * 6,
@@ -180,8 +180,8 @@
         scratch_shapes=[pltpu.SemaphoreType.DMA((8,))],
         compiler_params=pltpu.CompilerParams(vmem_limit_bytes=8 << 20),
         cost_estimate=pl.CostEstimate(flops=0, bytes_accessed=4 * 8 * mine.size, transcendentals=0),
-    )(mine, far, corner, cross, side, other_side)
-    return whole, corner
+    )(mine, far, beside, cross, three, small)
+    return whole, far
 
 
 def reduce_general(gradient):
@@ -221,10 +221,10 @@
     grad_total = reduce_blocks(gradient) if tuned else reduce_general(gradient)
     mine = adam(grad_total, master, moment_one, moment_two)[0].astype(jnp.bfloat16)
     if tuned:
-        secondary, corner = gather_blocks(mine)
+        secondary, early = gather_blocks(mine)
     else:
-        secondary = corner = lax.all_gather(mine, "hst", axis=1, tiled=True)
-    grad_total, _ = lax.optimization_barrier((grad_total, corner))
+        secondary = early = lax.all_gather(mine, "hst", axis=1, tiled=True)
+    grad_total, _ = lax.optimization_barrier((grad_total, early))
     new_master, new_one, new_two = adam(grad_total, master, moment_one, moment_two)
     return (grad_total, new_master, new_one, new_two, secondary)
 

time: 35.8 us -> 36.2 us (1.011)
  starting transfers between devices: 16.6 us -> 17.8 us
  waiting for transfers between devices: 13.7 us -> 12.8 us
    ppermute x13, starting transfers between devices: 16.6 us -> 17.8 us  [swap(): return lax.ppermute(value, ('hst', 'local'), flip_pairs(flips))]
    ppermute x13, waiting for transfers between devices: 13.7 us -> 12.8 us  [swap(): return lax.ppermute(value, ('hst', 'local'), flip_pairs(flips))]
  transfers between devices with their start and end apart: 13 -> 13, of which waited for: 10 -> 9; matrix products, arithmetic and copies ran while one was open for 3% -> 3% of each run, Pallas kernels for 1% -> 1%
where the time goes in v21:
time: 36.2 us; the launch traced here: 36.1 us
  starting transfers between devices  17.8 us (49%)
  waiting for transfers between devices  12.8 us (35%)
  Pallas kernels  3.04 us (8%)
  other arithmetic  1.61 us (4%)
  between operations  0.74 us (2%)
    ppermute x13, starting transfers between devices, swap(): return lax.ppermute(value, ('hst', 'local'), flip_pairs(flips))  17.8 us
    ppermute x13, waiting for transfers between devices, swap(): return lax.ppermute(value, ('hst', 'local'), flip_pairs(flips))  12.8 us
    pallas_call x2, Pallas kernels, call(): pl.pallas_call(kernel, in_specs=[pl.BlockSpec(memory_space=space)], out_s...  2.24 us
    sub x1, other arithmetic, adam(): new_master = master - learn_rate * (update + decay_rate * master)  0.84 us
    pallas_call x1, Pallas kernels, gather_blocks(): pl.pallas_call(join_kernel, in_specs=[pl.BlockSpec(memory_space=pl.ANY)]...  0.8 us
  transfers between devices with their start and end apart: 13, of which 9 were waited for; matrix products, arithmetic and copies ran while one was open for 3% of the time, Pallas kernels for 1%

profile of v21, /device:TPU:0, one launch (start us, length us, event | category | flops | bytes accessed | tf_op | source)
XLA Modules:
  0.0 36.1 jit_solution(7768122308210364214)
XLA Ops:
  0.6 1.8 %shard_map.83 = (bf16[4,8,3072]{2,1,0:T(8,128)(2,1)S(1)}, bf16[3,4,8,3072]{3,2,1,0:T(8,128)(2,1)S(1)}, bf16[16,49152]{1,0:T(8,128)(2,1)S(1)}) custom-call(bf16[16,49152]{1,0:T(8,128)(2,1)} %bitcast.30), custom_call_target="tpu_custom_call" | custom-call | flops 786432 | bytes 3145728 | tf_op jit(solution)/shard_map/pallas_call | solution.py:103
  2.4 0.5 %collective-permute-start = (bf16[4,8,3072]{2,1,0:T(8,128)(2,1)S(1)}, bf16[4,8,3072]{2,1,0:T(8,128)(2,1)S(1)}, u32[]{:S(2)}, u32[]{:S(2)}) collective-permute-start(bf16[4,8,3072]{2,1,0:T(8,128)(2,1)S(1)} %get-tuple-element.12), channel_id=1, source_target_pairs={{0,1},{1,0},{2,3},{3,2},{4,5},{5,4},{6,7},{7,6},{8,9},{9,8},{10,11... | collective-permute-start | bytes 589832 | tf_op jit(solution)/shard_map/ppermute | solution.py:25
  2.9 0.1 collective-permute-start.1
  3.0 0.5 %shard_map.84 = bf16[4,4,8,3072]{3,2,1,0:T(8,128)(2,1)S(1)} custom-call(bf16[16,49152]{1,0:T(8,128)(2,1)S(1)} %get-tuple-element.11.landed), custom_call_target="tpu_custom_call" | custom-call | flops 786432 | bytes 3145728 | tf_op jit(solution)/shard_map/pallas_call | solution.py:103
  3.5 0.5 %collective-permute-done = bf16[4,8,3072]{2,1,0:T(8,128)(2,1)S(1)} collective-permute-done((bf16[4,8,3072]{2,1,0:T(8,128)(2,1)S(1)}, bf16[4,8,3072]{2,1,0:T(8,128)(2,1)S(1)}, u32[]{:S(2)}, u32[]{:S(2)}) %collective-permute-start) | collective-permute-done | bytes 196640 | tf_op jit(solution)/shard_map/ppermute | solution.py:25
  4.0 0.1 fusion.1
  4.1 3.9 %collective-permute-start.2 = (f16[4,8,3072]{2,1,0:T(8,128)(2,1)S(1)}, f16[4,8,3072]{2,1,0:T(8,128)(2,1)S(1)}, u32[]{:S(2)}, u32[]{:S(2)}) collective-permute-start(f16[4,8,3072]{2,1,0:T(8,128)(2,1)S(1)} %fusion.1), channel_id=1, source_target_pairs={{0,6},{1,17},{2,4},{3,19},{4,2},{5,21},{6,0},{7,23},{8,14},{9,25},... | collective-permute-start | bytes 589832 | tf_op jit(solution)/shard_map/ppermute | solution.py:25
  7.9 0.0 collective-permute-done.1
  7.9 0.1 fusion.2
  8.1 0.6 %collective-permute-start.4 = (f16[4,8,3072]{2,1,0:T(8,128)(2,1)S(1)}, f16[4,8,3072]{2,1,0:T(8,128)(2,1)S(1)}, u32[]{:S(2)}, u32[]{:S(2)}) collective-permute-start(f16[4,8,3072]{2,1,0:T(8,128)(2,1)S(1)} %get-tuple-element.21), channel_id=1, source_target_pairs={{0,2},{1,25},{2,0},{3,27},{4,6},{5,29},{6,4},{7,31},{8,10},{9,17},... | collective-permute-start | bytes 589832 | tf_op jit(solution)/shard_map/ppermute | solution.py:25
  8.7 0.7 %collective-permute-start.3 = (f16[4,8,3072]{2,1,0:T(8,128)(2,1)S(1)}, f16[4,8,3072]{2,1,0:T(8,128)(2,1)S(1)}, u32[]{:S(2)}, u32[]{:S(2)}) collective-permute-start(f16[4,8,3072]{2,1,0:T(8,128)(2,1)S(1)} %get-tuple-element.20), channel_id=1, source_target_pairs={{0,4},{1,9},{2,6},{3,11},{4,0},{5,13},{6,2},{7,15},{8,12},{9,1},{1... | collective-permute-start | bytes 589832 | tf_op jit(solution)/shard_map/ppermute | solution.py:25
  9.4 2.2 %collective-permute-done.2 = f16[4,8,3072]{2,1,0:T(8,128)(2,1)S(1)} collective-permute-done((f16[4,8,3072]{2,1,0:T(8,128)(2,1)S(1)}, f16[4,8,3072]{2,1,0:T(8,128)(2,1)S(1)}, u32[]{:S(2)}, u32[]{:S(2)}) %collective-permute-start.2) | collective-permute-done | bytes 196640 | tf_op jit(solution)/shard_map/ppermute | solution.py:25
  11.6 0.1 bitcast_add_fusion
  11.7 2.6 %collective-permute-done.4 = f16[4,8,3072]{2,1,0:T(8,128)(2,1)S(1)} collective-permute-done((f16[4,8,3072]{2,1,0:T(8,128)(2,1)S(1)}, f16[4,8,3072]{2,1,0:T(8,128)(2,1)S(1)}, u32[]{:S(2)}, u32[]{:S(2)}) %collective-permute-start.4) | collective-permute-done | bytes 196640 | tf_op jit(solution)/shard_map/ppermute | solution.py:25
  14.2 0.1 collective-permute-done.3
  14.4 0.1 multiply_add_fusion
  14.5 3.7 %collective-permute-start.7 = (f16[8,3072]{1,0:T(8,128)(2,1)S(1)}, f16[8,3072]{1,0:T(8,128)(2,1)S(1)}, u32[]{:S(2)}, u32[]{:S(2)}) collective-permute-start(f16[8,3072]{1,0:T(8,128)(2,1)S(1)} %get-tuple-element.23), channel_id=1, source_target_pairs={{0,24},{1,7},{2,26},{3,5},{4,28},{5,3},{6,30},{7,1},{8,16},{9,15},... | collective-permute-start | bytes 147464 | tf_op jit(solution)/shard_map/ppermute | solution.py:25
  18.2 0.8 %collective-permute-start.5 = (f16[8,3072]{1,0:T(8,128)(2,1)S(1)}, f16[8,3072]{1,0:T(8,128)(2,1)S(1)}, u32[]{:S(2)}, u32[]{:S(2)}) collective-permute-start(f16[8,3072]{1,0:T(8,128)(2,1)S(1)} %get-tuple-element.22), channel_id=1, source_target_pairs={{0,8},{1,5},{2,10},{3,7},{4,12},{5,1},{6,14},{7,3},{8,0},{9,13},{1... | collective-permute-start | bytes 147464 | tf_op jit(solution)/shard_map/ppermute | solution.py:25
  19.0 1.5 %collective-permute-done.7 = f16[8,3072]{1,0:T(8,128)(2,1)S(1)} collective-permute-done((f16[8,3072]{1,0:T(8,128)(2,1)S(1)}, f16[8,3072]{1,0:T(8,128)(2,1)S(1)}, u32[]{:S(2)}, u32[]{:S(2)}) %collective-permute-start.7) | collective-permute-done | bytes 49184 | tf_op jit(solution)/shard_map/ppermute | solution.py:25
  20.5 2.7 %collective-permute-done.6 = f16[8,3072]{1,0:T(8,128)(2,1)S(1)} collective-permute-done((f16[8,3072]{1,0:T(8,128)(2,1)S(1)}, f16[8,3072]{1,0:T(8,128)(2,1)S(1)}, u32[]{:S(2)}, u32[]{:S(2)}) %collective-permute-start.6) | collective-permute-done | bytes 49184 | tf_op jit(solution)/shard_map/ppermute | solution.py:25
  23.3 0.2 subtract_convert_fusion
  23.5 0.0 copy-start.3
  23.5 2.1 %collective-permute-start.8 = (bf16[4,6144]{1,0:T(4,128)(2,1)S(1)}, bf16[4,6144]{1,0:T(4,128)(2,1)S(1)}, u32[]{:S(2)}, u32[]{:S(2)}) collective-permute-start(bf16[4,6144]{1,0:T(4,128)(2,1)S(1)} %get-tuple-element.25.mine), channel_id=1, source_target_pairs={{0,16},{1,17},{2,18},{3,19},{4,20},{5,21},{6,22},{7,23},{8,24},{9,... | collective-permute-start | bytes 147464 | tf_op jit(solution)/shard_map/ppermute | solution.py:25
  25.6 3.1 %collective-permute-start.10 = (bf16[4,6144]{1,0:T(4,128)(2,1)S(1)}, bf16[4,6144]{1,0:T(4,128)(2,1)S(1)}, u32[]{:S(2)}, u32[]{:S(2)}) collective-permute-start(bf16[4,6144]{1,0:T(4,128)(2,1)S(1)} %get-tuple-element.25.mine), channel_id=1, source_target_pairs={{0,28},{1,29},{2,30},{3,31},{4,24},{5,25},{6,26},{7,27},{8,20},{9,... | collective-permute-start | bytes 147464 | tf_op jit(solution)/shard_map/ppermute | solution.py:25
  28.7 0.5 %collective-permute-done.8.far = bf16[4,6144]{1,0:T(4,128)(2,1)S(1)} collective-permute-done((bf16[4,6144]{1,0:T(4,128)(2,1)S(1)}, bf16[4,6144]{1,0:T(4,128)(2,1)S(1)}, u32[]{:S(2)}, u32[]{:S(2)}) %collective-permute-start.8) | collective-permute-done | bytes 49184 | tf_op jit(solution)/shard_map/ppermute | solution.py:25
  29.2 0.5 %collective-permute-done.9.beside = bf16[4,6144]{1,0:T(4,128)(2,1)S(1)} collective-permute-done((bf16[4,6144]{1,0:T(4,128)(2,1)S(1)}, bf16[4,6144]{1,0:T(4,128)(2,1)S(1)}, u32[]{:S(2)}, u32[]{:S(2)}) %collective-permute-start.9) | collective-permute-done | bytes 49184 | tf_op jit(solution)/shard_map/ppermute | solution.py:25
  29.7 0.1 pad_maximum_fusion
  29.8 1.3 %collective-permute-start.11 = (bf16[3,4,6144]{2,1,0:T(4,128)(2,1)S(1)}, bf16[3,4,6144]{2,1,0:T(4,128)(2,1)S(1)}, u32[]{:S(2)}, u32[]{:S(2)}) collective-permute-start(bf16[3,4,6144]{2,1,0:T(4,128)(2,1)S(1)} %pad_maximum_fusion), channel_id=1, source_target_pairs={{0,4},{1,9},{2,6},{3,11},{4,0},{5,13},{6,2},{7,15},{8,12},{9,1},{1... | collective-permute-start | bytes 442376 | tf_op jit(solution)/shard_map/ppermute | solution.py:25
  31.1 1.1 %collective-permute-start.12 = (bf16[4,6144]{1,0:T(4,128)(2,1)S(1)}, bf16[4,6144]{1,0:T(4,128)(2,1)S(1)}, u32[]{:S(2)}, u32[]{:S(2)}) collective-permute-start(bf16[4,6144]{1,0:T(4,128)(2,1)S(1)} %collective-permute-done.8.far), channel_id=1, source_target_pairs={{0,8},{1,5},{2,10},{3,7},{4,12},{5,1},{6,14},{7,3},{8,0},{9,13},{1... | collective-permute-start | bytes 147464 | tf_op jit(solution)/shard_map/ppermute | solution.py:25
  32.2 0.8 %multiply_subtract_fusion = (f32[4,6144]{1,0:T(4,128)}, f32[4,6144]{1,0:T(4,128)}, f32[4,6144]{1,0:T(4,128)}) fusion(f32[4,6144]{1,0:T(4,128)S(1)} %copy-done, f32[4,6144]{1,0:T(4,128)S(1)} %get-tuple-element.6, f32[4,6144]{1,0:T(4,128)S(1)} %copy-done.2, f32[4,6144]{1,0:T(4,128)S(1)} %copy-done.1), kind=kLoop, calls=%fused_computation.23 | loop fusion | flops 368640 | bytes 688128 | tf_op jit(solution)/shard_map/sub | solution.py:214
  33.0 2.2 %collective-permute-done.12.small = bf16[4,6144]{1,0:T(4,128)(2,1)S(1)} collective-permute-done((bf16[4,6144]{1,0:T(4,128)(2,1)S(1)}, bf16[4,6144]{1,0:T(4,128)(2,1)S(1)}, u32[]{:S(2)}, u32[]{:S(2)}) %collective-permute-start.12) | collective-permute-done | bytes 49184 | tf_op jit(solution)/shard_map/ppermute | solution.py:25
  35.2 0.8 %shard_map.85 = bf16[4,49152]{1,0:T(4,128)(2,1)} custom-call(bf16[4,6144]{1,0:T(4,128)(2,1)S(1)} %get-tuple-element.25.mine, bf16[4,6144]{1,0:T(4,128)(2,1)S(1)} %collective-permute-done.8.far, bf16[4,6144]{1,0:T(4,128)(2,1)S(1)} %collective-permute-done.9.beside, bf16[4,6144]{1,0:T(4,128)(2,1)S(1)} %collective-permute-done.10.cross, ...), custom_call_target="tpu_custom_call" | custom-call | bytes 786432 | tf_op jit(solution)/shard_map/pallas_call | solution.py:175
  (15 shorter events, 0.1 us)
Async XLA Ops:
  2.4 1.6 %collective-permute-start = (bf16[4,8,3072]{2,1,0:T(8,128)(2,1)S(1)}, bf16[4,8,3072]{2,1,0:T(8,128)(2,1)S(1)}, u32[]{:S(2)}, u32[]{:S(2)}) collective-permute-start(bf16[4,8,3072]{2,1,0:T(8,128)(2,1)S(1)} %get-tuple-element.12), channel_id=1, source_target_pairs={{0,1},{1,0},{2,3},{3,2},{4,5},{5,4},{6,7},{7,6},{8,9},{9,8},{10,11... | collective-permute-start | bytes 589832 | tf_op jit(solution)/shard_map/ppermute | solution.py:25
  2.9 5.0 %collective-permute-start.1 = (bf16[3,4,8,3072]{3,2,1,0:T(8,128)(2,1)S(1)}, bf16[3,4,8,3072]{3,2,1,0:T(8,128)(2,1)S(1)}, u32[]{:S(2)}, u32[]{:S(2)}) collective-permute-start(bf16[3,4,8,3072]{3,2,1,0:T(8,128)(2,1)S(1)} %get-tuple-element.14), channel_id=1, source_target_pairs={{0,1},{1,0},{2,3},{3,2},{4,5},{5,4},{6,7},{7,6},{8,9},{9,8},{10,11... | collective-permute-start | bytes 1769480 | tf_op jit(solution)/shard_map/ppermute | solution.py:25
  4.1 7.5 %collective-permute-start.2 = (f16[4,8,3072]{2,1,0:T(8,128)(2,1)S(1)}, f16[4,8,3072]{2,1,0:T(8,128)(2,1)S(1)}, u32[]{:S(2)}, u32[]{:S(2)}) collective-permute-start(f16[4,8,3072]{2,1,0:T(8,128)(2,1)S(1)} %fusion.1), channel_id=1, source_target_pairs={{0,6},{1,17},{2,4},{3,19},{4,2},{5,21},{6,0},{7,23},{8,14},{9,25},... | collective-permute-start | bytes 589832 | tf_op jit(solution)/shard_map/ppermute | solution.py:25
  8.1 6.1 %collective-permute-start.4 = (f16[4,8,3072]{2,1,0:T(8,128)(2,1)S(1)}, f16[4,8,3072]{2,1,0:T(8,128)(2,1)S(1)}, u32[]{:S(2)}, u32[]{:S(2)}) collective-permute-start(f16[4,8,3072]{2,1,0:T(8,128)(2,1)S(1)} %get-tuple-element.21), channel_id=1, source_target_pairs={{0,2},{1,25},{2,0},{3,27},{4,6},{5,29},{6,4},{7,31},{8,10},{9,17},... | collective-permute-start | bytes 589832 | tf_op jit(solution)/shard_map/ppermute | solution.py:25
  8.7 14.5 %copy-start = (f32[4,6144]{1,0:T(4,128)S(1)}, f32[4,6144]{1,0:T(4,128)}, u32[]{:S(2)}) copy-start(f32[4,6144]{1,0:T(4,128)} %param.5) | copy-start | bytes 294916
  8.7 14.6 %copy-start.1 = (f32[4,6144]{1,0:T(4,128)S(1)}, f32[4,6144]{1,0:T(4,128)}, u32[]{:S(2)}) copy-start(f32[4,6144]{1,0:T(4,128)} %param.7) | copy-start | bytes 294916
  8.7 14.6 %copy-start.2 = (f32[4,6144]{1,0:T(4,128)S(1)}, f32[4,6144]{1,0:T(4,128)}, u32[]{:S(2)}) copy-start(f32[4,6144]{1,0:T(4,128)} %param.6) | copy-start | bytes 294916
  8.7 5.7 %collective-permute-start.3 = (f16[4,8,3072]{2,1,0:T(8,128)(2,1)S(1)}, f16[4,8,3072]{2,1,0:T(8,128)(2,1)S(1)}, u32[]{:S(2)}, u32[]{:S(2)}) collective-permute-start(f16[4,8,3072]{2,1,0:T(8,128)(2,1)S(1)} %get-tuple-element.20), channel_id=1, source_target_pairs={{0,4},{1,9},{2,6},{3,11},{4,0},{5,13},{6,2},{7,15},{8,12},{9,1},{1... | collective-permute-start | bytes 589832 | tf_op jit(solution)/shard_map/ppermute | solution.py:25
  14.5 6.0 %collective-permute-start.7 = (f16[8,3072]{1,0:T(8,128)(2,1)S(1)}, f16[8,3072]{1,0:T(8,128)(2,1)S(1)}, u32[]{:S(2)}, u32[]{:S(2)}) collective-permute-start(f16[8,3072]{1,0:T(8,128)(2,1)S(1)} %get-tuple-element.23), channel_id=1, source_target_pairs={{0,24},{1,7},{2,26},{3,5},{4,28},{5,3},{6,30},{7,1},{8,16},{9,15},... | collective-permute-start | bytes 147464 | tf_op jit(solution)/shard_map/ppermute | solution.py:25
  18.2 5.0 %collective-permute-start.6 = (f16[8,3072]{1,0:T(8,128)(2,1)S(1)}, f16[8,3072]{1,0:T(8,128)(2,1)S(1)}, u32[]{:S(2)}, u32[]{:S(2)}) collective-permute-start(f16[8,3072]{1,0:T(8,128)(2,1)S(1)} %get-tuple-element.24), channel_id=1, source_target_pairs={{0,16},{1,3},{2,18},{3,1},{4,20},{5,7},{6,22},{7,5},{8,24},{9,11},... | collective-permute-start | bytes 147464 | tf_op jit(solution)/shard_map/ppermute | solution.py:25
  18.2 5.0 %collective-permute-start.5 = (f16[8,3072]{1,0:T(8,128)(2,1)S(1)}, f16[8,3072]{1,0:T(8,128)(2,1)S(1)}, u32[]{:S(2)}, u32[]{:S(2)}) collective-permute-start(f16[8,3072]{1,0:T(8,128)(2,1)S(1)} %get-tuple-element.22), channel_id=1, source_target_pairs={{0,8},{1,5},{2,10},{3,7},{4,12},{5,1},{6,14},{7,3},{8,0},{9,13},{1... | collective-permute-start | bytes 147464 | tf_op jit(solution)/shard_map/ppermute | solution.py:25
  23.5 12.6 %copy-start.3 = (f32[4,6144]{1,0:T(4,128)}, f32[4,6144]{1,0:T(4,128)S(1)}, u32[]{:S(2)}) copy-start(f32[4,6144]{1,0:T(4,128)S(1)} %get-tuple-element.6) | copy-start | bytes 294916
  23.5 5.7 %collective-permute-start.8 = (bf16[4,6144]{1,0:T(4,128)(2,1)S(1)}, bf16[4,6144]{1,0:T(4,128)(2,1)S(1)}, u32[]{:S(2)}, u32[]{:S(2)}) collective-permute-start(bf16[4,6144]{1,0:T(4,128)(2,1)S(1)} %get-tuple-element.25.mine), channel_id=1, source_target_pairs={{0,16},{1,17},{2,18},{3,19},{4,20},{5,21},{6,22},{7,23},{8,24},{9,... | collective-permute-start | bytes 147464 | tf_op jit(solution)/shard_map/ppermute | solution.py:25
  25.6 4.1 %collective-permute-start.9 = (bf16[4,6144]{1,0:T(4,128)(2,1)S(1)}, bf16[4,6144]{1,0:T(4,128)(2,1)S(1)}, u32[]{:S(2)}, u32[]{:S(2)}) collective-permute-start(bf16[4,6144]{1,0:T(4,128)(2,1)S(1)} %get-tuple-element.25.mine), channel_id=1, source_target_pairs={{0,8},{1,5},{2,10},{3,7},{4,12},{5,1},{6,14},{7,3},{8,0},{9,13},{1... | collective-permute-start | bytes 147464 | tf_op jit(solution)/shard_map/ppermute | solution.py:25
  25.6 7.5 %collective-permute-start.10 = (bf16[4,6144]{1,0:T(4,128)(2,1)S(1)}, bf16[4,6144]{1,0:T(4,128)(2,1)S(1)}, u32[]{:S(2)}, u32[]{:S(2)}) collective-permute-start(bf16[4,6144]{1,0:T(4,128)(2,1)S(1)} %get-tuple-element.25.mine), channel_id=1, source_target_pairs={{0,28},{1,29},{2,30},{3,31},{4,24},{5,25},{6,26},{7,27},{8,20},{9,... | collective-permute-start | bytes 147464 | tf_op jit(solution)/shard_map/ppermute | solution.py:25
  29.8 5.4 %collective-permute-start.11 = (bf16[3,4,6144]{2,1,0:T(4,128)(2,1)S(1)}, bf16[3,4,6144]{2,1,0:T(4,128)(2,1)S(1)}, u32[]{:S(2)}, u32[]{:S(2)}) collective-permute-start(bf16[3,4,6144]{2,1,0:T(4,128)(2,1)S(1)} %pad_maximum_fusion), channel_id=1, source_target_pairs={{0,4},{1,9},{2,6},{3,11},{4,0},{5,13},{6,2},{7,15},{8,12},{9,1},{1... | collective-permute-start | bytes 442376 | tf_op jit(solution)/shard_map/ppermute | solution.py:25
  31.1 4.1 %collective-permute-start.12 = (bf16[4,6144]{1,0:T(4,128)(2,1)S(1)}, bf16[4,6144]{1,0:T(4,128)(2,1)S(1)}, u32[]{:S(2)}, u32[]{:S(2)}) collective-permute-start(bf16[4,6144]{1,0:T(4,128)(2,1)S(1)} %collective-permute-done.8.far), channel_id=1, source_target_pairs={{0,8},{1,5},{2,10},{3,7},{4,12},{5,1},{6,14},{7,3},{8,0},{9,13},{1... | collective-permute-start | bytes 147464 | tf_op jit(solution)/shard_map/ppermute | solution.py:25

commit v22 on v19

--- a/solution.py
+++ b/solution.py
@@ -144,7 +144,7 @@
     quarter = lax.optimization_barrier(pair(0) + widen(got[0]))
     quarter = quarter + widen(got[1]) + widen(got[2])
     me = jnp.where(core == 0, z, 2 * x + y)
-    got = [swap(narrow(pick(quarter, me ^ d)), over_z[d], over_xy[d]) for d in (1, 2, 3)]
+    got = [swap(narrow(pick(quarter, me ^ d)), over_z[d], over_xy[d]) for d in (1, 3, 2)]
     total = pick(quarter, me) + widen(got[0]) + widen(got[1]) + widen(got[2])
 
     return jnp.concatenate([total[: tile // 2], total[tile // 2 :]], axis=1)

time: 35.5 us -> 35.9 us (1.011)
  starting transfers between devices: 16.4 us -> 17.2 us
  waiting for transfers between devices: 13.5 us -> 13.1 us
    ppermute x13, starting transfers between devices: 16.4 us -> 17.2 us  [swap(): return lax.ppermute(value, ('hst', 'local'), flip_pairs(flips))]
  transfers between devices with their start and end apart: 13 -> 13, of which waited for: 10 -> 9; matrix products, arithmetic and copies ran while one was open for 3% -> 3% of each run, Pallas kernels for 1% -> 1%
where the time goes in v22:
time: 35.9 us; the launch traced here: 35.7 us
  starting transfers between devices  17.2 us (48%)
  waiting for transfers between devices  13.1 us (36%)
  Pallas kernels  3.04 us (8%)
  other arithmetic  1.56 us (4%)
  between operations  0.74 us (2%)
    ppermute x13, starting transfers between devices, swap(): return lax.ppermute(value, ('hst', 'local'), flip_pairs(flips))  17.2 us
    ppermute x13, waiting for transfers between devices, swap(): return lax.ppermute(value, ('hst', 'local'), flip_pairs(flips))  13.1 us
    pallas_call x2, Pallas kernels, call(): pl.pallas_call(kernel, in_specs=[pl.BlockSpec(memory_space=space)], out_s...  2.24 us
    sub x1, other arithmetic, adam(): new_master = master - learn_rate * (update + decay_rate * master)  0.84 us
    pallas_call x1, Pallas kernels, gather_blocks(): pl.pallas_call(join_kernel, in_specs=[pl.BlockSpec(memory_space=pl.ANY)]...  0.8 us
  transfers between devices with their start and end apart: 13, of which 9 were waited for; matrix products, arithmetic and copies ran while one was open for 3% of the time, Pallas kernels for 1%

profile of v22, /device:TPU:0, one launch (start us, length us, event | category | flops | bytes accessed | tf_op | source)
XLA Modules:
  0.0 35.7 jit_solution(11579898809890013579)
XLA Ops:
  0.6 1.8 %shard_map.83 = (bf16[4,8,3072]{2,1,0:T(8,128)(2,1)S(1)}, bf16[3,4,8,3072]{3,2,1,0:T(8,128)(2,1)S(1)}, bf16[16,49152]{1,0:T(8,128)(2,1)S(1)}) custom-call(bf16[16,49152]{1,0:T(8,128)(2,1)} %bitcast.28), custom_call_target="tpu_custom_call" | custom-call | flops 786432 | bytes 3145728 | tf_op jit(solution)/shard_map/pallas_call | solution.py:103
  2.4 0.5 %collective-permute-start = (bf16[4,8,3072]{2,1,0:T(8,128)(2,1)S(1)}, bf16[4,8,3072]{2,1,0:T(8,128)(2,1)S(1)}, u32[]{:S(2)}, u32[]{:S(2)}) collective-permute-start(bf16[4,8,3072]{2,1,0:T(8,128)(2,1)S(1)} %get-tuple-element.12), channel_id=1, source_target_pairs={{0,1},{1,0},{2,3},{3,2},{4,5},{5,4},{6,7},{7,6},{8,9},{9,8},{10,11... | collective-permute-start | bytes 589832 | tf_op jit(solution)/shard_map/ppermute | solution.py:25
  2.9 0.1 collective-permute-start.1
  3.0 0.5 %shard_map.84 = bf16[4,4,8,3072]{3,2,1,0:T(8,128)(2,1)S(1)} custom-call(bf16[16,49152]{1,0:T(8,128)(2,1)S(1)} %get-tuple-element.11.landed), custom_call_target="tpu_custom_call" | custom-call | flops 786432 | bytes 3145728 | tf_op jit(solution)/shard_map/pallas_call | solution.py:103
  3.5 0.5 %collective-permute-done = bf16[4,8,3072]{2,1,0:T(8,128)(2,1)S(1)} collective-permute-done((bf16[4,8,3072]{2,1,0:T(8,128)(2,1)S(1)}, bf16[4,8,3072]{2,1,0:T(8,128)(2,1)S(1)}, u32[]{:S(2)}, u32[]{:S(2)}) %collective-permute-start) | collective-permute-done | bytes 196640 | tf_op jit(solution)/shard_map/ppermute | solution.py:25
  4.0 0.1 fusion.1
  4.1 3.9 %collective-permute-start.2 = (f16[4,8,3072]{2,1,0:T(8,128)(2,1)S(1)}, f16[4,8,3072]{2,1,0:T(8,128)(2,1)S(1)}, u32[]{:S(2)}, u32[]{:S(2)}) collective-permute-start(f16[4,8,3072]{2,1,0:T(8,128)(2,1)S(1)} %fusion.1), channel_id=1, source_target_pairs={{0,6},{1,17},{2,4},{3,19},{4,2},{5,21},{6,0},{7,23},{8,14},{9,25},... | collective-permute-start | bytes 589832 | tf_op jit(solution)/shard_map/ppermute | solution.py:25
  7.9 0.1 fusion.2
  8.1 0.6 %collective-permute-start.4 = (f16[4,8,3072]{2,1,0:T(8,128)(2,1)S(1)}, f16[4,8,3072]{2,1,0:T(8,128)(2,1)S(1)}, u32[]{:S(2)}, u32[]{:S(2)}) collective-permute-start(f16[4,8,3072]{2,1,0:T(8,128)(2,1)S(1)} %get-tuple-element.21), channel_id=1, source_target_pairs={{0,2},{1,25},{2,0},{3,27},{4,6},{5,29},{6,4},{7,31},{8,10},{9,17},... | collective-permute-start | bytes 589832 | tf_op jit(solution)/shard_map/ppermute | solution.py:25
  8.7 0.7 %collective-permute-start.3 = (f16[4,8,3072]{2,1,0:T(8,128)(2,1)S(1)}, f16[4,8,3072]{2,1,0:T(8,128)(2,1)S(1)}, u32[]{:S(2)}, u32[]{:S(2)}) collective-permute-start(f16[4,8,3072]{2,1,0:T(8,128)(2,1)S(1)} %get-tuple-element.20), channel_id=1, source_target_pairs={{0,4},{1,9},{2,6},{3,11},{4,0},{5,13},{6,2},{7,15},{8,12},{9,1},{1... | collective-permute-start | bytes 589832 | tf_op jit(solution)/shard_map/ppermute | solution.py:25
  9.4 2.2 %collective-permute-done.2 = f16[4,8,3072]{2,1,0:T(8,128)(2,1)S(1)} collective-permute-done((f16[4,8,3072]{2,1,0:T(8,128)(2,1)S(1)}, f16[4,8,3072]{2,1,0:T(8,128)(2,1)S(1)}, u32[]{:S(2)}, u32[]{:S(2)}) %collective-permute-start.2) | collective-permute-done | bytes 196640 | tf_op jit(solution)/shard_map/ppermute | solution.py:25
  11.6 0.1 bitcast_add_fusion
  11.7 2.6 %collective-permute-done.4 = f16[4,8,3072]{2,1,0:T(8,128)(2,1)S(1)} collective-permute-done((f16[4,8,3072]{2,1,0:T(8,128)(2,1)S(1)}, f16[4,8,3072]{2,1,0:T(8,128)(2,1)S(1)}, u32[]{:S(2)}, u32[]{:S(2)}) %collective-permute-start.4) | collective-permute-done | bytes 196640 | tf_op jit(solution)/shard_map/ppermute | solution.py:25
  14.2 0.1 collective-permute-done.3
  14.4 0.1 multiply_add_fusion
  14.5 2.7 %collective-permute-start.7 = (f16[8,3072]{1,0:T(8,128)(2,1)S(1)}, f16[8,3072]{1,0:T(8,128)(2,1)S(1)}, u32[]{:S(2)}, u32[]{:S(2)}) collective-permute-start(f16[8,3072]{1,0:T(8,128)(2,1)S(1)} %get-tuple-element.23), channel_id=1, source_target_pairs={{0,16},{1,3},{2,18},{3,1},{4,20},{5,7},{6,22},{7,5},{8,24},{9,11},... | collective-permute-start | bytes 147464 | tf_op jit(solution)/shard_map/ppermute | solution.py:25
  17.2 1.4 %collective-permute-start.6 = (f16[8,3072]{1,0:T(8,128)(2,1)S(1)}, f16[8,3072]{1,0:T(8,128)(2,1)S(1)}, u32[]{:S(2)}, u32[]{:S(2)}) collective-permute-start(f16[8,3072]{1,0:T(8,128)(2,1)S(1)} %get-tuple-element.24), channel_id=1, source_target_pairs={{0,24},{1,7},{2,26},{3,5},{4,28},{5,3},{6,30},{7,1},{8,16},{9,15},... | collective-permute-start | bytes 147464 | tf_op jit(solution)/shard_map/ppermute | solution.py:25
  18.5 0.2 collective-permute-start.5
  18.7 0.8 %collective-permute-done.7 = f16[8,3072]{1,0:T(8,128)(2,1)S(1)} collective-permute-done((f16[8,3072]{1,0:T(8,128)(2,1)S(1)}, f16[8,3072]{1,0:T(8,128)(2,1)S(1)}, u32[]{:S(2)}, u32[]{:S(2)}) %collective-permute-start.7) | collective-permute-done | bytes 49184 | tf_op jit(solution)/shard_map/ppermute | solution.py:25
  19.6 3.6 %collective-permute-done.6 = f16[8,3072]{1,0:T(8,128)(2,1)S(1)} collective-permute-done((f16[8,3072]{1,0:T(8,128)(2,1)S(1)}, f16[8,3072]{1,0:T(8,128)(2,1)S(1)}, u32[]{:S(2)}, u32[]{:S(2)}) %collective-permute-start.6) | collective-permute-done | bytes 49184 | tf_op jit(solution)/shard_map/ppermute | solution.py:25
  23.2 0.2 subtract_convert_fusion
  23.4 1.2 %collective-permute-start.9 = (bf16[4,6144]{1,0:T(4,128)(2,1)S(1)}, bf16[4,6144]{1,0:T(4,128)(2,1)S(1)}, u32[]{:S(2)}, u32[]{:S(2)}) collective-permute-start(bf16[4,6144]{1,0:T(4,128)(2,1)S(1)} %get-tuple-element.25.mine), channel_id=1, source_target_pairs={{0,16},{1,17},{2,18},{3,19},{4,20},{5,21},{6,22},{7,23},{8,24},{9,... | collective-permute-start | bytes 147464 | tf_op jit(solution)/shard_map/ppermute | solution.py:25
  24.7 2.1 %collective-permute-start.8 = (bf16[4,6144]{1,0:T(4,128)(2,1)S(1)}, bf16[4,6144]{1,0:T(4,128)(2,1)S(1)}, u32[]{:S(2)}, u32[]{:S(2)}) collective-permute-start(bf16[4,6144]{1,0:T(4,128)(2,1)S(1)} %get-tuple-element.25.mine), channel_id=1, source_target_pairs={{0,12},{1,29},{2,14},{3,31},{4,8},{5,25},{6,10},{7,27},{8,4},{9,21... | collective-permute-start | bytes 147464 | tf_op jit(solution)/shard_map/ppermute | solution.py:25
  26.8 2.0 %collective-permute-start.10 = (bf16[4,6144]{1,0:T(4,128)(2,1)S(1)}, bf16[4,6144]{1,0:T(4,128)(2,1)S(1)}, u32[]{:S(2)}, u32[]{:S(2)}) collective-permute-start(bf16[4,6144]{1,0:T(4,128)(2,1)S(1)} %get-tuple-element.25.mine), channel_id=1, source_target_pairs={{0,28},{1,13},{2,30},{3,15},{4,24},{5,9},{6,26},{7,11},{8,20},{9,5... | collective-permute-start | bytes 147464 | tf_op jit(solution)/shard_map/ppermute | solution.py:25
  28.8 0.4 collective-permute-done.9.far
  29.1 0.1 pad_maximum_fusion.1
  29.2 0.4 %collective-permute-start.11 = (bf16[2,4,6144]{2,1,0:T(4,128)(2,1)S(1)}, bf16[2,4,6144]{2,1,0:T(4,128)(2,1)S(1)}, u32[]{:S(2)}, u32[]{:S(2)}) collective-permute-start(bf16[2,4,6144]{2,1,0:T(4,128)(2,1)S(1)} %pad_maximum_fusion.1), channel_id=1, source_target_pairs={{0,8},{1,5},{2,10},{3,7},{4,12},{5,1},{6,14},{7,3},{8,0},{9,13},{1... | collective-permute-start | bytes 294920 | tf_op jit(solution)/shard_map/ppermute | solution.py:25
  29.6 1.4 %collective-permute-start.12 = (bf16[2,4,6144]{2,1,0:T(4,128)(2,1)S(1)}, bf16[2,4,6144]{2,1,0:T(4,128)(2,1)S(1)}, u32[]{:S(2)}, u32[]{:S(2)}) collective-permute-start(bf16[2,4,6144]{2,1,0:T(4,128)(2,1)S(1)} %pad_maximum_fusion.1), channel_id=1, source_target_pairs={{0,4},{1,9},{2,6},{3,11},{4,0},{5,13},{6,2},{7,15},{8,12},{9,1},{1... | collective-permute-start | bytes 294920 | tf_op jit(solution)/shard_map/ppermute | solution.py:25
  31.0 0.8 %multiply_subtract_fusion = (f32[4,6144]{1,0:T(4,128)}, f32[4,6144]{1,0:T(4,128)}, f32[4,6144]{1,0:T(4,128)}) fusion(f32[4,6144]{1,0:T(4,128)S(1)} %copy-done, f32[4,6144]{1,0:T(4,128)S(1)} %get-tuple-element.6, f32[4,6144]{1,0:T(4,128)S(1)} %copy-done.2, f32[4,6144]{1,0:T(4,128)S(1)} %copy-done.1), kind=kLoop, calls=%fused_computation.23 | loop fusion | flops 368640 | bytes 688128 | tf_op jit(solution)/shard_map/sub | solution.py:214
  31.9 1.8 %collective-permute-done.10.cross = bf16[4,6144]{1,0:T(4,128)(2,1)S(1)} collective-permute-done((bf16[4,6144]{1,0:T(4,128)(2,1)S(1)}, bf16[4,6144]{1,0:T(4,128)(2,1)S(1)}, u32[]{:S(2)}, u32[]{:S(2)}) %collective-permute-start.10) | collective-permute-done | bytes 49184 | tf_op jit(solution)/shard_map/ppermute | solution.py:25
  33.7 1.2 %collective-permute-done.11.side = bf16[2,4,6144]{2,1,0:T(4,128)(2,1)S(1)} collective-permute-done((bf16[2,4,6144]{2,1,0:T(4,128)(2,1)S(1)}, bf16[2,4,6144]{2,1,0:T(4,128)(2,1)S(1)}, u32[]{:S(2)}, u32[]{:S(2)}) %collective-permute-start.11) | collective-permute-done | bytes 98336 | tf_op jit(solution)/shard_map/ppermute | solution.py:25
  34.9 0.8 %shard_map.85 = bf16[4,49152]{1,0:T(4,128)(2,1)} custom-call(bf16[4,6144]{1,0:T(4,128)(2,1)S(1)} %get-tuple-element.25.mine, bf16[4,6144]{1,0:T(4,128)(2,1)S(1)} %collective-permute-done.9.far, bf16[4,6144]{1,0:T(4,128)(2,1)S(1)} %collective-permute-done.8.corner, bf16[4,6144]{1,0:T(4,128)(2,1)S(1)} %collective-permute-done.10.cross, ...), custom_call_target="tpu_custom_call" | custom-call | bytes 786432 | tf_op jit(solution)/shard_map/pallas_call | solution.py:175
  (15 shorter events, 0.1 us)
Async XLA Ops:
  2.4 1.6 %collective-permute-start = (bf16[4,8,3072]{2,1,0:T(8,128)(2,1)S(1)}, bf16[4,8,3072]{2,1,0:T(8,128)(2,1)S(1)}, u32[]{:S(2)}, u32[]{:S(2)}) collective-permute-start(bf16[4,8,3072]{2,1,0:T(8,128)(2,1)S(1)} %get-tuple-element.12), channel_id=1, source_target_pairs={{0,1},{1,0},{2,3},{3,2},{4,5},{5,4},{6,7},{7,6},{8,9},{9,8},{10,11... | collective-permute-start | bytes 589832 | tf_op jit(solution)/shard_map/ppermute | solution.py:25
  2.9 5.0 %collective-permute-start.1 = (bf16[3,4,8,3072]{3,2,1,0:T(8,128)(2,1)S(1)}, bf16[3,4,8,3072]{3,2,1,0:T(8,128)(2,1)S(1)}, u32[]{:S(2)}, u32[]{:S(2)}) collective-permute-start(bf16[3,4,8,3072]{3,2,1,0:T(8,128)(2,1)S(1)} %get-tuple-element.14), channel_id=1, source_target_pairs={{0,1},{1,0},{2,3},{3,2},{4,5},{5,4},{6,7},{7,6},{8,9},{9,8},{10,11... | collective-permute-start | bytes 1769480 | tf_op jit(solution)/shard_map/ppermute | solution.py:25
  4.1 7.5 %collective-permute-start.2 = (f16[4,8,3072]{2,1,0:T(8,128)(2,1)S(1)}, f16[4,8,3072]{2,1,0:T(8,128)(2,1)S(1)}, u32[]{:S(2)}, u32[]{:S(2)}) collective-permute-start(f16[4,8,3072]{2,1,0:T(8,128)(2,1)S(1)} %fusion.1), channel_id=1, source_target_pairs={{0,6},{1,17},{2,4},{3,19},{4,2},{5,21},{6,0},{7,23},{8,14},{9,25},... | collective-permute-start | bytes 589832 | tf_op jit(solution)/shard_map/ppermute | solution.py:25
  8.1 6.1 %collective-permute-start.4 = (f16[4,8,3072]{2,1,0:T(8,128)(2,1)S(1)}, f16[4,8,3072]{2,1,0:T(8,128)(2,1)S(1)}, u32[]{:S(2)}, u32[]{:S(2)}) collective-permute-start(f16[4,8,3072]{2,1,0:T(8,128)(2,1)S(1)} %get-tuple-element.21), channel_id=1, source_target_pairs={{0,2},{1,25},{2,0},{3,27},{4,6},{5,29},{6,4},{7,31},{8,10},{9,17},... | collective-permute-start | bytes 589832 | tf_op jit(solution)/shard_map/ppermute | solution.py:25
  8.7 14.5 %copy-start = (f32[4,6144]{1,0:T(4,128)S(1)}, f32[4,6144]{1,0:T(4,128)}, u32[]{:S(2)}) copy-start(f32[4,6144]{1,0:T(4,128)} %param.5) | copy-start | bytes 294916
  8.7 14.5 %copy-start.1 = (f32[4,6144]{1,0:T(4,128)S(1)}, f32[4,6144]{1,0:T(4,128)}, u32[]{:S(2)}) copy-start(f32[4,6144]{1,0:T(4,128)} %param.7) | copy-start | bytes 294916
  8.7 14.5 %copy-start.2 = (f32[4,6144]{1,0:T(4,128)S(1)}, f32[4,6144]{1,0:T(4,128)}, u32[]{:S(2)}) copy-start(f32[4,6144]{1,0:T(4,128)} %param.6) | copy-start | bytes 294916
  8.7 5.7 %collective-permute-start.3 = (f16[4,8,3072]{2,1,0:T(8,128)(2,1)S(1)}, f16[4,8,3072]{2,1,0:T(8,128)(2,1)S(1)}, u32[]{:S(2)}, u32[]{:S(2)}) collective-permute-start(f16[4,8,3072]{2,1,0:T(8,128)(2,1)S(1)} %get-tuple-element.20), channel_id=1, source_target_pairs={{0,4},{1,9},{2,6},{3,11},{4,0},{5,13},{6,2},{7,15},{8,12},{9,1},{1... | collective-permute-start | bytes 589832 | tf_op jit(solution)/shard_map/ppermute | solution.py:25
  14.5 5.1 %collective-permute-start.7 = (f16[8,3072]{1,0:T(8,128)(2,1)S(1)}, f16[8,3072]{1,0:T(8,128)(2,1)S(1)}, u32[]{:S(2)}, u32[]{:S(2)}) collective-permute-start(f16[8,3072]{1,0:T(8,128)(2,1)S(1)} %get-tuple-element.23), channel_id=1, source_target_pairs={{0,16},{1,3},{2,18},{3,1},{4,20},{5,7},{6,22},{7,5},{8,24},{9,11},... | collective-permute-start | bytes 147464 | tf_op jit(solution)/shard_map/ppermute | solution.py:25
  17.2 6.0 %collective-permute-start.6 = (f16[8,3072]{1,0:T(8,128)(2,1)S(1)}, f16[8,3072]{1,0:T(8,128)(2,1)S(1)}, u32[]{:S(2)}, u32[]{:S(2)}) collective-permute-start(f16[8,3072]{1,0:T(8,128)(2,1)S(1)} %get-tuple-element.24), channel_id=1, source_target_pairs={{0,24},{1,7},{2,26},{3,5},{4,28},{5,3},{6,30},{7,1},{8,16},{9,15},... | collective-permute-start | bytes 147464 | tf_op jit(solution)/shard_map/ppermute | solution.py:25
  18.5 4.6 %collective-permute-start.5 = (f16[8,3072]{1,0:T(8,128)(2,1)S(1)}, f16[8,3072]{1,0:T(8,128)(2,1)S(1)}, u32[]{:S(2)}, u32[]{:S(2)}) collective-permute-start(f16[8,3072]{1,0:T(8,128)(2,1)S(1)} %get-tuple-element.22), channel_id=1, source_target_pairs={{0,8},{1,5},{2,10},{3,7},{4,12},{5,1},{6,14},{7,3},{8,0},{9,13},{1... | collective-permute-start | bytes 147464 | tf_op jit(solution)/shard_map/ppermute | solution.py:25
  23.4 12.3 %copy-start.3 = (f32[4,6144]{1,0:T(4,128)}, f32[4,6144]{1,0:T(4,128)S(1)}, u32[]{:S(2)}) copy-start(f32[4,6144]{1,0:T(4,128)S(1)} %get-tuple-element.6) | copy-start | bytes 294916
  23.4 5.7 %collective-permute-start.9 = (bf16[4,6144]{1,0:T(4,128)(2,1)S(1)}, bf16[4,6144]{1,0:T(4,128)(2,1)S(1)}, u32[]{:S(2)}, u32[]{:S(2)}) collective-permute-start(bf16[4,6144]{1,0:T(4,128)(2,1)S(1)} %get-tuple-element.25.mine), channel_id=1, source_target_pairs={{0,16},{1,17},{2,18},{3,19},{4,20},{5,21},{6,22},{7,23},{8,24},{9,... | collective-permute-start | bytes 147464 | tf_op jit(solution)/shard_map/ppermute | solution.py:25
  24.7 6.4 %collective-permute-start.8 = (bf16[4,6144]{1,0:T(4,128)(2,1)S(1)}, bf16[4,6144]{1,0:T(4,128)(2,1)S(1)}, u32[]{:S(2)}, u32[]{:S(2)}) collective-permute-start(bf16[4,6144]{1,0:T(4,128)(2,1)S(1)} %get-tuple-element.25.mine), channel_id=1, source_target_pairs={{0,12},{1,29},{2,14},{3,31},{4,8},{5,25},{6,10},{7,27},{8,4},{9,21... | collective-permute-start | bytes 147464 | tf_op jit(solution)/shard_map/ppermute | solution.py:25
  26.8 6.9 %collective-permute-start.10 = (bf16[4,6144]{1,0:T(4,128)(2,1)S(1)}, bf16[4,6144]{1,0:T(4,128)(2,1)S(1)}, u32[]{:S(2)}, u32[]{:S(2)}) collective-permute-start(bf16[4,6144]{1,0:T(4,128)(2,1)S(1)} %get-tuple-element.25.mine), channel_id=1, source_target_pairs={{0,28},{1,13},{2,30},{3,15},{4,24},{5,9},{6,26},{7,11},{8,20},{9,5... | collective-permute-start | bytes 147464 | tf_op jit(solution)/shard_map/ppermute | solution.py:25
  29.2 5.7 %collective-permute-start.11 = (bf16[2,4,6144]{2,1,0:T(4,128)(2,1)S(1)}, bf16[2,4,6144]{2,1,0:T(4,128)(2,1)S(1)}, u32[]{:S(2)}, u32[]{:S(2)}) collective-permute-start(bf16[2,4,6144]{2,1,0:T(4,128)(2,1)S(1)} %pad_maximum_fusion.1), channel_id=1, source_target_pairs={{0,8},{1,5},{2,10},{3,7},{4,12},{5,1},{6,14},{7,3},{8,0},{9,13},{1... | collective-permute-start | bytes 294920 | tf_op jit(solution)/shard_map/ppermute | solution.py:25
  29.6 5.3 %collective-permute-start.12 = (bf16[2,4,6144]{2,1,0:T(4,128)(2,1)S(1)}, bf16[2,4,6144]{2,1,0:T(4,128)(2,1)S(1)}, u32[]{:S(2)}, u32[]{:S(2)}) collective-permute-start(bf16[2,4,6144]{2,1,0:T(4,128)(2,1)S(1)} %pad_maximum_fusion.1), channel_id=1, source_target_pairs={{0,4},{1,9},{2,6},{3,11},{4,0},{5,13},{6,2},{7,15},{8,12},{9,1},{1... | collective-permute-start | bytes 294920 | tf_op jit(solution)/shard_map/ppermute | solution.py:25

commit v23 on v19

--- a/solution.py
+++ b/solution.py
@@ -62,7 +62,7 @@
         store(step, member, jnp.where(core == 0, rows[0], rows[1]))
 
 
-def theirs_kernel(whole, first, others, landed, arrived):
+def theirs_kernel(whole, first, every, landed, arrived):
     half = first.shape[2]
     core = place()[3]
     parts = [pl.ds(2 * i * half, 2 * half) for i in range(8)]
@@ -74,17 +74,12 @@
         copy.start()
 
     def store(step, member, rows):
-        @pl.when(step == 3)
-        def _():
-            first[member] = rows
-
-        @pl.when(step != 3)
-        def _():
-            others[jnp.minimum(step, 2), member] = rows
+        every[step, member] = rows
 
     for i in range(8):
         copies[i].wait()
         rows_of(1 - core, landed[:, parts[i]], i, store)
+    first[...] = every[3]
 
 
 def own_kernel(landed, own):
@@ -118,7 +113,7 @@
         theirs_kernel,
         gradient,
         pltpu.HBM,
-        [shape, (3, *shape), gradient.shape],
+        [shape, (4, *shape), gradient.shape],
         [pltpu.SemaphoreType.DMA((8,))],
     )
     first, others, landed = lax.optimization_barrier((first, others, landed))

time: 35.5 us -> 36.8 us (1.037)
  waiting for transfers between devices: 13.5 us -> 14.8 us
    ppermute x13, waiting for transfers between devices: 13.5 us -> 14.8 us  [swap(): return lax.ppermute(value, ('hst', 'local'), flip_pairs(flips))]
where the time goes in v23:
time: 36.8 us; the launch traced here: 36.7 us
  starting transfers between devices  16.6 us (45%)
  waiting for transfers between devices  14.8 us (40%)
  Pallas kernels  2.93 us (8%)
  other arithmetic  1.56 us (4%)
  between operations  0.74 us (2%)
    ppermute x13, starting transfers between devices, swap(): return lax.ppermute(value, ('hst', 'local'), flip_pairs(flips))  16.6 us
    ppermute x13, waiting for transfers between devices, swap(): return lax.ppermute(value, ('hst', 'local'), flip_pairs(flips))  14.8 us
    pallas_call x2, Pallas kernels, call(): pl.pallas_call(kernel, in_specs=[pl.BlockSpec(memory_space=space)], out_s...  2.13 us
    sub x1, other arithmetic, adam(): new_master = master - learn_rate * (update + decay_rate * master)  0.84 us
    pallas_call x1, Pallas kernels, gather_blocks(): pl.pallas_call(join_kernel, in_specs=[pl.BlockSpec(memory_space=pl.ANY)]...  0.8 us
  transfers between devices with their start and end apart: 13, of which 10 were waited for; matrix products, arithmetic and copies ran while one was open for 3% of the time, Pallas kernels for 1%

profile of v23, /device:TPU:0, one launch (start us, length us, event | category | flops | bytes accessed | tf_op | source)
XLA Modules:
  0.0 36.7 jit_solution(16611553911757744081)
XLA Ops:
  0.6 1.6 %shard_map.83 = (bf16[4,8,3072]{2,1,0:T(8,128)(2,1)S(1)}, bf16[4,4,8,3072]{3,2,1,0:T(8,128)(2,1)S(1)}, bf16[16,49152]{1,0:T(8,128)(2,1)S(1)}) custom-call(bf16[16,49152]{1,0:T(8,128)(2,1)} %bitcast.28), custom_call_target="tpu_custom_call" | custom-call | flops 786432 | bytes 3145728 | tf_op jit(solution)/shard_map/pallas_call | solution.py:98
  2.3 0.5 %collective-permute-start = (bf16[4,8,3072]{2,1,0:T(8,128)(2,1)S(1)}, bf16[4,8,3072]{2,1,0:T(8,128)(2,1)S(1)}, u32[]{:S(2)}, u32[]{:S(2)}) collective-permute-start(bf16[4,8,3072]{2,1,0:T(8,128)(2,1)S(1)} %get-tuple-element.12), channel_id=1, source_target_pairs={{0,1},{1,0},{2,3},{3,2},{4,5},{5,4},{6,7},{7,6},{8,9},{9,8},{10,11... | collective-permute-start | bytes 589832 | tf_op jit(solution)/shard_map/ppermute | solution.py:25
  2.8 0.1 collective-permute-start.1
  2.9 0.5 %shard_map.84 = bf16[4,4,8,3072]{3,2,1,0:T(8,128)(2,1)S(1)} custom-call(bf16[16,49152]{1,0:T(8,128)(2,1)S(1)} %get-tuple-element.11.landed), custom_call_target="tpu_custom_call" | custom-call | flops 786432 | bytes 3145728 | tf_op jit(solution)/shard_map/pallas_call | solution.py:98
  3.4 0.5 %collective-permute-done = bf16[4,8,3072]{2,1,0:T(8,128)(2,1)S(1)} collective-permute-done((bf16[4,8,3072]{2,1,0:T(8,128)(2,1)S(1)}, bf16[4,8,3072]{2,1,0:T(8,128)(2,1)S(1)}, u32[]{:S(2)}, u32[]{:S(2)}) %collective-permute-start) | collective-permute-done | bytes 196640 | tf_op jit(solution)/shard_map/ppermute | solution.py:25
  3.9 0.1 fusion.1
  3.9 3.9 %collective-permute-start.2 = (f16[4,8,3072]{2,1,0:T(8,128)(2,1)S(1)}, f16[4,8,3072]{2,1,0:T(8,128)(2,1)S(1)}, u32[]{:S(2)}, u32[]{:S(2)}) collective-permute-start(f16[4,8,3072]{2,1,0:T(8,128)(2,1)S(1)} %fusion.1), channel_id=1, source_target_pairs={{0,6},{1,17},{2,4},{3,19},{4,2},{5,21},{6,0},{7,23},{8,14},{9,25},... | collective-permute-start | bytes 589832 | tf_op jit(solution)/shard_map/ppermute | solution.py:25
  7.8 0.1 fusion.2
  8.0 0.6 %collective-permute-start.3 = (f16[4,8,3072]{2,1,0:T(8,128)(2,1)S(1)}, f16[4,8,3072]{2,1,0:T(8,128)(2,1)S(1)}, u32[]{:S(2)}, u32[]{:S(2)}) collective-permute-start(f16[4,8,3072]{2,1,0:T(8,128)(2,1)S(1)} %get-tuple-element.20), channel_id=1, source_target_pairs={{0,4},{1,9},{2,6},{3,11},{4,0},{5,13},{6,2},{7,15},{8,12},{9,1},{1... | collective-permute-start | bytes 589832 | tf_op jit(solution)/shard_map/ppermute | solution.py:25
  8.6 1.0 %collective-permute-start.4 = (f16[4,8,3072]{2,1,0:T(8,128)(2,1)S(1)}, f16[4,8,3072]{2,1,0:T(8,128)(2,1)S(1)}, u32[]{:S(2)}, u32[]{:S(2)}) collective-permute-start(f16[4,8,3072]{2,1,0:T(8,128)(2,1)S(1)} %get-tuple-element.21), channel_id=1, source_target_pairs={{0,2},{1,25},{2,0},{3,27},{4,6},{5,29},{6,4},{7,31},{8,10},{9,17},... | collective-permute-start | bytes 589832 | tf_op jit(solution)/shard_map/ppermute | solution.py:25
  9.6 1.9 %collective-permute-done.2 = f16[4,8,3072]{2,1,0:T(8,128)(2,1)S(1)} collective-permute-done((f16[4,8,3072]{2,1,0:T(8,128)(2,1)S(1)}, f16[4,8,3072]{2,1,0:T(8,128)(2,1)S(1)}, u32[]{:S(2)}, u32[]{:S(2)}) %collective-permute-start.2) | collective-permute-done | bytes 196640 | tf_op jit(solution)/shard_map/ppermute | solution.py:25
  11.5 0.1 bitcast_add_fusion
  11.6 2.2 %collective-permute-done.3 = f16[4,8,3072]{2,1,0:T(8,128)(2,1)S(1)} collective-permute-done((f16[4,8,3072]{2,1,0:T(8,128)(2,1)S(1)}, f16[4,8,3072]{2,1,0:T(8,128)(2,1)S(1)}, u32[]{:S(2)}, u32[]{:S(2)}) %collective-permute-start.3) | collective-permute-done | bytes 196640 | tf_op jit(solution)/shard_map/ppermute | solution.py:25
  13.7 0.5 %collective-permute-done.4 = f16[4,8,3072]{2,1,0:T(8,128)(2,1)S(1)} collective-permute-done((f16[4,8,3072]{2,1,0:T(8,128)(2,1)S(1)}, f16[4,8,3072]{2,1,0:T(8,128)(2,1)S(1)}, u32[]{:S(2)}, u32[]{:S(2)}) %collective-permute-start.4) | collective-permute-done | bytes 196640 | tf_op jit(solution)/shard_map/ppermute | solution.py:25
  14.2 0.1 multiply_add_fusion
  14.4 1.6 %collective-permute-start.5 = (f16[8,3072]{1,0:T(8,128)(2,1)S(1)}, f16[8,3072]{1,0:T(8,128)(2,1)S(1)}, u32[]{:S(2)}, u32[]{:S(2)}) collective-permute-start(f16[8,3072]{1,0:T(8,128)(2,1)S(1)} %get-tuple-element.22), channel_id=1, source_target_pairs={{0,8},{1,5},{2,10},{3,7},{4,12},{5,1},{6,14},{7,3},{8,0},{9,13},{1... | collective-permute-start | bytes 147464 | tf_op jit(solution)/shard_map/ppermute | solution.py:25
  16.0 2.5 %collective-permute-start.7 = (f16[8,3072]{1,0:T(8,128)(2,1)S(1)}, f16[8,3072]{1,0:T(8,128)(2,1)S(1)}, u32[]{:S(2)}, u32[]{:S(2)}) collective-permute-start(f16[8,3072]{1,0:T(8,128)(2,1)S(1)} %get-tuple-element.23), channel_id=1, source_target_pairs={{0,24},{1,7},{2,26},{3,5},{4,28},{5,3},{6,30},{7,1},{8,16},{9,15},... | collective-permute-start | bytes 147464 | tf_op jit(solution)/shard_map/ppermute | solution.py:25
  18.5 0.1 collective-permute-start.6
  18.6 3.3 %collective-permute-done.7 = f16[8,3072]{1,0:T(8,128)(2,1)S(1)} collective-permute-done((f16[8,3072]{1,0:T(8,128)(2,1)S(1)}, f16[8,3072]{1,0:T(8,128)(2,1)S(1)}, u32[]{:S(2)}, u32[]{:S(2)}) %collective-permute-start.7) | collective-permute-done | bytes 49184 | tf_op jit(solution)/shard_map/ppermute | solution.py:25
  21.9 2.1 %collective-permute-done.6 = f16[8,3072]{1,0:T(8,128)(2,1)S(1)} collective-permute-done((f16[8,3072]{1,0:T(8,128)(2,1)S(1)}, f16[8,3072]{1,0:T(8,128)(2,1)S(1)}, u32[]{:S(2)}, u32[]{:S(2)}) %collective-permute-start.6) | collective-permute-done | bytes 49184 | tf_op jit(solution)/shard_map/ppermute | solution.py:25
  24.1 0.2 subtract_convert_fusion
  24.3 0.1 collective-permute-start.9
  24.4 3.5 %collective-permute-start.10 = (bf16[4,6144]{1,0:T(4,128)(2,1)S(1)}, bf16[4,6144]{1,0:T(4,128)(2,1)S(1)}, u32[]{:S(2)}, u32[]{:S(2)}) collective-permute-start(bf16[4,6144]{1,0:T(4,128)(2,1)S(1)} %get-tuple-element.25.mine), channel_id=1, source_target_pairs={{0,28},{1,13},{2,30},{3,15},{4,24},{5,9},{6,26},{7,11},{8,20},{9,5... | collective-permute-start | bytes 147464 | tf_op jit(solution)/shard_map/ppermute | solution.py:25
  27.9 0.8 %collective-permute-start.8 = (bf16[4,6144]{1,0:T(4,128)(2,1)S(1)}, bf16[4,6144]{1,0:T(4,128)(2,1)S(1)}, u32[]{:S(2)}, u32[]{:S(2)}) collective-permute-start(bf16[4,6144]{1,0:T(4,128)(2,1)S(1)} %get-tuple-element.25.mine), channel_id=1, source_target_pairs={{0,12},{1,29},{2,14},{3,31},{4,8},{5,25},{6,10},{7,27},{8,4},{9,21... | collective-permute-start | bytes 147464 | tf_op jit(solution)/shard_map/ppermute | solution.py:25
  28.8 0.9 %collective-permute-done.9.far = bf16[4,6144]{1,0:T(4,128)(2,1)S(1)} collective-permute-done((bf16[4,6144]{1,0:T(4,128)(2,1)S(1)}, bf16[4,6144]{1,0:T(4,128)(2,1)S(1)}, u32[]{:S(2)}, u32[]{:S(2)}) %collective-permute-start.9) | collective-permute-done | bytes 49184 | tf_op jit(solution)/shard_map/ppermute | solution.py:25
  29.7 1.5 %collective-permute-start.12 = (bf16[2,4,6144]{2,1,0:T(4,128)(2,1)S(1)}, bf16[2,4,6144]{2,1,0:T(4,128)(2,1)S(1)}, u32[]{:S(2)}, u32[]{:S(2)}) collective-permute-start(bf16[2,4,6144]{2,1,0:T(4,128)(2,1)S(1)} %pad_maximum_fusion.1), channel_id=1, source_target_pairs={{0,4},{1,9},{2,6},{3,11},{4,0},{5,13},{6,2},{7,15},{8,12},{9,1},{1... | collective-permute-start | bytes 294920 | tf_op jit(solution)/shard_map/ppermute | solution.py:25
  31.2 0.3 collective-permute-start.11
  31.6 1.9 %collective-permute-done.8.corner = bf16[4,6144]{1,0:T(4,128)(2,1)S(1)} collective-permute-done((bf16[4,6144]{1,0:T(4,128)(2,1)S(1)}, bf16[4,6144]{1,0:T(4,128)(2,1)S(1)}, u32[]{:S(2)}, u32[]{:S(2)}) %collective-permute-start.8) | collective-permute-done | bytes 49184 | tf_op jit(solution)/shard_map/ppermute | solution.py:25
  33.4 0.8 %multiply_subtract_fusion = (f32[4,6144]{1,0:T(4,128)}, f32[4,6144]{1,0:T(4,128)}, f32[4,6144]{1,0:T(4,128)}) fusion(f32[4,6144]{1,0:T(4,128)S(1)} %copy-done, f32[4,6144]{1,0:T(4,128)S(1)} %get-tuple-element.6, f32[4,6144]{1,0:T(4,128)S(1)} %copy-done.2, f32[4,6144]{1,0:T(4,128)S(1)} %copy-done.1), kind=kLoop, calls=%fused_computation.23 | loop fusion | flops 368640 | bytes 688128 | tf_op jit(solution)/shard_map/sub | solution.py:209
  34.3 0.2 collective-permute-done.12.other_side
  34.5 1.4 %collective-permute-done.11.side = bf16[2,4,6144]{2,1,0:T(4,128)(2,1)S(1)} collective-permute-done((bf16[2,4,6144]{2,1,0:T(4,128)(2,1)S(1)}, bf16[2,4,6144]{2,1,0:T(4,128)(2,1)S(1)}, u32[]{:S(2)}, u32[]{:S(2)}) %collective-permute-start.11) | collective-permute-done | bytes 98336 | tf_op jit(solution)/shard_map/ppermute | solution.py:25
  35.8 0.8 %shard_map.85 = bf16[4,49152]{1,0:T(4,128)(2,1)} custom-call(bf16[4,6144]{1,0:T(4,128)(2,1)S(1)} %get-tuple-element.25.mine, bf16[4,6144]{1,0:T(4,128)(2,1)S(1)} %collective-permute-done.9.far, bf16[4,6144]{1,0:T(4,128)(2,1)S(1)} %collective-permute-done.8.corner, bf16[4,6144]{1,0:T(4,128)(2,1)S(1)} %collective-permute-done.10.cross, ...), custom_call_target="tpu_custom_call" | custom-call | bytes 786432 | tf_op jit(solution)/shard_map/pallas_call | solution.py:170
  (15 shorter events, 0.2 us)
Async XLA Ops:
  2.3 1.6 %collective-permute-start = (bf16[4,8,3072]{2,1,0:T(8,128)(2,1)S(1)}, bf16[4,8,3072]{2,1,0:T(8,128)(2,1)S(1)}, u32[]{:S(2)}, u32[]{:S(2)}) collective-permute-start(bf16[4,8,3072]{2,1,0:T(8,128)(2,1)S(1)} %get-tuple-element.12), channel_id=1, source_target_pairs={{0,1},{1,0},{2,3},{3,2},{4,5},{5,4},{6,7},{7,6},{8,9},{9,8},{10,11... | collective-permute-start | bytes 589832 | tf_op jit(solution)/shard_map/ppermute | solution.py:25
  2.8 5.0 %collective-permute-start.1 = (bf16[4,4,8,3072]{3,2,1,0:T(8,128)(2,1)S(1)}, bf16[4,4,8,3072]{3,2,1,0:T(8,128)(2,1)S(1)}, u32[]{:S(2)}, u32[]{:S(2)}) collective-permute-start(bf16[4,4,8,3072]{3,2,1,0:T(8,128)(2,1)S(1)} %get-tuple-element.14), channel_id=1, source_target_pairs={{0,1},{1,0},{2,3},{3,2},{4,5},{5,4},{6,7},{7,6},{8,9},{9,8},{10,11... | collective-permute-start | bytes 2359304 | tf_op jit(solution)/shard_map/ppermute | solution.py:25
  3.9 7.5 %collective-permute-start.2 = (f16[4,8,3072]{2,1,0:T(8,128)(2,1)S(1)}, f16[4,8,3072]{2,1,0:T(8,128)(2,1)S(1)}, u32[]{:S(2)}, u32[]{:S(2)}) collective-permute-start(f16[4,8,3072]{2,1,0:T(8,128)(2,1)S(1)} %fusion.1), channel_id=1, source_target_pairs={{0,6},{1,17},{2,4},{3,19},{4,2},{5,21},{6,0},{7,23},{8,14},{9,25},... | collective-permute-start | bytes 589832 | tf_op jit(solution)/shard_map/ppermute | solution.py:25
  8.0 5.7 %collective-permute-start.3 = (f16[4,8,3072]{2,1,0:T(8,128)(2,1)S(1)}, f16[4,8,3072]{2,1,0:T(8,128)(2,1)S(1)}, u32[]{:S(2)}, u32[]{:S(2)}) collective-permute-start(f16[4,8,3072]{2,1,0:T(8,128)(2,1)S(1)} %get-tuple-element.20), channel_id=1, source_target_pairs={{0,4},{1,9},{2,6},{3,11},{4,0},{5,13},{6,2},{7,15},{8,12},{9,1},{1... | collective-permute-start | bytes 589832 | tf_op jit(solution)/shard_map/ppermute | solution.py:25
  8.5 15.5 %copy-start = (f32[4,6144]{1,0:T(4,128)S(1)}, f32[4,6144]{1,0:T(4,128)}, u32[]{:S(2)}) copy-start(f32[4,6144]{1,0:T(4,128)} %param.5) | copy-start | bytes 294916
  8.6 15.5 %copy-start.1 = (f32[4,6144]{1,0:T(4,128)S(1)}, f32[4,6144]{1,0:T(4,128)}, u32[]{:S(2)}) copy-start(f32[4,6144]{1,0:T(4,128)} %param.7) | copy-start | bytes 294916
  8.6 15.5 %copy-start.2 = (f32[4,6144]{1,0:T(4,128)S(1)}, f32[4,6144]{1,0:T(4,128)}, u32[]{:S(2)}) copy-start(f32[4,6144]{1,0:T(4,128)} %param.6) | copy-start | bytes 294916
  8.6 5.7 %collective-permute-start.4 = (f16[4,8,3072]{2,1,0:T(8,128)(2,1)S(1)}, f16[4,8,3072]{2,1,0:T(8,128)(2,1)S(1)}, u32[]{:S(2)}, u32[]{:S(2)}) collective-permute-start(f16[4,8,3072]{2,1,0:T(8,128)(2,1)S(1)} %get-tuple-element.21), channel_id=1, source_target_pairs={{0,2},{1,25},{2,0},{3,27},{4,6},{5,29},{6,4},{7,31},{8,10},{9,17},... | collective-permute-start | bytes 589832 | tf_op jit(solution)/shard_map/ppermute | solution.py:25
  14.4 4.2 %collective-permute-start.5 = (f16[8,3072]{1,0:T(8,128)(2,1)S(1)}, f16[8,3072]{1,0:T(8,128)(2,1)S(1)}, u32[]{:S(2)}, u32[]{:S(2)}) collective-permute-start(f16[8,3072]{1,0:T(8,128)(2,1)S(1)} %get-tuple-element.22), channel_id=1, source_target_pairs={{0,8},{1,5},{2,10},{3,7},{4,12},{5,1},{6,14},{7,3},{8,0},{9,13},{1... | collective-permute-start | bytes 147464 | tf_op jit(solution)/shard_map/ppermute | solution.py:25
  16.0 5.9 %collective-permute-start.7 = (f16[8,3072]{1,0:T(8,128)(2,1)S(1)}, f16[8,3072]{1,0:T(8,128)(2,1)S(1)}, u32[]{:S(2)}, u32[]{:S(2)}) collective-permute-start(f16[8,3072]{1,0:T(8,128)(2,1)S(1)} %get-tuple-element.23), channel_id=1, source_target_pairs={{0,24},{1,7},{2,26},{3,5},{4,28},{5,3},{6,30},{7,1},{8,16},{9,15},... | collective-permute-start | bytes 147464 | tf_op jit(solution)/shard_map/ppermute | solution.py:25
  18.5 5.5 %collective-permute-start.6 = (f16[8,3072]{1,0:T(8,128)(2,1)S(1)}, f16[8,3072]{1,0:T(8,128)(2,1)S(1)}, u32[]{:S(2)}, u32[]{:S(2)}) collective-permute-start(f16[8,3072]{1,0:T(8,128)(2,1)S(1)} %get-tuple-element.24), channel_id=1, source_target_pairs={{0,16},{1,3},{2,18},{3,1},{4,20},{5,7},{6,22},{7,5},{8,24},{9,11},... | collective-permute-start | bytes 147464 | tf_op jit(solution)/shard_map/ppermute | solution.py:25
  24.3 12.4 %copy-start.3 = (f32[4,6144]{1,0:T(4,128)}, f32[4,6144]{1,0:T(4,128)S(1)}, u32[]{:S(2)}) copy-start(f32[4,6144]{1,0:T(4,128)S(1)} %get-tuple-element.6) | copy-start | bytes 294916
  24.3 5.4 %collective-permute-start.9 = (bf16[4,6144]{1,0:T(4,128)(2,1)S(1)}, bf16[4,6144]{1,0:T(4,128)(2,1)S(1)}, u32[]{:S(2)}, u32[]{:S(2)}) collective-permute-start(bf16[4,6144]{1,0:T(4,128)(2,1)S(1)} %get-tuple-element.25.mine), channel_id=1, source_target_pairs={{0,16},{1,17},{2,18},{3,19},{4,20},{5,21},{6,22},{7,23},{8,24},{9,... | collective-permute-start | bytes 147464 | tf_op jit(solution)/shard_map/ppermute | solution.py:25
  24.4 9.9 %collective-permute-start.10 = (bf16[4,6144]{1,0:T(4,128)(2,1)S(1)}, bf16[4,6144]{1,0:T(4,128)(2,1)S(1)}, u32[]{:S(2)}, u32[]{:S(2)}) collective-permute-start(bf16[4,6144]{1,0:T(4,128)(2,1)S(1)} %get-tuple-element.25.mine), channel_id=1, source_target_pairs={{0,28},{1,13},{2,30},{3,15},{4,24},{5,9},{6,26},{7,11},{8,20},{9,5... | collective-permute-start | bytes 147464 | tf_op jit(solution)/shard_map/ppermute | solution.py:25
  27.9 5.5 %collective-permute-start.8 = (bf16[4,6144]{1,0:T(4,128)(2,1)S(1)}, bf16[4,6144]{1,0:T(4,128)(2,1)S(1)}, u32[]{:S(2)}, u32[]{:S(2)}) collective-permute-start(bf16[4,6144]{1,0:T(4,128)(2,1)S(1)} %get-tuple-element.25.mine), channel_id=1, source_target_pairs={{0,12},{1,29},{2,14},{3,31},{4,8},{5,25},{6,10},{7,27},{8,4},{9,21... | collective-permute-start | bytes 147464 | tf_op jit(solution)/shard_map/ppermute | solution.py:25
  29.7 4.7 %collective-permute-start.12 = (bf16[2,4,6144]{2,1,0:T(4,128)(2,1)S(1)}, bf16[2,4,6144]{2,1,0:T(4,128)(2,1)S(1)}, u32[]{:S(2)}, u32[]{:S(2)}) collective-permute-start(bf16[2,4,6144]{2,1,0:T(4,128)(2,1)S(1)} %pad_maximum_fusion.1), channel_id=1, source_target_pairs={{0,4},{1,9},{2,6},{3,11},{4,0},{5,13},{6,2},{7,15},{8,12},{9,1},{1... | collective-permute-start | bytes 294920 | tf_op jit(solution)/shard_map/ppermute | solution.py:25
  31.2 4.6 %collective-permute-start.11 = (bf16[2,4,6144]{2,1,0:T(4,128)(2,1)S(1)}, bf16[2,4,6144]{2,1,0:T(4,128)(2,1)S(1)}, u32[]{:S(2)}, u32[]{:S(2)}) collective-permute-start(bf16[2,4,6144]{2,1,0:T(4,128)(2,1)S(1)} %pad_maximum_fusion.1), channel_id=1, source_target_pairs={{0,8},{1,5},{2,10},{3,7},{4,12},{5,1},{6,14},{7,3},{8,0},{9,13},{1... | collective-permute-start | bytes 294920 | tf_op jit(solution)/shard_map/ppermute | solution.py:25

commit v24 on v23

--- a/solution.py
+++ b/solution.py
@@ -135,11 +135,11 @@
     sent = {3: narrow(pair(3))}
     own, sent[3] = lax.optimization_barrier((own, sent[3]))
     sent.update({d: narrow(pair(d)) for d in (1, 2)})
-    got = [swap(sent[d], over_xy[d], over_z[d ^ (d // 2)]) for d in (3, 1, 2)]
+    got = [swap(sent[d], over_xy[d], over_z[d ^ (d // 2)]) for d in (3, 2, 1)]
     quarter = lax.optimization_barrier(pair(0) + widen(got[0]))
     quarter = quarter + widen(got[1]) + widen(got[2])
     me = jnp.where(core == 0, z, 2 * x + y)
-    got = [swap(narrow(pick(quarter, me ^ d)), over_z[d], over_xy[d]) for d in (1, 2, 3)]
+    got = [swap(narrow(pick(quarter, me ^ d)), over_z[d], over_xy[d]) for d in (3, 1, 2)]
     total = pick(quarter, me) + widen(got[0]) + widen(got[1]) + widen(got[2])
 
     return jnp.concatenate([total[: tile // 2], total[tile // 2 :]], axis=1)
@@ -149,9 +149,9 @@
     cols = mine.shape[1]
     me, core = lax.axis_index("hst"), place()[3]
     bits = lambda at_0, at_1: jnp.where(core == 0, at_0, at_1)
-    pieces = [(0, mine), (4, far), (bits(3, 7), corner), (bits(7, 3), cross)]
-    pieces += [(bits(2, 1) + 4 * i, side.at[i]) for i in (0, 1)]
-    pieces += [(bits(1, 2) + 4 * i, other_side.at[i]) for i in (0, 1)]
+    pieces = [(0, mine), (4, far), (bits(7, 3), corner), (bits(3, 7), cross)]
+    pieces += [(bits(1, 2) + 4 * i, side.at[i]) for i in (0, 1)]
+    pieces += [(bits(2, 1) + 4 * i, other_side.at[i]) for i in (0, 1)]
     copies = []
     for i, (away, block) in enumerate(pieces):
         at = pl.multiple_of((me ^ away) * cols, 128)
@@ -164,9 +164,9 @@
 def gather_blocks(mine):
     row_block, col_block = mine.shape
     far = swap(mine, Z_FAR, Z_FAR)
-    corner, cross = swap(mine, Z_NEAR + Y, Z_FAR + Z_NEAR + Y), swap(mine, Z_FAR + Z_NEAR + Y, Z_NEAR + Y)
+    corner, cross = swap(mine, Z_FAR + Z_NEAR + Y, Z_NEAR + Y), swap(mine, Z_NEAR + Y, Z_FAR + Z_NEAR + Y)
     pair = jnp.stack([mine, far])
-    side, other_side = swap(pair, Z_NEAR, Y), swap(pair, Y, Z_NEAR)
+    side, other_side = swap(pair, Y, Z_NEAR), swap(pair, Z_NEAR, Y)
     whole = pl.pallas_call(
         join_kernel,
         in_specs=[pl.BlockSpec(memory_space=pl.ANY)] * 6,

time: 36.8 us -> 35.3 us (0.959)
  waiting for transfers between devices: 14.8 us -> 13.2 us
    ppermute x13, waiting for transfers between devices: 14.8 us -> 13.2 us  [swap(): return lax.ppermute(value, ('hst', 'local'), flip_pairs(flips))]
  transfers between devices with their start and end apart: 13 -> 13, of which waited for: 10 -> 9; matrix products, arithmetic and copies ran while one was open for 3% -> 3% of each run, Pallas kernels for 1% -> 1%
where the time goes in v24:
time: 35.3 us; the launch traced here: 35.2 us
  starting transfers between devices  16.7 us (47%)
  waiting for transfers between devices  13.2 us (37%)
  Pallas kernels  2.93 us (8%)
  other arithmetic  1.56 us (4%)
  between operations  0.75 us (2%)
    ppermute x13, starting transfers between devices, swap(): return lax.ppermute(value, ('hst', 'local'), flip_pairs(flips))  16.7 us
    ppermute x13, waiting for transfers between devices, swap(): return lax.ppermute(value, ('hst', 'local'), flip_pairs(flips))  13.2 us
    pallas_call x2, Pallas kernels, call(): pl.pallas_call(kernel, in_specs=[pl.BlockSpec(memory_space=space)], out_s...  2.13 us
    sub x1, other arithmetic, adam(): new_master = master - learn_rate * (update + decay_rate * master)  0.84 us
    pallas_call x1, Pallas kernels, gather_blocks(): pl.pallas_call(join_kernel, in_specs=[pl.BlockSpec(memory_space=pl.ANY)]...  0.8 us
  transfers between devices with their start and end apart: 13, of which 9 were waited for; matrix products, arithmetic and copies ran while one was open for 3% of the time, Pallas kernels for 1%

profile of v24, /device:TPU:0, one launch (start us, length us, event | category | flops | bytes accessed | tf_op | source)
XLA Modules:
  0.0 35.2 jit_solution(2408578146985743319)
XLA Ops:
  0.6 1.6 %shard_map.83 = (bf16[4,8,3072]{2,1,0:T(8,128)(2,1)S(1)}, bf16[4,4,8,3072]{3,2,1,0:T(8,128)(2,1)S(1)}, bf16[16,49152]{1,0:T(8,128)(2,1)S(1)}) custom-call(bf16[16,49152]{1,0:T(8,128)(2,1)} %bitcast.28), custom_call_target="tpu_custom_call" | custom-call | flops 786432 | bytes 3145728 | tf_op jit(solution)/shard_map/pallas_call | solution.py:98
  2.3 0.5 %collective-permute-start = (bf16[4,8,3072]{2,1,0:T(8,128)(2,1)S(1)}, bf16[4,8,3072]{2,1,0:T(8,128)(2,1)S(1)}, u32[]{:S(2)}, u32[]{:S(2)}) collective-permute-start(bf16[4,8,3072]{2,1,0:T(8,128)(2,1)S(1)} %get-tuple-element.12), channel_id=1, source_target_pairs={{0,1},{1,0},{2,3},{3,2},{4,5},{5,4},{6,7},{7,6},{8,9},{9,8},{10,11... | collective-permute-start | bytes 589832 | tf_op jit(solution)/shard_map/ppermute | solution.py:25
  2.8 0.1 collective-permute-start.1
  2.9 0.5 %shard_map.84 = bf16[4,4,8,3072]{3,2,1,0:T(8,128)(2,1)S(1)} custom-call(bf16[16,49152]{1,0:T(8,128)(2,1)S(1)} %get-tuple-element.11.landed), custom_call_target="tpu_custom_call" | custom-call | flops 786432 | bytes 3145728 | tf_op jit(solution)/shard_map/pallas_call | solution.py:98
  3.4 0.5 %collective-permute-done = bf16[4,8,3072]{2,1,0:T(8,128)(2,1)S(1)} collective-permute-done((bf16[4,8,3072]{2,1,0:T(8,128)(2,1)S(1)}, bf16[4,8,3072]{2,1,0:T(8,128)(2,1)S(1)}, u32[]{:S(2)}, u32[]{:S(2)}) %collective-permute-start) | collective-permute-done | bytes 196640 | tf_op jit(solution)/shard_map/ppermute | solution.py:25
  3.9 0.1 fusion.1
  3.9 3.9 %collective-permute-start.2 = (f16[4,8,3072]{2,1,0:T(8,128)(2,1)S(1)}, f16[4,8,3072]{2,1,0:T(8,128)(2,1)S(1)}, u32[]{:S(2)}, u32[]{:S(2)}) collective-permute-start(f16[4,8,3072]{2,1,0:T(8,128)(2,1)S(1)} %fusion.1), channel_id=1, source_target_pairs={{0,6},{1,17},{2,4},{3,19},{4,2},{5,21},{6,0},{7,23},{8,14},{9,25},... | collective-permute-start | bytes 589832 | tf_op jit(solution)/shard_map/ppermute | solution.py:25
  7.8 0.1 fusion.2
  8.0 0.6 %collective-permute-start.3 = (f16[4,8,3072]{2,1,0:T(8,128)(2,1)S(1)}, f16[4,8,3072]{2,1,0:T(8,128)(2,1)S(1)}, u32[]{:S(2)}, u32[]{:S(2)}) collective-permute-start(f16[4,8,3072]{2,1,0:T(8,128)(2,1)S(1)} %get-tuple-element.20), channel_id=1, source_target_pairs={{0,2},{1,25},{2,0},{3,27},{4,6},{5,29},{6,4},{7,31},{8,10},{9,17},... | collective-permute-start | bytes 589832 | tf_op jit(solution)/shard_map/ppermute | solution.py:25
  8.6 1.0 %collective-permute-start.4 = (f16[4,8,3072]{2,1,0:T(8,128)(2,1)S(1)}, f16[4,8,3072]{2,1,0:T(8,128)(2,1)S(1)}, u32[]{:S(2)}, u32[]{:S(2)}) collective-permute-start(f16[4,8,3072]{2,1,0:T(8,128)(2,1)S(1)} %get-tuple-element.21), channel_id=1, source_target_pairs={{0,4},{1,9},{2,6},{3,11},{4,0},{5,13},{6,2},{7,15},{8,12},{9,1},{1... | collective-permute-start | bytes 589832 | tf_op jit(solution)/shard_map/ppermute | solution.py:25
  9.6 1.9 %collective-permute-done.2 = f16[4,8,3072]{2,1,0:T(8,128)(2,1)S(1)} collective-permute-done((f16[4,8,3072]{2,1,0:T(8,128)(2,1)S(1)}, f16[4,8,3072]{2,1,0:T(8,128)(2,1)S(1)}, u32[]{:S(2)}, u32[]{:S(2)}) %collective-permute-start.2) | collective-permute-done | bytes 196640 | tf_op jit(solution)/shard_map/ppermute | solution.py:25
  11.5 0.1 bitcast_add_fusion
  11.6 2.6 %collective-permute-done.3 = f16[4,8,3072]{2,1,0:T(8,128)(2,1)S(1)} collective-permute-done((f16[4,8,3072]{2,1,0:T(8,128)(2,1)S(1)}, f16[4,8,3072]{2,1,0:T(8,128)(2,1)S(1)}, u32[]{:S(2)}, u32[]{:S(2)}) %collective-permute-start.3) | collective-permute-done | bytes 196640 | tf_op jit(solution)/shard_map/ppermute | solution.py:25
  14.1 0.1 collective-permute-done.4
  14.3 0.1 multiply_add_fusion
  14.4 3.7 %collective-permute-start.5 = (f16[8,3072]{1,0:T(8,128)(2,1)S(1)}, f16[8,3072]{1,0:T(8,128)(2,1)S(1)}, u32[]{:S(2)}, u32[]{:S(2)}) collective-permute-start(f16[8,3072]{1,0:T(8,128)(2,1)S(1)} %get-tuple-element.22), channel_id=1, source_target_pairs={{0,24},{1,7},{2,26},{3,5},{4,28},{5,3},{6,30},{7,1},{8,16},{9,15},... | collective-permute-start | bytes 147464 | tf_op jit(solution)/shard_map/ppermute | solution.py:25
  18.1 0.8 %collective-permute-start.6 = (f16[8,3072]{1,0:T(8,128)(2,1)S(1)}, f16[8,3072]{1,0:T(8,128)(2,1)S(1)}, u32[]{:S(2)}, u32[]{:S(2)}) collective-permute-start(f16[8,3072]{1,0:T(8,128)(2,1)S(1)} %get-tuple-element.24), channel_id=1, source_target_pairs={{0,8},{1,5},{2,10},{3,7},{4,12},{5,1},{6,14},{7,3},{8,0},{9,13},{1... | collective-permute-start | bytes 147464 | tf_op jit(solution)/shard_map/ppermute | solution.py:25
  18.9 1.5 %collective-permute-done.5 = f16[8,3072]{1,0:T(8,128)(2,1)S(1)} collective-permute-done((f16[8,3072]{1,0:T(8,128)(2,1)S(1)}, f16[8,3072]{1,0:T(8,128)(2,1)S(1)}, u32[]{:S(2)}, u32[]{:S(2)}) %collective-permute-start.5) | collective-permute-done | bytes 49184 | tf_op jit(solution)/shard_map/ppermute | solution.py:25
  20.4 2.7 %collective-permute-done.7 = f16[8,3072]{1,0:T(8,128)(2,1)S(1)} collective-permute-done((f16[8,3072]{1,0:T(8,128)(2,1)S(1)}, f16[8,3072]{1,0:T(8,128)(2,1)S(1)}, u32[]{:S(2)}, u32[]{:S(2)}) %collective-permute-start.7) | collective-permute-done | bytes 49184 | tf_op jit(solution)/shard_map/ppermute | solution.py:25
  23.2 0.2 subtract_convert_fusion
  23.3 0.0 copy-start.3
  23.4 2.1 %collective-permute-start.9 = (bf16[4,6144]{1,0:T(4,128)(2,1)S(1)}, bf16[4,6144]{1,0:T(4,128)(2,1)S(1)}, u32[]{:S(2)}, u32[]{:S(2)}) collective-permute-start(bf16[4,6144]{1,0:T(4,128)(2,1)S(1)} %get-tuple-element.25.mine), channel_id=1, source_target_pairs={{0,16},{1,17},{2,18},{3,19},{4,20},{5,21},{6,22},{7,23},{8,24},{9,... | collective-permute-start | bytes 147464 | tf_op jit(solution)/shard_map/ppermute | solution.py:25
  25.5 0.7 %collective-permute-start.10 = (bf16[4,6144]{1,0:T(4,128)(2,1)S(1)}, bf16[4,6144]{1,0:T(4,128)(2,1)S(1)}, u32[]{:S(2)}, u32[]{:S(2)}) collective-permute-start(bf16[4,6144]{1,0:T(4,128)(2,1)S(1)} %get-tuple-element.25.mine), channel_id=1, source_target_pairs={{0,12},{1,29},{2,14},{3,31},{4,8},{5,25},{6,10},{7,27},{8,4},{9,21... | collective-permute-start | bytes 147464 | tf_op jit(solution)/shard_map/ppermute | solution.py:25
  26.2 2.5 %collective-permute-start.8 = (bf16[4,6144]{1,0:T(4,128)(2,1)S(1)}, bf16[4,6144]{1,0:T(4,128)(2,1)S(1)}, u32[]{:S(2)}, u32[]{:S(2)}) collective-permute-start(bf16[4,6144]{1,0:T(4,128)(2,1)S(1)} %get-tuple-element.25.mine), channel_id=1, source_target_pairs={{0,28},{1,13},{2,30},{3,15},{4,24},{5,9},{6,26},{7,11},{8,20},{9,5... | collective-permute-start | bytes 147464 | tf_op jit(solution)/shard_map/ppermute | solution.py:25
  28.7 0.6 %collective-permute-done.9.far = bf16[4,6144]{1,0:T(4,128)(2,1)S(1)} collective-permute-done((bf16[4,6144]{1,0:T(4,128)(2,1)S(1)}, bf16[4,6144]{1,0:T(4,128)(2,1)S(1)}, u32[]{:S(2)}, u32[]{:S(2)}) %collective-permute-start.9) | collective-permute-done | bytes 49184 | tf_op jit(solution)/shard_map/ppermute | solution.py:25
  29.3 0.1 pad_maximum_fusion.1
  29.4 0.1 collective-permute-start.12
  29.5 0.8 %collective-permute-start.11 = (bf16[2,4,6144]{2,1,0:T(4,128)(2,1)S(1)}, bf16[2,4,6144]{2,1,0:T(4,128)(2,1)S(1)}, u32[]{:S(2)}, u32[]{:S(2)}) collective-permute-start(bf16[2,4,6144]{2,1,0:T(4,128)(2,1)S(1)} %pad_maximum_fusion.1), channel_id=1, source_target_pairs={{0,4},{1,9},{2,6},{3,11},{4,0},{5,13},{6,2},{7,15},{8,12},{9,1},{1... | collective-permute-start | bytes 294920 | tf_op jit(solution)/shard_map/ppermute | solution.py:25
  30.2 2.9 %collective-permute-done.8.corner = bf16[4,6144]{1,0:T(4,128)(2,1)S(1)} collective-permute-done((bf16[4,6144]{1,0:T(4,128)(2,1)S(1)}, bf16[4,6144]{1,0:T(4,128)(2,1)S(1)}, u32[]{:S(2)}, u32[]{:S(2)}) %collective-permute-start.8) | collective-permute-done | bytes 49184 | tf_op jit(solution)/shard_map/ppermute | solution.py:25
  33.1 0.8 %multiply_subtract_fusion = (f32[4,6144]{1,0:T(4,128)}, f32[4,6144]{1,0:T(4,128)}, f32[4,6144]{1,0:T(4,128)}) fusion(f32[4,6144]{1,0:T(4,128)S(1)} %copy-done, f32[4,6144]{1,0:T(4,128)S(1)} %get-tuple-element.6, f32[4,6144]{1,0:T(4,128)S(1)} %copy-done.2, f32[4,6144]{1,0:T(4,128)S(1)} %copy-done.1), kind=kLoop, calls=%fused_computation.23 | loop fusion | flops 368640 | bytes 688128 | tf_op jit(solution)/shard_map/sub | solution.py:209
  34.0 0.4 %collective-permute-done.12.other_side = bf16[2,4,6144]{2,1,0:T(4,128)(2,1)S(1)} collective-permute-done((bf16[2,4,6144]{2,1,0:T(4,128)(2,1)S(1)}, bf16[2,4,6144]{2,1,0:T(4,128)(2,1)S(1)}, u32[]{:S(2)}, u32[]{:S(2)}) %collective-permute-start.12) | collective-permute-done | bytes 98336 | tf_op jit(solution)/shard_map/ppermute | solution.py:25
  34.4 0.8 %shard_map.85 = bf16[4,49152]{1,0:T(4,128)(2,1)} custom-call(bf16[4,6144]{1,0:T(4,128)(2,1)S(1)} %get-tuple-element.25.mine, bf16[4,6144]{1,0:T(4,128)(2,1)S(1)} %collective-permute-done.9.far, bf16[4,6144]{1,0:T(4,128)(2,1)S(1)} %collective-permute-done.8.corner, bf16[4,6144]{1,0:T(4,128)(2,1)S(1)} %collective-permute-done.10.cross, ...), custom_call_target="tpu_custom_call" | custom-call | bytes 786432 | tf_op jit(solution)/shard_map/pallas_call | solution.py:170
  (15 shorter events, 0.1 us)
Async XLA Ops:
  2.3 1.6 %collective-permute-start = (bf16[4,8,3072]{2,1,0:T(8,128)(2,1)S(1)}, bf16[4,8,3072]{2,1,0:T(8,128)(2,1)S(1)}, u32[]{:S(2)}, u32[]{:S(2)}) collective-permute-start(bf16[4,8,3072]{2,1,0:T(8,128)(2,1)S(1)} %get-tuple-element.12), channel_id=1, source_target_pairs={{0,1},{1,0},{2,3},{3,2},{4,5},{5,4},{6,7},{7,6},{8,9},{9,8},{10,11... | collective-permute-start | bytes 589832 | tf_op jit(solution)/shard_map/ppermute | solution.py:25
  2.8 5.0 %collective-permute-start.1 = (bf16[4,4,8,3072]{3,2,1,0:T(8,128)(2,1)S(1)}, bf16[4,4,8,3072]{3,2,1,0:T(8,128)(2,1)S(1)}, u32[]{:S(2)}, u32[]{:S(2)}) collective-permute-start(bf16[4,4,8,3072]{3,2,1,0:T(8,128)(2,1)S(1)} %get-tuple-element.14), channel_id=1, source_target_pairs={{0,1},{1,0},{2,3},{3,2},{4,5},{5,4},{6,7},{7,6},{8,9},{9,8},{10,11... | collective-permute-start | bytes 2359304 | tf_op jit(solution)/shard_map/ppermute | solution.py:25
  3.9 7.5 %collective-permute-start.2 = (f16[4,8,3072]{2,1,0:T(8,128)(2,1)S(1)}, f16[4,8,3072]{2,1,0:T(8,128)(2,1)S(1)}, u32[]{:S(2)}, u32[]{:S(2)}) collective-permute-start(f16[4,8,3072]{2,1,0:T(8,128)(2,1)S(1)} %fusion.1), channel_id=1, source_target_pairs={{0,6},{1,17},{2,4},{3,19},{4,2},{5,21},{6,0},{7,23},{8,14},{9,25},... | collective-permute-start | bytes 589832 | tf_op jit(solution)/shard_map/ppermute | solution.py:25
  8.0 6.1 %collective-permute-start.3 = (f16[4,8,3072]{2,1,0:T(8,128)(2,1)S(1)}, f16[4,8,3072]{2,1,0:T(8,128)(2,1)S(1)}, u32[]{:S(2)}, u32[]{:S(2)}) collective-permute-start(f16[4,8,3072]{2,1,0:T(8,128)(2,1)S(1)} %get-tuple-element.20), channel_id=1, source_target_pairs={{0,2},{1,25},{2,0},{3,27},{4,6},{5,29},{6,4},{7,31},{8,10},{9,17},... | collective-permute-start | bytes 589832 | tf_op jit(solution)/shard_map/ppermute | solution.py:25
  8.6 14.5 %copy-start = (f32[4,6144]{1,0:T(4,128)S(1)}, f32[4,6144]{1,0:T(4,128)}, u32[]{:S(2)}) copy-start(f32[4,6144]{1,0:T(4,128)} %param.5) | copy-start | bytes 294916
  8.6 14.6 %copy-start.1 = (f32[4,6144]{1,0:T(4,128)S(1)}, f32[4,6144]{1,0:T(4,128)}, u32[]{:S(2)}) copy-start(f32[4,6144]{1,0:T(4,128)} %param.7) | copy-start | bytes 294916
  8.6 14.6 %copy-start.2 = (f32[4,6144]{1,0:T(4,128)S(1)}, f32[4,6144]{1,0:T(4,128)}, u32[]{:S(2)}) copy-start(f32[4,6144]{1,0:T(4,128)} %param.6) | copy-start | bytes 294916
  8.6 5.7 %collective-permute-start.4 = (f16[4,8,3072]{2,1,0:T(8,128)(2,1)S(1)}, f16[4,8,3072]{2,1,0:T(8,128)(2,1)S(1)}, u32[]{:S(2)}, u32[]{:S(2)}) collective-permute-start(f16[4,8,3072]{2,1,0:T(8,128)(2,1)S(1)} %get-tuple-element.21), channel_id=1, source_target_pairs={{0,4},{1,9},{2,6},{3,11},{4,0},{5,13},{6,2},{7,15},{8,12},{9,1},{1... | collective-permute-start | bytes 589832 | tf_op jit(solution)/shard_map/ppermute | solution.py:25
  14.4 6.0 %collective-permute-start.5 = (f16[8,3072]{1,0:T(8,128)(2,1)S(1)}, f16[8,3072]{1,0:T(8,128)(2,1)S(1)}, u32[]{:S(2)}, u32[]{:S(2)}) collective-permute-start(f16[8,3072]{1,0:T(8,128)(2,1)S(1)} %get-tuple-element.22), channel_id=1, source_target_pairs={{0,24},{1,7},{2,26},{3,5},{4,28},{5,3},{6,30},{7,1},{8,16},{9,15},... | collective-permute-start | bytes 147464 | tf_op jit(solution)/shard_map/ppermute | solution.py:25
  18.1 5.0 %collective-permute-start.7 = (f16[8,3072]{1,0:T(8,128)(2,1)S(1)}, f16[8,3072]{1,0:T(8,128)(2,1)S(1)}, u32[]{:S(2)}, u32[]{:S(2)}) collective-permute-start(f16[8,3072]{1,0:T(8,128)(2,1)S(1)} %get-tuple-element.23), channel_id=1, source_target_pairs={{0,16},{1,3},{2,18},{3,1},{4,20},{5,7},{6,22},{7,5},{8,24},{9,11},... | collective-permute-start | bytes 147464 | tf_op jit(solution)/shard_map/ppermute | solution.py:25
  18.1 5.0 %collective-permute-start.6 = (f16[8,3072]{1,0:T(8,128)(2,1)S(1)}, f16[8,3072]{1,0:T(8,128)(2,1)S(1)}, u32[]{:S(2)}, u32[]{:S(2)}) collective-permute-start(f16[8,3072]{1,0:T(8,128)(2,1)S(1)} %get-tuple-element.24), channel_id=1, source_target_pairs={{0,8},{1,5},{2,10},{3,7},{4,12},{5,1},{6,14},{7,3},{8,0},{9,13},{1... | collective-permute-start | bytes 147464 | tf_op jit(solution)/shard_map/ppermute | solution.py:25
  23.3 11.8 %copy-start.3 = (f32[4,6144]{1,0:T(4,128)}, f32[4,6144]{1,0:T(4,128)S(1)}, u32[]{:S(2)}) copy-start(f32[4,6144]{1,0:T(4,128)S(1)} %get-tuple-element.6) | copy-start | bytes 294916
  23.4 6.0 %collective-permute-start.9 = (bf16[4,6144]{1,0:T(4,128)(2,1)S(1)}, bf16[4,6144]{1,0:T(4,128)(2,1)S(1)}, u32[]{:S(2)}, u32[]{:S(2)}) collective-permute-start(bf16[4,6144]{1,0:T(4,128)(2,1)S(1)} %get-tuple-element.25.mine), channel_id=1, source_target_pairs={{0,16},{1,17},{2,18},{3,19},{4,20},{5,21},{6,22},{7,23},{8,24},{9,... | collective-permute-start | bytes 147464 | tf_op jit(solution)/shard_map/ppermute | solution.py:25
  25.5 8.5 %collective-permute-start.10 = (bf16[4,6144]{1,0:T(4,128)(2,1)S(1)}, bf16[4,6144]{1,0:T(4,128)(2,1)S(1)}, u32[]{:S(2)}, u32[]{:S(2)}) collective-permute-start(bf16[4,6144]{1,0:T(4,128)(2,1)S(1)} %get-tuple-element.25.mine), channel_id=1, source_target_pairs={{0,12},{1,29},{2,14},{3,31},{4,8},{5,25},{6,10},{7,27},{8,4},{9,21... | collective-permute-start | bytes 147464 | tf_op jit(solution)/shard_map/ppermute | solution.py:25
  26.2 6.9 %collective-permute-start.8 = (bf16[4,6144]{1,0:T(4,128)(2,1)S(1)}, bf16[4,6144]{1,0:T(4,128)(2,1)S(1)}, u32[]{:S(2)}, u32[]{:S(2)}) collective-permute-start(bf16[4,6144]{1,0:T(4,128)(2,1)S(1)} %get-tuple-element.25.mine), channel_id=1, source_target_pairs={{0,28},{1,13},{2,30},{3,15},{4,24},{5,9},{6,26},{7,11},{8,20},{9,5... | collective-permute-start | bytes 147464 | tf_op jit(solution)/shard_map/ppermute | solution.py:25
  29.4 5.0 %collective-permute-start.12 = (bf16[2,4,6144]{2,1,0:T(4,128)(2,1)S(1)}, bf16[2,4,6144]{2,1,0:T(4,128)(2,1)S(1)}, u32[]{:S(2)}, u32[]{:S(2)}) collective-permute-start(bf16[2,4,6144]{2,1,0:T(4,128)(2,1)S(1)} %pad_maximum_fusion.1), channel_id=1, source_target_pairs={{0,8},{1,5},{2,10},{3,7},{4,12},{5,1},{6,14},{7,3},{8,0},{9,13},{1... | collective-permute-start | bytes 294920 | tf_op jit(solution)/shard_map/ppermute | solution.py:25
  29.5 4.9 %collective-permute-start.11 = (bf16[2,4,6144]{2,1,0:T(4,128)(2,1)S(1)}, bf16[2,4,6144]{2,1,0:T(4,128)(2,1)S(1)}, u32[]{:S(2)}, u32[]{:S(2)}) collective-permute-start(bf16[2,4,6144]{2,1,0:T(4,128)(2,1)S(1)} %pad_maximum_fusion.1), channel_id=1, source_target_pairs={{0,4},{1,9},{2,6},{3,11},{4,0},{5,13},{6,2},{7,15},{8,12},{9,1},{1... | collective-permute-start | bytes 294920 | tf_op jit(solution)/shard_map/ppermute | solution.py:25

commit v25 on v24

--- a/solution.py
+++ b/solution.py
@@ -65,7 +65,7 @@
 def theirs_kernel(whole, first, every, landed, arrived):
     half = first.shape[2]
     core = place()[3]
-    parts = [pl.ds(2 * i * half, 2 * half) for i in range(8)]
+    parts = [pl.ds(4 * i * half, 4 * half) for i in range(4)]
     copies = [
         pltpu.make_async_copy(whole.at[:, part], landed.at[:, part], arrived.at[i])
         for i, part in enumerate(parts)
@@ -77,8 +77,9 @@
         every[step, member] = rows
 
     for i in range(8):
-        copies[i].wait()
-        rows_of(1 - core, landed[:, parts[i]], i, store)
+        if i % 2 == 0:
+            copies[i // 2].wait()
+        rows_of(1 - core, landed[:, pl.ds(2 * i * half, 2 * half)], i, store)
     first[...] = every[3]
 
 
@@ -114,7 +115,7 @@
         gradient,
         pltpu.HBM,
         [shape, (4, *shape), gradient.shape],
-        [pltpu.SemaphoreType.DMA((8,))],
+        [pltpu.SemaphoreType.DMA((4,))],
     )
     first, others, landed = lax.optimization_barrier((first, others, landed))
     (own,) = call(own_kernel, landed, pltpu.VMEM, [(4, *shape)])

time: 35.3 us -> 35.3 us (level)
  no operation moved by 1% of the time
where the time goes in v25:
time: 35.3 us; the launch traced here: 35.1 us
  starting transfers between devices  16.7 us (47%)
  waiting for transfers between devices  13.2 us (37%)
  Pallas kernels  2.86 us (8%)
  other arithmetic  1.56 us (4%)
  between operations  0.75 us (2%)
    ppermute x13, starting transfers between devices, swap(): return lax.ppermute(value, ('hst', 'local'), flip_pairs(flips))  16.7 us
    ppermute x13, waiting for transfers between devices, swap(): return lax.ppermute(value, ('hst', 'local'), flip_pairs(flips))  13.2 us
    pallas_call x2, Pallas kernels, call(): pl.pallas_call(kernel, in_specs=[pl.BlockSpec(memory_space=space)], out_s...  2.06 us
    sub x1, other arithmetic, adam(): new_master = master - learn_rate * (update + decay_rate * master)  0.84 us
    pallas_call x1, Pallas kernels, gather_blocks(): pl.pallas_call(join_kernel, in_specs=[pl.BlockSpec(memory_space=pl.ANY)]...  0.8 us
  transfers between devices with their start and end apart: 13, of which 9 were waited for; matrix products, arithmetic and copies ran while one was open for 3% of the time, Pallas kernels for 1%

profile of v25, /device:TPU:0, one launch (start us, length us, event | category | flops | bytes accessed | tf_op | source)
XLA Modules:
  0.0 35.1 jit_solution(13489311987699769297)
XLA Ops:
  0.6 1.6 %shard_map.83 = (bf16[4,8,3072]{2,1,0:T(8,128)(2,1)S(1)}, bf16[4,4,8,3072]{3,2,1,0:T(8,128)(2,1)S(1)}, bf16[16,49152]{1,0:T(8,128)(2,1)S(1)}) custom-call(bf16[16,49152]{1,0:T(8,128)(2,1)} %bitcast.28), custom_call_target="tpu_custom_call" | custom-call | flops 786432 | bytes 3145728 | tf_op jit(solution)/shard_map/pallas_call | solution.py:99
  2.2 0.5 %collective-permute-start = (bf16[4,8,3072]{2,1,0:T(8,128)(2,1)S(1)}, bf16[4,8,3072]{2,1,0:T(8,128)(2,1)S(1)}, u32[]{:S(2)}, u32[]{:S(2)}) collective-permute-start(bf16[4,8,3072]{2,1,0:T(8,128)(2,1)S(1)} %get-tuple-element.12), channel_id=1, source_target_pairs={{0,1},{1,0},{2,3},{3,2},{4,5},{5,4},{6,7},{7,6},{8,9},{9,8},{10,11... | collective-permute-start | bytes 589832 | tf_op jit(solution)/shard_map/ppermute | solution.py:25
  2.7 0.1 collective-permute-start.1
  2.8 0.5 %shard_map.84 = bf16[4,4,8,3072]{3,2,1,0:T(8,128)(2,1)S(1)} custom-call(bf16[16,49152]{1,0:T(8,128)(2,1)S(1)} %get-tuple-element.11.landed), custom_call_target="tpu_custom_call" | custom-call | flops 786432 | bytes 3145728 | tf_op jit(solution)/shard_map/pallas_call | solution.py:99
  3.3 0.5 %collective-permute-done = bf16[4,8,3072]{2,1,0:T(8,128)(2,1)S(1)} collective-permute-done((bf16[4,8,3072]{2,1,0:T(8,128)(2,1)S(1)}, bf16[4,8,3072]{2,1,0:T(8,128)(2,1)S(1)}, u32[]{:S(2)}, u32[]{:S(2)}) %collective-permute-start) | collective-permute-done | bytes 196640 | tf_op jit(solution)/shard_map/ppermute | solution.py:25
  3.8 0.1 fusion.1
  3.9 3.9 %collective-permute-start.2 = (f16[4,8,3072]{2,1,0:T(8,128)(2,1)S(1)}, f16[4,8,3072]{2,1,0:T(8,128)(2,1)S(1)}, u32[]{:S(2)}, u32[]{:S(2)}) collective-permute-start(f16[4,8,3072]{2,1,0:T(8,128)(2,1)S(1)} %fusion.1), channel_id=1, source_target_pairs={{0,6},{1,17},{2,4},{3,19},{4,2},{5,21},{6,0},{7,23},{8,14},{9,25},... | collective-permute-start | bytes 589832 | tf_op jit(solution)/shard_map/ppermute | solution.py:25
  7.8 0.1 fusion.2
  7.9 0.6 %collective-permute-start.3 = (f16[4,8,3072]{2,1,0:T(8,128)(2,1)S(1)}, f16[4,8,3072]{2,1,0:T(8,128)(2,1)S(1)}, u32[]{:S(2)}, u32[]{:S(2)}) collective-permute-start(f16[4,8,3072]{2,1,0:T(8,128)(2,1)S(1)} %get-tuple-element.20), channel_id=1, source_target_pairs={{0,2},{1,25},{2,0},{3,27},{4,6},{5,29},{6,4},{7,31},{8,10},{9,17},... | collective-permute-start | bytes 589832 | tf_op jit(solution)/shard_map/ppermute | solution.py:25
  8.5 1.0 %collective-permute-start.4 = (f16[4,8,3072]{2,1,0:T(8,128)(2,1)S(1)}, f16[4,8,3072]{2,1,0:T(8,128)(2,1)S(1)}, u32[]{:S(2)}, u32[]{:S(2)}) collective-permute-start(f16[4,8,3072]{2,1,0:T(8,128)(2,1)S(1)} %get-tuple-element.21), channel_id=1, source_target_pairs={{0,4},{1,9},{2,6},{3,11},{4,0},{5,13},{6,2},{7,15},{8,12},{9,1},{1... | collective-permute-start | bytes 589832 | tf_op jit(solution)/shard_map/ppermute | solution.py:25
  9.5 1.9 %collective-permute-done.2 = f16[4,8,3072]{2,1,0:T(8,128)(2,1)S(1)} collective-permute-done((f16[4,8,3072]{2,1,0:T(8,128)(2,1)S(1)}, f16[4,8,3072]{2,1,0:T(8,128)(2,1)S(1)}, u32[]{:S(2)}, u32[]{:S(2)}) %collective-permute-start.2) | collective-permute-done | bytes 196640 | tf_op jit(solution)/shard_map/ppermute | solution.py:25
  11.4 0.1 bitcast_add_fusion
  11.5 2.6 %collective-permute-done.3 = f16[4,8,3072]{2,1,0:T(8,128)(2,1)S(1)} collective-permute-done((f16[4,8,3072]{2,1,0:T(8,128)(2,1)S(1)}, f16[4,8,3072]{2,1,0:T(8,128)(2,1)S(1)}, u32[]{:S(2)}, u32[]{:S(2)}) %collective-permute-start.3) | collective-permute-done | bytes 196640 | tf_op jit(solution)/shard_map/ppermute | solution.py:25
  14.0 0.1 collective-permute-done.4
  14.2 0.1 multiply_add_fusion
  14.3 3.7 %collective-permute-start.5 = (f16[8,3072]{1,0:T(8,128)(2,1)S(1)}, f16[8,3072]{1,0:T(8,128)(2,1)S(1)}, u32[]{:S(2)}, u32[]{:S(2)}) collective-permute-start(f16[8,3072]{1,0:T(8,128)(2,1)S(1)} %get-tuple-element.22), channel_id=1, source_target_pairs={{0,24},{1,7},{2,26},{3,5},{4,28},{5,3},{6,30},{7,1},{8,16},{9,15},... | collective-permute-start | bytes 147464 | tf_op jit(solution)/shard_map/ppermute | solution.py:25
  18.0 0.8 %collective-permute-start.6 = (f16[8,3072]{1,0:T(8,128)(2,1)S(1)}, f16[8,3072]{1,0:T(8,128)(2,1)S(1)}, u32[]{:S(2)}, u32[]{:S(2)}) collective-permute-start(f16[8,3072]{1,0:T(8,128)(2,1)S(1)} %get-tuple-element.24), channel_id=1, source_target_pairs={{0,8},{1,5},{2,10},{3,7},{4,12},{5,1},{6,14},{7,3},{8,0},{9,13},{1... | collective-permute-start | bytes 147464 | tf_op jit(solution)/shard_map/ppermute | solution.py:25
  18.8 1.5 %collective-permute-done.5 = f16[8,3072]{1,0:T(8,128)(2,1)S(1)} collective-permute-done((f16[8,3072]{1,0:T(8,128)(2,1)S(1)}, f16[8,3072]{1,0:T(8,128)(2,1)S(1)}, u32[]{:S(2)}, u32[]{:S(2)}) %collective-permute-start.5) | collective-permute-done | bytes 49184 | tf_op jit(solution)/shard_map/ppermute | solution.py:25
  20.3 2.7 %collective-permute-done.7 = f16[8,3072]{1,0:T(8,128)(2,1)S(1)} collective-permute-done((f16[8,3072]{1,0:T(8,128)(2,1)S(1)}, f16[8,3072]{1,0:T(8,128)(2,1)S(1)}, u32[]{:S(2)}, u32[]{:S(2)}) %collective-permute-start.7) | collective-permute-done | bytes 49184 | tf_op jit(solution)/shard_map/ppermute | solution.py:25
  23.1 0.2 subtract_convert_fusion
  23.3 0.0 copy-start.3
  23.3 2.1 %collective-permute-start.9 = (bf16[4,6144]{1,0:T(4,128)(2,1)S(1)}, bf16[4,6144]{1,0:T(4,128)(2,1)S(1)}, u32[]{:S(2)}, u32[]{:S(2)}) collective-permute-start(bf16[4,6144]{1,0:T(4,128)(2,1)S(1)} %get-tuple-element.25.mine), channel_id=1, source_target_pairs={{0,16},{1,17},{2,18},{3,19},{4,20},{5,21},{6,22},{7,23},{8,24},{9,... | collective-permute-start | bytes 147464 | tf_op jit(solution)/shard_map/ppermute | solution.py:25
  25.4 0.7 %collective-permute-start.10 = (bf16[4,6144]{1,0:T(4,128)(2,1)S(1)}, bf16[4,6144]{1,0:T(4,128)(2,1)S(1)}, u32[]{:S(2)}, u32[]{:S(2)}) collective-permute-start(bf16[4,6144]{1,0:T(4,128)(2,1)S(1)} %get-tuple-element.25.mine), channel_id=1, source_target_pairs={{0,12},{1,29},{2,14},{3,31},{4,8},{5,25},{6,10},{7,27},{8,4},{9,21... | collective-permute-start | bytes 147464 | tf_op jit(solution)/shard_map/ppermute | solution.py:25
  26.1 2.5 %collective-permute-start.8 = (bf16[4,6144]{1,0:T(4,128)(2,1)S(1)}, bf16[4,6144]{1,0:T(4,128)(2,1)S(1)}, u32[]{:S(2)}, u32[]{:S(2)}) collective-permute-start(bf16[4,6144]{1,0:T(4,128)(2,1)S(1)} %get-tuple-element.25.mine), channel_id=1, source_target_pairs={{0,28},{1,13},{2,30},{3,15},{4,24},{5,9},{6,26},{7,11},{8,20},{9,5... | collective-permute-start | bytes 147464 | tf_op jit(solution)/shard_map/ppermute | solution.py:25
  28.6 0.6 %collective-permute-done.9.far = bf16[4,6144]{1,0:T(4,128)(2,1)S(1)} collective-permute-done((bf16[4,6144]{1,0:T(4,128)(2,1)S(1)}, bf16[4,6144]{1,0:T(4,128)(2,1)S(1)}, u32[]{:S(2)}, u32[]{:S(2)}) %collective-permute-start.9) | collective-permute-done | bytes 49184 | tf_op jit(solution)/shard_map/ppermute | solution.py:25
  29.3 0.1 pad_maximum_fusion.1
  29.3 0.1 collective-permute-start.12
  29.4 0.8 %collective-permute-start.11 = (bf16[2,4,6144]{2,1,0:T(4,128)(2,1)S(1)}, bf16[2,4,6144]{2,1,0:T(4,128)(2,1)S(1)}, u32[]{:S(2)}, u32[]{:S(2)}) collective-permute-start(bf16[2,4,6144]{2,1,0:T(4,128)(2,1)S(1)} %pad_maximum_fusion.1), channel_id=1, source_target_pairs={{0,4},{1,9},{2,6},{3,11},{4,0},{5,13},{6,2},{7,15},{8,12},{9,1},{1... | collective-permute-start | bytes 294920 | tf_op jit(solution)/shard_map/ppermute | solution.py:25
  30.2 2.9 %collective-permute-done.8.corner = bf16[4,6144]{1,0:T(4,128)(2,1)S(1)} collective-permute-done((bf16[4,6144]{1,0:T(4,128)(2,1)S(1)}, bf16[4,6144]{1,0:T(4,128)(2,1)S(1)}, u32[]{:S(2)}, u32[]{:S(2)}) %collective-permute-start.8) | collective-permute-done | bytes 49184 | tf_op jit(solution)/shard_map/ppermute | solution.py:25
  33.1 0.8 %multiply_subtract_fusion = (f32[4,6144]{1,0:T(4,128)}, f32[4,6144]{1,0:T(4,128)}, f32[4,6144]{1,0:T(4,128)}) fusion(f32[4,6144]{1,0:T(4,128)S(1)} %copy-done, f32[4,6144]{1,0:T(4,128)S(1)} %get-tuple-element.6, f32[4,6144]{1,0:T(4,128)S(1)} %copy-done.2, f32[4,6144]{1,0:T(4,128)S(1)} %copy-done.1), kind=kLoop, calls=%fused_computation.23 | loop fusion | flops 368640 | bytes 688128 | tf_op jit(solution)/shard_map/sub | solution.py:210
  33.9 0.4 %collective-permute-done.12.other_side = bf16[2,4,6144]{2,1,0:T(4,128)(2,1)S(1)} collective-permute-done((bf16[2,4,6144]{2,1,0:T(4,128)(2,1)S(1)}, bf16[2,4,6144]{2,1,0:T(4,128)(2,1)S(1)}, u32[]{:S(2)}, u32[]{:S(2)}) %collective-permute-start.12) | collective-permute-done | bytes 98336 | tf_op jit(solution)/shard_map/ppermute | solution.py:25
  34.3 0.8 %shard_map.85 = bf16[4,49152]{1,0:T(4,128)(2,1)} custom-call(bf16[4,6144]{1,0:T(4,128)(2,1)S(1)} %get-tuple-element.25.mine, bf16[4,6144]{1,0:T(4,128)(2,1)S(1)} %collective-permute-done.9.far, bf16[4,6144]{1,0:T(4,128)(2,1)S(1)} %collective-permute-done.8.corner, bf16[4,6144]{1,0:T(4,128)(2,1)S(1)} %collective-permute-done.10.cross, ...), custom_call_target="tpu_custom_call" | custom-call | bytes 786432 | tf_op jit(solution)/shard_map/pallas_call | solution.py:171
  (15 shorter events, 0.1 us)
Async XLA Ops:
  2.2 1.6 %collective-permute-start = (bf16[4,8,3072]{2,1,0:T(8,128)(2,1)S(1)}, bf16[4,8,3072]{2,1,0:T(8,128)(2,1)S(1)}, u32[]{:S(2)}, u32[]{:S(2)}) collective-permute-start(bf16[4,8,3072]{2,1,0:T(8,128)(2,1)S(1)} %get-tuple-element.12), channel_id=1, source_target_pairs={{0,1},{1,0},{2,3},{3,2},{4,5},{5,4},{6,7},{7,6},{8,9},{9,8},{10,11... | collective-permute-start | bytes 589832 | tf_op jit(solution)/shard_map/ppermute | solution.py:25
  2.7 5.0 %collective-permute-start.1 = (bf16[4,4,8,3072]{3,2,1,0:T(8,128)(2,1)S(1)}, bf16[4,4,8,3072]{3,2,1,0:T(8,128)(2,1)S(1)}, u32[]{:S(2)}, u32[]{:S(2)}) collective-permute-start(bf16[4,4,8,3072]{3,2,1,0:T(8,128)(2,1)S(1)} %get-tuple-element.14), channel_id=1, source_target_pairs={{0,1},{1,0},{2,3},{3,2},{4,5},{5,4},{6,7},{7,6},{8,9},{9,8},{10,11... | collective-permute-start | bytes 2359304 | tf_op jit(solution)/shard_map/ppermute | solution.py:25
  3.9 7.5 %collective-permute-start.2 = (f16[4,8,3072]{2,1,0:T(8,128)(2,1)S(1)}, f16[4,8,3072]{2,1,0:T(8,128)(2,1)S(1)}, u32[]{:S(2)}, u32[]{:S(2)}) collective-permute-start(f16[4,8,3072]{2,1,0:T(8,128)(2,1)S(1)} %fusion.1), channel_id=1, source_target_pairs={{0,6},{1,17},{2,4},{3,19},{4,2},{5,21},{6,0},{7,23},{8,14},{9,25},... | collective-permute-start | bytes 589832 | tf_op jit(solution)/shard_map/ppermute | solution.py:25
  7.9 6.1 %collective-permute-start.3 = (f16[4,8,3072]{2,1,0:T(8,128)(2,1)S(1)}, f16[4,8,3072]{2,1,0:T(8,128)(2,1)S(1)}, u32[]{:S(2)}, u32[]{:S(2)}) collective-permute-start(f16[4,8,3072]{2,1,0:T(8,128)(2,1)S(1)} %get-tuple-element.20), channel_id=1, source_target_pairs={{0,2},{1,25},{2,0},{3,27},{4,6},{5,29},{6,4},{7,31},{8,10},{9,17},... | collective-permute-start | bytes 589832 | tf_op jit(solution)/shard_map/ppermute | solution.py:25
  8.5 14.5 %copy-start = (f32[4,6144]{1,0:T(4,128)S(1)}, f32[4,6144]{1,0:T(4,128)}, u32[]{:S(2)}) copy-start(f32[4,6144]{1,0:T(4,128)} %param.5) | copy-start | bytes 294916
  8.5 14.6 %copy-start.1 = (f32[4,6144]{1,0:T(4,128)S(1)}, f32[4,6144]{1,0:T(4,128)}, u32[]{:S(2)}) copy-start(f32[4,6144]{1,0:T(4,128)} %param.7) | copy-start | bytes 294916
  8.5 14.6 %copy-start.2 = (f32[4,6144]{1,0:T(4,128)S(1)}, f32[4,6144]{1,0:T(4,128)}, u32[]{:S(2)}) copy-start(f32[4,6144]{1,0:T(4,128)} %param.6) | copy-start | bytes 294916
  8.5 5.7 %collective-permute-start.4 = (f16[4,8,3072]{2,1,0:T(8,128)(2,1)S(1)}, f16[4,8,3072]{2,1,0:T(8,128)(2,1)S(1)}, u32[]{:S(2)}, u32[]{:S(2)}) collective-permute-start(f16[4,8,3072]{2,1,0:T(8,128)(2,1)S(1)} %get-tuple-element.21), channel_id=1, source_target_pairs={{0,4},{1,9},{2,6},{3,11},{4,0},{5,13},{6,2},{7,15},{8,12},{9,1},{1... | collective-permute-start | bytes 589832 | tf_op jit(solution)/shard_map/ppermute | solution.py:25
  14.3 6.0 %collective-permute-start.5 = (f16[8,3072]{1,0:T(8,128)(2,1)S(1)}, f16[8,3072]{1,0:T(8,128)(2,1)S(1)}, u32[]{:S(2)}, u32[]{:S(2)}) collective-permute-start(f16[8,3072]{1,0:T(8,128)(2,1)S(1)} %get-tuple-element.22), channel_id=1, source_target_pairs={{0,24},{1,7},{2,26},{3,5},{4,28},{5,3},{6,30},{7,1},{8,16},{9,15},... | collective-permute-start | bytes 147464 | tf_op jit(solution)/shard_map/ppermute | solution.py:25
  18.0 5.0 %collective-permute-start.7 = (f16[8,3072]{1,0:T(8,128)(2,1)S(1)}, f16[8,3072]{1,0:T(8,128)(2,1)S(1)}, u32[]{:S(2)}, u32[]{:S(2)}) collective-permute-start(f16[8,3072]{1,0:T(8,128)(2,1)S(1)} %get-tuple-element.23), channel_id=1, source_target_pairs={{0,16},{1,3},{2,18},{3,1},{4,20},{5,7},{6,22},{7,5},{8,24},{9,11},... | collective-permute-start | bytes 147464 | tf_op jit(solution)/shard_map/ppermute | solution.py:25
  18.0 5.0 %collective-permute-start.6 = (f16[8,3072]{1,0:T(8,128)(2,1)S(1)}, f16[8,3072]{1,0:T(8,128)(2,1)S(1)}, u32[]{:S(2)}, u32[]{:S(2)}) collective-permute-start(f16[8,3072]{1,0:T(8,128)(2,1)S(1)} %get-tuple-element.24), channel_id=1, source_target_pairs={{0,8},{1,5},{2,10},{3,7},{4,12},{5,1},{6,14},{7,3},{8,0},{9,13},{1... | collective-permute-start | bytes 147464 | tf_op jit(solution)/shard_map/ppermute | solution.py:25
  23.3 11.8 %copy-start.3 = (f32[4,6144]{1,0:T(4,128)}, f32[4,6144]{1,0:T(4,128)S(1)}, u32[]{:S(2)}) copy-start(f32[4,6144]{1,0:T(4,128)S(1)} %get-tuple-element.6) | copy-start | bytes 294916
  23.3 6.0 %collective-permute-start.9 = (bf16[4,6144]{1,0:T(4,128)(2,1)S(1)}, bf16[4,6144]{1,0:T(4,128)(2,1)S(1)}, u32[]{:S(2)}, u32[]{:S(2)}) collective-permute-start(bf16[4,6144]{1,0:T(4,128)(2,1)S(1)} %get-tuple-element.25.mine), channel_id=1, source_target_pairs={{0,16},{1,17},{2,18},{3,19},{4,20},{5,21},{6,22},{7,23},{8,24},{9,... | collective-permute-start | bytes 147464 | tf_op jit(solution)/shard_map/ppermute | solution.py:25
  25.4 8.5 %collective-permute-start.10 = (bf16[4,6144]{1,0:T(4,128)(2,1)S(1)}, bf16[4,6144]{1,0:T(4,128)(2,1)S(1)}, u32[]{:S(2)}, u32[]{:S(2)}) collective-permute-start(bf16[4,6144]{1,0:T(4,128)(2,1)S(1)} %get-tuple-element.25.mine), channel_id=1, source_target_pairs={{0,12},{1,29},{2,14},{3,31},{4,8},{5,25},{6,10},{7,27},{8,4},{9,21... | collective-permute-start | bytes 147464 | tf_op jit(solution)/shard_map/ppermute | solution.py:25
  26.1 6.9 %collective-permute-start.8 = (bf16[4,6144]{1,0:T(4,128)(2,1)S(1)}, bf16[4,6144]{1,0:T(4,128)(2,1)S(1)}, u32[]{:S(2)}, u32[]{:S(2)}) collective-permute-start(bf16[4,6144]{1,0:T(4,128)(2,1)S(1)} %get-tuple-element.25.mine), channel_id=1, source_target_pairs={{0,28},{1,13},{2,30},{3,15},{4,24},{5,9},{6,26},{7,11},{8,20},{9,5... | collective-permute-start | bytes 147464 | tf_op jit(solution)/shard_map/ppermute | solution.py:25
  29.3 5.0 %collective-permute-start.12 = (bf16[2,4,6144]{2,1,0:T(4,128)(2,1)S(1)}, bf16[2,4,6144]{2,1,0:T(4,128)(2,1)S(1)}, u32[]{:S(2)}, u32[]{:S(2)}) collective-permute-start(bf16[2,4,6144]{2,1,0:T(4,128)(2,1)S(1)} %pad_maximum_fusion.1), channel_id=1, source_target_pairs={{0,8},{1,5},{2,10},{3,7},{4,12},{5,1},{6,14},{7,3},{8,0},{9,13},{1... | collective-permute-start | bytes 294920 | tf_op jit(solution)/shard_map/ppermute | solution.py:25
  29.4 4.9 %collective-permute-start.11 = (bf16[2,4,6144]{2,1,0:T(4,128)(2,1)S(1)}, bf16[2,4,6144]{2,1,0:T(4,128)(2,1)S(1)}, u32[]{:S(2)}, u32[]{:S(2)}) collective-permute-start(bf16[2,4,6144]{2,1,0:T(4,128)(2,1)S(1)} %pad_maximum_fusion.1), channel_id=1, source_target_pairs={{0,4},{1,9},{2,6},{3,11},{4,0},{5,13},{6,2},{7,15},{8,12},{9,1},{1... | collective-permute-start | bytes 294920 | tf_op jit(solution)/shard_map/ppermute | solution.py:25
